TPU v7x, 32 devices: a whole 2x2x4 slice. The times are simulated.
32 devices in a mesh: groups: 2 (over y), ep: 4 (over z), kv: 2 (over x), tp: 2 (over core).
Axes of the slice: x: 2, y: 2, z: 4, core: 2. Of those that a mesh axis runs over, the one named last changes fastest.
Arguments:
- queries: bfloat16 [512, 4096], P(('groups', 'ep'), ('kv', 'tp')), parts along dimension 0, may hold values from -16 to 16
- new_kv: bfloat16 [512, 4, 256], P(('groups', 'ep'), 'kv'), parts along dimension 0, may hold values from -16 to 16
- cache_pool: bfloat16 [512, 16, 4, 256], P(('groups', 'ep'), None, 'kv'), parts along dimension 0, may hold values from -5 to 5
- hit_pages: int32 [128], P('groups'), parts along dimension 0, may hold values from 0 to 255, as said below
- span_lengths: int32 [8], P('groups'), parts along dimension 0, may hold values from 1 to 64, as said below
- out_weight: bfloat16 [4096, 4096], P(('kv', 'tp')), may hold values from -0.09375 to 0.09375
- hidden_in: bfloat16 [512, 4096], P(('groups', 'ep')), parts along dimension 0, may hold values from -1.2 to 1.2
- norm_gain: float32 [4096], replicated, may hold values from 0.1 to 1.9
- expert_ids: int32 [512, 4], P(('groups', 'ep')), parts along dimension 0, may hold values from 0 to 3, all different within a row; in each aligned block of 64 rows (0 to 63, 64 to 127, ...) at most 64 rows name the same one
- gate_weights: float32 [512, 4], P(('groups', 'ep')), parts along dimension 0, may hold values from 0.02 to 0.4
- gate_up: bfloat16 [4, 2, 1536, 4096], P('ep', None, ('kv', 'tp')), may hold values from -0.09375 to 0.09375
- down_weight: bfloat16 [4, 1536, 4096], P('ep', ('kv', 'tp')), may hold values from -0.15625 to 0.15625
- new_owner: int32 [32], P('groups'), parts along dimension 0, may hold values from 0 to 3, as said below
Outputs:
- layer_out: bfloat16 [512, 4096], P(('groups', 'ep', 'kv', 'tp')), parts along dimension 0
- decode_pages: bfloat16 [64, 16, 4, 256], P(('groups', 'ep'), None, 'kv'), parts along dimension 0
There are 2 independent parts, one for each index of `groups`. A program takes and returns all parts, laid end to end along the dimension named above; an argument that names none is the same for every part. Nothing has to cross between parts.
Inputs may be any that keep to these rules, and one draw needn't show every extreme that they name: `hit_pages`: distinct pool pages; rows p * 64 to (p+1) * 64 - 1 of the pool stand on index p of ep; at most 16 of the pages fall on one index, and some index holds exactly 16. `span_lengths`: the lengths sum to 192; some span holds exactly 64 tokens. `new_owner`: at most 8 pages go to one owner, and some owner receives exactly 8. `expert_ids`: each row names 4 different experts; in the rows of one index of ep no expert is named more than 64 times.
All inputs are finite; a program needn't handle non-finite values.
Results may differ from a plain program's by a relative error of at most 0.03.
Values may be sent and summed in bfloat16 or wider, within the bound.
No kernel may reach another device: no remote copies, remote signals or barrier semaphores. Data moves between devices by JAX's collectives and lax.ppermute only.
A program may use at most 128 MiB of HBM per device.

v0:
```python
import math

import jax
import jax.numpy as jnp
from jax import lax
from jax.sharding import PartitionSpec as P

HD = 128
HQ = 32
KVH = 4
HOLD_MOST = 16


MASKED = -1e30
EPSILON = 1e-06


def expert_rows(arrived, gate_up, down_weight):
    flat_rows = arrived.reshape(-1, arrived.shape[-1])
    contract = (((1,), (1,)), ((), ()))
    gate_part = lax.dot_general(
        flat_rows, gate_up[0, 0], contract, preferred_element_type=jnp.float32
    )
    up_part = lax.dot_general(
        flat_rows, gate_up[0, 1], contract, preferred_element_type=jnp.float32
    )
    hidden = (jax.nn.silu(gate_part) * up_part).astype(jnp.bfloat16)
    down_part = jnp.dot(hidden, down_weight[0], preferred_element_type=jnp.float32).astype(
        jnp.bfloat16
    )
    return down_part.reshape(arrived.shape)


def normalize(resid_wide, norm_gain):
    return (
        resid_wide
        * lax.rsqrt(jnp.mean(resid_wide * resid_wide, axis=1, keepdims=True) + EPSILON)
        * norm_gain
    ).astype(jnp.bfloat16)


def local(
    queries,
    new_kv,
    cache_pool,
    hit_pages,
    span_lengths,
    out_weight,
    hidden_in,
    norm_gain,
    expert_ids,
    gate_weights,
    gate_up,
    down_weight,
    new_owner,
):
    tokens = queries.shape[0]
    model_width = hidden_in.shape[1]
    ep_count = lax.axis_size("ep")
    blocks = lax.axis_size("kv") * lax.axis_size("tp")
    ep_index = lax.axis_index("ep")
    kv_index = lax.axis_index("kv")
    block_index = kv_index * lax.axis_size("tp") + lax.axis_index("tp")
    keyval_local = new_kv.shape[1]
    heads_local = queries.shape[1] // HD
    keyval_pick = block_index * heads_local // (HQ // KVH) - kv_index * keyval_local
    starts = jnp.cumsum(span_lengths) - span_lengths
    slots_here = jnp.arange(tokens, dtype=jnp.int32)
    all_positions = (starts[:, None] + slots_here[None, :]).reshape(-1)
    all_filled = (slots_here[None, :] < span_lengths[:, None]).reshape(-1)
    own_positions = starts[ep_index] + slots_here
    own_filled = slots_here < span_lengths[ep_index]
    pool_pages = cache_pool.shape[0]
    page_size = cache_pool.shape[1]
    owned_hits = hit_pages // pool_pages == ep_index
    hit_rank = jnp.cumsum(owned_hits.astype(jnp.int32)) - 1
    hit_pick = owned_hits[None, :] & (
        hit_rank[None, :] == jnp.arange(HOLD_MOST, dtype=jnp.int32)[:, None]
    )
    local_page = jnp.sum(jnp.where(hit_pick, hit_pages[None, :] - ep_index * pool_pages, 0), axis=1)
    present = jnp.any(hit_pick, axis=1).astype(jnp.bfloat16)
    chosen = jnp.take(cache_pool, local_page, axis=0)
    suffix = lax.all_gather(new_kv, "ep", axis=0, tiled=True)
    pulled, pulled_flags = (
        lax.all_gather(chosen, "ep", axis=0, tiled=True),
        lax.all_gather(present, "ep", axis=0, tiled=True),
    )
    prefix_keys = lax.dynamic_index_in_dim(pulled, keyval_pick, 2, keepdims=False).reshape(
        -1, 2 * HD
    )
    suffix_keys = lax.dynamic_index_in_dim(suffix, keyval_pick, 1, keepdims=False)
    all_keys = jnp.concatenate([prefix_keys, suffix_keys], axis=0)
    prefix_open = jnp.repeat(pulled_flags > 0, page_size)
    causal = all_filled[None, :] & (all_positions[None, :] <= own_positions[:, None])
    allowed = jnp.concatenate(
        [jnp.broadcast_to(prefix_open[None, :], (tokens, prefix_open.shape[0])), causal], axis=1
    )
    grouped = queries.reshape(tokens, heads_local, HD)
    scores = jnp.einsum(
        "thd,kd->htk", grouped, all_keys[:, :HD], preferred_element_type=jnp.float32
    ) * (1.0 / math.sqrt(HD))
    scores = jnp.where(allowed[None], scores, MASKED)
    attention_weights = jax.nn.softmax(scores, axis=-1).astype(jnp.bfloat16)
    attended = jnp.einsum(
        "htk,kd->thd", attention_weights, all_keys[:, HD:], preferred_element_type=jnp.float32
    )
    attended = attended.astype(jnp.bfloat16).reshape(tokens, heads_local * HD)
    projected = jnp.dot(attended, out_weight, preferred_element_type=jnp.float32)
    row_count = tokens // blocks
    top_count = expert_ids.shape[1]
    rows_filled = lax.dynamic_slice_in_dim(own_filled, block_index * row_count, row_count, 0)
    heads_out = lax.psum(projected.astype(jnp.bfloat16), ("kv", "tp")).astype(jnp.float32)
    residual = (hidden_in.astype(jnp.float32) + heads_out).astype(jnp.bfloat16)
    resid_wide = residual.astype(jnp.float32)
    normed = normalize(resid_wide, norm_gain)
    capacity = min(tokens, (tokens * top_count // ep_count + tokens // 8) // 8 * 8)
    flat_ids = expert_ids.reshape(-1)
    onehot = flat_ids[:, None] == jnp.arange(ep_count, dtype=jnp.int32)[None, :]
    running = jnp.cumsum(onehot.astype(jnp.int32), axis=0) - 1
    slot_index = jnp.sum(jnp.where(onehot, running, 0), axis=1)
    target = flat_ids * capacity + slot_index
    source = (
        jnp.zeros((ep_count * capacity,), jnp.int32)
        .at[target]
        .set(jnp.arange(tokens * top_count, dtype=jnp.int32) // top_count)
    )
    outgoing = jnp.take(normed, source, axis=0).reshape(ep_count, capacity, model_width)
    returned = lax.all_to_all(
        expert_rows(
            lax.all_to_all(outgoing, "ep", split_axis=0, concat_axis=0, tiled=True),
            gate_up,
            down_weight,
        ),
        "ep",
        split_axis=0,
        concat_axis=0,
        tiled=True,
    )
    first_slot = 0
    values = returned.reshape(ep_count * capacity, model_width)
    inside = (slot_index >= first_slot) & (slot_index < first_slot + capacity)
    spot_index = flat_ids * capacity + jnp.clip(slot_index - first_slot, 0, capacity - 1)
    picked = jnp.take(values, spot_index, axis=0).astype(jnp.float32)
    weight = jnp.where(inside, gate_weights.reshape(-1), 0.0)
    mixture_part = jnp.sum(
        (weight[:, None] * picked).reshape(tokens, top_count, model_width), axis=1
    )
    mixture = lax.psum_scatter(
        mixture_part.astype(jnp.bfloat16), ("kv", "tp"), scatter_dimension=0, tiled=True
    ).astype(jnp.float32)
    own_rows = lax.dynamic_slice_in_dim(resid_wide, block_index * row_count, row_count, 0)
    layer_out = jnp.where(rows_filled[:, None], own_rows + mixture, 0.0).astype(jnp.bfloat16)
    own_most = 2 * (tokens // page_size)
    page_count = new_owner.shape[0]
    kept_pages = jnp.where(all_filled[:, None, None], suffix, jnp.zeros_like(suffix)).reshape(
        page_count, page_size, keyval_local, 2 * HD
    )
    owned_pages = new_owner == ep_index
    owner_rank = jnp.cumsum(owned_pages.astype(jnp.int32)) - 1
    choose = owned_pages[None, :] & (
        owner_rank[None, :] == jnp.arange(own_most, dtype=jnp.int32)[:, None]
    )
    page_index = jnp.sum(
        jnp.where(choose, jnp.arange(page_count, dtype=jnp.int32)[None, :], 0), axis=1
    )
    has_page = jnp.any(choose, axis=1)
    decode_pages = jnp.where(
        has_page[:, None, None, None],
        jnp.take(kept_pages, page_index, axis=0),
        jnp.zeros((), jnp.bfloat16),
    )
    return (layer_out, decode_pages)


def solution(mesh):
    placed = (
        P(("groups", "ep"), ("kv", "tp")),
        P(("groups", "ep"), "kv", None),
        P(("groups", "ep"), None, "kv", None),
        P("groups"),
        P("groups"),
        P(("kv", "tp"), None),
        P(("groups", "ep"), None),
        P(),
        P(("groups", "ep"), None),
        P(("groups", "ep"), None),
        P("ep", None, ("kv", "tp"), None),
        P("ep", ("kv", "tp"), None),
        P("groups"),
    )
    return jax.shard_map(
        local,
        mesh=mesh,
        in_specs=placed,
        out_specs=(P(("groups", "ep", "kv", "tp"), None), P(("groups", "ep"), None, "kv", None)),
        check_vma=False,
    )
```

profile of v0, /device:TPU:0, one launch (start us, length us, event | category | flops | bytes accessed | tf_op | source)
XLA Modules:
  0.0 275.5 jit_solution(10178715060644506464)
XLA Ops:
  9.3 2.3 gather_fusion
  20.5 13.6 %all-reduce = bf16[64]{0:T(256)(128)(2,1)S(1)} all-reduce(bf16[64]{0:T(256)(128)(2,1)S(1)} %dynamic-update-slice), channel_id=1, replica_groups=mesh['groups'=2,'ep'=4,'kv'=2,'tp'=2] {'ep'}, use_global_device_ids=true, to_apply=%add | all-reduce | flops 64 | bytes 256
  36.0 1.4 scatter_custom_fusion
  39.0 14.9 %all_gather.10 = bf16[256,2,256]{2,0,1:T(8,128)(2,1)S(1)} all-gather(bf16[64,2,256]{2,0,1:T(8,128)(2,1)S(1)} %copy.80), channel_id=1, replica_groups=mesh['groups'=2,'ep'=4,'kv'=2,'tp'=2] {'ep'}, dimensions={0}, use_global_device_ids=true | all-gather | bytes 327680 | tf_op jit(solution)/shard_map/all_gather | solution.py:83
  56.0 1.9 constant_dynamic-slice_fusion
  57.9 3.5 %fusion.70 = (f32[8,64]{1,0:T(8,128)S(1)}, f32[8,64,1280]{2,1,0:T(8,128)}) fusion(pred[64,1280]{1,0:T(8,128)(4,1)} %pad_add_fusion, bf16[256,256]{1,0:T(8,128)(2,1)S(1)} %dynamic-slice_bitcast_fusion, bf16[1024,256]{1,0:T(8,128)(2,1)} %bitcast.113, bf16[64,1024]{1,0:T(8,128)(2,1)} %param.13), kind=kOutput, calls=%fused_computation.126 | convolution fusion | flops 171050240 | bytes 3491840 | tf_op jit(solution)/shard_map/sub | solution.py:103
  61.4 2.4 fusion.20
  63.8 5.8 %convolution_convert_fusion.1 = bf16[64,4096]{1,0:T(8,128)(2,1)} fusion(bf16[1024,4096]{1,0:T(8,128)(2,1)} %param.18, bf16[8,8,8,128]{3,2,1,0:T(8,128)(2,1)S(1)} %fusion.20), kind=kOutput, calls=%fused_computation.7 | convolution fusion | flops 537133056 | bytes 9043968 | tf_op jit(solution)/shard_map/dot_general | solution.py:108
  69.7 31.5 %all-reduce.3.cloned.1.call-done = bf16[64,4096]{1,0:T(8,128)(2,1)} async-done(((bf16[64,4096]{1,0:T(8,128)(2,1)}), bf16[64,4096]{1,0:T(8,128)(2,1)}) %all-reduce.3.cloned.1.call-update) | async-done | bytes 524304 | tf_op jit(solution)/shard_map/psum | solution.py:112
  101.2 2.4 fusion.23
  103.7 2.2 multiply_convert_fusion
  105.9 6.3 %gather_fusion.1 = bf16[256,4096]{1,0:T(8,128)(2,1)} fusion(bf16[64,4096]{1,0:T(8,128)(2,1)} %multiply_convert_fusion, s32[1024]{0:T(1024)S(1)} %pad_clamp_fusion.2), kind=kCustom, calls=%fused_computation.1 | custom fusion | bytes 4195328 | tf_op jit(solution)/shard_map/jit(_take)/gather | solution.py:127
  112.2 1.8 broadcast_select_fusion
  114.1 51.7 %all_to_all.10 = bf16[4,64,4096]{2,1,0:T(8,128)(2,1)S(1)} all-to-all(bf16[4,64,4096]{2,1,0:T(8,128)(2,1)S(1)} %broadcast_select_fusion), channel_id=1, replica_groups=mesh['groups'=2,'ep'=4,'kv'=2,'tp'=2] {'ep'}, dimensions={0} | all-to-all | bytes 4194304 | tf_op jit(solution)/shard_map/all_to_all | solution.py:130
  167.0 4.0 %fusion.8 = f32[256,384]{1,0:T(8,128)} fusion(bf16[256,4096]{1,0:T(8,128)(2,1)S(1)} %bitcast.110, bf16[1,2,384,4096]{3,2,1,0:T(8,128)(2,1)} %param.23), kind=kOutput, calls=%fused_computation.17 | convolution fusion | flops 805306368 | bytes 5636096 | tf_op jit(solution)/shard_map/dot_general | solution.py:21
  171.0 6.4 %convolution_convert_fusion = bf16[256,4096]{1,0:T(8,128)(2,1)} fusion(bf16[1,384,4096]{2,1,0:T(8,128)(2,1)S(1)} %copy-done, bf16[256,4096]{1,0:T(8,128)(2,1)} %bitcast.111, bf16[1,2,384,4096]{3,2,1,0:T(8,128)(2,1)} %param.23, f32[256,384]{1,0:T(8,128)} %fusion.8), kind=kOutput, calls=%fused_computation.6 | convolution fusion | flops 1612251136 | bytes 10878976 | tf_op jit(solution)/shard_map/dot_general | solution.py:28
  177.4 4.6 %all-to-all-start.1 = ((bf16[4,64,4096]{2,1,0:T(8,128)(2,1)}), bf16[4,64,4096]{2,1,0:T(8,128)(2,1)}, u32[]{:S(2)}, u32[]{:S(2)}) async-start(bf16[4,64,4096]{2,1,0:T(8,128)(2,1)} %bitcast.109), calls=%async_computation.1 | async-start | bytes 4194304 | tf_op jit(solution)/shard_map/all_to_all | solution.py:128
  183.7 45.7 %all-to-all-done.1 = bf16[4,64,4096]{2,1,0:T(8,128)(2,1)} async-done(((bf16[4,64,4096]{2,1,0:T(8,128)(2,1)}), bf16[4,64,4096]{2,1,0:T(8,128)(2,1)}, u32[]{:S(2)}, u32[]{:S(2)}) %all-to-all-start.1) | async-done | bytes 2097184 | tf_op jit(solution)/shard_map/all_to_all | solution.py:128
  229.4 7.1 %gather_fusion.2 = bf16[256,4096]{1,0:T(8,128)(2,1)} fusion(bf16[256,4096]{1,0:T(8,128)(2,1)} %bitcast.24, s32[1024]{0:T(1024)S(1)} %pad_clamp_fusion.1), kind=kCustom, calls=%fused_computation.2 | custom fusion | bytes 4195328 | tf_op jit(solution)/shard_map/jit(_take)/gather | solution.py:143
  236.5 4.1 %gather.24 = bf16[64,4,4096]{2,1,0:T(4,128)(2,1)} reshape(bf16[256,4096]{1,0:T(8,128)(2,1)} %gather_fusion.2) | data formatting | bytes 4194304 | tf_op jit(solution)/shard_map/jit(_take)/gather | solution.py:143
  240.6 6.7 %multiply_reduce_fusion = bf16[64,4096]{1,0:T(8,128)(2,1)} fusion(bf16[64,4,4096]{2,1,0:T(4,128)(2,1)} %gather.24, f32[64,4]{1,0:T(8,128)S(1)} %broadcast_select_fusion.3, pred[64,4]{1,0:T(8,128)(4,1)S(1)} %copy.89), kind=kLoop, calls=%fused_computation.8 | loop fusion | flops 3932160 | bytes 2622720 | tf_op jit(solution)/shard_map/reduce_sum | solution.py:145
  248.7 1.5 gather_fusion.3
  252.0 15.3 %reduce-scatter.2.cloned.1.call-done = bf16[16,4096]{1,0:T(8,128)(2,1)} async-done(((bf16[64,4096]{1,0:T(8,128)(2,1)}), bf16[16,4096]{1,0:T(8,128)(2,1)}) %reduce-scatter.2.cloned.1.call-update) | async-done | bytes 131088 | tf_op jit(solution)/shard_map/reduce_scatter | solution.py:148
  267.2 1.8 select_convert_fusion
  (110 shorter events, 21.8 us)
Async XLA Ops:
  7.2 163.8 %copy-start = (bf16[1,384,4096]{2,1,0:T(8,128)(2,1)S(1)}, bf16[1,384,4096]{2,1,0:T(8,128)(2,1)}, u32[]{:S(2)}) copy-start(bf16[1,384,4096]{2,1,0:T(8,128)(2,1)} %param.24) | copy-start | bytes 9437188
  7.2 48.8 %all-gather.2.cloned.1.call-start = ((), (), s32[]{:S(2)}) async-start(), calls=%async_computation.3 | async-start | bytes 1310720 | tf_op jit(solution)/shard_map/all_gather | solution.py:85
  12.7 88.5 %all-reduce.3.cloned.1.call-start = ((), (), s32[]{:S(2)}) async-start(), calls=%async_computation.4 | async-start | bytes 1048576 | tf_op jit(solution)/shard_map/psum | solution.py:112
  37.4 1.5 copy-start.7
  63.8 5.9 %copy-start.8 = (s32[256]{0:T(256)S(1)}, s32[256]{0:T(256)}, u32[]{:S(2)}) copy-start(s32[256]{0:T(256)} %copy-done.7) | copy-start | bytes 3076
  69.6 34.1 %copy-start.4 = (f32[4096]{0:T(1024)S(1)}, f32[4096]{0:T(1024)}, u32[]{:S(2)}) copy-start(f32[4096]{0:T(1024)} %param.20) | copy-start | bytes 49156
  105.9 6.3 %copy-start.9 = (pred[4,64]{1,0:T(4,128)(4,1)S(1)}, pred[4,64]{1,0:T(4,128)(4,1)}, u32[]{:S(2)}) copy-start(pred[4,64]{1,0:T(4,128)(4,1)} %broadcast_in_dim.169) | copy-start | bytes 772
  165.7 1.3 copy-start.1
  177.4 4.7 %copy-start.10 = (s32[16]{0:T(128)S(1)}, s32[16]{0:T(128)}, u32[]{:S(2)}) copy-start(s32[16]{0:T(128)} %param.25) | copy-start | bytes 196
  177.4 5.1 %copy-start.3 = (s32[64,4]{0,1:T(4,128)S(1)}, s32[64,4]{0,1:T(4,128)}, u32[]{:S(2)}) copy-start(s32[64,4]{0,1:T(4,128)} %param.21) | copy-start | bytes 3076
  177.4 5.3 %copy-start.6 = (f32[64,4]{0,1:T(4,128)S(1)}, f32[64,4]{0,1:T(4,128)}, u32[]{:S(2)}) copy-start(f32[64,4]{0,1:T(4,128)} %param.22) | copy-start | bytes 3076
  177.4 5.5 %copy-start.5 = (pred[256]{0:T(512)(128)(4,1)S(1)}, pred[256]{0:T(512)(128)(4,1)}, u32[]{:S(2)}) copy-start(pred[256]{0:T(512)(128)(4,1)} %lt.128) | copy-start | bytes 772
  177.4 52.0 %all-to-all-start.1 = ((bf16[4,64,4096]{2,1,0:T(8,128)(2,1)}), bf16[4,64,4096]{2,1,0:T(8,128)(2,1)}, u32[]{:S(2)}, u32[]{:S(2)}) async-start(bf16[4,64,4096]{2,1,0:T(8,128)(2,1)} %bitcast.109), calls=%async_computation.1 | async-start | bytes 4194304 | tf_op jit(solution)/shard_map/all_to_all | solution.py:128
  182.0 85.2 %reduce-scatter.2.cloned.1.call-start = ((), (), s32[]{:S(2)}) async-start(), calls=%async_computation.5 | async-start | bytes 655360 | tf_op jit(solution)/shard_map/reduce_scatter | solution.py:148
  240.6 6.8 %copy-start.11 = (s32[4]{0:T(128)S(1)}, s32[4]{0:T(128)}, u32[]{:S(2)}) copy-start(s32[4]{0:T(128)} %param.17) | copy-start | bytes 52
  240.6 7.4 %copy-start.2 = (bf16[256,2,256]{2,0,1:T(8,128)(2,1)S(1)}, bf16[256,2,256]{2,0,1:T(8,128)(2,1)}, u32[]{:S(2)}) copy-start(bf16[256,2,256]{2,0,1:T(8,128)(2,1)} %broadcast_select_fusion.2) | copy-start | bytes 786436
Sparse Core Ops, SparseCore 0:
  12.8 33.1 all-gather.1
  69.8 31.3 all-reduce.2
  247.4 19.7 reduce-scatter.1
where the time goes:
time: 276 us
  waiting for transfers between devices  92.5 us (34%)
  blocking collectives  80.2 us (29%)
  local copies, waits for them, and re-layouts  35.5 us (13%)
  other arithmetic  25.7 us (9%)
  matrix products  22.1 us (8%)
  between operations  14.8 us (5%)
  starting transfers between devices  4.71 us (2%)
    all_to_all x1, blocking collectives, local(): lax.all_to_all(outgoing, 'ep', split_axis=0, concat_axis=0, tiled=True)  51.7 us
    all_to_all x1, waiting for transfers between devices, local(): lax.all_to_all(expert_rows(lax.all_to_all(outgoing, 'ep', split_axis=0, c...  45.7 us
    psum x1, waiting for transfers between devices, local(): lax.psum(projected.astype(jnp.bfloat16), ('kv', 'tp')).astype(jnp.float32)  31.5 us
    reduce_scatter x1, waiting for transfers between devices, local(): lax.psum_scatter(mixture_part.astype(jnp.bfloat16), ('kv', 'tp'), scatter...  15.3 us
    all_gather x1, blocking collectives, local(): suffix = lax.all_gather(new_kv, 'ep', axis=0, tiled=True)  14.9 us
    unnamed x1, blocking collectives  13.6 us
    gather x2, local copies, waits for them, and re-layouts, local(): picked = jnp.take(values, spot_index, axis=0).astype(jnp.float32)  11.2 us
    reduce_sum x1, other arithmetic, local(): jnp.sum((weight[:, None] * picked).reshape(tokens, top_count, model_width...  6.66 us
  transfers between devices with their start and end apart: 4, of which 3 were waited for; matrix products, arithmetic and copies ran while one was open for 7% of the time, Pallas kernels for 0%

commit v1 on v0

v1 whole, which is shorter than its diff:
```python
import math

import jax
import jax.numpy as jnp
from jax import lax
from jax.sharding import PartitionSpec as P

HD = 128
HQ = 32
KVH = 4
HOLD_MOST = 16
WEIGHT_ROWS = 16

MASKED = -1e30
EPSILON = 1e-06


def three_parts(wide):
    high = lax.reduce_precision(wide, 8, 7)
    rest = wide - high
    middle = lax.reduce_precision(rest, 8, 7)
    low = rest - middle
    return [part.astype(jnp.bfloat16) for part in (high, middle, low)]


def local(
    queries,
    new_kv,
    cache_pool,
    hit_pages,
    span_lengths,
    out_weight,
    hidden_in,
    norm_gain,
    expert_ids,
    gate_weights,
    gate_up,
    down_weight,
    new_owner,
):
    tokens = queries.shape[0]
    model_width = hidden_in.shape[1]
    ep_count = lax.axis_size("ep")
    tp_count = lax.axis_size("tp")
    blocks = lax.axis_size("kv") * tp_count
    ep_index = lax.axis_index("ep")
    kv_index = lax.axis_index("kv")
    tp_index = lax.axis_index("tp")
    block_index = kv_index * tp_count + tp_index
    keyval_local = new_kv.shape[1]
    heads_local = queries.shape[1] // HD
    keyval_pick = block_index * heads_local // (HQ // KVH) - kv_index * keyval_local
    row_count = tokens // blocks
    pool_pages = cache_pool.shape[0]
    page_size = cache_pool.shape[1]
    held = HOLD_MOST * page_size

    hits = hit_pages.shape[0]
    owned_hits = hit_pages // pool_pages == ep_index
    earlier = jnp.arange(hits)[None, :] < jnp.arange(hits)[:, None]
    hit_rank = jnp.sum((earlier & owned_hits[None, :]).astype(jnp.int32), axis=1)
    hit_pick = owned_hits[None, :] & (
        hit_rank[None, :] == jnp.arange(HOLD_MOST, dtype=jnp.int32)[:, None]
    )
    local_page = jnp.sum(jnp.where(hit_pick, hit_pages[None, :] - ep_index * pool_pages, 0), axis=1)
    chosen = cache_pool.at[local_page].get(mode="promise_in_bounds")
    own_pages = lax.dynamic_index_in_dim(chosen, keyval_pick, 2, keepdims=False).reshape(held, 2 * HD)
    own_suffix = lax.dynamic_index_in_dim(new_kv, keyval_pick, 1, keepdims=False)

    by_expert = jnp.sum(
        jnp.where(
            expert_ids[:, :, None] == jnp.arange(ep_count, dtype=jnp.int32)[None, None, :],
            gate_weights[:, :, None],
            0.0,
        ),
        axis=1,
    )
    weight_part = jnp.stack(three_parts(by_expert.T)).reshape(-1, 2 * HD)
    weight_rows = weight_part.shape[0]
    weight_part = jnp.pad(weight_part, ((0, -weight_rows % WEIGHT_ROWS), (0, 0)))
    payload = jnp.concatenate([own_pages, own_suffix, weight_part], axis=0)
    arrived = [payload]
    for step in range(1, ep_count):
        arrived.append(
            lax.ppermute(payload, "ep", [(i, (i + step) % ep_count) for i in range(ep_count)])
        )
    sources = [(ep_index - step) % ep_count for step in range(ep_count)]

    starts = jnp.cumsum(span_lengths) - span_lengths
    slots_here = jnp.arange(tokens, dtype=jnp.int32)
    own_positions = starts[ep_index] + slots_here
    own_filled = slots_here < span_lengths[ep_index]
    holder = hit_pages // pool_pages
    keys = []
    allowed = []
    for source, block in zip(sources, arrived):
        keys.append(block[: held + tokens])
        count = jnp.sum((holder == source).astype(jnp.int32))
        open_rows = jnp.arange(held, dtype=jnp.int32) < count * page_size
        causal = (slots_here < span_lengths[source])[None, :] & (
            (starts[source] + slots_here)[None, :] <= own_positions[:, None]
        )
        allowed += [jnp.broadcast_to(open_rows[None, :], (tokens, held)), causal]
    keys = jnp.concatenate(keys, axis=0)
    allowed = jnp.concatenate(allowed, axis=1)
    grouped = queries.reshape(tokens, heads_local, HD)
    scores = jnp.einsum(
        "thd,kd->htk", grouped, keys[:, :HD], preferred_element_type=jnp.float32
    ) * (1.0 / math.sqrt(HD))
    scores = jnp.where(allowed[None], scores, MASKED)
    attention_weights = jax.nn.softmax(scores, axis=-1).astype(jnp.bfloat16)
    attended = jnp.einsum(
        "htk,kd->thd", attention_weights, keys[:, HD:], preferred_element_type=jnp.float32
    )
    attended = attended.astype(jnp.bfloat16).reshape(tokens, heads_local * HD)
    projected = jnp.dot(attended, out_weight, preferred_element_type=jnp.float32)

    projected_rows = projected.astype(jnp.bfloat16)
    heads_out = lax.dynamic_slice_in_dim(projected, block_index * row_count, row_count, 0)
    for step in range(1, blocks):
        sent = lax.dynamic_slice_in_dim(
            projected_rows, (block_index ^ step) * row_count, row_count, 0
        )
        heads_out = heads_out + lax.ppermute(
            sent, ("kv", "tp"), [(i, i ^ step) for i in range(blocks)]
        ).astype(jnp.float32)
    own_hidden = lax.dynamic_slice_in_dim(hidden_in, block_index * row_count, row_count, 0)
    residual = (own_hidden.astype(jnp.float32) + heads_out).astype(jnp.bfloat16)
    resid_wide = residual.astype(jnp.float32)
    normed = (
        resid_wide
        * lax.rsqrt(jnp.mean(resid_wide * resid_wide, axis=1, keepdims=True) + EPSILON)
        * norm_gain
    ).astype(jnp.bfloat16)

    all_normed = lax.all_gather(normed, ("ep", "kv", "tp"), axis=0, tiled=True)
    contract = (((1,), (1,)), ((), ()))
    gate_part = lax.dot_general(
        all_normed, gate_up[0, 0], contract, preferred_element_type=jnp.float32
    )
    up_part = lax.dot_general(
        all_normed, gate_up[0, 1], contract, preferred_element_type=jnp.float32
    )
    hidden = (jax.nn.silu(gate_part) * up_part).astype(jnp.bfloat16)
    down_part = jnp.dot(hidden, down_weight[0], preferred_element_type=jnp.float32)
    row_weights = []
    for block in arrived:
        parts = block[held + tokens : held + tokens + weight_rows].astype(jnp.float32)
        parts = parts.reshape(3, ep_count, tokens)
        row_weights.append(lax.dynamic_index_in_dim(jnp.sum(parts, axis=0), ep_index, 0, False))
    row_weights = jnp.stack(row_weights)
    row_weights = row_weights[(ep_index - jnp.arange(ep_count)) % ep_count].reshape(-1)
    mixture = lax.psum_scatter(
        (row_weights[:, None] * down_part).astype(jnp.bfloat16),
        ("ep", "kv", "tp"),
        scatter_dimension=0,
        tiled=True,
    ).astype(jnp.float32)
    rows_filled = lax.dynamic_slice_in_dim(own_filled, block_index * row_count, row_count, 0)
    layer_out = jnp.where(rows_filled[:, None], resid_wide + mixture, 0.0).astype(jnp.bfloat16)

    own_most = 2 * (tokens // page_size)
    page_count = new_owner.shape[0]
    pages_here = tokens // page_size
    owned_pages = new_owner == ep_index
    page_ids = jnp.arange(page_count, dtype=jnp.int32)
    owner_rank = jnp.sum(
        ((page_ids[None, :] < page_ids[:, None]) & owned_pages[None, :]).astype(jnp.int32), axis=1
    )
    choose = owned_pages[None, :] & (
        owner_rank[None, :] == jnp.arange(own_most, dtype=jnp.int32)[:, None]
    )
    page_index = jnp.sum(jnp.where(choose, page_ids[None, :], 0), axis=1)
    has_page = jnp.any(choose, axis=1)
    suffix = jnp.concatenate([block[held : held + tokens] for block in arrived], axis=0)
    spot = (ep_index - page_index // pages_here) % ep_count * pages_here + page_index % pages_here
    taken = suffix.reshape(page_count, page_size, 2 * HD).at[spot].get(mode="promise_in_bounds")
    slot_in_span = (page_index % pages_here)[:, None] * page_size + jnp.arange(page_size)[None, :]
    kept = has_page[:, None] & (slot_in_span < span_lengths[page_index // pages_here][:, None])
    head_pages = jnp.where(kept[:, :, None], taken, jnp.zeros((), jnp.bfloat16))
    if keyval_local == 1:
        decode_pages = head_pages[:, :, None, :]
    else:
        other = lax.ppermute(head_pages, "tp", [(i, i ^ 1) for i in range(tp_count)])
        first = tp_index == 0
        decode_pages = jnp.stack(
            [jnp.where(first, head_pages, other), jnp.where(first, other, head_pages)], axis=2
        )
    return (layer_out, decode_pages)


def solution(mesh):
    placed = (
        P(("groups", "ep"), ("kv", "tp")),
        P(("groups", "ep"), "kv", None),
        P(("groups", "ep"), None, "kv", None),
        P("groups"),
        P("groups"),
        P(("kv", "tp"), None),
        P(("groups", "ep"), None),
        P(),
        P(("groups", "ep"), None),
        P(("groups", "ep"), None),
        P("ep", None, ("kv", "tp"), None),
        P("ep", ("kv", "tp"), None),
        P("groups"),
    )
    return jax.shard_map(
        local,
        mesh=mesh,
        in_specs=placed,
        out_specs=(P(("groups", "ep", "kv", "tp"), None), P(("groups", "ep"), None, "kv", None)),
        check_vma=False,
    )
```

time: 276 us -> 185 us (0.67)
  blocking collectives: 80.2 us -> 0 us
  local copies, waits for them, and re-layouts: 35.5 us -> 15.9 us
  waiting for transfers between devices: 92.5 us -> 103 us
  other arithmetic: 25.7 us -> 17.8 us
  starting transfers between devices: 4.71 us -> 8.61 us
    all_to_all x1 -> x0, blocking collectives: 51.7 us -> none  [local(): lax.all_to_all(outgoing, 'ep', split_axis=0, concat_axis=0, tiled=True)]
    all_to_all x1 -> x0, waiting for transfers between devices: 45.7 us -> none  [local(): lax.all_to_all(expert_rows(lax.all_to_all(outgoing, 'ep', split_axis=0, c...]
    all_gather x1, waiting for transfers between devices: 0.01 us -> 40.9 us  [local(): all_normed = lax.all_gather(normed, ('ep', 'kv', 'tp'), axis=0, tiled=True)]
    reduce_scatter x1, waiting for transfers between devices: 15.3 us -> 54.9 us  [local(): lax.psum_scatter((row_weights[:, None] * down_part).astype(jnp.bfloat16),...]
    psum x1 -> x0, waiting for transfers between devices: 31.5 us -> none  [local(): lax.psum(projected.astype(jnp.bfloat16), ('kv', 'tp')).astype(jnp.float32)]
    gather x5 -> x4, local copies, waits for them, and re-layouts: 21.4 us -> 4.05 us  [the longest x1 2.3 us: local(): chosen = cache_pool.at[local_page].get(mode='promise_in_bounds')]
    all_gather x1 -> x0, blocking collectives: 14.9 us -> none  [local(): suffix = lax.all_gather(new_kv, 'ep', axis=0, tiled=True)]
    unnamed x1 -> x0, blocking collectives: 13.6 us -> none
  transfers between devices with their start and end apart: 4 -> 9, of which waited for: 3 -> 5; matrix products, arithmetic and copies ran while one was open for 7% -> 11% of each run, Pallas kernels for 0% -> 0%
where the time goes in v1:
time: 185 us; the launch traced here: 184 us
  waiting for transfers between devices  103 us (56%)
  matrix products  21.9 us (12%)
  other arithmetic  17.8 us (10%)
  between operations  17 us (9%)
  local copies, waits for them, and re-layouts  15.9 us (9%)
  starting transfers between devices  8.61 us (5%)
    reduce_scatter x1, waiting for transfers between devices, local(): lax.psum_scatter((row_weights[:, None] * down_part).astype(jnp.bfloat16),...  54.9 us
    all_gather x1, waiting for transfers between devices, local(): all_normed = lax.all_gather(normed, ('ep', 'kv', 'tp'), axis=0, tiled=True)  40.9 us
    ppermute x3, waiting for transfers between devices, local(): lax.ppermute(sent, ('kv', 'tp'), [(i, i ^ step) for i in range(blocks)])  6.78 us
    dot_general x1, matrix products, local(): jnp.dot(hidden, down_weight[0], preferred_element_type=jnp.float32)  6.41 us
    ppermute x3, starting transfers between devices, local(): lax.ppermute(payload, 'ep', [(i, (i + step) % ep_count) for i in range(ep...  6.06 us
    dot_general x1, matrix products, local(): jnp.dot(attended, out_weight, preferred_element_type=jnp.float32)  5.95 us
    unnamed x16, local copies, waits for them, and re-layouts  5.28 us
    dot_general x1, matrix products, local(): lax.dot_general(all_normed, gate_up[0, 0], contract, preferred_element_ty...  4.54 us
  transfers between devices with their start and end apart: 9, of which 5 were waited for; matrix products, arithmetic and copies ran while one was open for 11% of the time, Pallas kernels for 0%

profile of v1, /device:TPU:0, one launch (start us, length us, event | category | flops | bytes accessed | tf_op | source)
XLA Modules:
  0.0 184.0 jit_solution(8470083182087059299)
XLA Ops:
  7.2 0.8 broadcast_compare_fusion.1
  10.0 0.9 constant_dynamic-slice_fusion.7
  10.9 2.3 %gather_fusion = bf16[16,16,2,256]{3,2,1,0:T(2,128)(2,1)S(1)} fusion(bf16[64,16,2,256]{3,2,1,0:T(2,128)(2,1)} %param.15, s32[1024]{0:T(1024)S(1)} %pad_clamp_fusion.3), kind=kCustom, calls=%fused_computation | custom fusion | bytes 524352 | tf_op jit(solution)/shard_map/gather | solution.py:66
  15.5 5.0 %collective-permute-start.2 = (bf16[336,256]{1,0:T(8,128)(2,1)}, bf16[336,256]{1,0:T(8,128)(2,1)S(1)}, u32[]{:S(2)}, u32[]{:S(2)}) collective-permute-start(bf16[336,256]{1,0:T(8,128)(2,1)} %pad_maximum_fusion), channel_id=1, source_target_pairs={{0,12},{4,0},{8,4},{12,8},{1,13},{5,1},{9,5},{13,9},{2,14},{6,2},{... | collective-permute-start | bytes 516104 | tf_op jit(solution)/shard_map/ppermute | solution.py:85
  20.6 1.0 collective-permute-start
  21.6 0.8 reduce-window.9
  26.4 1.5 fusion.85
  34.1 1.6 slice_dynamic-update-slice_fusion.2
  35.7 1.6 slice_dynamic-update-slice_fusion.1
  38.0 2.1 %fusion.87 = f32[8,64]{1,0:T(8,128)S(1)} fusion(pred[64,1280]{1,0:T(8,128)(4,1)S(1)} %concatenate.18, bf16[1280,256]{1,0:T(8,128)(2,1)} %slice_dynamic-update-slice_fusion, bf16[64,1024]{1,0:T(8,128)(2,1)} %param.13), kind=kOutput, calls=%fused_computation.180 | convolution fusion | flops 170394880 | bytes 542720 | tf_op jit(solution)/shard_map/sub | solution.py:111
  40.0 2.9 %fusion.21 = bf16[8,8,8,128]{3,2,1,0:T(8,128)(2,1)S(1)} fusion(f32[8,64]{1,0:T(8,128)S(1)} %fusion.87, bf16[1280,256]{1,0:T(8,128)(2,1)} %slice_dynamic-update-slice_fusion, pred[64,1280]{1,0:T(8,128)(4,1)} %copy-done.2, bf16[64,1024]{1,0:T(8,128)(2,1)} %param.13), kind=kOutput, calls=%fused_computation.24 | convolution fusion | flops 338888448 | bytes 1001472 | tf_op jit(solution)/shard_map/htk,kd->thd/dot_general | solution.py:112
  43.0 5.9 %fusion.90 = (bf16[64,4096]{1,0:T(8,128)(2,1)S(1)}, f32[64,4096]{1,0:T(8,128)}) fusion(bf16[1024,4096]{1,0:T(8,128)(2,1)} %param.18, bf16[8,8,8,128]{3,2,1,0:T(8,128)(2,1)S(1)} %fusion.21), kind=kOutput, calls=%fused_computation.181 | convolution fusion | flops 537133056 | bytes 10092544 | tf_op jit(solution)/shard_map/dot_general | solution.py:116
  49.6 1.6 collective-permute-start.5
  51.8 3.6 %collective-permute-done.5 = bf16[16,4096]{1,0:T(8,128)(2,1)} collective-permute-done((bf16[16,4096]{1,0:T(8,128)(2,1)}, bf16[16,4096]{1,0:T(8,128)(2,1)}, u32[]{:S(2)}, u32[]{:S(2)}) %collective-permute-start.5) | collective-permute-done | bytes 131104 | tf_op jit(solution)/shard_map/ppermute | solution.py:124
  55.4 3.2 %collective-permute-done.4 = bf16[16,4096]{1,0:T(8,128)(2,1)} collective-permute-done((bf16[16,4096]{1,0:T(8,128)(2,1)S(1)}, bf16[16,4096]{1,0:T(8,128)(2,1)}, u32[]{:S(2)}, u32[]{:S(2)}) %collective-permute-start.4) | collective-permute-done | bytes 131104 | tf_op jit(solution)/shard_map/ppermute | solution.py:124
  58.6 1.4 fusion.29
  63.1 40.9 %all-gather.2.cloned.1.call-done = bf16[256,4096]{1,0:T(8,128)(2,1)} async-done(((bf16[16,4096]{1,0:T(8,128)(2,1)}), bf16[256,4096]{1,0:T(8,128)(2,1)}) %all-gather.2.cloned.1.call-update) | async-done | bytes 2097168 | tf_op jit(solution)/shard_map/all_gather | solution.py:136
  104.0 4.5 %fusion.9 = f32[256,384]{1,0:T(8,128)} fusion(bf16[256,4096]{1,0:T(8,128)(2,1)} %all-gather.2.cloned.1.call-done, bf16[1,2,384,4096]{3,2,1,0:T(8,128)(2,1)} %param.23), kind=kOutput, calls=%fused_computation.15 | convolution fusion | flops 805306368 | bytes 5636096 | tf_op jit(solution)/shard_map/dot_general | solution.py:138
  108.6 6.4 %fusion.1 = bf16[256,4096]{1,0:T(8,128)(2,1)} fusion(bf16[1,384,4096]{2,1,0:T(8,128)(2,1)S(1)} %copy-done, f32[256]{0:T(256)S(1)} %mul.113, bf16[256,4096]{1,0:T(8,128)(2,1)} %all-gather.2.cloned.1.call-done, bf16[1,2,384,4096]{3,2,1,0:T(8,128)(2,1)} %param.23, f32[256,384]{1,0:T(8,128)} %fusion.9), kind=kOutput, calls=%fused_computation.6 | convolution fusion | flops 1613299712 | bytes 10880000 | tf_op jit(solution)/shard_map/dot_general | solution.py:145
  116.2 0.8 slice.72
  117.0 0.8 slice.71
  119.9 0.8 copy.34
  120.7 54.9 %reduce-scatter.2.cloned.1.call-done = bf16[16,4096]{1,0:T(8,128)(2,1)} async-done(((bf16[256,4096]{1,0:T(8,128)(2,1)}), bf16[16,4096]{1,0:T(8,128)(2,1)}) %reduce-scatter.2.cloned.1.call-update) | async-done | bytes 131088 | tf_op jit(solution)/shard_map/reduce_scatter | solution.py:153
  175.5 1.6 fusion.33
  (95 shorter events, 20.0 us)
Async XLA Ops:
  7.2 101.4 %copy-start = (bf16[1,384,4096]{2,1,0:T(8,128)(2,1)S(1)}, bf16[1,384,4096]{2,1,0:T(8,128)(2,1)}, u32[]{:S(2)}) copy-start(bf16[1,384,4096]{2,1,0:T(8,128)(2,1)} %param.24) | copy-start | bytes 9437188
  7.2 96.9 %all-gather.2.cloned.1.call-start = ((), (), s32[]{:S(2)}) async-start(), calls=%async_computation.1 | async-start | bytes 2228224 | tf_op jit(solution)/shard_map/all_gather | solution.py:136
  15.5 21.8 %collective-permute-start.2 = (bf16[336,256]{1,0:T(8,128)(2,1)}, bf16[336,256]{1,0:T(8,128)(2,1)S(1)}, u32[]{:S(2)}, u32[]{:S(2)}) collective-permute-start(bf16[336,256]{1,0:T(8,128)(2,1)} %pad_maximum_fusion), channel_id=1, source_target_pairs={{0,12},{4,0},{8,4},{12,8},{1,13},{5,1},{9,5},{13,9},{2,14},{6,2},{... | collective-permute-start | bytes 516104 | tf_op jit(solution)/shard_map/ppermute | solution.py:85
  20.6 15.2 %collective-permute-start.1 = (bf16[336,256]{1,0:T(8,128)(2,1)}, bf16[336,256]{1,0:T(8,128)(2,1)}, u32[]{:S(2)}, u32[]{:S(2)}) collective-permute-start(bf16[336,256]{1,0:T(8,128)(2,1)} %pad_maximum_fusion), channel_id=1, source_target_pairs={{0,8},{4,12},{8,0},{12,4},{1,9},{5,13},{9,1},{13,5},{2,10},{6,14},... | collective-permute-start | bytes 516104 | tf_op jit(solution)/shard_map/ppermute | solution.py:85
  20.6 13.5 %collective-permute-start = (bf16[336,256]{1,0:T(8,128)(2,1)}, bf16[336,256]{1,0:T(8,128)(2,1)}, u32[]{:S(2)}, u32[]{:S(2)}) collective-permute-start(bf16[336,256]{1,0:T(8,128)(2,1)} %pad_maximum_fusion), channel_id=1, source_target_pairs={{0,4},{4,8},{8,12},{12,0},{1,5},{5,9},{9,13},{13,1},{2,6},{6,10},{... | collective-permute-start | bytes 516104 | tf_op jit(solution)/shard_map/ppermute | solution.py:85
  34.1 3.9 %copy-start.2 = (pred[64,1280]{1,0:T(8,128)(4,1)}, pred[64,1280]{1,0:T(8,128)(4,1)S(1)}, u32[]{:S(2)}) copy-start(pred[64,1280]{1,0:T(8,128)(4,1)S(1)} %concatenate.18) | copy-start | bytes 245764
  42.9 17.0 %copy-start.3 = (f32[4096]{0:T(1024)S(1)}, f32[4096]{0:T(1024)}, u32[]{:S(2)}) copy-start(f32[4096]{0:T(1024)} %param.20) | copy-start | bytes 49156
  49.6 2.1 %collective-permute-start.3 = (bf16[16,4096]{1,0:T(8,128)(2,1)}, bf16[16,4096]{1,0:T(8,128)(2,1)}, u32[]{:S(2)}, u32[]{:S(2)}) collective-permute-start(bf16[16,4096]{1,0:T(8,128)(2,1)} %get-tuple-element.18), channel_id=1, source_target_pairs={{0,1},{1,0},{2,3},{3,2},{4,5},{5,4},{6,7},{7,6},{8,9},{9,8},{10,11... | collective-permute-start | bytes 393224 | tf_op jit(solution)/shard_map/ppermute | solution.py:124
  49.6 5.8 %collective-permute-start.5 = (bf16[16,4096]{1,0:T(8,128)(2,1)}, bf16[16,4096]{1,0:T(8,128)(2,1)}, u32[]{:S(2)}, u32[]{:S(2)}) collective-permute-start(bf16[16,4096]{1,0:T(8,128)(2,1)} %get-tuple-element.19), channel_id=1, source_target_pairs={{0,3},{1,2},{2,1},{3,0},{4,7},{5,6},{6,5},{7,4},{8,11},{9,10},{10,... | collective-permute-start | bytes 393224 | tf_op jit(solution)/shard_map/ppermute | solution.py:124
  51.2 7.3 %collective-permute-start.4 = (bf16[16,4096]{1,0:T(8,128)(2,1)S(1)}, bf16[16,4096]{1,0:T(8,128)(2,1)}, u32[]{:S(2)}, u32[]{:S(2)}) collective-permute-start(bf16[16,4096]{1,0:T(8,128)(2,1)S(1)} %get-tuple-element.20), channel_id=1, source_target_pairs={{0,2},{1,3},{2,0},{3,1},{4,6},{5,7},{6,4},{7,5},{8,10},{9,11},{10,... | collective-permute-start | bytes 393224 | tf_op jit(solution)/shard_map/ppermute | solution.py:124
  60.7 114.8 %reduce-scatter.2.cloned.1.call-start = ((), (), s32[]{:S(2)}) async-start(), calls=%async_computation.2 | async-start | bytes 2228224 | tf_op jit(solution)/shard_map/reduce_scatter | solution.py:153
  108.6 6.4 %copy-start.4 = (s32[16]{0:T(128)S(1)}, s32[16]{0:T(128)}, u32[]{:S(2)}) copy-start(s32[16]{0:T(128)} %param.25) | copy-start | bytes 196
  108.6 6.7 %copy-start.1 = (s32[4]{0:T(128)S(1)}, s32[4]{0:T(128)}, u32[]{:S(2)}) copy-start(s32[4]{0:T(128)} %param.17) | copy-start | bytes 52
  118.4 1.4 collective-permute-start.6
Sparse Core Ops, SparseCore 0:
  60.8 43.1 all-gather.1
  115.2 60.3 reduce-scatter.1

commit v2 on v1

--- a/solution.py
+++ b/solution.py
@@ -3,6 +3,8 @@
 import jax
 import jax.numpy as jnp
 from jax import lax
+from jax.experimental import pallas as pl
+from jax.experimental.pallas import tpu as pltpu
 from jax.sharding import PartitionSpec as P
 
 HD = 128
@@ -21,6 +23,89 @@
     middle = lax.reduce_precision(rest, 8, 7)
     low = rest - middle
     return [part.astype(jnp.bfloat16) for part in (high, middle, low)]
+
+
+def piece_order(blocks):
+    order = [0]
+    bit = 2
+    while bit < blocks:
+        order += [piece ^ bit for piece in order]
+        bit *= 2
+    return order + [piece ^ 1 for piece in order]
+
+
+TRANSPOSED = (((1,), (1,)), ((), ()))
+CHUNKS = 4
+
+
+def expert_kernel(count, *refs):
+    row_refs = refs[:count]
+    weight_ref, gate_up, down_weight, kept_ref, sent_ref = refs[count : count + 5]
+    gate_up_held, down_held, gate_up_sem, down_sem = refs[count + 5 :]
+    width = gate_up_held.shape[-1]
+    first = [
+        pltpu.make_async_copy(
+            gate_up.at[0, :, :, pl.ds(i * width, width)], gate_up_held.at[i], gate_up_sem.at[i]
+        )
+        for i in range(CHUNKS)
+    ]
+    second = [
+        pltpu.make_async_copy(
+            down_weight.at[0, :, pl.ds(i * width, width)], down_held.at[i], down_sem.at[i]
+        )
+        for i in range(CHUNKS)
+    ]
+    for copy in first + second:
+        copy.start()
+    gate_part = up_part = 0.0
+    for i in range(CHUNKS):
+        rows = jnp.concatenate([ref[:, i * width : (i + 1) * width] for ref in row_refs], axis=0)
+        first[i].wait()
+        gate_part += lax.dot_general(
+            rows, gate_up_held[i, 0], TRANSPOSED, preferred_element_type=jnp.float32
+        )
+        up_part += lax.dot_general(
+            rows, gate_up_held[i, 1], TRANSPOSED, preferred_element_type=jnp.float32
+        )
+    hidden = gate_part / (1.0 + jnp.exp(-gate_part)) * up_part
+    hidden = (hidden * weight_ref[...]).astype(jnp.bfloat16)
+    half = kept_ref.shape[0]
+    for i in range(CHUNKS):
+        second[i].wait()
+        out = jnp.dot(hidden, down_held[i], preferred_element_type=jnp.float32)
+        out = out.astype(jnp.bfloat16)
+        kept_ref[:, i * width : (i + 1) * width] = out[:half]
+        sent_ref[:, i * width : (i + 1) * width] = out[half:]
+
+
+def expert_call(have, row_weight, gate_up, down_weight):
+    if have[0].shape[0] % 16:
+        have = [jnp.concatenate(have, axis=0)]
+    tokens = sum(piece.shape[0] for piece in have)
+    model_width = have[0].shape[1]
+    hidden_units = down_weight.shape[1]
+    width = model_width // CHUNKS
+    whole = pl.BlockSpec(memory_space=pltpu.VMEM)
+    half = jax.ShapeDtypeStruct((tokens // 2, model_width), jnp.bfloat16)
+    return pl.pallas_call(
+        lambda *refs: expert_kernel(len(have), *refs),
+        out_shape=(half, half),
+        in_specs=[whole] * (len(have) + 1) + [pl.BlockSpec(memory_space=pl.ANY)] * 2,
+        out_specs=(whole, whole),
+        scratch_shapes=[
+            pltpu.VMEM((CHUNKS, 2, hidden_units, width), jnp.bfloat16),
+            pltpu.VMEM((CHUNKS, hidden_units, width), jnp.bfloat16),
+            pltpu.SemaphoreType.DMA((CHUNKS,)),
+            pltpu.SemaphoreType.DMA((CHUNKS,)),
+        ],
+        compiler_params=pltpu.CompilerParams(vmem_limit_bytes=24 * 2**20),
+        cost_estimate=pl.CostEstimate(
+            flops=6 * tokens * hidden_units * model_width,
+            bytes_accessed=6 * hidden_units * model_width,
+            transcendentals=tokens * hidden_units,
+        ),
+        name="experts",
+    )(*have, row_weight, gate_up, down_weight)
 
 
 def local(
@@ -82,9 +167,9 @@
     arrived = [payload]
     for step in range(1, ep_count):
         arrived.append(
-            lax.ppermute(payload, "ep", [(i, (i + step) % ep_count) for i in range(ep_count)])
-        )
-    sources = [(ep_index - step) % ep_count for step in range(ep_count)]
+            lax.ppermute(payload, "ep", [(i, i ^ step) for i in range(ep_count)])
+        )
+    sources = [ep_index ^ step for step in range(ep_count)]
 
     starts = jnp.cumsum(span_lengths) - span_lengths
     slots_here = jnp.arange(tokens, dtype=jnp.int32)
@@ -133,31 +218,41 @@
         * norm_gain
     ).astype(jnp.bfloat16)
 
-    all_normed = lax.all_gather(normed, ("ep", "kv", "tp"), axis=0, tiled=True)
-    contract = (((1,), (1,)), ((), ()))
-    gate_part = lax.dot_general(
-        all_normed, gate_up[0, 0], contract, preferred_element_type=jnp.float32
-    )
-    up_part = lax.dot_general(
-        all_normed, gate_up[0, 1], contract, preferred_element_type=jnp.float32
-    )
-    hidden = (jax.nn.silu(gate_part) * up_part).astype(jnp.bfloat16)
-    down_part = jnp.dot(hidden, down_weight[0], preferred_element_type=jnp.float32)
+    pieces = [block_index ^ piece for piece in piece_order(blocks)]
+    pieces = jnp.stack(pieces)
     row_weights = []
     for block in arrived:
         parts = block[held + tokens : held + tokens + weight_rows].astype(jnp.float32)
-        parts = parts.reshape(3, ep_count, tokens)
-        row_weights.append(lax.dynamic_index_in_dim(jnp.sum(parts, axis=0), ep_index, 0, False))
-    row_weights = jnp.stack(row_weights)
-    row_weights = row_weights[(ep_index - jnp.arange(ep_count)) % ep_count].reshape(-1)
-    mixture = lax.psum_scatter(
-        (row_weights[:, None] * down_part).astype(jnp.bfloat16),
-        ("ep", "kv", "tp"),
-        scatter_dimension=0,
-        tiled=True,
-    ).astype(jnp.float32)
+        parts = jnp.sum(parts.reshape(3, ep_count, tokens), axis=0)
+        parts = lax.dynamic_index_in_dim(parts, ep_index, 0, False)
+        row_weights.append(parts.reshape(blocks, row_count)[pieces].reshape(tokens, 1))
+    exchange = lambda value, bit: lax.ppermute(
+        value, ("kv", "tp"), [(i, i ^ bit) for i in range(blocks)]
+    )
+    across = lambda value, step: lax.ppermute(
+        value, "ep", [(i, i ^ step) for i in range(ep_count)]
+    )
+    bits = [1 << place for place in range(1, blocks.bit_length() - 1)]
+    mixture = resid_wide
+    for step in range(ep_count):
+        have = [normed if step == 0 else across(normed, step)]
+        for bit in bits + [1]:
+            have += [exchange(piece, bit) for piece in have]
+        kept, sent = expert_call(have, row_weights[step], gate_up, down_weight)
+        got = exchange(sent, 1)
+        for bit in reversed(bits):
+            half = kept.shape[0] // 2
+            give = (kept[half:].astype(jnp.float32) + got[half:].astype(jnp.float32)).astype(
+                jnp.bfloat16
+            )
+            kept = kept[:half].astype(jnp.float32) + got[:half].astype(jnp.float32)
+            got = exchange(give, bit)
+        own = kept.astype(jnp.float32) + got.astype(jnp.float32)
+        if step > 0:
+            own = across(own.astype(jnp.bfloat16), step).astype(jnp.float32)
+        mixture = mixture + own
     rows_filled = lax.dynamic_slice_in_dim(own_filled, block_index * row_count, row_count, 0)
-    layer_out = jnp.where(rows_filled[:, None], resid_wide + mixture, 0.0).astype(jnp.bfloat16)
+    layer_out = jnp.where(rows_filled[:, None], mixture, 0.0).astype(jnp.bfloat16)
 
     own_most = 2 * (tokens // page_size)
     page_count = new_owner.shape[0]
@@ -173,7 +268,7 @@
     page_index = jnp.sum(jnp.where(choose, page_ids[None, :], 0), axis=1)
     has_page = jnp.any(choose, axis=1)
     suffix = jnp.concatenate([block[held : held + tokens] for block in arrived], axis=0)
-    spot = (ep_index - page_index // pages_here) % ep_count * pages_here + page_index % pages_here
+    spot = (ep_index ^ (page_index // pages_here)) * pages_here + page_index % pages_here
     taken = suffix.reshape(page_count, page_size, 2 * HD).at[spot].get(mode="promise_in_bounds")
     slot_in_span = (page_index % pages_here)[:, None] * page_size + jnp.arange(page_size)[None, :]
     kept = has_page[:, None] & (slot_in_span < span_lengths[page_index // pages_here][:, None])

time: 185 us -> 125 us (0.68)
  waiting for transfers between devices: 103 us -> 26.3 us
  starting transfers between devices: 8.61 us -> 28.1 us
  Pallas kernels: 0 us -> 19.2 us
  matrix products: 21.9 us -> 7.85 us
  between operations: 17 us -> 3.83 us
  local copies, waits for them, and re-layouts: 15.9 us -> 21.8 us
    reduce_scatter x1 -> x0, waiting for transfers between devices: 54.9 us -> none  [local(): lax.psum_scatter((row_weights[:, None] * down_part).astype(jnp.bfloat16),...]
    all_gather x1 -> x0, waiting for transfers between devices: 40.9 us -> none  [local(): all_normed = lax.all_gather(normed, ('ep', 'kv', 'tp'), axis=0, tiled=True)]
    ppermute x3 -> x29, starting transfers between devices: 6.06 us -> 26 us  [the longest x6 10.9 us: local(): lax.ppermute(value, 'ep', [(i, i ^ step) for i in range(ep_count)])]
    ppermute x3 -> x29, waiting for transfers between devices: 0.01 us -> 19.8 us  [the longest x6 11.7 us: local(): lax.ppermute(value, 'ep', [(i, i ^ step) for i in range(ep_count)])]
    pallas_call x0 -> x4, Pallas kernels: none -> 19.2 us  [expert_call(): pl.pallas_call(lambda *refs: expert_kernel(len(have), *refs), out_shape=(...]
    dot_general x2 -> x0, matrix products: 11 us -> none  [the longest x1 6.41 us: local(): jnp.dot(hidden, down_weight[0], preferred_element_type=jnp.float32)]
    unnamed x16 -> x32, local copies, waits for them, and re-layouts: 5.28 us -> 13 us
  transfers between devices with their start and end apart: 9 -> 33, of which waited for: 5 -> 9; matrix products, arithmetic and copies ran while one was open for 11% -> 15% of each run, Pallas kernels for 0% -> 15%
where the time goes in v2:
time: 125 us; the launch traced here: 124 us
  starting transfers between devices  28.1 us (22%)
  waiting for transfers between devices  26.3 us (21%)
  local copies, waits for them, and re-layouts  21.8 us (17%)
  Pallas kernels  19.2 us (15%)
  other arithmetic  17.2 us (14%)
  matrix products  7.85 us (6%)
  between operations  3.83 us (3%)
    pallas_call x4, Pallas kernels, expert_call(): pl.pallas_call(lambda *refs: expert_kernel(len(have), *refs), out_shape=(...  19.2 us
    unnamed x32, local copies, waits for them, and re-layouts  13 us
    ppermute x6, waiting for transfers between devices, local(): lax.ppermute(value, 'ep', [(i, i ^ step) for i in range(ep_count)])  11.7 us
    ppermute x6, starting transfers between devices, local(): lax.ppermute(value, 'ep', [(i, i ^ step) for i in range(ep_count)])  10.9 us
    ppermute x20, starting transfers between devices, local(): lax.ppermute(value, ('kv', 'tp'), [(i, i ^ bit) for i in range(blocks)])  9.46 us
    ppermute x20, waiting for transfers between devices, local(): lax.ppermute(value, ('kv', 'tp'), [(i, i ^ bit) for i in range(blocks)])  7.66 us
    ppermute x3, waiting for transfers between devices, local(): lax.ppermute(sent, ('kv', 'tp'), [(i, i ^ step) for i in range(blocks)])  6.59 us
    ppermute x3, starting transfers between devices, local(): lax.ppermute(payload, 'ep', [(i, i ^ step) for i in range(ep_count)])  5.68 us
  transfers between devices with their start and end apart: 33, of which 9 were waited for; matrix products, arithmetic and copies ran while one was open for 15% of the time, Pallas kernels for 15%

profile of v2, /device:TPU:0, one launch (start us, length us, event | category | flops | bytes accessed | tf_op | source)
XLA Modules:
  0.0 124.3 jit_solution(18434106547150967190)
XLA Ops:
  6.5 3.1 %collective-permute-start = (bf16[336,256]{1,0:T(8,128)(2,1)S(1)}, bf16[336,256]{1,0:T(8,128)(2,1)S(1)}, u32[]{:S(2)}, u32[]{:S(2)}) collective-permute-start(bf16[336,256]{1,0:T(8,128)(2,1)S(1)} %pad_maximum_fusion), channel_id=1, source_target_pairs={{0,4},{4,0},{8,12},{12,8},{1,5},{5,1},{9,13},{13,9},{2,6},{6,2},{1... | collective-permute-start | bytes 516104 | tf_op jit(solution)/shard_map/ppermute | solution.py:170
  9.6 2.6 %collective-permute-start.1 = (bf16[336,256]{1,0:T(8,128)(2,1)S(1)}, bf16[336,256]{1,0:T(8,128)(2,1)S(1)}, u32[]{:S(2)}, u32[]{:S(2)}) collective-permute-start(bf16[336,256]{1,0:T(8,128)(2,1)S(1)} %pad_maximum_fusion), channel_id=1, source_target_pairs={{0,8},{4,12},{8,0},{12,4},{1,9},{5,13},{9,1},{13,5},{2,10},{6,14},... | collective-permute-start | bytes 516104 | tf_op jit(solution)/shard_map/ppermute | solution.py:170
  26.3 1.8 %fusion.7 = bf16[8,8,8,128]{3,2,1,0:T(8,128)(2,1)S(1)} fusion(f32[8,64]{1,0:T(8,128)S(1)} %fusion.67, bf16[1280,256]{1,0:T(8,128)(2,1)S(1)} %slice_dynamic-update-slice_fusion, pred[64,1280]{1,0:T(8,128)(4,1)S(1)} %concatenate.37, bf16[64,1024]{1,0:T(8,128)(2,1)S(1)} %copy-done.12), kind=kOutput, calls=%fused_computation.16 | convolution fusion | flops 338888448 | bytes 1001472 | tf_op jit(solution)/shard_map/htk,kd->thd/dot_general | solution.py:197
  28.1 5.0 %fusion.70 = (bf16[64,4096]{1,0:T(8,128)(2,1)S(1)}, f32[64,4096]{1,0:T(8,128)S(1)}) fusion(bf16[1024,4096]{1,0:T(8,128)(2,1)} %param.18, bf16[8,8,8,128]{3,2,1,0:T(8,128)(2,1)S(1)} %fusion.7), kind=kOutput, calls=%fused_computation.167 | convolution fusion | flops 537133056 | bytes 10092544 | tf_op jit(solution)/shard_map/dot_general | solution.py:201
  35.2 3.7 %collective-permute-done.5 = bf16[16,4096]{1,0:T(8,128)(2,1)S(1)} collective-permute-done((bf16[16,4096]{1,0:T(8,128)(2,1)S(1)}, bf16[16,4096]{1,0:T(8,128)(2,1)S(1)}, u32[]{:S(2)}, u32[]{:S(2)}) %collective-permute-start.5) | collective-permute-done | bytes 131104 | tf_op jit(solution)/shard_map/ppermute | solution.py:209
  39.0 2.9 %collective-permute-done.4 = bf16[16,4096]{1,0:T(8,128)(2,1)S(1)} collective-permute-done((bf16[16,4096]{1,0:T(8,128)(2,1)S(1)}, bf16[16,4096]{1,0:T(8,128)(2,1)S(1)}, u32[]{:S(2)}, u32[]{:S(2)}) %collective-permute-start.4) | collective-permute-done | bytes 131104 | tf_op jit(solution)/shard_map/ppermute | solution.py:209
  43.0 3.5 %collective-permute-start.25 = (bf16[16,4096]{1,0:T(8,128)(2,1)S(1)}, bf16[16,4096]{1,0:T(8,128)(2,1)S(1)}, u32[]{:S(2)}, u32[]{:S(2)}) collective-permute-start(bf16[16,4096]{1,0:T(8,128)(2,1)S(1)} %fusion.10.refs_0_), channel_id=1, source_target_pairs={{0,12},{4,8},{8,4},{12,0},{1,13},{5,9},{9,5},{13,1},{2,14},{6,10},... | collective-permute-start | bytes 393224 | tf_op jit(solution)/shard_map/ppermute | solution.py:232
  48.4 2.1 %collective-permute-done.25.refs_0_ = bf16[16,4096]{1,0:T(8,128)(2,1)S(1)} collective-permute-done((bf16[16,4096]{1,0:T(8,128)(2,1)S(1)}, bf16[16,4096]{1,0:T(8,128)(2,1)S(1)}, u32[]{:S(2)}, u32[]{:S(2)}) %collective-permute-start.25) | collective-permute-done | bytes 131104 | tf_op jit(solution)/shard_map/ppermute | solution.py:232
  51.6 2.8 %collective-permute-done.6.refs_1_ = bf16[16,4096]{1,0:T(8,128)(2,1)S(1)} collective-permute-done((bf16[16,4096]{1,0:T(8,128)(2,1)S(1)}, bf16[16,4096]{1,0:T(8,128)(2,1)S(1)}, u32[]{:S(2)}, u32[]{:S(2)}) %collective-permute-start.6) | collective-permute-done | bytes 131104 | tf_op jit(solution)/shard_map/ppermute | solution.py:229
  55.3 3.5 %collective-permute-done.18.refs_0_ = bf16[16,4096]{1,0:T(8,128)(2,1)S(1)} collective-permute-done((bf16[16,4096]{1,0:T(8,128)(2,1)S(1)}, bf16[16,4096]{1,0:T(8,128)(2,1)S(1)}, u32[]{:S(2)}, u32[]{:S(2)}) %collective-permute-start.18) | collective-permute-done | bytes 131104 | tf_op jit(solution)/shard_map/ppermute | solution.py:232
  62.1 2.8 %copy-done.1 = bf16[1,2,384,4096]{3,2,1,0:T(8,128)(2,1)S(1)} copy-done((bf16[1,2,384,4096]{3,2,1,0:T(8,128)(2,1)S(1)}, bf16[1,2,384,4096]{3,2,1,0:T(8,128)(2,1)}, u32[]{:S(2)}) %copy-start.1) | copy-done | bytes 6291480
  64.9 1.9 %copy-done.4 = bf16[1,384,4096]{2,1,0:T(8,128)(2,1)S(1)} copy-done((bf16[1,384,4096]{2,1,0:T(8,128)(2,1)S(1)}, bf16[1,384,4096]{2,1,0:T(8,128)(2,1)}, u32[]{:S(2)}) %copy-start.4) | copy-done | bytes 3145752
  66.8 4.8 %experts.4 = (bf16[32,4096]{1,0:T(8,128)(2,1)S(1)}, bf16[32,4096]{1,0:T(8,128)(2,1)S(1)}) custom-call(bf16[16,4096]{1,0:T(8,128)(2,1)S(1)} %fusion.10.refs_0_, bf16[16,4096]{1,0:T(8,128)(2,1)S(1)} %collective-permute-done.6.refs_1_, bf16[16,4096]{1,0:T(8,128)(2,1)S(1)} %collective-permute-done.7.refs_2_, ...), custom_call_target="tpu_custom_call" | custom-call | flops 603979776 | bytes 9437184 | tf_op jit(solution)/shard_map/experts/pallas_call | solution.py:90
  75.8 2.8 %copy-done.2 = bf16[1,2,384,4096]{3,2,1,0:T(8,128)(2,1)S(1)} copy-done((bf16[1,2,384,4096]{3,2,1,0:T(8,128)(2,1)S(1)}, bf16[1,2,384,4096]{3,2,1,0:T(8,128)(2,1)}, u32[]{:S(2)}) %copy-start.2) | copy-done | bytes 6291480
  78.6 1.9 %copy-done.5 = bf16[1,384,4096]{2,1,0:T(8,128)(2,1)S(1)} copy-done((bf16[1,384,4096]{2,1,0:T(8,128)(2,1)S(1)}, bf16[1,384,4096]{2,1,0:T(8,128)(2,1)}, u32[]{:S(2)}) %copy-start.5) | copy-done | bytes 3145752
  80.5 4.8 %experts.7 = (bf16[32,4096]{1,0:T(8,128)(2,1)S(1)}, bf16[32,4096]{1,0:T(8,128)(2,1)S(1)}) custom-call(bf16[16,4096]{1,0:T(8,128)(2,1)S(1)} %collective-permute-done.25.refs_0_, bf16[16,4096]{1,0:T(8,128)(2,1)S(1)} %collective-permute-done.26.refs_1_, bf16[16,4096]{1,0:T(8,128)(2,1)S(1)} %collective-permute-done.27.refs_2_, ...), custom_call_target="tpu_custom_call" | custom-call | flops 603979776 | bytes 9437184 | tf_op jit(solution)/shard_map/experts/pallas_call | solution.py:90
  85.9 2.8 %copy-done.3 = bf16[1,2,384,4096]{3,2,1,0:T(8,128)(2,1)S(1)} copy-done((bf16[1,2,384,4096]{3,2,1,0:T(8,128)(2,1)S(1)}, bf16[1,2,384,4096]{3,2,1,0:T(8,128)(2,1)}, u32[]{:S(2)}) %copy-start.3) | copy-done | bytes 6291480
  88.7 4.8 %experts.6 = (bf16[32,4096]{1,0:T(8,128)(2,1)S(1)}, bf16[32,4096]{1,0:T(8,128)(2,1)S(1)}) custom-call(bf16[16,4096]{1,0:T(8,128)(2,1)S(1)} %collective-permute-done.18.refs_0_, bf16[16,4096]{1,0:T(8,128)(2,1)S(1)} %collective-permute-done.19.refs_1_, bf16[16,4096]{1,0:T(8,128)(2,1)S(1)} %collective-permute-done.20.refs_2_, ...), custom_call_target="tpu_custom_call" | custom-call | flops 603979776 | bytes 9437184 | tf_op jit(solution)/shard_map/experts/pallas_call | solution.py:90
  93.7 4.8 %experts.5 = (bf16[32,4096]{1,0:T(8,128)(2,1)S(1)}, bf16[32,4096]{1,0:T(8,128)(2,1)S(1)}) custom-call(bf16[16,4096]{1,0:T(8,128)(2,1)S(1)} %collective-permute-done.11.refs_0_, bf16[16,4096]{1,0:T(8,128)(2,1)S(1)} %collective-permute-done.12.refs_1_, bf16[16,4096]{1,0:T(8,128)(2,1)S(1)} %collective-permute-done.13.refs_2_, ...), custom_call_target="tpu_custom_call" | custom-call | flops 603979776 | bytes 9437184 | tf_op jit(solution)/shard_map/experts/pallas_call | solution.py:90
  104.4 4.8 %collective-permute-done.30 = bf16[16,4096]{1,0:T(8,128)(2,1)S(1)} collective-permute-done((bf16[16,4096]{1,0:T(8,128)(2,1)S(1)}, bf16[16,4096]{1,0:T(8,128)(2,1)S(1)}, u32[]{:S(2)}, u32[]{:S(2)}) %collective-permute-start.30) | collective-permute-done | bytes 131104 | tf_op jit(solution)/shard_map/ppermute | solution.py:229
  109.2 3.0 %collective-permute-start.31 = (bf16[16,4096]{1,0:T(8,128)(2,1)S(1)}, bf16[16,4096]{1,0:T(8,128)(2,1)S(1)}, u32[]{:S(2)}, u32[]{:S(2)}) collective-permute-start(bf16[16,4096]{1,0:T(8,128)(2,1)S(1)} %add_convert_fusion), channel_id=1, source_target_pairs={{0,12},{4,8},{8,4},{12,0},{1,13},{5,9},{9,5},{13,1},{2,14},{6,10},... | collective-permute-start | bytes 393224 | tf_op jit(solution)/shard_map/ppermute | solution.py:232
  112.2 2.6 %collective-permute-start.24 = (bf16[16,4096]{1,0:T(8,128)(2,1)S(1)}, bf16[16,4096]{1,0:T(8,128)(2,1)S(1)}, u32[]{:S(2)}, u32[]{:S(2)}) collective-permute-start(bf16[16,4096]{1,0:T(8,128)(2,1)S(1)} %add_convert_fusion.2), channel_id=1, source_target_pairs={{0,8},{4,12},{8,0},{12,4},{1,9},{5,13},{9,1},{13,5},{2,10},{6,14},... | collective-permute-start | bytes 393224 | tf_op jit(solution)/shard_map/ppermute | solution.py:232
  117.5 5.1 %collective-permute-done.24 = bf16[16,4096]{1,0:T(8,128)(2,1)S(1)} collective-permute-done((bf16[16,4096]{1,0:T(8,128)(2,1)S(1)}, bf16[16,4096]{1,0:T(8,128)(2,1)S(1)}, u32[]{:S(2)}, u32[]{:S(2)}) %collective-permute-start.24) | collective-permute-done | bytes 131104 | tf_op jit(solution)/shard_map/ppermute | solution.py:232
  122.6 1.7 %fusion.15 = bf16[16,4096]{1,0:T(8,128)(2,1)} fusion(bf16[16,4096]{1,0:T(8,128)(2,1)S(1)} %get-tuple-element.28, bf16[16,4096]{1,0:T(8,128)(2,1)S(1)} %collective-permute-done.31, bf16[16,4096]{1,0:T(8,128)(2,1)S(1)} %collective-permute-done.24, bf16[16,4096]{1,0:T(8,128)(2,1)S(1)} %collective-permute-done.17, ...), kind=kLoop, calls=%fused_computation.29 | loop fusion | flops 983040 | bytes 1048592 | tf_op jit(solution)/shard_map/convert_element_type | solution.py:255
  (172 shorter events, 41.0 us)
Async XLA Ops:
  6.5 18.3 %collective-permute-start = (bf16[336,256]{1,0:T(8,128)(2,1)S(1)}, bf16[336,256]{1,0:T(8,128)(2,1)S(1)}, u32[]{:S(2)}, u32[]{:S(2)}) collective-permute-start(bf16[336,256]{1,0:T(8,128)(2,1)S(1)} %pad_maximum_fusion), channel_id=1, source_target_pairs={{0,4},{4,0},{8,12},{12,8},{1,5},{5,1},{9,13},{13,9},{2,6},{6,2},{1... | collective-permute-start | bytes 516104 | tf_op jit(solution)/shard_map/ppermute | solution.py:170
  9.6 15.6 %collective-permute-start.1 = (bf16[336,256]{1,0:T(8,128)(2,1)S(1)}, bf16[336,256]{1,0:T(8,128)(2,1)S(1)}, u32[]{:S(2)}, u32[]{:S(2)}) collective-permute-start(bf16[336,256]{1,0:T(8,128)(2,1)S(1)} %pad_maximum_fusion), channel_id=1, source_target_pairs={{0,8},{4,12},{8,0},{12,4},{1,9},{5,13},{9,1},{13,5},{2,10},{6,14},... | collective-permute-start | bytes 516104 | tf_op jit(solution)/shard_map/ppermute | solution.py:170
  12.2 13.0 %collective-permute-start.2 = (bf16[336,256]{1,0:T(8,128)(2,1)S(1)}, bf16[336,256]{1,0:T(8,128)(2,1)S(1)}, u32[]{:S(2)}, u32[]{:S(2)}) collective-permute-start(bf16[336,256]{1,0:T(8,128)(2,1)S(1)} %pad_maximum_fusion), channel_id=1, source_target_pairs={{0,12},{4,8},{8,4},{12,0},{1,13},{5,9},{9,5},{13,1},{2,14},{6,10},... | collective-permute-start | bytes 516104 | tf_op jit(solution)/shard_map/ppermute | solution.py:170
  47.3 11.5 %collective-permute-start.18 = (bf16[16,4096]{1,0:T(8,128)(2,1)S(1)}, bf16[16,4096]{1,0:T(8,128)(2,1)S(1)}, u32[]{:S(2)}, u32[]{:S(2)}) collective-permute-start(bf16[16,4096]{1,0:T(8,128)(2,1)S(1)} %fusion.10.refs_0_), channel_id=1, source_target_pairs={{0,8},{4,12},{8,0},{12,4},{1,9},{5,13},{9,1},{13,5},{2,10},{6,14},... | collective-permute-start | bytes 393224 | tf_op jit(solution)/shard_map/ppermute | solution.py:232
  48.1 10.7 %collective-permute-start.11 = (bf16[16,4096]{1,0:T(8,128)(2,1)S(1)}, bf16[16,4096]{1,0:T(8,128)(2,1)S(1)}, u32[]{:S(2)}, u32[]{:S(2)}) collective-permute-start(bf16[16,4096]{1,0:T(8,128)(2,1)S(1)} %fusion.10.refs_0_), channel_id=1, source_target_pairs={{0,4},{4,0},{8,12},{12,8},{1,5},{5,1},{9,13},{13,9},{2,6},{6,2},{1... | collective-permute-start | bytes 393224 | tf_op jit(solution)/shard_map/ppermute | solution.py:232
  48.3 10.9 %collective-permute-start.7 = (bf16[16,4096]{1,0:T(8,128)(2,1)S(1)}, bf16[16,4096]{1,0:T(8,128)(2,1)S(1)}, u32[]{:S(2)}, u32[]{:S(2)}) collective-permute-start(bf16[16,4096]{1,0:T(8,128)(2,1)S(1)} %fusion.10.refs_0_), channel_id=1, source_target_pairs={{0,1},{1,0},{2,3},{3,2},{4,5},{5,4},{6,7},{7,6},{8,9},{9,8},{10,11... | collective-permute-start | bytes 393224 | tf_op jit(solution)/shard_map/ppermute | solution.py:229
  50.5 10.4 %collective-permute-start.26 = (bf16[16,4096]{1,0:T(8,128)(2,1)S(1)}, bf16[16,4096]{1,0:T(8,128)(2,1)S(1)}, u32[]{:S(2)}, u32[]{:S(2)}) collective-permute-start(bf16[16,4096]{1,0:T(8,128)(2,1)S(1)} %collective-permute-done.25.refs_0_), channel_id=1, source_target_pairs={{0,2},{1,3},{2,0},{3,1},{4,6},{5,7},{6,4},{7,5},{8,10},{9,11},{10,... | collective-permute-start | bytes 393224 | tf_op jit(solution)/shard_map/ppermute | solution.py:229
  58.8 12.8 %collective-permute-start.27 = (bf16[16,4096]{1,0:T(8,128)(2,1)S(1)}, bf16[16,4096]{1,0:T(8,128)(2,1)S(1)}, u32[]{:S(2)}, u32[]{:S(2)}) collective-permute-start(bf16[16,4096]{1,0:T(8,128)(2,1)S(1)} %collective-permute-done.25.refs_0_), channel_id=1, source_target_pairs={{0,1},{1,0},{2,3},{3,2},{4,5},{5,4},{6,7},{7,6},{8,9},{9,8},{10,11... | collective-permute-start | bytes 393224 | tf_op jit(solution)/shard_map/ppermute | solution.py:229
  58.8 12.9 %collective-permute-start.19 = (bf16[16,4096]{1,0:T(8,128)(2,1)S(1)}, bf16[16,4096]{1,0:T(8,128)(2,1)S(1)}, u32[]{:S(2)}, u32[]{:S(2)}) collective-permute-start(bf16[16,4096]{1,0:T(8,128)(2,1)S(1)} %collective-permute-done.18.refs_0_), channel_id=1, source_target_pairs={{0,2},{1,3},{2,0},{3,1},{4,6},{5,7},{6,4},{7,5},{8,10},{9,11},{10,... | collective-permute-start | bytes 393224 | tf_op jit(solution)/shard_map/ppermute | solution.py:229
  59.3 12.9 %collective-permute-start.12 = (bf16[16,4096]{1,0:T(8,128)(2,1)S(1)}, bf16[16,4096]{1,0:T(8,128)(2,1)S(1)}, u32[]{:S(2)}, u32[]{:S(2)}) collective-permute-start(bf16[16,4096]{1,0:T(8,128)(2,1)S(1)} %collective-permute-done.11.refs_0_), channel_id=1, source_target_pairs={{0,2},{1,3},{2,0},{3,1},{4,6},{5,7},{6,4},{7,5},{8,10},{9,11},{10,... | collective-permute-start | bytes 393224 | tf_op jit(solution)/shard_map/ppermute | solution.py:229
  60.9 11.4 %collective-permute-start.28 = (bf16[16,4096]{1,0:T(8,128)(2,1)S(1)}, bf16[16,4096]{1,0:T(8,128)(2,1)S(1)}, u32[]{:S(2)}, u32[]{:S(2)}) collective-permute-start(bf16[16,4096]{1,0:T(8,128)(2,1)S(1)} %collective-permute-done.26.refs_1_), channel_id=1, source_target_pairs={{0,1},{1,0},{2,3},{3,2},{4,5},{5,4},{6,7},{7,6},{8,9},{9,8},{10,11... | collective-permute-start | bytes 393224 | tf_op jit(solution)/shard_map/ppermute | solution.py:229
  61.6 23.8 %collective-permute-start.20 = (bf16[16,4096]{1,0:T(8,128)(2,1)S(1)}, bf16[16,4096]{1,0:T(8,128)(2,1)S(1)}, u32[]{:S(2)}, u32[]{:S(2)}) collective-permute-start(bf16[16,4096]{1,0:T(8,128)(2,1)S(1)} %collective-permute-done.18.refs_0_), channel_id=1, source_target_pairs={{0,1},{1,0},{2,3},{3,2},{4,5},{5,4},{6,7},{7,6},{8,9},{9,8},{10,11... | collective-permute-start | bytes 393224 | tf_op jit(solution)/shard_map/ppermute | solution.py:229
  71.6 21.9 %collective-permute-start.13 = (bf16[16,4096]{1,0:T(8,128)(2,1)S(1)}, bf16[16,4096]{1,0:T(8,128)(2,1)S(1)}, u32[]{:S(2)}, u32[]{:S(2)}) collective-permute-start(bf16[16,4096]{1,0:T(8,128)(2,1)S(1)} %collective-permute-done.11.refs_0_), channel_id=1, source_target_pairs={{0,1},{1,0},{2,3},{3,2},{4,5},{5,4},{6,7},{7,6},{8,9},{9,8},{10,11... | collective-permute-start | bytes 393224 | tf_op jit(solution)/shard_map/ppermute | solution.py:229
  71.7 27.3 %collective-permute-start.9 = (bf16[32,4096]{1,0:T(8,128)(2,1)S(1)}, bf16[32,4096]{1,0:T(8,128)(2,1)}, u32[]{:S(2)}, u32[]{:S(2)}) collective-permute-start(bf16[32,4096]{1,0:T(8,128)(2,1)S(1)} %get-tuple-element.11), channel_id=1, source_target_pairs={{0,1},{1,0},{2,3},{3,2},{4,5},{5,4},{6,7},{7,6},{8,9},{9,8},{10,11... | collective-permute-start | bytes 786440 | tf_op jit(solution)/shard_map/ppermute | solution.py:229
  72.2 13.3 %collective-permute-start.21 = (bf16[16,4096]{1,0:T(8,128)(2,1)S(1)}, bf16[16,4096]{1,0:T(8,128)(2,1)S(1)}, u32[]{:S(2)}, u32[]{:S(2)}) collective-permute-start(bf16[16,4096]{1,0:T(8,128)(2,1)S(1)} %collective-permute-done.19.refs_1_), channel_id=1, source_target_pairs={{0,1},{1,0},{2,3},{3,2},{4,5},{5,4},{6,7},{7,6},{8,9},{9,8},{10,11... | collective-permute-start | bytes 393224 | tf_op jit(solution)/shard_map/ppermute | solution.py:229
  72.3 21.4 %collective-permute-start.14 = (bf16[16,4096]{1,0:T(8,128)(2,1)S(1)}, bf16[16,4096]{1,0:T(8,128)(2,1)S(1)}, u32[]{:S(2)}, u32[]{:S(2)}) collective-permute-start(bf16[16,4096]{1,0:T(8,128)(2,1)S(1)} %collective-permute-done.12.refs_1_), channel_id=1, source_target_pairs={{0,1},{1,0},{2,3},{3,2},{4,5},{5,4},{6,7},{7,6},{8,9},{9,8},{10,11... | collective-permute-start | bytes 393224 | tf_op jit(solution)/shard_map/ppermute | solution.py:229
  85.3 30.3 %collective-permute-start.32 = (bf16[8,16,256]{2,1,0:T(8,128)(2,1)S(1)}, bf16[8,16,256]{2,1,0:T(8,128)(2,1)S(1)}, u32[]{:S(2)}, u32[]{:S(2)}) collective-permute-start(bf16[8,16,256]{2,1,0:T(8,128)(2,1)S(1)} %copy-done.10), channel_id=1, source_target_pairs={{0,1},{1,0},{2,3},{3,2},{4,5},{5,4},{6,7},{7,6},{8,9},{9,8},{10,11... | collective-permute-start | bytes 196616 | tf_op jit(solution)/shard_map/ppermute | solution.py:279
  85.5 14.9 %collective-permute-start.29 = (bf16[32,4096]{1,0:T(8,128)(2,1)S(1)}, bf16[32,4096]{1,0:T(8,128)(2,1)S(1)}, u32[]{:S(2)}, u32[]{:S(2)}) collective-permute-start(bf16[32,4096]{1,0:T(8,128)(2,1)S(1)} %get-tuple-element.17), channel_id=1, source_target_pairs={{0,1},{1,0},{2,3},{3,2},{4,5},{5,4},{6,7},{7,6},{8,9},{9,8},{10,11... | collective-permute-start | bytes 786440 | tf_op jit(solution)/shard_map/ppermute | solution.py:229
  93.5 8.6 %collective-permute-start.22 = (bf16[32,4096]{1,0:T(8,128)(2,1)S(1)}, bf16[32,4096]{1,0:T(8,128)(2,1)S(1)}, u32[]{:S(2)}, u32[]{:S(2)}) collective-permute-start(bf16[32,4096]{1,0:T(8,128)(2,1)S(1)} %get-tuple-element.15), channel_id=1, source_target_pairs={{0,1},{1,0},{2,3},{3,2},{4,5},{5,4},{6,7},{7,6},{8,9},{9,8},{10,11... | collective-permute-start | bytes 786440 | tf_op jit(solution)/shard_map/ppermute | solution.py:229
  99.9 16.6 %collective-permute-start.10 = (bf16[16,4096]{1,0:T(8,128)(2,1)S(1)}, bf16[16,4096]{1,0:T(8,128)(2,1)S(1)}, u32[]{:S(2)}, u32[]{:S(2)}) collective-permute-start(bf16[16,4096]{1,0:T(8,128)(2,1)S(1)} %add_convert_fusion.6), channel_id=1, source_target_pairs={{0,2},{1,3},{2,0},{3,1},{4,6},{5,7},{6,4},{7,5},{8,10},{9,11},{10,... | collective-permute-start | bytes 393224 | tf_op jit(solution)/shard_map/ppermute | solution.py:229
  100.5 8.7 %collective-permute-start.30 = (bf16[16,4096]{1,0:T(8,128)(2,1)S(1)}, bf16[16,4096]{1,0:T(8,128)(2,1)S(1)}, u32[]{:S(2)}, u32[]{:S(2)}) collective-permute-start(bf16[16,4096]{1,0:T(8,128)(2,1)S(1)} %add_convert_fusion.1), channel_id=1, source_target_pairs={{0,2},{1,3},{2,0},{3,1},{4,6},{5,7},{6,4},{7,5},{8,10},{9,11},{10,... | collective-permute-start | bytes 393224 | tf_op jit(solution)/shard_map/ppermute | solution.py:229
  102.2 10.0 %collective-permute-start.23 = (bf16[16,4096]{1,0:T(8,128)(2,1)S(1)}, bf16[16,4096]{1,0:T(8,128)(2,1)S(1)}, u32[]{:S(2)}, u32[]{:S(2)}) collective-permute-start(bf16[16,4096]{1,0:T(8,128)(2,1)S(1)} %add_convert_fusion.3), channel_id=1, source_target_pairs={{0,2},{1,3},{2,0},{3,1},{4,6},{5,7},{6,4},{7,5},{8,10},{9,11},{10,... | collective-permute-start | bytes 393224 | tf_op jit(solution)/shard_map/ppermute | solution.py:229
  102.7 12.1 %collective-permute-start.16 = (bf16[16,4096]{1,0:T(8,128)(2,1)S(1)}, bf16[16,4096]{1,0:T(8,128)(2,1)S(1)}, u32[]{:S(2)}, u32[]{:S(2)}) collective-permute-start(bf16[16,4096]{1,0:T(8,128)(2,1)S(1)} %add_convert_fusion.5), channel_id=1, source_target_pairs={{0,2},{1,3},{2,0},{3,1},{4,6},{5,7},{6,4},{7,5},{8,10},{9,11},{10,... | collective-permute-start | bytes 393224 | tf_op jit(solution)/shard_map/ppermute | solution.py:229
  112.2 10.4 %collective-permute-start.24 = (bf16[16,4096]{1,0:T(8,128)(2,1)S(1)}, bf16[16,4096]{1,0:T(8,128)(2,1)S(1)}, u32[]{:S(2)}, u32[]{:S(2)}) collective-permute-start(bf16[16,4096]{1,0:T(8,128)(2,1)S(1)} %add_convert_fusion.2), channel_id=1, source_target_pairs={{0,8},{4,12},{8,0},{12,4},{1,9},{5,13},{9,1},{13,5},{2,10},{6,14},... | collective-permute-start | bytes 393224 | tf_op jit(solution)/shard_map/ppermute | solution.py:232
  (22 other events, 192.7 us)

commit v3 on v2

--- a/solution.py
+++ b/solution.py
@@ -35,77 +35,193 @@
 
 
 TRANSPOSED = (((1,), (1,)), ((), ()))
-CHUNKS = 4
+WHOLE = pl.BlockSpec(memory_space=pltpu.VMEM)
+ANYWHERE = pl.BlockSpec(memory_space=pl.ANY)
+SCALARS = pl.BlockSpec(memory_space=pltpu.SMEM)
+COLUMNS = 1024
+ROWS = 256
+VMEM_LIMIT = 16 * 2**20
+
+
+def hold_kernel(*refs):
+    count = (len(refs) - 2) // 2
+    sources, held, sem = refs[:count], refs[count + 1 : -1], refs[-1]
+    copies = [
+        pltpu.make_async_copy(source, target, sem.at[i])
+        for i, (source, target) in enumerate(zip(sources, held))
+    ]
+    for copy in copies:
+        copy.start()
+    for copy in copies:
+        copy.wait()
+
+
+def hold_call(arrays, after):
+    size = sum(math.prod(array.shape) * 2 for array in arrays)
+    return pl.pallas_call(
+        hold_kernel,
+        out_shape=[jax.ShapeDtypeStruct(array.shape, array.dtype) for array in arrays],
+        in_specs=[ANYWHERE] * (len(arrays) + 1),
+        out_specs=[WHOLE] * len(arrays),
+        scratch_shapes=[pltpu.SemaphoreType.DMA((len(arrays),))],
+        compiler_params=pltpu.CompilerParams(vmem_limit_bytes=VMEM_LIMIT),
+        cost_estimate=pl.CostEstimate(flops=0, bytes_accessed=2 * size, transcendentals=0),
+        name="hold",
+    )(*arrays, after)
+
+
+def attend_kernel(ep_count, held, tokens, all_open, lens, place, counts, queries, *refs):
+    blocks = refs[:ep_count]
+    out_weight = refs[ep_count]
+    own_ref, *sent_refs = refs[ep_count + 1 : -2]
+    scores, projected = refs[-2:]
+    heads = queries.shape[1] // HD
+    ep_index = place[0]
+    block_index = place[1]
+    suffix = ep_count * tokens
+
+    own_start = jnp.int32(0)
+    for j in range(ep_count):
+        own_start = own_start + jnp.where(j < ep_index, lens[j], 0)
+    column = lax.broadcasted_iota(jnp.int32, (tokens, suffix), 1)
+    slot = column % tokens
+    query_position = own_start + lax.broadcasted_iota(jnp.int32, (tokens, suffix), 0)
+    seen = jnp.zeros((tokens, suffix), jnp.int32)
+    for step in range(ep_count):
+        source = ep_index ^ step
+        start = jnp.int32(0)
+        for j in range(ep_count):
+            start = start + jnp.where(j < source, lens[j], 0)
+        last = jnp.minimum(query_position - start, lens[source] - 1)
+        here = (column // tokens == step) & (slot <= last)
+        seen = seen + here.astype(jnp.int32)
+    bias = jnp.where(seen > 0, 0.0, MASKED)
+
+    suffix_keys = jnp.concatenate([block[held : held + tokens, :HD] for block in blocks], axis=0)
+    suffix_values = jnp.concatenate([block[held : held + tokens, HD:] for block in blocks], axis=0)
+    scale = math.log2(math.e) / math.sqrt(HD)
+    rows = min(ROWS, heads * tokens)
+    together = rows // tokens
+    attended = []
+    for first in range(0, heads, together):
+        grouped = jnp.concatenate(
+            [queries[:, h * HD : (h + 1) * HD] for h in range(first, first + together)], axis=0
+        )
+        highest = None
+        for step in range(ep_count):
+            part = scale * lax.dot_general(
+                grouped, blocks[step][:held, :HD], TRANSPOSED, preferred_element_type=jnp.float32
+            )
+            if not all_open:
+                entry = lax.broadcasted_iota(jnp.int32, part.shape, 1)
+                part = jnp.where(entry < counts[step], part, MASKED)
+            scores[:, step * held : (step + 1) * held] = part
+            top = jnp.max(part, axis=1, keepdims=True)
+            highest = top if highest is None else jnp.maximum(highest, top)
+        part = scale * lax.dot_general(
+            grouped, suffix_keys, TRANSPOSED, preferred_element_type=jnp.float32
+        )
+        part = part + jnp.concatenate([bias] * together, axis=0)
+        highest = jnp.maximum(highest, jnp.max(part, axis=1, keepdims=True))
+        part = jnp.exp2(part - highest)
+        total = jnp.sum(part, axis=1, keepdims=True)
+        mixed = jnp.dot(
+            part.astype(jnp.bfloat16), suffix_values, preferred_element_type=jnp.float32
+        )
+        for step in range(ep_count):
+            part = jnp.exp2(scores[:, step * held : (step + 1) * held] - highest)
+            total += jnp.sum(part, axis=1, keepdims=True)
+            mixed += jnp.dot(
+                part.astype(jnp.bfloat16),
+                blocks[step][:held, HD:],
+                preferred_element_type=jnp.float32,
+            )
+        mixed = (mixed / total).astype(jnp.bfloat16)
+        attended += [mixed[h * tokens : (h + 1) * tokens] for h in range(together)]
+    attended = jnp.concatenate(attended, axis=1)
+    for at in range(0, out_weight.shape[1], COLUMNS):
+        projected[:, at : at + COLUMNS] = jnp.dot(
+            attended, out_weight[:, at : at + COLUMNS], preferred_element_type=jnp.float32
+        )
+    count = own_ref.shape[0]
+    own_ref[...] = projected[pl.ds(pl.multiple_of(block_index * count, count), count), :]
+    for step, ref in enumerate(sent_refs, 1):
+        at = pl.multiple_of((block_index ^ step) * count, count)
+        ref[...] = projected[pl.ds(at, count), :].astype(jnp.bfloat16)
+
+
+def attend_call(lens, place, counts, queries, arrived, out_weight, held, blocks, all_open):
+    tokens = queries.shape[0]
+    ep_count = len(arrived)
+    model_width = out_weight.shape[1]
+    heads = queries.shape[1] // HD
+    row_count = tokens // blocks
+    keys = ep_count * (held + tokens)
+    return pl.pallas_call(
+        lambda *refs: attend_kernel(ep_count, held, tokens, all_open, *refs),
+        out_shape=[jax.ShapeDtypeStruct((row_count, model_width), jnp.float32)]
+        + [jax.ShapeDtypeStruct((row_count, model_width), jnp.bfloat16)] * (blocks - 1),
+        in_specs=[SCALARS] * 3 + [WHOLE] * (ep_count + 2),
+        out_specs=[WHOLE] * blocks,
+        scratch_shapes=[
+            pltpu.VMEM((min(ROWS, heads * tokens), ep_count * held), jnp.float32),
+            pltpu.VMEM((tokens, model_width), jnp.float32),
+        ],
+        compiler_params=pltpu.CompilerParams(vmem_limit_bytes=VMEM_LIMIT),
+        cost_estimate=pl.CostEstimate(
+            flops=4 * heads * tokens * keys * HD + 2 * tokens * heads * HD * model_width,
+            bytes_accessed=2 * heads * HD * model_width,
+            transcendentals=heads * tokens * keys,
+        ),
+        name="attend",
+    )(lens, place, counts, queries, *arrived, out_weight)
 
 
 def expert_kernel(count, *refs):
     row_refs = refs[:count]
-    weight_ref, gate_up, down_weight, kept_ref, sent_ref = refs[count : count + 5]
-    gate_up_held, down_held, gate_up_sem, down_sem = refs[count + 5 :]
-    width = gate_up_held.shape[-1]
-    first = [
-        pltpu.make_async_copy(
-            gate_up.at[0, :, :, pl.ds(i * width, width)], gate_up_held.at[i], gate_up_sem.at[i]
-        )
-        for i in range(CHUNKS)
-    ]
-    second = [
-        pltpu.make_async_copy(
-            down_weight.at[0, :, pl.ds(i * width, width)], down_held.at[i], down_sem.at[i]
-        )
-        for i in range(CHUNKS)
-    ]
-    for copy in first + second:
-        copy.start()
+    weight_ref, gate_up, down_weight = refs[count : count + 3]
+    kept_ref, sent_ref = refs[-2:]
+    model_width = kept_ref.shape[1]
     gate_part = up_part = 0.0
-    for i in range(CHUNKS):
-        rows = jnp.concatenate([ref[:, i * width : (i + 1) * width] for ref in row_refs], axis=0)
-        first[i].wait()
+    for at in range(0, model_width, COLUMNS):
+        rows = jnp.concatenate([ref[:, at : at + COLUMNS] for ref in row_refs], axis=0)
         gate_part += lax.dot_general(
-            rows, gate_up_held[i, 0], TRANSPOSED, preferred_element_type=jnp.float32
+            rows, gate_up[0, 0, :, at : at + COLUMNS], TRANSPOSED, preferred_element_type=jnp.float32
         )
         up_part += lax.dot_general(
-            rows, gate_up_held[i, 1], TRANSPOSED, preferred_element_type=jnp.float32
+            rows, gate_up[0, 1, :, at : at + COLUMNS], TRANSPOSED, preferred_element_type=jnp.float32
         )
     hidden = gate_part / (1.0 + jnp.exp(-gate_part)) * up_part
     hidden = (hidden * weight_ref[...]).astype(jnp.bfloat16)
     half = kept_ref.shape[0]
-    for i in range(CHUNKS):
-        second[i].wait()
-        out = jnp.dot(hidden, down_held[i], preferred_element_type=jnp.float32)
-        out = out.astype(jnp.bfloat16)
-        kept_ref[:, i * width : (i + 1) * width] = out[:half]
-        sent_ref[:, i * width : (i + 1) * width] = out[half:]
-
-
-def expert_call(have, row_weight, gate_up, down_weight):
+    for at in range(0, model_width, COLUMNS):
+        out = jnp.dot(
+            hidden, down_weight[0, :, at : at + COLUMNS], preferred_element_type=jnp.float32
+        ).astype(jnp.bfloat16)
+        kept_ref[:, at : at + COLUMNS] = out[:half]
+        sent_ref[:, at : at + COLUMNS] = out[half:]
+
+
+def expert_call(have, row_weight, gate_up, down_weight, after):
     if have[0].shape[0] % 16:
         have = [jnp.concatenate(have, axis=0)]
     tokens = sum(piece.shape[0] for piece in have)
     model_width = have[0].shape[1]
     hidden_units = down_weight.shape[1]
-    width = model_width // CHUNKS
-    whole = pl.BlockSpec(memory_space=pltpu.VMEM)
     half = jax.ShapeDtypeStruct((tokens // 2, model_width), jnp.bfloat16)
     return pl.pallas_call(
         lambda *refs: expert_kernel(len(have), *refs),
         out_shape=(half, half),
-        in_specs=[whole] * (len(have) + 1) + [pl.BlockSpec(memory_space=pl.ANY)] * 2,
-        out_specs=(whole, whole),
-        scratch_shapes=[
-            pltpu.VMEM((CHUNKS, 2, hidden_units, width), jnp.bfloat16),
-            pltpu.VMEM((CHUNKS, hidden_units, width), jnp.bfloat16),
-            pltpu.SemaphoreType.DMA((CHUNKS,)),
-            pltpu.SemaphoreType.DMA((CHUNKS,)),
-        ],
-        compiler_params=pltpu.CompilerParams(vmem_limit_bytes=24 * 2**20),
+        in_specs=[WHOLE] * (len(have) + 3) + [ANYWHERE] * len(after),
+        out_specs=(WHOLE, WHOLE),
+        compiler_params=pltpu.CompilerParams(vmem_limit_bytes=VMEM_LIMIT),
         cost_estimate=pl.CostEstimate(
             flops=6 * tokens * hidden_units * model_width,
             bytes_accessed=6 * hidden_units * model_width,
             transcendentals=tokens * hidden_units,
         ),
         name="experts",
-    )(*have, row_weight, gate_up, down_weight)
+    )(*have, row_weight, gate_up, down_weight, *after)
 
 
 def local(
@@ -171,41 +287,19 @@
         )
     sources = [ep_index ^ step for step in range(ep_count)]
 
-    starts = jnp.cumsum(span_lengths) - span_lengths
-    slots_here = jnp.arange(tokens, dtype=jnp.int32)
-    own_positions = starts[ep_index] + slots_here
-    own_filled = slots_here < span_lengths[ep_index]
+    held_out, held_gate_up, held_down = hold_call([out_weight, gate_up, down_weight], payload)
+    all_open = hits == HOLD_MOST * ep_count
     holder = hit_pages // pool_pages
-    keys = []
-    allowed = []
-    for source, block in zip(sources, arrived):
-        keys.append(block[: held + tokens])
-        count = jnp.sum((holder == source).astype(jnp.int32))
-        open_rows = jnp.arange(held, dtype=jnp.int32) < count * page_size
-        causal = (slots_here < span_lengths[source])[None, :] & (
-            (starts[source] + slots_here)[None, :] <= own_positions[:, None]
-        )
-        allowed += [jnp.broadcast_to(open_rows[None, :], (tokens, held)), causal]
-    keys = jnp.concatenate(keys, axis=0)
-    allowed = jnp.concatenate(allowed, axis=1)
-    grouped = queries.reshape(tokens, heads_local, HD)
-    scores = jnp.einsum(
-        "thd,kd->htk", grouped, keys[:, :HD], preferred_element_type=jnp.float32
-    ) * (1.0 / math.sqrt(HD))
-    scores = jnp.where(allowed[None], scores, MASKED)
-    attention_weights = jax.nn.softmax(scores, axis=-1).astype(jnp.bfloat16)
-    attended = jnp.einsum(
-        "htk,kd->thd", attention_weights, keys[:, HD:], preferred_element_type=jnp.float32
-    )
-    attended = attended.astype(jnp.bfloat16).reshape(tokens, heads_local * HD)
-    projected = jnp.dot(attended, out_weight, preferred_element_type=jnp.float32)
-
-    projected_rows = projected.astype(jnp.bfloat16)
-    heads_out = lax.dynamic_slice_in_dim(projected, block_index * row_count, row_count, 0)
-    for step in range(1, blocks):
-        sent = lax.dynamic_slice_in_dim(
-            projected_rows, (block_index ^ step) * row_count, row_count, 0
-        )
+    counts = jnp.sum(
+        (holder[None, :] == jnp.stack(sources)[:, None]).astype(jnp.int32) * page_size, axis=1
+    )
+    if all_open:
+        counts = jnp.zeros((1,), jnp.int32)
+    place = jnp.stack([ep_index, block_index]).astype(jnp.int32)
+    heads_out, *sent_rows = attend_call(
+        span_lengths, place, counts, queries, arrived, held_out, held, blocks, all_open
+    )
+    for step, sent in enumerate(sent_rows, 1):
         heads_out = heads_out + lax.ppermute(
             sent, ("kv", "tp"), [(i, i ^ step) for i in range(blocks)]
         ).astype(jnp.float32)
@@ -233,25 +327,36 @@
         value, "ep", [(i, i ^ step) for i in range(ep_count)]
     )
     bits = [1 << place for place in range(1, blocks.bit_length() - 1)]
-    mixture = resid_wide
+    haves = []
     for step in range(ep_count):
         have = [normed if step == 0 else across(normed, step)]
         for bit in bits + [1]:
             have += [exchange(piece, bit) for piece in have]
-        kept, sent = expert_call(have, row_weights[step], gate_up, down_weight)
+        haves.append(have)
+    mixture = resid_wide
+    given = []
+    finished = []
+    for step in range(ep_count):
+        after = given[step - 2 : step - 1] if step >= 2 else []
+        after = after + (finished[step - 3 : step - 2] if step >= 3 else [])
+        kept, sent = expert_call(haves[step], row_weights[step], held_gate_up, held_down, after)
         got = exchange(sent, 1)
         for bit in reversed(bits):
             half = kept.shape[0] // 2
             give = (kept[half:].astype(jnp.float32) + got[half:].astype(jnp.float32)).astype(
                 jnp.bfloat16
             )
+            if bit == bits[-1]:
+                given.append(give)
             kept = kept[:half].astype(jnp.float32) + got[:half].astype(jnp.float32)
             got = exchange(give, bit)
-        own = kept.astype(jnp.float32) + got.astype(jnp.float32)
+        own = (kept.astype(jnp.float32) + got.astype(jnp.float32)).astype(jnp.bfloat16)
+        finished.append(own)
         if step > 0:
-            own = across(own.astype(jnp.bfloat16), step).astype(jnp.float32)
-        mixture = mixture + own
-    rows_filled = lax.dynamic_slice_in_dim(own_filled, block_index * row_count, row_count, 0)
+            own = across(own, step)
+        mixture = mixture + own.astype(jnp.float32)
+    own_slots = block_index * row_count + jnp.arange(row_count, dtype=jnp.int32)
+    rows_filled = own_slots < span_lengths[ep_index]
     layer_out = jnp.where(rows_filled[:, None], mixture, 0.0).astype(jnp.bfloat16)
 
     own_most = 2 * (tokens // page_size)

time: 125 us -> 99.5 us (0.80)
  other arithmetic: 17.2 us -> 6.91 us
  matrix products: 7.85 us -> 0 us
  waiting for transfers between devices: 26.3 us -> 19.9 us
  Pallas kernels: 19.2 us -> 15.2 us
  starting transfers between devices: 28.1 us -> 31.7 us
  between operations: 3.83 us -> 1.14 us
  local copies, waits for them, and re-layouts: 21.8 us -> 24.1 us
    pallas_call x4, Pallas kernels: 19.2 us -> 10.6 us  [expert_call(): pl.pallas_call(lambda *refs: expert_kernel(len(have), *refs), out_shape=(...]
    dot_general x2 -> x0, matrix products: 6.77 us -> none  [the longest x1 4.99 us: local(): jnp.dot(attended, out_weight, preferred_element_type=jnp.float32)]
    ppermute x6, waiting for transfers between devices: 11.7 us -> 5.6 us  [local(): lax.ppermute(value, 'ep', [(i, i ^ step) for i in range(ep_count)])]
    pallas_call x0 -> x2, Pallas kernels: none -> 4.61 us  [the longest x1 3.4 us: attend_call(): pl.pallas_call(lambda *refs: attend_kernel(ep_count, held, tokens, all_op...]
    ppermute x20, starting transfers between devices: 9.46 us -> 12.4 us  [local(): lax.ppermute(value, ('kv', 'tp'), [(i, i ^ bit) for i in range(blocks)])]
    add x4 -> x0, other arithmetic: 2.43 us -> none  [local(): starts[source] + slots_here]
    unnamed x32 -> x25, local copies, waits for them, and re-layouts: 13 us -> 15.3 us
    reduce_sum x2 -> x0, other arithmetic: 2.13 us -> none  [local(): count = jnp.sum((holder == source).astype(jnp.int32))]
  transfers between devices with their start and end apart: 33 -> 33, of which waited for: 9 -> 8; matrix products, arithmetic and copies ran while one was open for 15% -> 10% of each run, Pallas kernels for 15% -> 12%
where the time goes in v3:
time: 99.5 us; the launch traced here: 99.1 us
  starting transfers between devices  31.7 us (32%)
  local copies, waits for them, and re-layouts  24.1 us (24%)
  waiting for transfers between devices  19.9 us (20%)
  Pallas kernels  15.2 us (15%)
  other arithmetic  6.91 us (7%)
  between operations  1.14 us (1%)
    unnamed x25, local copies, waits for them, and re-layouts  15.3 us
    ppermute x20, starting transfers between devices, local(): lax.ppermute(value, ('kv', 'tp'), [(i, i ^ bit) for i in range(blocks)])  12.4 us
    ppermute x6, starting transfers between devices, local(): lax.ppermute(value, 'ep', [(i, i ^ step) for i in range(ep_count)])  11.5 us
    pallas_call x4, Pallas kernels, expert_call(): pl.pallas_call(lambda *refs: expert_kernel(len(have), *refs), out_shape=(...  10.6 us
    ppermute x20, waiting for transfers between devices, local(): lax.ppermute(value, ('kv', 'tp'), [(i, i ^ bit) for i in range(blocks)])  8 us
    ppermute x3, waiting for transfers between devices, local(): lax.ppermute(sent, ('kv', 'tp'), [(i, i ^ step) for i in range(blocks)])  6.29 us
    ppermute x3, starting transfers between devices, local(): lax.ppermute(payload, 'ep', [(i, i ^ step) for i in range(ep_count)])  5.68 us
    ppermute x6, waiting for transfers between devices, local(): lax.ppermute(value, 'ep', [(i, i ^ step) for i in range(ep_count)])  5.6 us
  transfers between devices with their start and end apart: 33, of which 8 were waited for; matrix products, arithmetic and copies ran while one was open for 10% of the time, Pallas kernels for 12%

profile of v3, /device:TPU:0, one launch (start us, length us, event | category | flops | bytes accessed | tf_op | source)
XLA Modules:
  0.0 99.1 jit_solution(14884699795044966262)
XLA Ops:
  5.7 3.1 %collective-permute-start = (bf16[336,256]{1,0:T(8,128)(2,1)S(1)}, bf16[336,256]{1,0:T(8,128)(2,1)S(1)}, u32[]{:S(2)}, u32[]{:S(2)}) collective-permute-start(bf16[336,256]{1,0:T(8,128)(2,1)S(1)} %pad_maximum_fusion.refs_3_.refs_4_), channel_id=1, source_target_pairs={{0,4},{4,0},{8,12},{12,8},{1,5},{5,1},{9,13},{13,9},{2,6},{6,2},{1... | collective-permute-start | bytes 516104 | tf_op jit(solution)/shard_map/ppermute | solution.py:286
  8.8 2.6 %collective-permute-start.1 = (bf16[336,256]{1,0:T(8,128)(2,1)S(1)}, bf16[336,256]{1,0:T(8,128)(2,1)S(1)}, u32[]{:S(2)}, u32[]{:S(2)}) collective-permute-start(bf16[336,256]{1,0:T(8,128)(2,1)S(1)} %pad_maximum_fusion.refs_3_.refs_4_), channel_id=1, source_target_pairs={{0,8},{4,12},{8,0},{12,4},{1,9},{5,13},{9,1},{13,5},{2,10},{6,14},... | collective-permute-start | bytes 516104 | tf_op jit(solution)/shard_map/ppermute | solution.py:286
  15.8 3.4 %copy-done.6 = bf16[1024,4096]{1,0:T(8,128)(2,1)S(1)} copy-done((bf16[1024,4096]{1,0:T(8,128)(2,1)S(1)}, bf16[1024,4096]{1,0:T(8,128)(2,1)}, u32[]{:S(2)}) %copy-start.6) | copy-done | bytes 8388632
  19.1 2.8 %copy-done.7 = bf16[1,2,384,4096]{3,2,1,0:T(8,128)(2,1)S(1)} copy-done((bf16[1,2,384,4096]{3,2,1,0:T(8,128)(2,1)S(1)}, bf16[1,2,384,4096]{3,2,1,0:T(8,128)(2,1)}, u32[]{:S(2)}) %copy-start.7) | copy-done | bytes 6291480
  21.9 1.9 %copy-done.8 = bf16[1,384,4096]{2,1,0:T(8,128)(2,1)S(1)} copy-done((bf16[1,384,4096]{2,1,0:T(8,128)(2,1)S(1)}, bf16[1,384,4096]{2,1,0:T(8,128)(2,1)}, u32[]{:S(2)}) %copy-start.8) | copy-done | bytes 3145752
  25.1 1.7 %copy-done.4 = bf16[1,384,4096]{2,1,0:T(8,128)(2,1)} copy-done((bf16[1,384,4096]{2,1,0:T(8,128)(2,1)}, bf16[1,384,4096]{2,1,0:T(8,128)(2,1)S(1)}, u32[]{:S(2)}) %copy-start.4) | copy-done | bytes 3145752
  26.9 3.4 %attend.1 = (f32[16,4096]{1,0:T(8,128)S(1)}, bf16[16,4096]{1,0:T(8,128)(2,1)S(1)}, bf16[16,4096]{1,0:T(8,128)(2,1)S(1)}, bf16[16,4096]{1,0:T(8,128)(2,1)S(1)}) custom-call(s32[4]{0:T(128)S(1)} %copy-done.1, s32[2]{0:T(128)S(1)} %pad_add_fusion.refs_1_, s32[1]{0:T(128)} %constant.104.clone.1.refs_2_, bf16[64,1024]{1,0:T(8,128)(2,1)S(1)} %copy-done.9, ...), custom_call_target="tpu_custom_call" | custom-call | flops 872415232 | bytes 8388608 | tf_op jit(solution)/shard_map/attend/pallas_call | solution.py:160
  30.4 1.8 %collective-permute-start.4 = (bf16[16,4096]{1,0:T(8,128)(2,1)S(1)}, bf16[16,4096]{1,0:T(8,128)(2,1)S(1)}, u32[]{:S(2)}, u32[]{:S(2)}) collective-permute-start(bf16[16,4096]{1,0:T(8,128)(2,1)S(1)} %get-tuple-element.20), channel_id=1, source_target_pairs={{0,2},{1,3},{2,0},{3,1},{4,6},{5,7},{6,4},{7,5},{8,10},{9,11},{10,... | collective-permute-start | bytes 393224 | tf_op jit(solution)/shard_map/ppermute | solution.py:303
  32.3 4.4 %collective-permute-done.4 = bf16[16,4096]{1,0:T(8,128)(2,1)S(1)} collective-permute-done((bf16[16,4096]{1,0:T(8,128)(2,1)S(1)}, bf16[16,4096]{1,0:T(8,128)(2,1)S(1)}, u32[]{:S(2)}, u32[]{:S(2)}) %collective-permute-start.4) | collective-permute-done | bytes 131104 | tf_op jit(solution)/shard_map/ppermute | solution.py:303
  36.7 1.9 %collective-permute-done.5 = bf16[16,4096]{1,0:T(8,128)(2,1)S(1)} collective-permute-done((bf16[16,4096]{1,0:T(8,128)(2,1)S(1)}, bf16[16,4096]{1,0:T(8,128)(2,1)S(1)}, u32[]{:S(2)}, u32[]{:S(2)}) %collective-permute-start.5) | collective-permute-done | bytes 131104 | tf_op jit(solution)/shard_map/ppermute | solution.py:303
  39.9 1.8 %collective-permute-start.6 = (bf16[16,4096]{1,0:T(8,128)(2,1)S(1)}, bf16[16,4096]{1,0:T(8,128)(2,1)S(1)}, u32[]{:S(2)}, u32[]{:S(2)}) collective-permute-start(bf16[16,4096]{1,0:T(8,128)(2,1)S(1)} %fusion.2.refs_0_), channel_id=1, source_target_pairs={{0,2},{1,3},{2,0},{3,1},{4,6},{5,7},{6,4},{7,5},{8,10},{9,11},{10,... | collective-permute-start | bytes 393224 | tf_op jit(solution)/shard_map/ppermute | solution.py:323
  42.5 3.6 %collective-permute-start.18 = (bf16[16,4096]{1,0:T(8,128)(2,1)S(1)}, bf16[16,4096]{1,0:T(8,128)(2,1)S(1)}, u32[]{:S(2)}, u32[]{:S(2)}) collective-permute-start(bf16[16,4096]{1,0:T(8,128)(2,1)S(1)} %fusion.2.refs_0_), channel_id=1, source_target_pairs={{0,8},{4,12},{8,0},{12,4},{1,9},{5,13},{9,1},{13,5},{2,10},{6,14},... | collective-permute-start | bytes 393224 | tf_op jit(solution)/shard_map/ppermute | solution.py:326
  51.3 3.7 %collective-permute-start.25 = (bf16[16,4096]{1,0:T(8,128)(2,1)S(1)}, bf16[16,4096]{1,0:T(8,128)(2,1)S(1)}, u32[]{:S(2)}, u32[]{:S(2)}) collective-permute-start(bf16[16,4096]{1,0:T(8,128)(2,1)S(1)} %fusion.2.refs_0_), channel_id=1, source_target_pairs={{0,12},{4,8},{8,4},{12,0},{1,13},{5,9},{9,5},{13,1},{2,14},{6,10},... | collective-permute-start | bytes 393224 | tf_op jit(solution)/shard_map/ppermute | solution.py:326
  55.5 2.8 %copy-done.3 = bf16[1,2,384,4096]{3,2,1,0:T(8,128)(2,1)S(1)} copy-done((bf16[1,2,384,4096]{3,2,1,0:T(8,128)(2,1)S(1)}, bf16[1,2,384,4096]{3,2,1,0:T(8,128)(2,1)}, u32[]{:S(2)}) %copy-start.3) | copy-done | bytes 6291480
  58.3 1.9 %copy-done.5 = bf16[1,384,4096]{2,1,0:T(8,128)(2,1)S(1)} copy-done((bf16[1,384,4096]{2,1,0:T(8,128)(2,1)S(1)}, bf16[1,384,4096]{2,1,0:T(8,128)(2,1)}, u32[]{:S(2)}) %copy-start.5) | copy-done | bytes 3145752
  60.2 2.7 %experts.4 = (bf16[32,4096]{1,0:T(8,128)(2,1)S(1)}, bf16[32,4096]{1,0:T(8,128)(2,1)S(1)}) custom-call(bf16[16,4096]{1,0:T(8,128)(2,1)S(1)} %fusion.2.refs_0_, bf16[16,4096]{1,0:T(8,128)(2,1)S(1)} %collective-permute-done.6.refs_1_, bf16[16,4096]{1,0:T(8,128)(2,1)S(1)} %collective-permute-done.7.refs_2_, bf16[16,4096]{1,0:T(8,128)(2,1)S(1)} %collective-permute-done.8.refs_3_, ...), custom_call_target="tpu_custom_call" | custom-call | flops 603979776 | bytes 9437184 | tf_op jit(solution)/shard_map/experts/pallas_call | solution.py:212
  65.7 2.7 %experts.5 = (bf16[32,4096]{1,0:T(8,128)(2,1)S(1)}, bf16[32,4096]{1,0:T(8,128)(2,1)S(1)}) custom-call(bf16[16,4096]{1,0:T(8,128)(2,1)S(1)} %collective-permute-done.11.refs_0_, bf16[16,4096]{1,0:T(8,128)(2,1)S(1)} %collective-permute-done.12.refs_1_, bf16[16,4096]{1,0:T(8,128)(2,1)S(1)} %collective-permute-done.13.refs_2_, ...), custom_call_target="tpu_custom_call" | custom-call | flops 603979776 | bytes 9437184 | tf_op jit(solution)/shard_map/experts/pallas_call | solution.py:212
  69.7 1.5 %collective-permute-start.10 = (bf16[16,4096]{1,0:T(8,128)(2,1)S(1)}, bf16[16,4096]{1,0:T(8,128)(2,1)S(1)}, u32[]{:S(2)}, u32[]{:S(2)}) collective-permute-start(bf16[16,4096]{1,0:T(8,128)(2,1)S(1)} %add_convert_fusion.7.refs_7_), channel_id=1, source_target_pairs={{0,2},{1,3},{2,0},{3,1},{4,6},{5,7},{6,4},{7,5},{8,10},{9,11},{10,... | collective-permute-start | bytes 393224 | tf_op jit(solution)/shard_map/ppermute | solution.py:323
  71.2 2.7 %experts.6 = (bf16[32,4096]{1,0:T(8,128)(2,1)S(1)}, bf16[32,4096]{1,0:T(8,128)(2,1)S(1)}) custom-call(bf16[16,4096]{1,0:T(8,128)(2,1)S(1)} %collective-permute-done.18.refs_0_, bf16[16,4096]{1,0:T(8,128)(2,1)S(1)} %collective-permute-done.19.refs_1_, bf16[16,4096]{1,0:T(8,128)(2,1)S(1)} %collective-permute-done.20.refs_2_, ...), custom_call_target="tpu_custom_call" | custom-call | flops 603979776 | bytes 9437184 | tf_op jit(solution)/shard_map/experts/pallas_call | solution.py:212
  77.2 2.7 %experts.7 = (bf16[32,4096]{1,0:T(8,128)(2,1)S(1)}, bf16[32,4096]{1,0:T(8,128)(2,1)S(1)}) custom-call(bf16[16,4096]{1,0:T(8,128)(2,1)S(1)} %collective-permute-done.25.refs_0_, bf16[16,4096]{1,0:T(8,128)(2,1)S(1)} %collective-permute-done.26.refs_1_, bf16[16,4096]{1,0:T(8,128)(2,1)S(1)} %collective-permute-done.27.refs_2_, ...), custom_call_target="tpu_custom_call" | custom-call | flops 603979776 | bytes 9437184 | tf_op jit(solution)/shard_map/experts/pallas_call | solution.py:212
  80.9 1.6 %collective-permute-start.23 = (bf16[16,4096]{1,0:T(8,128)(2,1)S(1)}, bf16[16,4096]{1,0:T(8,128)(2,1)S(1)}, u32[]{:S(2)}, u32[]{:S(2)}) collective-permute-start(bf16[16,4096]{1,0:T(8,128)(2,1)S(1)} %add_convert_fusion.3), channel_id=1, source_target_pairs={{0,2},{1,3},{2,0},{3,1},{4,6},{5,7},{6,4},{7,5},{8,10},{9,11},{10,... | collective-permute-start | bytes 393224 | tf_op jit(solution)/shard_map/ppermute | solution.py:323
  83.1 4.3 %collective-permute-done.23 = bf16[16,4096]{1,0:T(8,128)(2,1)S(1)} collective-permute-done((bf16[16,4096]{1,0:T(8,128)(2,1)S(1)}, bf16[16,4096]{1,0:T(8,128)(2,1)S(1)}, u32[]{:S(2)}, u32[]{:S(2)}) %collective-permute-start.23) | collective-permute-done | bytes 131104 | tf_op jit(solution)/shard_map/ppermute | solution.py:323
  89.0 2.9 %collective-permute-start.31 = (bf16[16,4096]{1,0:T(8,128)(2,1)S(1)}, bf16[16,4096]{1,0:T(8,128)(2,1)S(1)}, u32[]{:S(2)}, u32[]{:S(2)}) collective-permute-start(bf16[16,4096]{1,0:T(8,128)(2,1)S(1)} %add_convert_fusion), channel_id=1, source_target_pairs={{0,12},{4,8},{8,4},{12,0},{1,13},{5,9},{9,5},{13,1},{2,14},{6,10},... | collective-permute-start | bytes 393224 | tf_op jit(solution)/shard_map/ppermute | solution.py:326
  92.7 5.6 %collective-permute-done.24 = bf16[16,4096]{1,0:T(8,128)(2,1)S(1)} collective-permute-done((bf16[16,4096]{1,0:T(8,128)(2,1)S(1)}, bf16[16,4096]{1,0:T(8,128)(2,1)S(1)}, u32[]{:S(2)}, u32[]{:S(2)}) %collective-permute-start.24) | collective-permute-done | bytes 131104 | tf_op jit(solution)/shard_map/ppermute | solution.py:326
  (144 shorter events, 31.0 us)
Async XLA Ops:
  5.7 21.1 %collective-permute-start = (bf16[336,256]{1,0:T(8,128)(2,1)S(1)}, bf16[336,256]{1,0:T(8,128)(2,1)S(1)}, u32[]{:S(2)}, u32[]{:S(2)}) collective-permute-start(bf16[336,256]{1,0:T(8,128)(2,1)S(1)} %pad_maximum_fusion.refs_3_.refs_4_), channel_id=1, source_target_pairs={{0,4},{4,0},{8,12},{12,8},{1,5},{5,1},{9,13},{13,9},{2,6},{6,2},{1... | collective-permute-start | bytes 516104 | tf_op jit(solution)/shard_map/ppermute | solution.py:286
  8.8 18.0 %collective-permute-start.1 = (bf16[336,256]{1,0:T(8,128)(2,1)S(1)}, bf16[336,256]{1,0:T(8,128)(2,1)S(1)}, u32[]{:S(2)}, u32[]{:S(2)}) collective-permute-start(bf16[336,256]{1,0:T(8,128)(2,1)S(1)} %pad_maximum_fusion.refs_3_.refs_4_), channel_id=1, source_target_pairs={{0,8},{4,12},{8,0},{12,4},{1,9},{5,13},{9,1},{13,5},{2,10},{6,14},... | collective-permute-start | bytes 516104 | tf_op jit(solution)/shard_map/ppermute | solution.py:286
  11.4 15.4 %collective-permute-start.2 = (bf16[336,256]{1,0:T(8,128)(2,1)S(1)}, bf16[336,256]{1,0:T(8,128)(2,1)S(1)}, u32[]{:S(2)}, u32[]{:S(2)}) collective-permute-start(bf16[336,256]{1,0:T(8,128)(2,1)S(1)} %pad_maximum_fusion.refs_3_.refs_4_), channel_id=1, source_target_pairs={{0,12},{4,8},{8,4},{12,0},{1,13},{5,9},{9,5},{13,1},{2,14},{6,10},... | collective-permute-start | bytes 516104 | tf_op jit(solution)/shard_map/ppermute | solution.py:286
  30.4 6.4 %collective-permute-start.4 = (bf16[16,4096]{1,0:T(8,128)(2,1)S(1)}, bf16[16,4096]{1,0:T(8,128)(2,1)S(1)}, u32[]{:S(2)}, u32[]{:S(2)}) collective-permute-start(bf16[16,4096]{1,0:T(8,128)(2,1)S(1)} %get-tuple-element.20), channel_id=1, source_target_pairs={{0,2},{1,3},{2,0},{3,1},{4,6},{5,7},{6,4},{7,5},{8,10},{9,11},{10,... | collective-permute-start | bytes 393224 | tf_op jit(solution)/shard_map/ppermute | solution.py:303
  32.1 6.5 %collective-permute-start.5 = (bf16[16,4096]{1,0:T(8,128)(2,1)S(1)}, bf16[16,4096]{1,0:T(8,128)(2,1)S(1)}, u32[]{:S(2)}, u32[]{:S(2)}) collective-permute-start(bf16[16,4096]{1,0:T(8,128)(2,1)S(1)} %get-tuple-element.21), channel_id=1, source_target_pairs={{0,3},{1,2},{2,1},{3,0},{4,7},{5,6},{6,5},{7,4},{8,11},{9,10},{10,... | collective-permute-start | bytes 393224 | tf_op jit(solution)/shard_map/ppermute | solution.py:303
  39.9 6.2 %collective-permute-start.6 = (bf16[16,4096]{1,0:T(8,128)(2,1)S(1)}, bf16[16,4096]{1,0:T(8,128)(2,1)S(1)}, u32[]{:S(2)}, u32[]{:S(2)}) collective-permute-start(bf16[16,4096]{1,0:T(8,128)(2,1)S(1)} %fusion.2.refs_0_), channel_id=1, source_target_pairs={{0,2},{1,3},{2,0},{3,1},{4,6},{5,7},{6,4},{7,5},{8,10},{9,11},{10,... | collective-permute-start | bytes 393224 | tf_op jit(solution)/shard_map/ppermute | solution.py:323
  41.7 7.8 %collective-permute-start.11 = (bf16[16,4096]{1,0:T(8,128)(2,1)S(1)}, bf16[16,4096]{1,0:T(8,128)(2,1)S(1)}, u32[]{:S(2)}, u32[]{:S(2)}) collective-permute-start(bf16[16,4096]{1,0:T(8,128)(2,1)S(1)} %fusion.2.refs_0_), channel_id=1, source_target_pairs={{0,4},{4,0},{8,12},{12,8},{1,5},{5,1},{9,13},{13,9},{2,6},{6,2},{1... | collective-permute-start | bytes 393224 | tf_op jit(solution)/shard_map/ppermute | solution.py:326
  42.4 12.5 %collective-permute-start.7 = (bf16[16,4096]{1,0:T(8,128)(2,1)S(1)}, bf16[16,4096]{1,0:T(8,128)(2,1)S(1)}, u32[]{:S(2)}, u32[]{:S(2)}) collective-permute-start(bf16[16,4096]{1,0:T(8,128)(2,1)S(1)} %fusion.2.refs_0_), channel_id=1, source_target_pairs={{0,1},{1,0},{2,3},{3,2},{4,5},{5,4},{6,7},{7,6},{8,9},{9,8},{10,11... | collective-permute-start | bytes 393224 | tf_op jit(solution)/shard_map/ppermute | solution.py:323
  42.5 12.5 %collective-permute-start.18 = (bf16[16,4096]{1,0:T(8,128)(2,1)S(1)}, bf16[16,4096]{1,0:T(8,128)(2,1)S(1)}, u32[]{:S(2)}, u32[]{:S(2)}) collective-permute-start(bf16[16,4096]{1,0:T(8,128)(2,1)S(1)} %fusion.2.refs_0_), channel_id=1, source_target_pairs={{0,8},{4,12},{8,0},{12,4},{1,9},{5,13},{9,1},{13,5},{2,10},{6,14},... | collective-permute-start | bytes 393224 | tf_op jit(solution)/shard_map/ppermute | solution.py:326
  46.0 9.5 %collective-permute-start.8 = (bf16[16,4096]{1,0:T(8,128)(2,1)S(1)}, bf16[16,4096]{1,0:T(8,128)(2,1)S(1)}, u32[]{:S(2)}, u32[]{:S(2)}) collective-permute-start(bf16[16,4096]{1,0:T(8,128)(2,1)S(1)} %collective-permute-done.6.refs_1_), channel_id=1, source_target_pairs={{0,1},{1,0},{2,3},{3,2},{4,5},{5,4},{6,7},{7,6},{8,9},{9,8},{10,11... | collective-permute-start | bytes 393224 | tf_op jit(solution)/shard_map/ppermute | solution.py:323
  49.5 13.6 %collective-permute-start.12 = (bf16[16,4096]{1,0:T(8,128)(2,1)S(1)}, bf16[16,4096]{1,0:T(8,128)(2,1)S(1)}, u32[]{:S(2)}, u32[]{:S(2)}) collective-permute-start(bf16[16,4096]{1,0:T(8,128)(2,1)S(1)} %collective-permute-done.11.refs_0_), channel_id=1, source_target_pairs={{0,2},{1,3},{2,0},{3,1},{4,6},{5,7},{6,4},{7,5},{8,10},{9,11},{10,... | collective-permute-start | bytes 393224 | tf_op jit(solution)/shard_map/ppermute | solution.py:323
  51.3 12.3 %collective-permute-start.25 = (bf16[16,4096]{1,0:T(8,128)(2,1)S(1)}, bf16[16,4096]{1,0:T(8,128)(2,1)S(1)}, u32[]{:S(2)}, u32[]{:S(2)}) collective-permute-start(bf16[16,4096]{1,0:T(8,128)(2,1)S(1)} %fusion.2.refs_0_), channel_id=1, source_target_pairs={{0,12},{4,8},{8,4},{12,0},{1,13},{5,9},{9,5},{13,1},{2,14},{6,10},... | collective-permute-start | bytes 393224 | tf_op jit(solution)/shard_map/ppermute | solution.py:326
  54.9 8.9 %collective-permute-start.13 = (bf16[16,4096]{1,0:T(8,128)(2,1)S(1)}, bf16[16,4096]{1,0:T(8,128)(2,1)S(1)}, u32[]{:S(2)}, u32[]{:S(2)}) collective-permute-start(bf16[16,4096]{1,0:T(8,128)(2,1)S(1)} %collective-permute-done.11.refs_0_), channel_id=1, source_target_pairs={{0,1},{1,0},{2,3},{3,2},{4,5},{5,4},{6,7},{7,6},{8,9},{9,8},{10,11... | collective-permute-start | bytes 393224 | tf_op jit(solution)/shard_map/ppermute | solution.py:323
  54.9 9.2 %collective-permute-start.19 = (bf16[16,4096]{1,0:T(8,128)(2,1)S(1)}, bf16[16,4096]{1,0:T(8,128)(2,1)S(1)}, u32[]{:S(2)}, u32[]{:S(2)}) collective-permute-start(bf16[16,4096]{1,0:T(8,128)(2,1)S(1)} %collective-permute-done.18.refs_0_), channel_id=1, source_target_pairs={{0,2},{1,3},{2,0},{3,1},{4,6},{5,7},{6,4},{7,5},{8,10},{9,11},{10,... | collective-permute-start | bytes 393224 | tf_op jit(solution)/shard_map/ppermute | solution.py:323
  63.6 28.2 %collective-permute-start.32 = (bf16[8,16,256]{2,1,0:T(8,128)(2,1)S(1)}, bf16[8,16,256]{2,1,0:T(8,128)(2,1)S(1)}, u32[]{:S(2)}, u32[]{:S(2)}) collective-permute-start(bf16[8,16,256]{2,1,0:T(8,128)(2,1)S(1)} %broadcast_select_fusion), channel_id=1, source_target_pairs={{0,1},{1,0},{2,3},{3,2},{4,5},{5,4},{6,7},{7,6},{8,9},{9,8},{10,11... | collective-permute-start | bytes 196616 | tf_op jit(solution)/shard_map/ppermute | solution.py:384
  68.9 8.2 %collective-permute-start.27 = (bf16[16,4096]{1,0:T(8,128)(2,1)S(1)}, bf16[16,4096]{1,0:T(8,128)(2,1)S(1)}, u32[]{:S(2)}, u32[]{:S(2)}) collective-permute-start(bf16[16,4096]{1,0:T(8,128)(2,1)S(1)} %collective-permute-done.25.refs_0_), channel_id=1, source_target_pairs={{0,1},{1,0},{2,3},{3,2},{4,5},{5,4},{6,7},{7,6},{8,9},{9,8},{10,11... | collective-permute-start | bytes 393224 | tf_op jit(solution)/shard_map/ppermute | solution.py:323
  69.7 7.5 %collective-permute-start.28 = (bf16[16,4096]{1,0:T(8,128)(2,1)S(1)}, bf16[16,4096]{1,0:T(8,128)(2,1)S(1)}, u32[]{:S(2)}, u32[]{:S(2)}) collective-permute-start(bf16[16,4096]{1,0:T(8,128)(2,1)S(1)} %collective-permute-done.26.refs_1_), channel_id=1, source_target_pairs={{0,1},{1,0},{2,3},{3,2},{4,5},{5,4},{6,7},{7,6},{8,9},{9,8},{10,11... | collective-permute-start | bytes 393224 | tf_op jit(solution)/shard_map/ppermute | solution.py:323
  69.7 5.9 %collective-permute-start.10 = (bf16[16,4096]{1,0:T(8,128)(2,1)S(1)}, bf16[16,4096]{1,0:T(8,128)(2,1)S(1)}, u32[]{:S(2)}, u32[]{:S(2)}) collective-permute-start(bf16[16,4096]{1,0:T(8,128)(2,1)S(1)} %add_convert_fusion.7.refs_7_), channel_id=1, source_target_pairs={{0,2},{1,3},{2,0},{3,1},{4,6},{5,7},{6,4},{7,5},{8,10},{9,11},{10,... | collective-permute-start | bytes 393224 | tf_op jit(solution)/shard_map/ppermute | solution.py:323
  73.9 7.0 %collective-permute-start.22 = (bf16[32,4096]{1,0:T(8,128)(2,1)S(1)}, bf16[32,4096]{1,0:T(8,128)(2,1)S(1)}, u32[]{:S(2)}, u32[]{:S(2)}) collective-permute-start(bf16[32,4096]{1,0:T(8,128)(2,1)S(1)} %get-tuple-element.29), channel_id=1, source_target_pairs={{0,1},{1,0},{2,3},{3,2},{4,5},{5,4},{6,7},{7,6},{8,9},{9,8},{10,11... | collective-permute-start | bytes 786440 | tf_op jit(solution)/shard_map/ppermute | solution.py:323
  80.8 11.9 %collective-permute-start.17 = (bf16[16,4096]{1,0:T(8,128)(2,1)S(1)}, bf16[16,4096]{1,0:T(8,128)(2,1)S(1)}, u32[]{:S(2)}, u32[]{:S(2)}) collective-permute-start(bf16[16,4096]{1,0:T(8,128)(2,1)S(1)} %add_convert_fusion.4), channel_id=1, source_target_pairs={{0,4},{4,0},{8,12},{12,8},{1,5},{5,1},{9,13},{13,9},{2,6},{6,2},{1... | collective-permute-start | bytes 393224 | tf_op jit(solution)/shard_map/ppermute | solution.py:326
  80.9 6.5 %collective-permute-start.23 = (bf16[16,4096]{1,0:T(8,128)(2,1)S(1)}, bf16[16,4096]{1,0:T(8,128)(2,1)S(1)}, u32[]{:S(2)}, u32[]{:S(2)}) collective-permute-start(bf16[16,4096]{1,0:T(8,128)(2,1)S(1)} %add_convert_fusion.3), channel_id=1, source_target_pairs={{0,2},{1,3},{2,0},{3,1},{4,6},{5,7},{6,4},{7,5},{8,10},{9,11},{10,... | collective-permute-start | bytes 393224 | tf_op jit(solution)/shard_map/ppermute | solution.py:323
  82.5 6.4 %collective-permute-start.30 = (bf16[16,4096]{1,0:T(8,128)(2,1)S(1)}, bf16[16,4096]{1,0:T(8,128)(2,1)S(1)}, u32[]{:S(2)}, u32[]{:S(2)}) collective-permute-start(bf16[16,4096]{1,0:T(8,128)(2,1)S(1)} %add_convert_fusion.1), channel_id=1, source_target_pairs={{0,2},{1,3},{2,0},{3,1},{4,6},{5,7},{6,4},{7,5},{8,10},{9,11},{10,... | collective-permute-start | bytes 393224 | tf_op jit(solution)/shard_map/ppermute | solution.py:323
  87.5 10.9 %collective-permute-start.24 = (bf16[16,4096]{1,0:T(8,128)(2,1)S(1)}, bf16[16,4096]{1,0:T(8,128)(2,1)S(1)}, u32[]{:S(2)}, u32[]{:S(2)}) collective-permute-start(bf16[16,4096]{1,0:T(8,128)(2,1)S(1)} %add_convert_fusion.2), channel_id=1, source_target_pairs={{0,8},{4,12},{8,0},{12,4},{1,9},{5,13},{9,1},{13,5},{2,10},{6,14},... | collective-permute-start | bytes 393224 | tf_op jit(solution)/shard_map/ppermute | solution.py:326
  89.0 9.4 %collective-permute-start.31 = (bf16[16,4096]{1,0:T(8,128)(2,1)S(1)}, bf16[16,4096]{1,0:T(8,128)(2,1)S(1)}, u32[]{:S(2)}, u32[]{:S(2)}) collective-permute-start(bf16[16,4096]{1,0:T(8,128)(2,1)S(1)} %add_convert_fusion), channel_id=1, source_target_pairs={{0,12},{4,8},{8,4},{12,0},{1,13},{5,9},{9,5},{13,1},{2,14},{6,10},... | collective-permute-start | bytes 393224 | tf_op jit(solution)/shard_map/ppermute | solution.py:326
  (20 other events, 76.9 us)

commit v4 on v3

--- a/solution.py
+++ b/solution.py
@@ -41,6 +41,7 @@
 COLUMNS = 1024
 ROWS = 256
 VMEM_LIMIT = 16 * 2**20
+LITTLE = pl.CostEstimate(flops=1024, bytes_accessed=1024, transcendentals=0)
 
 
 def hold_kernel(*refs):
@@ -57,7 +58,6 @@
 
 
 def hold_call(arrays, after):
-    size = sum(math.prod(array.shape) * 2 for array in arrays)
     return pl.pallas_call(
         hold_kernel,
         out_shape=[jax.ShapeDtypeStruct(array.shape, array.dtype) for array in arrays],
@@ -65,7 +65,7 @@
         out_specs=[WHOLE] * len(arrays),
         scratch_shapes=[pltpu.SemaphoreType.DMA((len(arrays),))],
         compiler_params=pltpu.CompilerParams(vmem_limit_bytes=VMEM_LIMIT),
-        cost_estimate=pl.CostEstimate(flops=0, bytes_accessed=2 * size, transcendentals=0),
+        cost_estimate=LITTLE,
         name="hold",
     )(*arrays, after)
 
@@ -156,7 +156,6 @@
     model_width = out_weight.shape[1]
     heads = queries.shape[1] // HD
     row_count = tokens // blocks
-    keys = ep_count * (held + tokens)
     return pl.pallas_call(
         lambda *refs: attend_kernel(ep_count, held, tokens, all_open, *refs),
         out_shape=[jax.ShapeDtypeStruct((row_count, model_width), jnp.float32)]
@@ -168,19 +167,29 @@
             pltpu.VMEM((tokens, model_width), jnp.float32),
         ],
         compiler_params=pltpu.CompilerParams(vmem_limit_bytes=VMEM_LIMIT),
-        cost_estimate=pl.CostEstimate(
-            flops=4 * heads * tokens * keys * HD + 2 * tokens * heads * HD * model_width,
-            bytes_accessed=2 * heads * HD * model_width,
-            transcendentals=heads * tokens * keys,
-        ),
+        cost_estimate=LITTLE,
         name="attend",
     )(lens, place, counts, queries, *arrived, out_weight)
 
 
-def expert_kernel(count, *refs):
+def expert_kernel(count, ep_count, blocks, weight_at, place, payload, *refs):
     row_refs = refs[:count]
-    weight_ref, gate_up, down_weight = refs[count : count + 3]
+    gate_up, down_weight = refs[count : count + 2]
     kept_ref, sent_ref = refs[-2:]
+    tokens = 2 * kept_ref.shape[0]
+    row_count = tokens // blocks
+
+    parts = payload[weight_at:, :].astype(jnp.float32)
+    part_row = lax.broadcasted_iota(jnp.int32, parts.shape, 0)
+    chosen = (part_row % ep_count == place[0]) & (part_row < 3 * ep_count)
+    by_token = jnp.sum(jnp.where(chosen, parts, 0.0), axis=0, keepdims=True)
+    row = lax.broadcasted_iota(jnp.int32, (tokens, parts.shape[1]), 0)
+    token = row % row_count
+    for spot, piece in enumerate(piece_order(blocks)):
+        token = token + jnp.where(row // row_count == spot, (place[1] ^ piece) * row_count, 0)
+    here = lax.broadcasted_iota(jnp.int32, (tokens, parts.shape[1]), 1) == token
+    row_weight = jnp.sum(jnp.where(here, by_token, 0.0), axis=1, keepdims=True)
+
     model_width = kept_ref.shape[1]
     gate_part = up_part = 0.0
     for at in range(0, model_width, COLUMNS):
@@ -192,7 +201,7 @@
             rows, gate_up[0, 1, :, at : at + COLUMNS], TRANSPOSED, preferred_element_type=jnp.float32
         )
     hidden = gate_part / (1.0 + jnp.exp(-gate_part)) * up_part
-    hidden = (hidden * weight_ref[...]).astype(jnp.bfloat16)
+    hidden = (hidden * row_weight).astype(jnp.bfloat16)
     half = kept_ref.shape[0]
     for at in range(0, model_width, COLUMNS):
         out = jnp.dot(
@@ -202,7 +211,7 @@
         sent_ref[:, at : at + COLUMNS] = out[half:]
 
 
-def expert_call(have, row_weight, gate_up, down_weight, after):
+def expert_call(place, payload, have, gate_up, down_weight, after, ep_count, blocks, weight_at):
     if have[0].shape[0] % 16:
         have = [jnp.concatenate(have, axis=0)]
     tokens = sum(piece.shape[0] for piece in have)
@@ -210,18 +219,14 @@
     hidden_units = down_weight.shape[1]
     half = jax.ShapeDtypeStruct((tokens // 2, model_width), jnp.bfloat16)
     return pl.pallas_call(
-        lambda *refs: expert_kernel(len(have), *refs),
+        lambda *refs: expert_kernel(len(have), ep_count, blocks, weight_at, *refs),
         out_shape=(half, half),
-        in_specs=[WHOLE] * (len(have) + 3) + [ANYWHERE] * len(after),
+        in_specs=[SCALARS] + [WHOLE] * (len(have) + 3) + [ANYWHERE] * len(after),
         out_specs=(WHOLE, WHOLE),
         compiler_params=pltpu.CompilerParams(vmem_limit_bytes=VMEM_LIMIT),
-        cost_estimate=pl.CostEstimate(
-            flops=6 * tokens * hidden_units * model_width,
-            bytes_accessed=6 * hidden_units * model_width,
-            transcendentals=tokens * hidden_units,
-        ),
+        cost_estimate=LITTLE,
         name="experts",
-    )(*have, row_weight, gate_up, down_weight, *after)
+    )(place, payload, *have, gate_up, down_weight, *after)
 
 
 def local(
@@ -276,9 +281,11 @@
         ),
         axis=1,
     )
-    weight_part = jnp.stack(three_parts(by_expert.T)).reshape(-1, 2 * HD)
+    weight_part = jnp.concatenate(three_parts(by_expert.T), axis=0)
     weight_rows = weight_part.shape[0]
-    weight_part = jnp.pad(weight_part, ((0, -weight_rows % WEIGHT_ROWS), (0, 0)))
+    weight_part = jnp.pad(
+        weight_part, ((0, -weight_rows % WEIGHT_ROWS), (0, 2 * HD - weight_part.shape[1]))
+    )
     payload = jnp.concatenate([own_pages, own_suffix, weight_part], axis=0)
     arrived = [payload]
     for step in range(1, ep_count):
@@ -287,7 +294,7 @@
         )
     sources = [ep_index ^ step for step in range(ep_count)]
 
-    held_out, held_gate_up, held_down = hold_call([out_weight, gate_up, down_weight], payload)
+    held_out = hold_call([out_weight], payload)[0]
     all_open = hits == HOLD_MOST * ep_count
     holder = hit_pages // pool_pages
     counts = jnp.sum(
@@ -312,14 +319,6 @@
         * norm_gain
     ).astype(jnp.bfloat16)
 
-    pieces = [block_index ^ piece for piece in piece_order(blocks)]
-    pieces = jnp.stack(pieces)
-    row_weights = []
-    for block in arrived:
-        parts = block[held + tokens : held + tokens + weight_rows].astype(jnp.float32)
-        parts = jnp.sum(parts.reshape(3, ep_count, tokens), axis=0)
-        parts = lax.dynamic_index_in_dim(parts, ep_index, 0, False)
-        row_weights.append(parts.reshape(blocks, row_count)[pieces].reshape(tokens, 1))
     exchange = lambda value, bit: lax.ppermute(
         value, ("kv", "tp"), [(i, i ^ bit) for i in range(blocks)]
     )
@@ -327,19 +326,29 @@
         value, "ep", [(i, i ^ step) for i in range(ep_count)]
     )
     bits = [1 << place for place in range(1, blocks.bit_length() - 1)]
-    haves = []
-    for step in range(ep_count):
-        have = [normed if step == 0 else across(normed, step)]
+    held_gate_up, held_down = hold_call([gate_up, down_weight], normed)
+    order = list(range(ep_count - 1, -1, -1))
+    gathered = {step: [normed if step == 0 else across(normed, step)] for step in order}
+    for step in order:
         for bit in bits + [1]:
-            have += [exchange(piece, bit) for piece in have]
-        haves.append(have)
+            gathered[step] += [exchange(piece, bit) for piece in gathered[step]]
     mixture = resid_wide
     given = []
     finished = []
-    for step in range(ep_count):
-        after = given[step - 2 : step - 1] if step >= 2 else []
-        after = after + (finished[step - 3 : step - 2] if step >= 3 else [])
-        kept, sent = expert_call(haves[step], row_weights[step], held_gate_up, held_down, after)
+    for turn, step in enumerate(order):
+        after = given[turn - 2 : turn - 1] if turn >= 2 else []
+        after = after + (finished[turn - 3 : turn - 2] if turn >= 3 else [])
+        kept, sent = expert_call(
+            place,
+            arrived[step],
+            gathered[step],
+            held_gate_up,
+            held_down,
+            after,
+            ep_count,
+            blocks,
+            held + tokens,
+        )
         got = exchange(sent, 1)
         for bit in reversed(bits):
             half = kept.shape[0] // 2

time: 99.5 us -> 118 us (1.19)
  waiting for transfers between devices: 19.9 us -> 29.8 us
  local copies, waits for them, and re-layouts: 24.1 us -> 27.1 us
  Pallas kernels: 15.2 us -> 17.6 us
  other arithmetic: 6.91 us -> 8.56 us
  starting transfers between devices: 31.7 us -> 33 us
    unnamed x25 -> x45, local copies, waits for them, and re-layouts: 15.3 us -> 23 us
    ppermute x3, waiting for transfers between devices: 0.01 us -> 5.38 us  [local(): lax.ppermute(payload, 'ep', [(i, i ^ step) for i in range(ep_count)])]
    ppermute x6, waiting for transfers between devices: 5.6 us -> 10.7 us  [local(): lax.ppermute(value, 'ep', [(i, i ^ step) for i in range(ep_count)])]
    gather x4 -> x0, local copies, waits for them, and re-layouts: 2.24 us -> none  [local(): parts.reshape(blocks, row_count)[pieces].reshape(tokens, 1)]
    pallas_call x4, Pallas kernels: 10.6 us -> 12.8 us  [expert_call(): pl.pallas_call(lambda *refs: expert_kernel(len(have), ep_count, blocks, w...]
    ppermute x6, starting transfers between devices: 11.5 us -> 13 us  [local(): lax.ppermute(value, 'ep', [(i, i ^ step) for i in range(ep_count)])]
  transfers between devices with their start and end apart: 33 -> 33, of which waited for: 8 -> 10; matrix products, arithmetic and copies ran while one was open for 10% -> 6% of each run, Pallas kernels for 12% -> 12%
where the time goes in v4:
time: 118 us; the launch traced here: 117 us
  starting transfers between devices  33 us (28%)
  waiting for transfers between devices  29.8 us (25%)
  local copies, waits for them, and re-layouts  27.1 us (23%)
  Pallas kernels  17.6 us (15%)
  other arithmetic  8.56 us (7%)
    unnamed x45, local copies, waits for them, and re-layouts  23 us
    ppermute x6, starting transfers between devices, local(): lax.ppermute(value, 'ep', [(i, i ^ step) for i in range(ep_count)])  13 us
    pallas_call x4, Pallas kernels, expert_call(): pl.pallas_call(lambda *refs: expert_kernel(len(have), ep_count, blocks, w...  12.8 us
    ppermute x20, starting transfers between devices, local(): lax.ppermute(value, ('kv', 'tp'), [(i, i ^ bit) for i in range(blocks)])  11.8 us
    ppermute x6, waiting for transfers between devices, local(): lax.ppermute(value, 'ep', [(i, i ^ step) for i in range(ep_count)])  10.7 us
    ppermute x20, waiting for transfers between devices, local(): lax.ppermute(value, ('kv', 'tp'), [(i, i ^ bit) for i in range(blocks)])  7.36 us
    ppermute x3, waiting for transfers between devices, local(): lax.ppermute(sent, ('kv', 'tp'), [(i, i ^ step) for i in range(blocks)])  6.38 us
    ppermute x3, starting transfers between devices, local(): lax.ppermute(payload, 'ep', [(i, i ^ step) for i in range(ep_count)])  5.68 us
  transfers between devices with their start and end apart: 33, of which 10 were waited for; matrix products, arithmetic and copies ran while one was open for 6% of the time, Pallas kernels for 12%

profile of v4, /device:TPU:0, one launch (start us, length us, event | category | flops | bytes accessed | tf_op | source)
XLA Modules:
  0.0 117.2 jit_solution(14328522366566553682)
XLA Ops:
  5.5 3.1 %collective-permute-start = (bf16[336,256]{1,0:T(8,128)(2,1)S(1)}, bf16[336,256]{1,0:T(8,128)(2,1)S(1)}, u32[]{:S(2)}, u32[]{:S(2)}) collective-permute-start(bf16[336,256]{1,0:T(8,128)(2,1)S(1)} %pad_maximum_fusion.refs_1_.refs_4_), channel_id=1, source_target_pairs={{0,4},{4,0},{8,12},{12,8},{1,5},{5,1},{9,13},{13,9},{2,6},{6,2},{1... | collective-permute-start | bytes 516104 | tf_op jit(solution)/shard_map/ppermute | solution.py:293
  8.6 2.6 %collective-permute-start.1 = (bf16[336,256]{1,0:T(8,128)(2,1)S(1)}, bf16[336,256]{1,0:T(8,128)(2,1)S(1)}, u32[]{:S(2)}, u32[]{:S(2)}) collective-permute-start(bf16[336,256]{1,0:T(8,128)(2,1)S(1)} %pad_maximum_fusion.refs_1_.refs_4_), channel_id=1, source_target_pairs={{0,8},{4,12},{8,0},{12,4},{1,9},{5,13},{9,1},{13,5},{2,10},{6,14},... | collective-permute-start | bytes 516104 | tf_op jit(solution)/shard_map/ppermute | solution.py:293
  11.2 3.4 %copy-done.8 = bf16[1024,4096]{1,0:T(8,128)(2,1)S(1)} copy-done((bf16[1024,4096]{1,0:T(8,128)(2,1)S(1)}, bf16[1024,4096]{1,0:T(8,128)(2,1)}, u32[]{:S(2)}) %copy-start.8) | copy-done | bytes 8388632
  15.1 3.3 %copy-done.6 = bf16[1024,4096]{1,0:T(8,128)(2,1)} copy-done((bf16[1024,4096]{1,0:T(8,128)(2,1)}, bf16[1024,4096]{1,0:T(8,128)(2,1)S(1)}, u32[]{:S(2)}) %copy-start.6) | copy-done | bytes 8388632
  18.8 5.4 %collective-permute-done.1.refs_6_.refs_1_ = bf16[336,256]{1,0:T(8,128)(2,1)S(1)} collective-permute-done((bf16[336,256]{1,0:T(8,128)(2,1)S(1)}, bf16[336,256]{1,0:T(8,128)(2,1)S(1)}, u32[]{:S(2)}, u32[]{:S(2)}) %collective-permute-start.1) | collective-permute-done | bytes 172064 | tf_op jit(solution)/shard_map/ppermute | solution.py:293
  24.2 3.4 %copy-done.7 = bf16[1024,4096]{1,0:T(8,128)(2,1)S(1)} copy-done((bf16[1024,4096]{1,0:T(8,128)(2,1)S(1)}, bf16[1024,4096]{1,0:T(8,128)(2,1)}, u32[]{:S(2)}) %copy-start.7) | copy-done | bytes 8388632
  27.6 3.4 %attend.1 = (f32[16,4096]{1,0:T(8,128)S(1)}, bf16[16,4096]{1,0:T(8,128)(2,1)S(1)}, bf16[16,4096]{1,0:T(8,128)(2,1)S(1)}, bf16[16,4096]{1,0:T(8,128)(2,1)S(1)}) custom-call(s32[4]{0:T(128)S(1)} %copy-done.1, s32[2]{0:T(128)S(1)} %pad_add_fusion.refs_1_.refs_0_, s32[1]{0:T(128)} %constant.90.clone.1.refs_2_, bf16[64,1024]{1,0:T(8,128)(2,1)S(1)} %copy-done.15, ...), custom_call_target="tpu_custom_call" | custom-call | flops 1024 | bytes 1024 | tf_op jit(solution)/shard_map/attend/pallas_call | solution.py:159
  33.0 4.5 %collective-permute-done.4 = bf16[16,4096]{1,0:T(8,128)(2,1)S(1)} collective-permute-done((bf16[16,4096]{1,0:T(8,128)(2,1)S(1)}, bf16[16,4096]{1,0:T(8,128)(2,1)S(1)}, u32[]{:S(2)}, u32[]{:S(2)}) %collective-permute-start.4) | collective-permute-done | bytes 131104 | tf_op jit(solution)/shard_map/ppermute | solution.py:310
  40.6 2.4 %collective-permute-start.6 = (bf16[16,4096]{1,0:T(8,128)(2,1)S(1)}, bf16[16,4096]{1,0:T(8,128)(2,1)S(1)}, u32[]{:S(2)}, u32[]{:S(2)}) collective-permute-start(bf16[16,4096]{1,0:T(8,128)(2,1)S(1)} %fusion.2.refs_2_), channel_id=1, source_target_pairs={{0,12},{4,8},{8,4},{12,0},{1,13},{5,9},{9,5},{13,1},{2,14},{6,10},... | collective-permute-start | bytes 393224 | tf_op jit(solution)/shard_map/ppermute | solution.py:325
  43.0 5.2 %collective-permute-done.6.refs_2_ = bf16[16,4096]{1,0:T(8,128)(2,1)S(1)} collective-permute-done((bf16[16,4096]{1,0:T(8,128)(2,1)S(1)}, bf16[16,4096]{1,0:T(8,128)(2,1)S(1)}, u32[]{:S(2)}, u32[]{:S(2)}) %collective-permute-start.6) | collective-permute-done | bytes 131104 | tf_op jit(solution)/shard_map/ppermute | solution.py:325
  50.5 4.3 %collective-permute-start.13 = (bf16[16,4096]{1,0:T(8,128)(2,1)S(1)}, bf16[16,4096]{1,0:T(8,128)(2,1)S(1)}, u32[]{:S(2)}, u32[]{:S(2)}) collective-permute-start(bf16[16,4096]{1,0:T(8,128)(2,1)S(1)} %fusion.2.refs_2_), channel_id=1, source_target_pairs={{0,8},{4,12},{8,0},{12,4},{1,9},{5,13},{9,1},{13,5},{2,10},{6,14},... | collective-permute-start | bytes 393224 | tf_op jit(solution)/shard_map/ppermute | solution.py:325
  57.6 3.5 %collective-permute-done.13.refs_2_ = bf16[16,4096]{1,0:T(8,128)(2,1)S(1)} collective-permute-done((bf16[16,4096]{1,0:T(8,128)(2,1)S(1)}, bf16[16,4096]{1,0:T(8,128)(2,1)S(1)}, u32[]{:S(2)}, u32[]{:S(2)}) %collective-permute-start.13) | collective-permute-done | bytes 131104 | tf_op jit(solution)/shard_map/ppermute | solution.py:325
  62.8 2.8 %copy-done.9 = bf16[1,2,384,4096]{3,2,1,0:T(8,128)(2,1)S(1)} copy-done((bf16[1,2,384,4096]{3,2,1,0:T(8,128)(2,1)S(1)}, bf16[1,2,384,4096]{3,2,1,0:T(8,128)(2,1)}, u32[]{:S(2)}) %copy-start.9) | copy-done | bytes 6291480
  68.4 3.2 %experts.4 = (bf16[32,4096]{1,0:T(8,128)(2,1)S(1)}, bf16[32,4096]{1,0:T(8,128)(2,1)S(1)}) custom-call(s32[2]{0:T(128)S(1)} %pad_add_fusion.refs_1_.refs_0_, bf16[336,256]{1,0:T(8,128)(2,1)S(1)} %collective-permute-done.2.refs_7_.refs_1_, bf16[16,4096]{1,0:T(8,128)(2,1)S(1)} %collective-permute-done.6.refs_2_, ...), custom_call_target="tpu_custom_call" | custom-call | flops 1024 | bytes 1024 | tf_op jit(solution)/shard_map/experts/pallas_call | solution.py:221
  71.6 2.7 %copy-done.2 = bf16[1,2,384,4096]{3,2,1,0:T(8,128)(2,1)} copy-done((bf16[1,2,384,4096]{3,2,1,0:T(8,128)(2,1)}, bf16[1,2,384,4096]{3,2,1,0:T(8,128)(2,1)S(1)}, u32[]{:S(2)}) %copy-start.2) | copy-done | bytes 6291480
  78.2 3.4 %collective-permute-done.21.refs_3_ = bf16[16,4096]{1,0:T(8,128)(2,1)S(1)} collective-permute-done((bf16[16,4096]{1,0:T(8,128)(2,1)S(1)}, bf16[16,4096]{1,0:T(8,128)(2,1)S(1)}, u32[]{:S(2)}, u32[]{:S(2)}) %collective-permute-start.21) | collective-permute-done | bytes 131104 | tf_op jit(solution)/shard_map/ppermute | solution.py:322
  82.1 2.8 %copy-done.3 = bf16[1,2,384,4096]{3,2,1,0:T(8,128)(2,1)S(1)} copy-done((bf16[1,2,384,4096]{3,2,1,0:T(8,128)(2,1)S(1)}, bf16[1,2,384,4096]{3,2,1,0:T(8,128)(2,1)}, u32[]{:S(2)}) %copy-start.3) | copy-done | bytes 6291480
  86.7 3.2 %experts.5 = (bf16[32,4096]{1,0:T(8,128)(2,1)S(1)}, bf16[32,4096]{1,0:T(8,128)(2,1)S(1)}) custom-call(s32[2]{0:T(128)S(1)} %pad_add_fusion.refs_1_.refs_0_, bf16[336,256]{1,0:T(8,128)(2,1)S(1)} %copy-done.14, bf16[16,4096]{1,0:T(8,128)(2,1)S(1)} %collective-permute-done.13.refs_2_, bf16[16,4096]{1,0:T(8,128)(2,1)S(1)} %collective-permute-done.14.refs_3_, ...), custom_call_target="tpu_custom_call" | custom-call | flops 1024 | bytes 1024 | tf_op jit(solution)/shard_map/experts/pallas_call | solution.py:221
  94.2 3.2 %experts.6 = (bf16[32,4096]{1,0:T(8,128)(2,1)S(1)}, bf16[32,4096]{1,0:T(8,128)(2,1)S(1)}) custom-call(s32[2]{0:T(128)S(1)} %pad_add_fusion.refs_1_.refs_0_, bf16[336,256]{1,0:T(8,128)(2,1)S(1)} %copy-done.12, bf16[16,4096]{1,0:T(8,128)(2,1)S(1)} %collective-permute-done.20.refs_2_, bf16[16,4096]{1,0:T(8,128)(2,1)S(1)} %collective-permute-done.21.refs_3_, ...), custom_call_target="tpu_custom_call" | custom-call | flops 1024 | bytes 1024 | tf_op jit(solution)/shard_map/experts/pallas_call | solution.py:221
  100.2 3.2 %experts.7 = (bf16[32,4096]{1,0:T(8,128)(2,1)S(1)}, bf16[32,4096]{1,0:T(8,128)(2,1)S(1)}) custom-call(s32[2]{0:T(128)S(1)} %pad_add_fusion.refs_1_.refs_0_, bf16[336,256]{1,0:T(8,128)(2,1)S(1)} %pad_maximum_fusion.refs_1_.refs_4_, bf16[16,4096]{1,0:T(8,128)(2,1)S(1)} %fusion.2.refs_2_, bf16[16,4096]{1,0:T(8,128)(2,1)S(1)} %collective-permute-done.27.refs_3_, ...), custom_call_target="tpu_custom_call" | custom-call | flops 1024 | bytes 1024 | tf_op jit(solution)/shard_map/experts/pallas_call | solution.py:221
  103.8 2.1 %collective-permute-start.25 = (bf16[16,4096]{1,0:T(8,128)(2,1)S(1)}, bf16[16,4096]{1,0:T(8,128)(2,1)S(1)}, u32[]{:S(2)}, u32[]{:S(2)}) collective-permute-start(bf16[16,4096]{1,0:T(8,128)(2,1)S(1)} %add_convert_fusion.3), channel_id=1, source_target_pairs={{0,2},{1,3},{2,0},{3,1},{4,6},{5,7},{6,4},{7,5},{8,10},{9,11},{10,... | collective-permute-start | bytes 393224 | tf_op jit(solution)/shard_map/ppermute | solution.py:322
  107.1 3.1 %collective-permute-done.25 = bf16[16,4096]{1,0:T(8,128)(2,1)S(1)} collective-permute-done((bf16[16,4096]{1,0:T(8,128)(2,1)S(1)}, bf16[16,4096]{1,0:T(8,128)(2,1)S(1)}, u32[]{:S(2)}, u32[]{:S(2)}) %collective-permute-start.25) | collective-permute-done | bytes 131104 | tf_op jit(solution)/shard_map/ppermute | solution.py:322
  110.2 3.2 %collective-permute-start.26 = (bf16[16,4096]{1,0:T(8,128)(2,1)S(1)}, bf16[16,4096]{1,0:T(8,128)(2,1)S(1)}, u32[]{:S(2)}, u32[]{:S(2)}) collective-permute-start(bf16[16,4096]{1,0:T(8,128)(2,1)S(1)} %add_convert_fusion.2), channel_id=1, source_target_pairs={{0,4},{4,0},{8,12},{12,8},{1,5},{5,1},{9,13},{13,9},{2,6},{6,2},{1... | collective-permute-start | bytes 393224 | tf_op jit(solution)/shard_map/ppermute | solution.py:325
  114.4 2.0 %collective-permute-done.26 = bf16[16,4096]{1,0:T(8,128)(2,1)S(1)} collective-permute-done((bf16[16,4096]{1,0:T(8,128)(2,1)S(1)}, bf16[16,4096]{1,0:T(8,128)(2,1)S(1)}, u32[]{:S(2)}, u32[]{:S(2)}) %collective-permute-start.26) | collective-permute-done | bytes 131104 | tf_op jit(solution)/shard_map/ppermute | solution.py:325
  (141 shorter events, 36.8 us)
Async XLA Ops:
  5.5 13.3 %collective-permute-start = (bf16[336,256]{1,0:T(8,128)(2,1)S(1)}, bf16[336,256]{1,0:T(8,128)(2,1)S(1)}, u32[]{:S(2)}, u32[]{:S(2)}) collective-permute-start(bf16[336,256]{1,0:T(8,128)(2,1)S(1)} %pad_maximum_fusion.refs_1_.refs_4_), channel_id=1, source_target_pairs={{0,4},{4,0},{8,12},{12,8},{1,5},{5,1},{9,13},{13,9},{2,6},{6,2},{1... | collective-permute-start | bytes 516104 | tf_op jit(solution)/shard_map/ppermute | solution.py:293
  8.6 15.6 %collective-permute-start.1 = (bf16[336,256]{1,0:T(8,128)(2,1)S(1)}, bf16[336,256]{1,0:T(8,128)(2,1)S(1)}, u32[]{:S(2)}, u32[]{:S(2)}) collective-permute-start(bf16[336,256]{1,0:T(8,128)(2,1)S(1)} %pad_maximum_fusion.refs_1_.refs_4_), channel_id=1, source_target_pairs={{0,8},{4,12},{8,0},{12,4},{1,9},{5,13},{9,1},{13,5},{2,10},{6,14},... | collective-permute-start | bytes 516104 | tf_op jit(solution)/shard_map/ppermute | solution.py:293
  11.2 13.0 %collective-permute-start.2 = (bf16[336,256]{1,0:T(8,128)(2,1)S(1)}, bf16[336,256]{1,0:T(8,128)(2,1)S(1)}, u32[]{:S(2)}, u32[]{:S(2)}) collective-permute-start(bf16[336,256]{1,0:T(8,128)(2,1)S(1)} %pad_maximum_fusion.refs_1_.refs_4_), channel_id=1, source_target_pairs={{0,12},{4,8},{8,4},{12,0},{1,13},{5,9},{9,5},{13,1},{2,14},{6,10},... | collective-permute-start | bytes 516104 | tf_op jit(solution)/shard_map/ppermute | solution.py:293
  31.1 6.4 %collective-permute-start.4 = (bf16[16,4096]{1,0:T(8,128)(2,1)S(1)}, bf16[16,4096]{1,0:T(8,128)(2,1)S(1)}, u32[]{:S(2)}, u32[]{:S(2)}) collective-permute-start(bf16[16,4096]{1,0:T(8,128)(2,1)S(1)} %get-tuple-element.18), channel_id=1, source_target_pairs={{0,2},{1,3},{2,0},{3,1},{4,6},{5,7},{6,4},{7,5},{8,10},{9,11},{10,... | collective-permute-start | bytes 393224 | tf_op jit(solution)/shard_map/ppermute | solution.py:310
  32.6 6.7 %collective-permute-start.5 = (bf16[16,4096]{1,0:T(8,128)(2,1)S(1)}, bf16[16,4096]{1,0:T(8,128)(2,1)S(1)}, u32[]{:S(2)}, u32[]{:S(2)}) collective-permute-start(bf16[16,4096]{1,0:T(8,128)(2,1)S(1)} %get-tuple-element.19), channel_id=1, source_target_pairs={{0,3},{1,2},{2,1},{3,0},{4,7},{5,6},{6,5},{7,4},{8,11},{9,10},{10,... | collective-permute-start | bytes 393224 | tf_op jit(solution)/shard_map/ppermute | solution.py:310
  40.6 7.6 %collective-permute-start.6 = (bf16[16,4096]{1,0:T(8,128)(2,1)S(1)}, bf16[16,4096]{1,0:T(8,128)(2,1)S(1)}, u32[]{:S(2)}, u32[]{:S(2)}) collective-permute-start(bf16[16,4096]{1,0:T(8,128)(2,1)S(1)} %fusion.2.refs_2_), channel_id=1, source_target_pairs={{0,12},{4,8},{8,4},{12,0},{1,13},{5,9},{9,5},{13,1},{2,14},{6,10},... | collective-permute-start | bytes 393224 | tf_op jit(solution)/shard_map/ppermute | solution.py:325
  48.2 6.5 %collective-permute-start.7 = (bf16[16,4096]{1,0:T(8,128)(2,1)S(1)}, bf16[16,4096]{1,0:T(8,128)(2,1)S(1)}, u32[]{:S(2)}, u32[]{:S(2)}) collective-permute-start(bf16[16,4096]{1,0:T(8,128)(2,1)S(1)} %collective-permute-done.6.refs_2_), channel_id=1, source_target_pairs={{0,2},{1,3},{2,0},{3,1},{4,6},{5,7},{6,4},{7,5},{8,10},{9,11},{10,... | collective-permute-start | bytes 393224 | tf_op jit(solution)/shard_map/ppermute | solution.py:322
  50.5 10.6 %collective-permute-start.13 = (bf16[16,4096]{1,0:T(8,128)(2,1)S(1)}, bf16[16,4096]{1,0:T(8,128)(2,1)S(1)}, u32[]{:S(2)}, u32[]{:S(2)}) collective-permute-start(bf16[16,4096]{1,0:T(8,128)(2,1)S(1)} %fusion.2.refs_2_), channel_id=1, source_target_pairs={{0,8},{4,12},{8,0},{12,4},{1,9},{5,13},{9,1},{13,5},{2,10},{6,14},... | collective-permute-start | bytes 393224 | tf_op jit(solution)/shard_map/ppermute | solution.py:325
  54.7 13.6 %collective-permute-start.8 = (bf16[16,4096]{1,0:T(8,128)(2,1)S(1)}, bf16[16,4096]{1,0:T(8,128)(2,1)S(1)}, u32[]{:S(2)}, u32[]{:S(2)}) collective-permute-start(bf16[16,4096]{1,0:T(8,128)(2,1)S(1)} %collective-permute-done.6.refs_2_), channel_id=1, source_target_pairs={{0,1},{1,0},{2,3},{3,2},{4,5},{5,4},{6,7},{7,6},{8,9},{9,8},{10,11... | collective-permute-start | bytes 393224 | tf_op jit(solution)/shard_map/ppermute | solution.py:322
  54.7 13.6 %collective-permute-start.9 = (bf16[16,4096]{1,0:T(8,128)(2,1)S(1)}, bf16[16,4096]{1,0:T(8,128)(2,1)S(1)}, u32[]{:S(2)}, u32[]{:S(2)}) collective-permute-start(bf16[16,4096]{1,0:T(8,128)(2,1)S(1)} %collective-permute-done.7.refs_3_), channel_id=1, source_target_pairs={{0,1},{1,0},{2,3},{3,2},{4,5},{5,4},{6,7},{7,6},{8,9},{9,8},{10,11... | collective-permute-start | bytes 393224 | tf_op jit(solution)/shard_map/ppermute | solution.py:322
  55.9 19.5 %collective-permute-start.20 = (bf16[16,4096]{1,0:T(8,128)(2,1)S(1)}, bf16[16,4096]{1,0:T(8,128)(2,1)S(1)}, u32[]{:S(2)}, u32[]{:S(2)}) collective-permute-start(bf16[16,4096]{1,0:T(8,128)(2,1)S(1)} %fusion.2.refs_2_), channel_id=1, source_target_pairs={{0,4},{4,0},{8,12},{12,8},{1,5},{5,1},{9,13},{13,9},{2,6},{6,2},{1... | collective-permute-start | bytes 393224 | tf_op jit(solution)/shard_map/ppermute | solution.py:325
  61.1 15.9 %collective-permute-start.14 = (bf16[16,4096]{1,0:T(8,128)(2,1)S(1)}, bf16[16,4096]{1,0:T(8,128)(2,1)S(1)}, u32[]{:S(2)}, u32[]{:S(2)}) collective-permute-start(bf16[16,4096]{1,0:T(8,128)(2,1)S(1)} %collective-permute-done.13.refs_2_), channel_id=1, source_target_pairs={{0,2},{1,3},{2,0},{3,1},{4,6},{5,7},{6,4},{7,5},{8,10},{9,11},{10,... | collective-permute-start | bytes 393224 | tf_op jit(solution)/shard_map/ppermute | solution.py:322
  74.3 15.7 %collective-permute-start.10 = (bf16[32,4096]{1,0:T(8,128)(2,1)S(1)}, bf16[32,4096]{1,0:T(8,128)(2,1)}, u32[]{:S(2)}, u32[]{:S(2)}) collective-permute-start(bf16[32,4096]{1,0:T(8,128)(2,1)S(1)} %get-tuple-element.23), channel_id=1, source_target_pairs={{0,1},{1,0},{2,3},{3,2},{4,5},{5,4},{6,7},{7,6},{8,9},{9,8},{10,11... | collective-permute-start | bytes 786440 | tf_op jit(solution)/shard_map/ppermute | solution.py:322
  77.0 36.4 %collective-permute-start.32 = (bf16[8,16,256]{2,1,0:T(8,128)(2,1)S(1)}, bf16[8,16,256]{2,1,0:T(8,128)(2,1)S(1)}, u32[]{:S(2)}, u32[]{:S(2)}) collective-permute-start(bf16[8,16,256]{2,1,0:T(8,128)(2,1)S(1)} %broadcast_select_fusion), channel_id=1, source_target_pairs={{0,1},{1,0},{2,3},{3,2},{4,5},{5,4},{6,7},{7,6},{8,9},{9,8},{10,11... | collective-permute-start | bytes 196616 | tf_op jit(solution)/shard_map/ppermute | solution.py:393
  77.6 15.8 %collective-permute-start.27 = (bf16[16,4096]{1,0:T(8,128)(2,1)S(1)}, bf16[16,4096]{1,0:T(8,128)(2,1)S(1)}, u32[]{:S(2)}, u32[]{:S(2)}) collective-permute-start(bf16[16,4096]{1,0:T(8,128)(2,1)S(1)} %fusion.2.refs_2_), channel_id=1, source_target_pairs={{0,2},{1,3},{2,0},{3,1},{4,6},{5,7},{6,4},{7,5},{8,10},{9,11},{10,... | collective-permute-start | bytes 393224 | tf_op jit(solution)/shard_map/ppermute | solution.py:322
  81.5 11.9 %collective-permute-start.22 = (bf16[16,4096]{1,0:T(8,128)(2,1)S(1)}, bf16[16,4096]{1,0:T(8,128)(2,1)S(1)}, u32[]{:S(2)}, u32[]{:S(2)}) collective-permute-start(bf16[16,4096]{1,0:T(8,128)(2,1)S(1)} %collective-permute-done.20.refs_2_), channel_id=1, source_target_pairs={{0,1},{1,0},{2,3},{3,2},{4,5},{5,4},{6,7},{7,6},{8,9},{9,8},{10,11... | collective-permute-start | bytes 393224 | tf_op jit(solution)/shard_map/ppermute | solution.py:322
  81.5 12.4 %collective-permute-start.23 = (bf16[16,4096]{1,0:T(8,128)(2,1)S(1)}, bf16[16,4096]{1,0:T(8,128)(2,1)S(1)}, u32[]{:S(2)}, u32[]{:S(2)}) collective-permute-start(bf16[16,4096]{1,0:T(8,128)(2,1)S(1)} %collective-permute-done.21.refs_3_), channel_id=1, source_target_pairs={{0,1},{1,0},{2,3},{3,2},{4,5},{5,4},{6,7},{7,6},{8,9},{9,8},{10,11... | collective-permute-start | bytes 393224 | tf_op jit(solution)/shard_map/ppermute | solution.py:322
  91.6 6.3 %collective-permute-start.11 = (bf16[16,4096]{1,0:T(8,128)(2,1)S(1)}, bf16[16,4096]{1,0:T(8,128)(2,1)S(1)}, u32[]{:S(2)}, u32[]{:S(2)}) collective-permute-start(bf16[16,4096]{1,0:T(8,128)(2,1)S(1)} %add_convert_fusion.7.refs_8_), channel_id=1, source_target_pairs={{0,2},{1,3},{2,0},{3,1},{4,6},{5,7},{6,4},{7,5},{8,10},{9,11},{10,... | collective-permute-start | bytes 393224 | tf_op jit(solution)/shard_map/ppermute | solution.py:322
  93.5 6.7 %collective-permute-start.29 = (bf16[16,4096]{1,0:T(8,128)(2,1)S(1)}, bf16[16,4096]{1,0:T(8,128)(2,1)S(1)}, u32[]{:S(2)}, u32[]{:S(2)}) collective-permute-start(bf16[16,4096]{1,0:T(8,128)(2,1)S(1)} %collective-permute-done.27.refs_3_), channel_id=1, source_target_pairs={{0,1},{1,0},{2,3},{3,2},{4,5},{5,4},{6,7},{7,6},{8,9},{9,8},{10,11... | collective-permute-start | bytes 393224 | tf_op jit(solution)/shard_map/ppermute | solution.py:322
  94.0 9.7 %collective-permute-start.18 = (bf16[16,4096]{1,0:T(8,128)(2,1)S(1)}, bf16[16,4096]{1,0:T(8,128)(2,1)S(1)}, u32[]{:S(2)}, u32[]{:S(2)}) collective-permute-start(bf16[16,4096]{1,0:T(8,128)(2,1)S(1)} %add_convert_fusion.5.refs_8_), channel_id=1, source_target_pairs={{0,2},{1,3},{2,0},{3,1},{4,6},{5,7},{6,4},{7,5},{8,10},{9,11},{10,... | collective-permute-start | bytes 393224 | tf_op jit(solution)/shard_map/ppermute | solution.py:322
  98.8 15.6 %collective-permute-start.12 = (bf16[16,4096]{1,0:T(8,128)(2,1)S(1)}, bf16[16,4096]{1,0:T(8,128)(2,1)S(1)}, u32[]{:S(2)}, u32[]{:S(2)}) collective-permute-start(bf16[16,4096]{1,0:T(8,128)(2,1)S(1)} %add_convert_fusion.6.refs_9_), channel_id=1, source_target_pairs={{0,12},{4,8},{8,4},{12,0},{1,13},{5,9},{9,5},{13,1},{2,14},{6,10},... | collective-permute-start | bytes 393224 | tf_op jit(solution)/shard_map/ppermute | solution.py:325
  103.7 10.7 %collective-permute-start.19 = (bf16[16,4096]{1,0:T(8,128)(2,1)S(1)}, bf16[16,4096]{1,0:T(8,128)(2,1)S(1)}, u32[]{:S(2)}, u32[]{:S(2)}) collective-permute-start(bf16[16,4096]{1,0:T(8,128)(2,1)S(1)} %add_convert_fusion.4), channel_id=1, source_target_pairs={{0,8},{4,12},{8,0},{12,4},{1,9},{5,13},{9,1},{13,5},{2,10},{6,14},... | collective-permute-start | bytes 393224 | tf_op jit(solution)/shard_map/ppermute | solution.py:325
  103.8 6.4 %collective-permute-start.25 = (bf16[16,4096]{1,0:T(8,128)(2,1)S(1)}, bf16[16,4096]{1,0:T(8,128)(2,1)S(1)}, u32[]{:S(2)}, u32[]{:S(2)}) collective-permute-start(bf16[16,4096]{1,0:T(8,128)(2,1)S(1)} %add_convert_fusion.3), channel_id=1, source_target_pairs={{0,2},{1,3},{2,0},{3,1},{4,6},{5,7},{6,4},{7,5},{8,10},{9,11},{10,... | collective-permute-start | bytes 393224 | tf_op jit(solution)/shard_map/ppermute | solution.py:322
  106.0 8.4 %collective-permute-start.31 = (bf16[16,4096]{1,0:T(8,128)(2,1)S(1)}, bf16[16,4096]{1,0:T(8,128)(2,1)S(1)}, u32[]{:S(2)}, u32[]{:S(2)}) collective-permute-start(bf16[16,4096]{1,0:T(8,128)(2,1)S(1)} %add_convert_fusion.1), channel_id=1, source_target_pairs={{0,2},{1,3},{2,0},{3,1},{4,6},{5,7},{6,4},{7,5},{8,10},{9,11},{10,... | collective-permute-start | bytes 393224 | tf_op jit(solution)/shard_map/ppermute | solution.py:322
  (32 other events, 287.2 us)

commit v5 on v4

--- a/solution.py
+++ b/solution.py
@@ -40,41 +40,22 @@
 SCALARS = pl.BlockSpec(memory_space=pltpu.SMEM)
 COLUMNS = 1024
 ROWS = 256
-VMEM_LIMIT = 16 * 2**20
-LITTLE = pl.CostEstimate(flops=1024, bytes_accessed=1024, transcendentals=0)
-
-
-def hold_kernel(*refs):
-    count = (len(refs) - 2) // 2
-    sources, held, sem = refs[:count], refs[count + 1 : -1], refs[-1]
-    copies = [
-        pltpu.make_async_copy(source, target, sem.at[i])
-        for i, (source, target) in enumerate(zip(sources, held))
-    ]
-    for copy in copies:
-        copy.start()
-    for copy in copies:
-        copy.wait()
-
-
-def hold_call(arrays, after):
-    return pl.pallas_call(
-        hold_kernel,
-        out_shape=[jax.ShapeDtypeStruct(array.shape, array.dtype) for array in arrays],
-        in_specs=[ANYWHERE] * (len(arrays) + 1),
-        out_specs=[WHOLE] * len(arrays),
-        scratch_shapes=[pltpu.SemaphoreType.DMA((len(arrays),))],
-        compiler_params=pltpu.CompilerParams(vmem_limit_bytes=VMEM_LIMIT),
-        cost_estimate=LITTLE,
-        name="hold",
-    )(*arrays, after)
-
-
-def attend_kernel(ep_count, held, tokens, all_open, lens, place, counts, queries, *refs):
+VMEM_LIMIT = 60 * 2**20 + 2**17
+
+
+def attend_kernel(ep_count, held, tokens, row_blocks, all_open, lens, place, counts, queries, *refs):
     blocks = refs[:ep_count]
     out_weight = refs[ep_count]
-    own_ref, *sent_refs = refs[ep_count + 1 : -2]
-    scores, projected = refs[-2:]
+    kept_ref, sent_ref = refs[ep_count + 1 : ep_count + 3]
+    scores, projected, fetched, fetch_sem = refs[ep_count + 3 :]
+    fetches = []
+    for i in range(fetched.shape[0]):
+        fetches.append(
+            pltpu.make_async_copy(
+                out_weight.at[:, pl.ds(i * COLUMNS, COLUMNS)], fetched.at[i], fetch_sem.at[i]
+            )
+        )
+        fetches[i].start()
     heads = queries.shape[1] // HD
     ep_index = place[0]
     block_index = place[1]
@@ -139,15 +120,16 @@
         mixed = (mixed / total).astype(jnp.bfloat16)
         attended += [mixed[h * tokens : (h + 1) * tokens] for h in range(together)]
     attended = jnp.concatenate(attended, axis=1)
-    for at in range(0, out_weight.shape[1], COLUMNS):
-        projected[:, at : at + COLUMNS] = jnp.dot(
-            attended, out_weight[:, at : at + COLUMNS], preferred_element_type=jnp.float32
-        )
-    count = own_ref.shape[0]
-    own_ref[...] = projected[pl.ds(pl.multiple_of(block_index * count, count), count), :]
-    for step, ref in enumerate(sent_refs, 1):
-        at = pl.multiple_of((block_index ^ step) * count, count)
-        ref[...] = projected[pl.ds(at, count), :].astype(jnp.bfloat16)
+    for i, fetch in enumerate(fetches):
+        fetch.wait()
+        projected[:, i * COLUMNS : (i + 1) * COLUMNS] = jnp.dot(
+            attended, fetched[i], preferred_element_type=jnp.float32
+        )
+    count = tokens // row_blocks
+    for spot, piece in enumerate(piece_order(row_blocks)):
+        rows = projected[pl.ds(pl.multiple_of((block_index ^ piece) * count, count), count), :]
+        ref, spot = (kept_ref, spot) if 2 * spot < row_blocks else (sent_ref, spot - row_blocks // 2)
+        ref[spot * count : (spot + 1) * count, :] = rows.astype(ref.dtype)
 
 
 def attend_call(lens, place, counts, queries, arrived, out_weight, held, blocks, all_open):
@@ -155,27 +137,50 @@
     ep_count = len(arrived)
     model_width = out_weight.shape[1]
     heads = queries.shape[1] // HD
-    row_count = tokens // blocks
+    keys = ep_count * (held + tokens)
     return pl.pallas_call(
-        lambda *refs: attend_kernel(ep_count, held, tokens, all_open, *refs),
-        out_shape=[jax.ShapeDtypeStruct((row_count, model_width), jnp.float32)]
-        + [jax.ShapeDtypeStruct((row_count, model_width), jnp.bfloat16)] * (blocks - 1),
-        in_specs=[SCALARS] * 3 + [WHOLE] * (ep_count + 2),
-        out_specs=[WHOLE] * blocks,
+        lambda *refs: attend_kernel(ep_count, held, tokens, blocks, all_open, *refs),
+        out_shape=[
+            jax.ShapeDtypeStruct((tokens // 2, model_width), jnp.float32),
+            jax.ShapeDtypeStruct((tokens // 2, model_width), jnp.bfloat16),
+        ],
+        in_specs=[SCALARS] * 3 + [WHOLE] * (ep_count + 1) + [ANYWHERE],
+        out_specs=[WHOLE] * 2,
         scratch_shapes=[
             pltpu.VMEM((min(ROWS, heads * tokens), ep_count * held), jnp.float32),
             pltpu.VMEM((tokens, model_width), jnp.float32),
+            pltpu.VMEM((model_width // COLUMNS, heads * HD, COLUMNS), jnp.bfloat16),
+            pltpu.SemaphoreType.DMA((model_width // COLUMNS,)),
         ],
         compiler_params=pltpu.CompilerParams(vmem_limit_bytes=VMEM_LIMIT),
-        cost_estimate=LITTLE,
+        cost_estimate=pl.CostEstimate(
+            flops=4 * heads * tokens * keys * HD + 2 * tokens * heads * HD * model_width,
+            bytes_accessed=2 * heads * HD * model_width,
+            transcendentals=heads * tokens * keys,
+        ),
         name="attend",
     )(lens, place, counts, queries, *arrived, out_weight)
 
 
 def expert_kernel(count, ep_count, blocks, weight_at, place, payload, *refs):
     row_refs = refs[:count]
-    gate_up, down_weight = refs[count : count + 2]
-    kept_ref, sent_ref = refs[-2:]
+    gate_up_hbm, down_hbm = refs[count : count + 2]
+    kept_ref, sent_ref, gate_up, down_weight, gate_up_sem, down_sem = refs[-6:]
+    chunks = gate_up.shape[0]
+    first = []
+    second = []
+    for i in range(chunks):
+        columns = pl.ds(i * COLUMNS, COLUMNS)
+        first.append(
+            pltpu.make_async_copy(
+                gate_up_hbm.at[0, :, :, columns], gate_up.at[i], gate_up_sem.at[i]
+            )
+        )
+        second.append(
+            pltpu.make_async_copy(down_hbm.at[0, :, columns], down_weight.at[i], down_sem.at[i])
+        )
+    for fetch in first + second:
+        fetch.start()
     tokens = 2 * kept_ref.shape[0]
     row_count = tokens // blocks
 
@@ -190,23 +195,25 @@
     here = lax.broadcasted_iota(jnp.int32, (tokens, parts.shape[1]), 1) == token
     row_weight = jnp.sum(jnp.where(here, by_token, 0.0), axis=1, keepdims=True)
 
-    model_width = kept_ref.shape[1]
     gate_part = up_part = 0.0
-    for at in range(0, model_width, COLUMNS):
+    for i in range(chunks):
+        at = i * COLUMNS
         rows = jnp.concatenate([ref[:, at : at + COLUMNS] for ref in row_refs], axis=0)
+        first[i].wait()
         gate_part += lax.dot_general(
-            rows, gate_up[0, 0, :, at : at + COLUMNS], TRANSPOSED, preferred_element_type=jnp.float32
+            rows, gate_up[i, 0], TRANSPOSED, preferred_element_type=jnp.float32
         )
         up_part += lax.dot_general(
-            rows, gate_up[0, 1, :, at : at + COLUMNS], TRANSPOSED, preferred_element_type=jnp.float32
+            rows, gate_up[i, 1], TRANSPOSED, preferred_element_type=jnp.float32
         )
     hidden = gate_part / (1.0 + jnp.exp(-gate_part)) * up_part
     hidden = (hidden * row_weight).astype(jnp.bfloat16)
     half = kept_ref.shape[0]
-    for at in range(0, model_width, COLUMNS):
-        out = jnp.dot(
-            hidden, down_weight[0, :, at : at + COLUMNS], preferred_element_type=jnp.float32
-        ).astype(jnp.bfloat16)
+    for i in range(chunks):
+        at = i * COLUMNS
+        second[i].wait()
+        out = jnp.dot(hidden, down_weight[i], preferred_element_type=jnp.float32)
+        out = out.astype(jnp.bfloat16)
         kept_ref[:, at : at + COLUMNS] = out[:half]
         sent_ref[:, at : at + COLUMNS] = out[half:]
 
@@ -221,10 +228,20 @@
     return pl.pallas_call(
         lambda *refs: expert_kernel(len(have), ep_count, blocks, weight_at, *refs),
         out_shape=(half, half),
-        in_specs=[SCALARS] + [WHOLE] * (len(have) + 3) + [ANYWHERE] * len(after),
+        in_specs=[SCALARS] + [WHOLE] * (len(have) + 1) + [ANYWHERE] * (len(after) + 2),
         out_specs=(WHOLE, WHOLE),
+        scratch_shapes=[
+            pltpu.VMEM((model_width // COLUMNS, 2, hidden_units, COLUMNS), jnp.bfloat16),
+            pltpu.VMEM((model_width // COLUMNS, hidden_units, COLUMNS), jnp.bfloat16),
+            pltpu.SemaphoreType.DMA((model_width // COLUMNS,)),
+            pltpu.SemaphoreType.DMA((model_width // COLUMNS,)),
+        ],
         compiler_params=pltpu.CompilerParams(vmem_limit_bytes=VMEM_LIMIT),
-        cost_estimate=LITTLE,
+        cost_estimate=pl.CostEstimate(
+            flops=6 * tokens * hidden_units * model_width,
+            bytes_accessed=6 * hidden_units * model_width,
+            transcendentals=tokens * hidden_units,
+        ),
         name="experts",
     )(place, payload, *have, gate_up, down_weight, *after)
 
@@ -294,7 +311,6 @@
         )
     sources = [ep_index ^ step for step in range(ep_count)]
 
-    held_out = hold_call([out_weight], payload)[0]
     all_open = hits == HOLD_MOST * ep_count
     holder = hit_pages // pool_pages
     counts = jnp.sum(
@@ -303,13 +319,30 @@
     if all_open:
         counts = jnp.zeros((1,), jnp.int32)
     place = jnp.stack([ep_index, block_index]).astype(jnp.int32)
-    heads_out, *sent_rows = attend_call(
-        span_lengths, place, counts, queries, arrived, held_out, held, blocks, all_open
-    )
-    for step, sent in enumerate(sent_rows, 1):
-        heads_out = heads_out + lax.ppermute(
-            sent, ("kv", "tp"), [(i, i ^ step) for i in range(blocks)]
-        ).astype(jnp.float32)
+    exchange = lambda value, bit: lax.ppermute(
+        value, ("kv", "tp"), [(i, i ^ bit) for i in range(blocks)]
+    )
+    across = lambda value, step: lax.ppermute(
+        value, "ep", [(i, i ^ step) for i in range(ep_count)]
+    )
+    bits = [1 << place for place in range(1, blocks.bit_length() - 1)]
+
+    def scatter(kept, sent):
+        got = exchange(sent, 1)
+        gives = []
+        for bit in reversed(bits):
+            half = kept.shape[0] // 2
+            give = kept[half:].astype(jnp.float32) + got[half:].astype(jnp.float32)
+            gives.append(give.astype(jnp.bfloat16))
+            kept = kept[:half].astype(jnp.float32) + got[:half].astype(jnp.float32)
+            got = exchange(gives[-1], bit)
+        return kept.astype(jnp.float32) + got.astype(jnp.float32), gives
+
+    heads_out, _ = scatter(
+        *attend_call(
+            span_lengths, place, counts, queries, arrived, out_weight, held, blocks, all_open
+        )
+    )
     own_hidden = lax.dynamic_slice_in_dim(hidden_in, block_index * row_count, row_count, 0)
     residual = (own_hidden.astype(jnp.float32) + heads_out).astype(jnp.bfloat16)
     resid_wide = residual.astype(jnp.float32)
@@ -319,55 +352,6 @@
         * norm_gain
     ).astype(jnp.bfloat16)
 
-    exchange = lambda value, bit: lax.ppermute(
-        value, ("kv", "tp"), [(i, i ^ bit) for i in range(blocks)]
-    )
-    across = lambda value, step: lax.ppermute(
-        value, "ep", [(i, i ^ step) for i in range(ep_count)]
-    )
-    bits = [1 << place for place in range(1, blocks.bit_length() - 1)]
-    held_gate_up, held_down = hold_call([gate_up, down_weight], normed)
-    order = list(range(ep_count - 1, -1, -1))
-    gathered = {step: [normed if step == 0 else across(normed, step)] for step in order}
-    for step in order:
-        for bit in bits + [1]:
-            gathered[step] += [exchange(piece, bit) for piece in gathered[step]]
-    mixture = resid_wide
-    given = []
-    finished = []
-    for turn, step in enumerate(order):
-        after = given[turn - 2 : turn - 1] if turn >= 2 else []
-        after = after + (finished[turn - 3 : turn - 2] if turn >= 3 else [])
-        kept, sent = expert_call(
-            place,
-            arrived[step],
-            gathered[step],
-            held_gate_up,
-            held_down,
-            after,
-            ep_count,
-            blocks,
-            held + tokens,
-        )
-        got = exchange(sent, 1)
-        for bit in reversed(bits):
-            half = kept.shape[0] // 2
-            give = (kept[half:].astype(jnp.float32) + got[half:].astype(jnp.float32)).astype(
-                jnp.bfloat16
-            )
-            if bit == bits[-1]:
-                given.append(give)
-            kept = kept[:half].astype(jnp.float32) + got[:half].astype(jnp.float32)
-            got = exchange(give, bit)
-        own = (kept.astype(jnp.float32) + got.astype(jnp.float32)).astype(jnp.bfloat16)
-        finished.append(own)
-        if step > 0:
-            own = across(own, step)
-        mixture = mixture + own.astype(jnp.float32)
-    own_slots = block_index * row_count + jnp.arange(row_count, dtype=jnp.int32)
-    rows_filled = own_slots < span_lengths[ep_index]
-    layer_out = jnp.where(rows_filled[:, None], mixture, 0.0).astype(jnp.bfloat16)
-
     own_most = 2 * (tokens // page_size)
     page_count = new_owner.shape[0]
     pages_here = tokens // page_size
@@ -387,6 +371,48 @@
     slot_in_span = (page_index % pages_here)[:, None] * page_size + jnp.arange(page_size)[None, :]
     kept = has_page[:, None] & (slot_in_span < span_lengths[page_index // pages_here][:, None])
     head_pages = jnp.where(kept[:, :, None], taken, jnp.zeros((), jnp.bfloat16))
+
+    order = [0] + list(range(ep_count - 1, 0, -1))
+    given = []
+    finished = []
+
+    def experts_of(step, piece, turn):
+        have = [piece]
+        for bit in bits + [1]:
+            have += [exchange(part, bit) for part in have]
+        after = given[turn - 2 : turn - 1] if turn >= 2 else []
+        after = after + (finished[turn - 3 : turn - 2] if turn >= 3 else [])
+        return expert_call(
+            place,
+            arrived[step],
+            have,
+            gate_up,
+            down_weight,
+            after,
+            ep_count,
+            blocks,
+            held + tokens,
+        )
+
+    kept, sent = experts_of(0, normed, 0)
+    sent, head_pages, *crossed = lax.optimization_barrier(
+        [sent, head_pages] + [across(normed, step) for step in order[1:]]
+    )
+    mixture = resid_wide
+    for turn, step in enumerate(order):
+        if turn > 0:
+            kept, sent = experts_of(step, crossed[turn - 1], turn)
+        own, gives = scatter(kept, sent)
+        own = own.astype(jnp.bfloat16)
+        given.append(gives[0] if gives else own)
+        finished.append(own)
+        if step > 0:
+            own = across(own, step)
+        mixture = mixture + own.astype(jnp.float32)
+    own_slots = block_index * row_count + jnp.arange(row_count, dtype=jnp.int32)
+    rows_filled = own_slots < span_lengths[ep_index]
+    layer_out = jnp.where(rows_filled[:, None], mixture, 0.0).astype(jnp.bfloat16)
+
     if keyval_local == 1:
         decode_pages = head_pages[:, :, None, :]
     else:

time: 118 us -> 121 us (1.025)
  Pallas kernels: 17.6 us -> 35.8 us
  local copies, waits for them, and re-layouts: 27.1 us -> 11.6 us
  starting transfers between devices: 33 us -> 26.1 us
  waiting for transfers between devices: 29.8 us -> 33.8 us
  other arithmetic: 8.56 us -> 11.5 us
    unnamed x45 -> x61, local copies, waits for them, and re-layouts: 23 us -> 5.24 us
    pallas_call x4, Pallas kernels: 12.8 us -> 29.3 us  [expert_call(): pl.pallas_call(lambda *refs: expert_kernel(len(have), ep_count, blocks, w...]
    ppermute x20 -> x22, waiting for transfers between devices: 7.36 us -> 14 us  [local(): lax.ppermute(value, ('kv', 'tp'), [(i, i ^ bit) for i in range(blocks)])]
    ppermute x3 -> x0, waiting for transfers between devices: 6.38 us -> none  [local(): lax.ppermute(sent, ('kv', 'tp'), [(i, i ^ step) for i in range(blocks)])]
    ppermute x3, waiting for transfers between devices: 5.38 us -> 11.5 us  [local(): lax.ppermute(payload, 'ep', [(i, i ^ step) for i in range(ep_count)])]
    ppermute x6, starting transfers between devices: 13 us -> 8.09 us  [local(): lax.ppermute(value, 'ep', [(i, i ^ step) for i in range(ep_count)])]
    convert_element_type x7 -> x9, other arithmetic: 2.25 us -> 4.68 us  [the longest x5 2.93 us: scatter(): gives.append(give.astype(jnp.bfloat16))]
    ppermute x6, waiting for transfers between devices: 10.7 us -> 8.25 us  [local(): lax.ppermute(value, 'ep', [(i, i ^ step) for i in range(ep_count)])]
  transfers between devices with their start and end apart: 33 -> 32, of which waited for: 10 -> 12; matrix products, arithmetic and copies ran while one was open for 6% -> 9% of each run, Pallas kernels for 12% -> 24%
where the time goes in v5:
time: 121 us; the launch traced here: 120 us
  Pallas kernels  35.8 us (30%)
  waiting for transfers between devices  33.8 us (28%)
  starting transfers between devices  26.1 us (22%)
  local copies, waits for them, and re-layouts  11.6 us (10%)
  other arithmetic  11.5 us (10%)
  between operations  1.25 us (1%)
    pallas_call x4, Pallas kernels, expert_call(): pl.pallas_call(lambda *refs: expert_kernel(len(have), ep_count, blocks, w...  29.3 us
    ppermute x22, waiting for transfers between devices, local(): lax.ppermute(value, ('kv', 'tp'), [(i, i ^ bit) for i in range(blocks)])  14 us
    ppermute x22, starting transfers between devices, local(): lax.ppermute(value, ('kv', 'tp'), [(i, i ^ bit) for i in range(blocks)])  12.3 us
    ppermute x3, waiting for transfers between devices, local(): lax.ppermute(payload, 'ep', [(i, i ^ step) for i in range(ep_count)])  11.5 us
    ppermute x6, waiting for transfers between devices, local(): lax.ppermute(value, 'ep', [(i, i ^ step) for i in range(ep_count)])  8.25 us
    ppermute x6, starting transfers between devices, local(): lax.ppermute(value, 'ep', [(i, i ^ step) for i in range(ep_count)])  8.09 us
    pallas_call x1, Pallas kernels, attend_call(): pl.pallas_call(lambda *refs: attend_kernel(ep_count, held, tokens, blocks...  6.44 us
    ppermute x3, starting transfers between devices, local(): lax.ppermute(payload, 'ep', [(i, i ^ step) for i in range(ep_count)])  5.68 us
  transfers between devices with their start and end apart: 32, of which 12 were waited for; matrix products, arithmetic and copies ran while one was open for 9% of the time, Pallas kernels for 24%

profile of v5, /device:TPU:0, one launch (start us, length us, event | category | flops | bytes accessed | tf_op | source)
XLA Modules:
  0.0 120.0 jit_solution(10314796471516887450)
XLA Ops:
  5.5 3.1 %collective-permute-start = (bf16[336,256]{1,0:T(8,128)(2,1)S(1)}, bf16[336,256]{1,0:T(8,128)(2,1)S(1)}, u32[]{:S(2)}, u32[]{:S(2)}) collective-permute-start(bf16[336,256]{1,0:T(8,128)(2,1)S(1)} %pad_maximum_fusion.refs_4_.refs_1_), channel_id=1, source_target_pairs={{0,4},{4,0},{8,12},{12,8},{1,5},{5,1},{9,13},{13,9},{2,6},{6,2},{1... | collective-permute-start | bytes 516104 | tf_op jit(solution)/shard_map/ppermute | solution.py:310
  8.6 2.6 %collective-permute-start.1 = (bf16[336,256]{1,0:T(8,128)(2,1)S(1)}, bf16[336,256]{1,0:T(8,128)(2,1)S(1)}, u32[]{:S(2)}, u32[]{:S(2)}) collective-permute-start(bf16[336,256]{1,0:T(8,128)(2,1)S(1)} %pad_maximum_fusion.refs_4_.refs_1_), channel_id=1, source_target_pairs={{0,8},{4,12},{8,0},{12,4},{1,9},{5,13},{9,1},{13,5},{2,10},{6,14},... | collective-permute-start | bytes 516104 | tf_op jit(solution)/shard_map/ppermute | solution.py:310
  12.7 3.0 %collective-permute-done.refs_5_.refs_1_ = bf16[336,256]{1,0:T(8,128)(2,1)S(1)} collective-permute-done((bf16[336,256]{1,0:T(8,128)(2,1)S(1)}, bf16[336,256]{1,0:T(8,128)(2,1)S(1)}, u32[]{:S(2)}, u32[]{:S(2)}) %collective-permute-start) | collective-permute-done | bytes 172064 | tf_op jit(solution)/shard_map/ppermute | solution.py:310
  15.7 8.5 %collective-permute-done.1.refs_6_.refs_1_ = bf16[336,256]{1,0:T(8,128)(2,1)S(1)} collective-permute-done((bf16[336,256]{1,0:T(8,128)(2,1)S(1)}, bf16[336,256]{1,0:T(8,128)(2,1)S(1)}, u32[]{:S(2)}, u32[]{:S(2)}) %collective-permute-start.1) | collective-permute-done | bytes 172064 | tf_op jit(solution)/shard_map/ppermute | solution.py:310
  25.5 6.4 %attend.1 = (f32[32,4096]{1,0:T(8,128)}, bf16[32,4096]{1,0:T(8,128)(2,1)}) custom-call(s32[4]{0:T(128)} %refs_0_.1, s32[2]{0:T(128)} %pad_add_fusion.refs_1_.refs_0_, s32[1]{0:T(128)} %constant.90.clone.1.refs_2_, bf16[64,1024]{1,0:T(8,128)(2,1)} %refs_3_.1, bf16[336,256]{1,0:T(8,128)(2,1)} %copy-done.2, bf16[336,256]{1,0:T(8,128)(2,1)} %copy-done.4, ...), custom_call_target="tpu_custom_call" | custom-call | flops 872415232 | bytes 8388608 | tf_op jit(solution)/shard_map/attend/pallas_call | solution.py:141
  32.1 1.7 %collective-permute-done.3 = bf16[32,4096]{1,0:T(8,128)(2,1)S(1)} collective-permute-done((bf16[32,4096]{1,0:T(8,128)(2,1)}, bf16[32,4096]{1,0:T(8,128)(2,1)S(1)}, u32[]{:S(2)}, u32[]{:S(2)}) %collective-permute-start.3) | collective-permute-done | bytes 262176 | tf_op jit(solution)/shard_map/ppermute | solution.py:322
  34.8 1.6 %collective-permute-start.4 = (bf16[16,4096]{1,0:T(8,128)(2,1)S(1)}, bf16[16,4096]{1,0:T(8,128)(2,1)S(1)}, u32[]{:S(2)}, u32[]{:S(2)}) collective-permute-start(bf16[16,4096]{1,0:T(8,128)(2,1)S(1)} %add_convert_fusion.9), channel_id=1, source_target_pairs={{0,2},{1,3},{2,0},{3,1},{4,6},{5,7},{6,4},{7,5},{8,10},{9,11},{10,... | collective-permute-start | bytes 393224 | tf_op jit(solution)/shard_map/ppermute | solution.py:322
  37.1 3.3 %collective-permute-done.4 = bf16[16,4096]{1,0:T(8,128)(2,1)S(1)} collective-permute-done((bf16[16,4096]{1,0:T(8,128)(2,1)S(1)}, bf16[16,4096]{1,0:T(8,128)(2,1)S(1)}, u32[]{:S(2)}, u32[]{:S(2)}) %collective-permute-start.4) | collective-permute-done | bytes 131104 | tf_op jit(solution)/shard_map/ppermute | solution.py:322
  41.7 1.6 %collective-permute-start.5 = (bf16[16,4096]{1,0:T(8,128)(2,1)S(1)}, bf16[16,4096]{1,0:T(8,128)(2,1)S(1)}, u32[]{:S(2)}, u32[]{:S(2)}) collective-permute-start(bf16[16,4096]{1,0:T(8,128)(2,1)S(1)} %fusion.2.refs_2_), channel_id=1, source_target_pairs={{0,2},{1,3},{2,0},{3,1},{4,6},{5,7},{6,4},{7,5},{8,10},{9,11},{10,... | collective-permute-start | bytes 393224 | tf_op jit(solution)/shard_map/ppermute | solution.py:322
  46.2 2.2 %collective-permute-start.10 = (bf16[16,4096]{1,0:T(8,128)(2,1)S(1)}, bf16[16,4096]{1,0:T(8,128)(2,1)S(1)}, u32[]{:S(2)}, u32[]{:S(2)}) collective-permute-start(bf16[16,4096]{1,0:T(8,128)(2,1)S(1)} %fusion.2.refs_2_), channel_id=1, source_target_pairs={{0,4},{4,0},{8,12},{12,8},{1,5},{5,1},{9,13},{13,9},{2,6},{6,2},{1... | collective-permute-start | bytes 393224 | tf_op jit(solution)/shard_map/ppermute | solution.py:325
  48.5 2.5 %collective-permute-start.8 = (bf16[16,4096]{1,0:T(8,128)(2,1)S(1)}, bf16[16,4096]{1,0:T(8,128)(2,1)S(1)}, u32[]{:S(2)}, u32[]{:S(2)}) collective-permute-start(bf16[16,4096]{1,0:T(8,128)(2,1)S(1)} %fusion.2.refs_2_), channel_id=1, source_target_pairs={{0,12},{4,8},{8,4},{12,0},{1,13},{5,9},{9,5},{13,1},{2,14},{6,10},... | collective-permute-start | bytes 393224 | tf_op jit(solution)/shard_map/ppermute | solution.py:325
  53.0 7.4 %experts.4 = (bf16[32,4096]{1,0:T(8,128)(2,1)}, bf16[32,4096]{1,0:T(8,128)(2,1)}) custom-call(s32[2]{0:T(128)} %pad_add_fusion.refs_1_.refs_0_, bf16[336,256]{1,0:T(8,128)(2,1)} %copy-done.2, bf16[16,4096]{1,0:T(8,128)(2,1)} %copy-done.9, bf16[16,4096]{1,0:T(8,128)(2,1)} %copy-done.23, bf16[16,4096]{1,0:T(8,128)(2,1)} %copy-done.26, ...), custom_call_target="tpu_custom_call" | custom-call | flops 603979776 | bytes 9437184 | tf_op jit(solution)/shard_map/experts/pallas_call | solution.py:228
  60.5 2.3 %collective-permute-done.9.refs_2_ = bf16[16,4096]{1,0:T(8,128)(2,1)S(1)} collective-permute-done((bf16[16,4096]{1,0:T(8,128)(2,1)S(1)}, bf16[16,4096]{1,0:T(8,128)(2,1)S(1)}, u32[]{:S(2)}, u32[]{:S(2)}) %collective-permute-start.9) | collective-permute-done | bytes 131104 | tf_op jit(solution)/shard_map/ppermute | solution.py:325
  65.8 3.2 %collective-permute-done.13.refs_3_ = bf16[16,4096]{1,0:T(8,128)(2,1)S(1)} collective-permute-done((bf16[16,4096]{1,0:T(8,128)(2,1)S(1)}, bf16[16,4096]{1,0:T(8,128)(2,1)S(1)}, u32[]{:S(2)}, u32[]{:S(2)}) %collective-permute-start.13) | collective-permute-done | bytes 131104 | tf_op jit(solution)/shard_map/ppermute | solution.py:322
  69.6 2.3 %collective-permute-done.19.refs_3_ = bf16[16,4096]{1,0:T(8,128)(2,1)S(1)} collective-permute-done((bf16[16,4096]{1,0:T(8,128)(2,1)S(1)}, bf16[16,4096]{1,0:T(8,128)(2,1)S(1)}, u32[]{:S(2)}, u32[]{:S(2)}) %collective-permute-start.19) | collective-permute-done | bytes 131104 | tf_op jit(solution)/shard_map/ppermute | solution.py:322
  75.2 7.3 %experts.5 = (bf16[32,4096]{1,0:T(8,128)(2,1)}, bf16[32,4096]{1,0:T(8,128)(2,1)}) custom-call(s32[2]{0:T(128)} %pad_add_fusion.refs_1_.refs_0_, bf16[336,256]{1,0:T(8,128)(2,1)} %copy-done.6, bf16[16,4096]{1,0:T(8,128)(2,1)} %copy-done.15, bf16[16,4096]{1,0:T(8,128)(2,1)} %copy-done.20, bf16[16,4096]{1,0:T(8,128)(2,1)} %copy-done.22, ...), custom_call_target="tpu_custom_call" | custom-call | flops 603979776 | bytes 9437184 | tf_op jit(solution)/shard_map/experts/pallas_call | solution.py:228
  83.8 7.3 %experts.6 = (bf16[32,4096]{1,0:T(8,128)(2,1)}, bf16[32,4096]{1,0:T(8,128)(2,1)}) custom-call(s32[2]{0:T(128)} %pad_add_fusion.refs_1_.refs_0_, bf16[336,256]{1,0:T(8,128)(2,1)} %copy-done.5, bf16[16,4096]{1,0:T(8,128)(2,1)} %copy-done.14, bf16[16,4096]{1,0:T(8,128)(2,1)} %copy-done.17, bf16[16,4096]{1,0:T(8,128)(2,1)} %copy-done.18, ...), custom_call_target="tpu_custom_call" | custom-call | flops 603979776 | bytes 9437184 | tf_op jit(solution)/shard_map/experts/pallas_call | solution.py:228
  92.1 1.5 %collective-permute-start.17 = (bf16[16,4096]{1,0:T(8,128)(2,1)S(1)}, bf16[16,4096]{1,0:T(8,128)(2,1)S(1)}, u32[]{:S(2)}, u32[]{:S(2)}) collective-permute-start(bf16[16,4096]{1,0:T(8,128)(2,1)S(1)} %add_convert_fusion.5.refs_8_), channel_id=1, source_target_pairs={{0,2},{1,3},{2,0},{3,1},{4,6},{5,7},{6,4},{7,5},{8,10},{9,11},{10,... | collective-permute-start | bytes 393224 | tf_op jit(solution)/shard_map/ppermute | solution.py:322
  94.9 7.3 %experts.7 = (bf16[32,4096]{1,0:T(8,128)(2,1)}, bf16[32,4096]{1,0:T(8,128)(2,1)}) custom-call(s32[2]{0:T(128)} %pad_add_fusion.refs_1_.refs_0_, bf16[336,256]{1,0:T(8,128)(2,1)} %copy-done.4, bf16[16,4096]{1,0:T(8,128)(2,1)} %copy-done.13, bf16[16,4096]{1,0:T(8,128)(2,1)} %copy-done.16, bf16[16,4096]{1,0:T(8,128)(2,1)} %copy-done.19, ...), custom_call_target="tpu_custom_call" | custom-call | flops 603979776 | bytes 9437184 | tf_op jit(solution)/shard_map/experts/pallas_call | solution.py:228
  103.2 2.0 %collective-permute-start.18 = (bf16[16,4096]{1,0:T(8,128)(2,1)S(1)}, bf16[16,4096]{1,0:T(8,128)(2,1)S(1)}, u32[]{:S(2)}, u32[]{:S(2)}) collective-permute-start(bf16[16,4096]{1,0:T(8,128)(2,1)S(1)} %add_convert_fusion.4), channel_id=1, source_target_pairs={{0,12},{4,8},{8,4},{12,0},{1,13},{5,9},{9,5},{13,1},{2,14},{6,10},... | collective-permute-start | bytes 393224 | tf_op jit(solution)/shard_map/ppermute | solution.py:325
  106.1 1.6 %collective-permute-start.29 = (bf16[16,4096]{1,0:T(8,128)(2,1)S(1)}, bf16[16,4096]{1,0:T(8,128)(2,1)S(1)}, u32[]{:S(2)}, u32[]{:S(2)}) collective-permute-start(bf16[16,4096]{1,0:T(8,128)(2,1)S(1)} %add_convert_fusion.1), channel_id=1, source_target_pairs={{0,2},{1,3},{2,0},{3,1},{4,6},{5,7},{6,4},{7,5},{8,10},{9,11},{10,... | collective-permute-start | bytes 393224 | tf_op jit(solution)/shard_map/ppermute | solution.py:322
  109.7 1.6 %collective-permute-done.29 = bf16[16,4096]{1,0:T(8,128)(2,1)S(1)} collective-permute-done((bf16[16,4096]{1,0:T(8,128)(2,1)S(1)}, bf16[16,4096]{1,0:T(8,128)(2,1)S(1)}, u32[]{:S(2)}, u32[]{:S(2)}) %collective-permute-start.29) | collective-permute-done | bytes 131104 | tf_op jit(solution)/shard_map/ppermute | solution.py:322
  113.3 3.2 %collective-permute-done.24 = bf16[16,4096]{1,0:T(8,128)(2,1)S(1)} collective-permute-done((bf16[16,4096]{1,0:T(8,128)(2,1)S(1)}, bf16[16,4096]{1,0:T(8,128)(2,1)S(1)}, u32[]{:S(2)}, u32[]{:S(2)}) %collective-permute-start.24) | collective-permute-done | bytes 131104 | tf_op jit(solution)/shard_map/ppermute | solution.py:325
  116.5 2.7 %collective-permute-done.30 = bf16[16,4096]{1,0:T(8,128)(2,1)S(1)} collective-permute-done((bf16[16,4096]{1,0:T(8,128)(2,1)S(1)}, bf16[16,4096]{1,0:T(8,128)(2,1)S(1)}, u32[]{:S(2)}, u32[]{:S(2)}) %collective-permute-start.30) | collective-permute-done | bytes 131104 | tf_op jit(solution)/shard_map/ppermute | solution.py:325
  (152 shorter events, 32.6 us)
Async XLA Ops:
  5.5 10.2 %collective-permute-start = (bf16[336,256]{1,0:T(8,128)(2,1)S(1)}, bf16[336,256]{1,0:T(8,128)(2,1)S(1)}, u32[]{:S(2)}, u32[]{:S(2)}) collective-permute-start(bf16[336,256]{1,0:T(8,128)(2,1)S(1)} %pad_maximum_fusion.refs_4_.refs_1_), channel_id=1, source_target_pairs={{0,4},{4,0},{8,12},{12,8},{1,5},{5,1},{9,13},{13,9},{2,6},{6,2},{1... | collective-permute-start | bytes 516104 | tf_op jit(solution)/shard_map/ppermute | solution.py:310
  8.6 15.6 %collective-permute-start.1 = (bf16[336,256]{1,0:T(8,128)(2,1)S(1)}, bf16[336,256]{1,0:T(8,128)(2,1)S(1)}, u32[]{:S(2)}, u32[]{:S(2)}) collective-permute-start(bf16[336,256]{1,0:T(8,128)(2,1)S(1)} %pad_maximum_fusion.refs_4_.refs_1_), channel_id=1, source_target_pairs={{0,8},{4,12},{8,0},{12,4},{1,9},{5,13},{9,1},{13,5},{2,10},{6,14},... | collective-permute-start | bytes 516104 | tf_op jit(solution)/shard_map/ppermute | solution.py:310
  11.2 13.0 %collective-permute-start.2 = (bf16[336,256]{1,0:T(8,128)(2,1)S(1)}, bf16[336,256]{1,0:T(8,128)(2,1)S(1)}, u32[]{:S(2)}, u32[]{:S(2)}) collective-permute-start(bf16[336,256]{1,0:T(8,128)(2,1)S(1)} %pad_maximum_fusion.refs_4_.refs_1_), channel_id=1, source_target_pairs={{0,12},{4,8},{8,4},{12,0},{1,13},{5,9},{9,5},{13,1},{2,14},{6,10},... | collective-permute-start | bytes 516104 | tf_op jit(solution)/shard_map/ppermute | solution.py:310
  41.7 9.3 %collective-permute-start.5 = (bf16[16,4096]{1,0:T(8,128)(2,1)S(1)}, bf16[16,4096]{1,0:T(8,128)(2,1)S(1)}, u32[]{:S(2)}, u32[]{:S(2)}) collective-permute-start(bf16[16,4096]{1,0:T(8,128)(2,1)S(1)} %fusion.2.refs_2_), channel_id=1, source_target_pairs={{0,2},{1,3},{2,0},{3,1},{4,6},{5,7},{6,4},{7,5},{8,10},{9,11},{10,... | collective-permute-start | bytes 393224 | tf_op jit(solution)/shard_map/ppermute | solution.py:322
  46.2 14.2 %collective-permute-start.10 = (bf16[16,4096]{1,0:T(8,128)(2,1)S(1)}, bf16[16,4096]{1,0:T(8,128)(2,1)S(1)}, u32[]{:S(2)}, u32[]{:S(2)}) collective-permute-start(bf16[16,4096]{1,0:T(8,128)(2,1)S(1)} %fusion.2.refs_2_), channel_id=1, source_target_pairs={{0,4},{4,0},{8,12},{12,8},{1,5},{5,1},{9,13},{13,9},{2,6},{6,2},{1... | collective-permute-start | bytes 393224 | tf_op jit(solution)/shard_map/ppermute | solution.py:325
  48.5 12.0 %collective-permute-start.8 = (bf16[16,4096]{1,0:T(8,128)(2,1)S(1)}, bf16[16,4096]{1,0:T(8,128)(2,1)S(1)}, u32[]{:S(2)}, u32[]{:S(2)}) collective-permute-start(bf16[16,4096]{1,0:T(8,128)(2,1)S(1)} %fusion.2.refs_2_), channel_id=1, source_target_pairs={{0,12},{4,8},{8,4},{12,0},{1,13},{5,9},{9,5},{13,1},{2,14},{6,10},... | collective-permute-start | bytes 393224 | tf_op jit(solution)/shard_map/ppermute | solution.py:325
  51.0 11.8 %collective-permute-start.9 = (bf16[16,4096]{1,0:T(8,128)(2,1)S(1)}, bf16[16,4096]{1,0:T(8,128)(2,1)S(1)}, u32[]{:S(2)}, u32[]{:S(2)}) collective-permute-start(bf16[16,4096]{1,0:T(8,128)(2,1)S(1)} %fusion.2.refs_2_), channel_id=1, source_target_pairs={{0,8},{4,12},{8,0},{12,4},{1,9},{5,13},{9,1},{13,5},{2,10},{6,14},... | collective-permute-start | bytes 393224 | tf_op jit(solution)/shard_map/ppermute | solution.py:325
  62.8 9.1 %collective-permute-start.11 = (bf16[32,4096]{1,0:T(8,128)(2,1)}, bf16[32,4096]{1,0:T(8,128)(2,1)S(1)}, u32[]{:S(2)}, u32[]{:S(2)}) collective-permute-start(bf16[32,4096]{1,0:T(8,128)(2,1)} %get-tuple-element.21), channel_id=1, source_target_pairs={{0,1},{1,0},{2,3},{3,2},{4,5},{5,4},{6,7},{7,6},{8,9},{9,8},{10,11... | collective-permute-start | bytes 786440 | tf_op jit(solution)/shard_map/ppermute | solution.py:322
  62.8 6.3 %collective-permute-start.13 = (bf16[16,4096]{1,0:T(8,128)(2,1)S(1)}, bf16[16,4096]{1,0:T(8,128)(2,1)S(1)}, u32[]{:S(2)}, u32[]{:S(2)}) collective-permute-start(bf16[16,4096]{1,0:T(8,128)(2,1)S(1)} %collective-permute-done.8.refs_2_), channel_id=1, source_target_pairs={{0,2},{1,3},{2,0},{3,1},{4,6},{5,7},{6,4},{7,5},{8,10},{9,11},{10,... | collective-permute-start | bytes 393224 | tf_op jit(solution)/shard_map/ppermute | solution.py:322
  63.3 8.6 %collective-permute-start.19 = (bf16[16,4096]{1,0:T(8,128)(2,1)S(1)}, bf16[16,4096]{1,0:T(8,128)(2,1)S(1)}, u32[]{:S(2)}, u32[]{:S(2)}) collective-permute-start(bf16[16,4096]{1,0:T(8,128)(2,1)S(1)} %collective-permute-done.9.refs_2_), channel_id=1, source_target_pairs={{0,2},{1,3},{2,0},{3,1},{4,6},{5,7},{6,4},{7,5},{8,10},{9,11},{10,... | collective-permute-start | bytes 393224 | tf_op jit(solution)/shard_map/ppermute | solution.py:322
  65.3 8.0 %collective-permute-start.14 = (bf16[16,4096]{1,0:T(8,128)(2,1)S(1)}, bf16[16,4096]{1,0:T(8,128)(2,1)S(1)}, u32[]{:S(2)}, u32[]{:S(2)}) collective-permute-start(bf16[16,4096]{1,0:T(8,128)(2,1)S(1)} %collective-permute-done.8.refs_2_), channel_id=1, source_target_pairs={{0,1},{1,0},{2,3},{3,2},{4,5},{5,4},{6,7},{7,6},{8,9},{9,8},{10,11... | collective-permute-start | bytes 393224 | tf_op jit(solution)/shard_map/ppermute | solution.py:322
  65.3 17.2 %collective-permute-start.20 = (bf16[16,4096]{1,0:T(8,128)(2,1)S(1)}, bf16[16,4096]{1,0:T(8,128)(2,1)S(1)}, u32[]{:S(2)}, u32[]{:S(2)}) collective-permute-start(bf16[16,4096]{1,0:T(8,128)(2,1)S(1)} %collective-permute-done.9.refs_2_), channel_id=1, source_target_pairs={{0,1},{1,0},{2,3},{3,2},{4,5},{5,4},{6,7},{7,6},{8,9},{9,8},{10,11... | collective-permute-start | bytes 393224 | tf_op jit(solution)/shard_map/ppermute | solution.py:322
  69.1 13.6 %collective-permute-start.25 = (bf16[16,4096]{1,0:T(8,128)(2,1)S(1)}, bf16[16,4096]{1,0:T(8,128)(2,1)S(1)}, u32[]{:S(2)}, u32[]{:S(2)}) collective-permute-start(bf16[16,4096]{1,0:T(8,128)(2,1)S(1)} %collective-permute-done.10.refs_2_), channel_id=1, source_target_pairs={{0,2},{1,3},{2,0},{3,1},{4,6},{5,7},{6,4},{7,5},{8,10},{9,11},{10,... | collective-permute-start | bytes 393224 | tf_op jit(solution)/shard_map/ppermute | solution.py:322
  71.9 11.3 %collective-permute-start.21 = (bf16[16,4096]{1,0:T(8,128)(2,1)S(1)}, bf16[16,4096]{1,0:T(8,128)(2,1)S(1)}, u32[]{:S(2)}, u32[]{:S(2)}) collective-permute-start(bf16[16,4096]{1,0:T(8,128)(2,1)S(1)} %collective-permute-done.19.refs_3_), channel_id=1, source_target_pairs={{0,1},{1,0},{2,3},{3,2},{4,5},{5,4},{6,7},{7,6},{8,9},{9,8},{10,11... | collective-permute-start | bytes 393224 | tf_op jit(solution)/shard_map/ppermute | solution.py:322
  73.4 17.8 %collective-permute-start.12 = (bf16[16,4096]{1,0:T(8,128)(2,1)S(1)}, bf16[16,4096]{1,0:T(8,128)(2,1)S(1)}, u32[]{:S(2)}, u32[]{:S(2)}) collective-permute-start(bf16[16,4096]{1,0:T(8,128)(2,1)S(1)} %add_convert_fusion.7.refs_8_), channel_id=1, source_target_pairs={{0,2},{1,3},{2,0},{3,1},{4,6},{5,7},{6,4},{7,5},{8,10},{9,11},{10,... | collective-permute-start | bytes 393224 | tf_op jit(solution)/shard_map/ppermute | solution.py:322
  74.5 19.1 %collective-permute-start.26 = (bf16[16,4096]{1,0:T(8,128)(2,1)S(1)}, bf16[16,4096]{1,0:T(8,128)(2,1)S(1)}, u32[]{:S(2)}, u32[]{:S(2)}) collective-permute-start(bf16[16,4096]{1,0:T(8,128)(2,1)S(1)} %collective-permute-done.10.refs_2_), channel_id=1, source_target_pairs={{0,1},{1,0},{2,3},{3,2},{4,5},{5,4},{6,7},{7,6},{8,9},{9,8},{10,11... | collective-permute-start | bytes 393224 | tf_op jit(solution)/shard_map/ppermute | solution.py:322
  82.5 29.9 %collective-permute-start.31 = (bf16[8,16,256]{2,1,0:T(8,128)(2,1)S(1)}, bf16[8,16,256]{2,1,0:T(8,128)(2,1)S(1)}, u32[]{:S(2)}, u32[]{:S(2)}) collective-permute-start(bf16[8,16,256]{2,1,0:T(8,128)(2,1)S(1)} %broadcast_select_fusion), channel_id=1, source_target_pairs={{0,1},{1,0},{2,3},{3,2},{4,5},{5,4},{6,7},{7,6},{8,9},{9,8},{10,11... | collective-permute-start | bytes 196616 | tf_op jit(solution)/shard_map/ppermute | solution.py:419
  82.6 11.0 %collective-permute-start.27 = (bf16[16,4096]{1,0:T(8,128)(2,1)S(1)}, bf16[16,4096]{1,0:T(8,128)(2,1)S(1)}, u32[]{:S(2)}, u32[]{:S(2)}) collective-permute-start(bf16[16,4096]{1,0:T(8,128)(2,1)S(1)} %collective-permute-done.25.refs_3_), channel_id=1, source_target_pairs={{0,1},{1,0},{2,3},{3,2},{4,5},{5,4},{6,7},{7,6},{8,9},{9,8},{10,11... | collective-permute-start | bytes 393224 | tf_op jit(solution)/shard_map/ppermute | solution.py:322
  83.1 8.9 %collective-permute-start.16 = (bf16[32,4096]{1,0:T(8,128)(2,1)}, bf16[32,4096]{1,0:T(8,128)(2,1)S(1)}, u32[]{:S(2)}, u32[]{:S(2)}) collective-permute-start(bf16[32,4096]{1,0:T(8,128)(2,1)} %get-tuple-element.24), channel_id=1, source_target_pairs={{0,1},{1,0},{2,3},{3,2},{4,5},{5,4},{6,7},{7,6},{8,9},{9,8},{10,11... | collective-permute-start | bytes 786440 | tf_op jit(solution)/shard_map/ppermute | solution.py:322
  91.1 11.3 %collective-permute-start.22 = (bf16[32,4096]{1,0:T(8,128)(2,1)}, bf16[32,4096]{1,0:T(8,128)(2,1)S(1)}, u32[]{:S(2)}, u32[]{:S(2)}) collective-permute-start(bf16[32,4096]{1,0:T(8,128)(2,1)} %get-tuple-element.27), channel_id=1, source_target_pairs={{0,1},{1,0},{2,3},{3,2},{4,5},{5,4},{6,7},{7,6},{8,9},{9,8},{10,11... | collective-permute-start | bytes 786440 | tf_op jit(solution)/shard_map/ppermute | solution.py:322
  92.1 11.1 %collective-permute-start.17 = (bf16[16,4096]{1,0:T(8,128)(2,1)S(1)}, bf16[16,4096]{1,0:T(8,128)(2,1)S(1)}, u32[]{:S(2)}, u32[]{:S(2)}) collective-permute-start(bf16[16,4096]{1,0:T(8,128)(2,1)S(1)} %add_convert_fusion.5.refs_8_), channel_id=1, source_target_pairs={{0,2},{1,3},{2,0},{3,1},{4,6},{5,7},{6,4},{7,5},{8,10},{9,11},{10,... | collective-permute-start | bytes 393224 | tf_op jit(solution)/shard_map/ppermute | solution.py:322
  103.2 10.1 %collective-permute-start.18 = (bf16[16,4096]{1,0:T(8,128)(2,1)S(1)}, bf16[16,4096]{1,0:T(8,128)(2,1)S(1)}, u32[]{:S(2)}, u32[]{:S(2)}) collective-permute-start(bf16[16,4096]{1,0:T(8,128)(2,1)S(1)} %add_convert_fusion.4), channel_id=1, source_target_pairs={{0,12},{4,8},{8,4},{12,0},{1,13},{5,9},{9,5},{13,1},{2,14},{6,10},... | collective-permute-start | bytes 393224 | tf_op jit(solution)/shard_map/ppermute | solution.py:325
  108.4 8.1 %collective-permute-start.24 = (bf16[16,4096]{1,0:T(8,128)(2,1)S(1)}, bf16[16,4096]{1,0:T(8,128)(2,1)S(1)}, u32[]{:S(2)}, u32[]{:S(2)}) collective-permute-start(bf16[16,4096]{1,0:T(8,128)(2,1)S(1)} %add_convert_fusion.2), channel_id=1, source_target_pairs={{0,8},{4,12},{8,0},{12,4},{1,9},{5,13},{9,1},{13,5},{2,10},{6,14},... | collective-permute-start | bytes 393224 | tf_op jit(solution)/shard_map/ppermute | solution.py:325
  112.3 6.9 %collective-permute-start.30 = (bf16[16,4096]{1,0:T(8,128)(2,1)S(1)}, bf16[16,4096]{1,0:T(8,128)(2,1)S(1)}, u32[]{:S(2)}, u32[]{:S(2)}) collective-permute-start(bf16[16,4096]{1,0:T(8,128)(2,1)S(1)} %add_convert_fusion), channel_id=1, source_target_pairs={{0,4},{4,0},{8,12},{12,8},{1,5},{5,1},{9,13},{13,9},{2,6},{6,2},{1... | collective-permute-start | bytes 393224 | tf_op jit(solution)/shard_map/ppermute | solution.py:325
  (37 other events, 314.7 us)

commit v6 on v5

--- a/solution.py
+++ b/solution.py
@@ -40,22 +40,41 @@
 SCALARS = pl.BlockSpec(memory_space=pltpu.SMEM)
 COLUMNS = 1024
 ROWS = 256
-VMEM_LIMIT = 60 * 2**20 + 2**17
+VMEM_LIMIT = 16 * 2**20
+
+
+def hold_kernel(*refs):
+    count = (len(refs) - 2) // 2
+    sources, held, sem = refs[:count], refs[count + 1 : -1], refs[-1]
+    copies = [
+        pltpu.make_async_copy(source, target, sem.at[i])
+        for i, (source, target) in enumerate(zip(sources, held))
+    ]
+    for copy in copies:
+        copy.start()
+    for copy in copies:
+        copy.wait()
+
+
+def hold_call(arrays, after):
+    size = sum(math.prod(array.shape) * 2 for array in arrays)
+    return pl.pallas_call(
+        hold_kernel,
+        out_shape=[jax.ShapeDtypeStruct(array.shape, array.dtype) for array in arrays],
+        in_specs=[ANYWHERE] * (len(arrays) + 1),
+        out_specs=[WHOLE] * len(arrays),
+        scratch_shapes=[pltpu.SemaphoreType.DMA((len(arrays),))],
+        compiler_params=pltpu.CompilerParams(vmem_limit_bytes=VMEM_LIMIT),
+        cost_estimate=pl.CostEstimate(flops=0, bytes_accessed=2 * size, transcendentals=0),
+        name="hold",
+    )(*arrays, after)
 
 
 def attend_kernel(ep_count, held, tokens, row_blocks, all_open, lens, place, counts, queries, *refs):
     blocks = refs[:ep_count]
     out_weight = refs[ep_count]
     kept_ref, sent_ref = refs[ep_count + 1 : ep_count + 3]
-    scores, projected, fetched, fetch_sem = refs[ep_count + 3 :]
-    fetches = []
-    for i in range(fetched.shape[0]):
-        fetches.append(
-            pltpu.make_async_copy(
-                out_weight.at[:, pl.ds(i * COLUMNS, COLUMNS)], fetched.at[i], fetch_sem.at[i]
-            )
-        )
-        fetches[i].start()
+    scores, projected = refs[ep_count + 3 :]
     heads = queries.shape[1] // HD
     ep_index = place[0]
     block_index = place[1]
@@ -120,10 +139,9 @@
         mixed = (mixed / total).astype(jnp.bfloat16)
         attended += [mixed[h * tokens : (h + 1) * tokens] for h in range(together)]
     attended = jnp.concatenate(attended, axis=1)
-    for i, fetch in enumerate(fetches):
-        fetch.wait()
-        projected[:, i * COLUMNS : (i + 1) * COLUMNS] = jnp.dot(
-            attended, fetched[i], preferred_element_type=jnp.float32
+    for at in range(0, out_weight.shape[1], COLUMNS):
+        projected[:, at : at + COLUMNS] = jnp.dot(
+            attended, out_weight[:, at : at + COLUMNS], preferred_element_type=jnp.float32
         )
     count = tokens // row_blocks
     for spot, piece in enumerate(piece_order(row_blocks)):
@@ -144,13 +162,11 @@
             jax.ShapeDtypeStruct((tokens // 2, model_width), jnp.float32),
             jax.ShapeDtypeStruct((tokens // 2, model_width), jnp.bfloat16),
         ],
-        in_specs=[SCALARS] * 3 + [WHOLE] * (ep_count + 1) + [ANYWHERE],
+        in_specs=[SCALARS] * 3 + [WHOLE] * (ep_count + 2),
         out_specs=[WHOLE] * 2,
         scratch_shapes=[
             pltpu.VMEM((min(ROWS, heads * tokens), ep_count * held), jnp.float32),
             pltpu.VMEM((tokens, model_width), jnp.float32),
-            pltpu.VMEM((model_width // COLUMNS, heads * HD, COLUMNS), jnp.bfloat16),
-            pltpu.SemaphoreType.DMA((model_width // COLUMNS,)),
         ],
         compiler_params=pltpu.CompilerParams(vmem_limit_bytes=VMEM_LIMIT),
         cost_estimate=pl.CostEstimate(
@@ -164,23 +180,8 @@
 
 def expert_kernel(count, ep_count, blocks, weight_at, place, payload, *refs):
     row_refs = refs[:count]
-    gate_up_hbm, down_hbm = refs[count : count + 2]
-    kept_ref, sent_ref, gate_up, down_weight, gate_up_sem, down_sem = refs[-6:]
-    chunks = gate_up.shape[0]
-    first = []
-    second = []
-    for i in range(chunks):
-        columns = pl.ds(i * COLUMNS, COLUMNS)
-        first.append(
-            pltpu.make_async_copy(
-                gate_up_hbm.at[0, :, :, columns], gate_up.at[i], gate_up_sem.at[i]
-            )
-        )
-        second.append(
-            pltpu.make_async_copy(down_hbm.at[0, :, columns], down_weight.at[i], down_sem.at[i])
-        )
-    for fetch in first + second:
-        fetch.start()
+    gate_up, down_weight = refs[count : count + 2]
+    kept_ref, sent_ref = refs[-2:]
     tokens = 2 * kept_ref.shape[0]
     row_count = tokens // blocks
 
@@ -196,24 +197,21 @@
     row_weight = jnp.sum(jnp.where(here, by_token, 0.0), axis=1, keepdims=True)
 
     gate_part = up_part = 0.0
-    for i in range(chunks):
-        at = i * COLUMNS
+    for at in range(0, kept_ref.shape[1], COLUMNS):
         rows = jnp.concatenate([ref[:, at : at + COLUMNS] for ref in row_refs], axis=0)
-        first[i].wait()
         gate_part += lax.dot_general(
-            rows, gate_up[i, 0], TRANSPOSED, preferred_element_type=jnp.float32
+            rows, gate_up[0, 0, :, at : at + COLUMNS], TRANSPOSED, preferred_element_type=jnp.float32
         )
         up_part += lax.dot_general(
-            rows, gate_up[i, 1], TRANSPOSED, preferred_element_type=jnp.float32
+            rows, gate_up[0, 1, :, at : at + COLUMNS], TRANSPOSED, preferred_element_type=jnp.float32
         )
     hidden = gate_part / (1.0 + jnp.exp(-gate_part)) * up_part
     hidden = (hidden * row_weight).astype(jnp.bfloat16)
     half = kept_ref.shape[0]
-    for i in range(chunks):
-        at = i * COLUMNS
-        second[i].wait()
-        out = jnp.dot(hidden, down_weight[i], preferred_element_type=jnp.float32)
-        out = out.astype(jnp.bfloat16)
+    for at in range(0, kept_ref.shape[1], COLUMNS):
+        out = jnp.dot(
+            hidden, down_weight[0, :, at : at + COLUMNS], preferred_element_type=jnp.float32
+        ).astype(jnp.bfloat16)
         kept_ref[:, at : at + COLUMNS] = out[:half]
         sent_ref[:, at : at + COLUMNS] = out[half:]
 
@@ -228,14 +226,8 @@
     return pl.pallas_call(
         lambda *refs: expert_kernel(len(have), ep_count, blocks, weight_at, *refs),
         out_shape=(half, half),
-        in_specs=[SCALARS] + [WHOLE] * (len(have) + 1) + [ANYWHERE] * (len(after) + 2),
+        in_specs=[SCALARS] + [WHOLE] * (len(have) + 3) + [ANYWHERE] * len(after),
         out_specs=(WHOLE, WHOLE),
-        scratch_shapes=[
-            pltpu.VMEM((model_width // COLUMNS, 2, hidden_units, COLUMNS), jnp.bfloat16),
-            pltpu.VMEM((model_width // COLUMNS, hidden_units, COLUMNS), jnp.bfloat16),
-            pltpu.SemaphoreType.DMA((model_width // COLUMNS,)),
-            pltpu.SemaphoreType.DMA((model_width // COLUMNS,)),
-        ],
         compiler_params=pltpu.CompilerParams(vmem_limit_bytes=VMEM_LIMIT),
         cost_estimate=pl.CostEstimate(
             flops=6 * tokens * hidden_units * model_width,
@@ -311,6 +303,7 @@
         )
     sources = [ep_index ^ step for step in range(ep_count)]
 
+    held_out = hold_call([out_weight], payload)[0]
     all_open = hits == HOLD_MOST * ep_count
     holder = hit_pages // pool_pages
     counts = jnp.sum(
@@ -340,9 +333,30 @@
 
     heads_out, _ = scatter(
         *attend_call(
-            span_lengths, place, counts, queries, arrived, out_weight, held, blocks, all_open
-        )
-    )
+            span_lengths, place, counts, queries, arrived, held_out, held, blocks, all_open
+        )
+    )
+    own_most = 2 * (tokens // page_size)
+    page_count = new_owner.shape[0]
+    pages_here = tokens // page_size
+    owned_pages = new_owner == ep_index
+    page_ids = jnp.arange(page_count, dtype=jnp.int32)
+    owner_rank = jnp.sum(
+        ((page_ids[None, :] < page_ids[:, None]) & owned_pages[None, :]).astype(jnp.int32), axis=1
+    )
+    choose = owned_pages[None, :] & (
+        owner_rank[None, :] == jnp.arange(own_most, dtype=jnp.int32)[:, None]
+    )
+    page_index = jnp.sum(jnp.where(choose, page_ids[None, :], 0), axis=1)
+    has_page = jnp.any(choose, axis=1)
+    suffix = jnp.concatenate([block[held : held + tokens] for block in arrived], axis=0)
+    spot = (ep_index ^ (page_index // pages_here)) * pages_here + page_index % pages_here
+    taken = suffix.reshape(page_count, page_size, 2 * HD).at[spot].get(mode="promise_in_bounds")
+    slot_in_span = (page_index % pages_here)[:, None] * page_size + jnp.arange(page_size)[None, :]
+    kept = has_page[:, None] & (slot_in_span < span_lengths[page_index // pages_here][:, None])
+    head_pages = jnp.where(kept[:, :, None], taken, jnp.zeros((), jnp.bfloat16))
+    heads_out, head_pages = lax.optimization_barrier([heads_out, head_pages])
+
     own_hidden = lax.dynamic_slice_in_dim(hidden_in, block_index * row_count, row_count, 0)
     residual = (own_hidden.astype(jnp.float32) + heads_out).astype(jnp.bfloat16)
     resid_wide = residual.astype(jnp.float32)
@@ -352,56 +366,29 @@
         * norm_gain
     ).astype(jnp.bfloat16)
 
-    own_most = 2 * (tokens // page_size)
-    page_count = new_owner.shape[0]
-    pages_here = tokens // page_size
-    owned_pages = new_owner == ep_index
-    page_ids = jnp.arange(page_count, dtype=jnp.int32)
-    owner_rank = jnp.sum(
-        ((page_ids[None, :] < page_ids[:, None]) & owned_pages[None, :]).astype(jnp.int32), axis=1
-    )
-    choose = owned_pages[None, :] & (
-        owner_rank[None, :] == jnp.arange(own_most, dtype=jnp.int32)[:, None]
-    )
-    page_index = jnp.sum(jnp.where(choose, page_ids[None, :], 0), axis=1)
-    has_page = jnp.any(choose, axis=1)
-    suffix = jnp.concatenate([block[held : held + tokens] for block in arrived], axis=0)
-    spot = (ep_index ^ (page_index // pages_here)) * pages_here + page_index % pages_here
-    taken = suffix.reshape(page_count, page_size, 2 * HD).at[spot].get(mode="promise_in_bounds")
-    slot_in_span = (page_index % pages_here)[:, None] * page_size + jnp.arange(page_size)[None, :]
-    kept = has_page[:, None] & (slot_in_span < span_lengths[page_index // pages_here][:, None])
-    head_pages = jnp.where(kept[:, :, None], taken, jnp.zeros((), jnp.bfloat16))
-
-    order = [0] + list(range(ep_count - 1, 0, -1))
+    order = list(range(ep_count - 1, -1, -1))
+    crossed = lax.optimization_barrier([across(normed, step) for step in order[:-1]])
+    held_gate_up, held_down = hold_call([gate_up, down_weight], crossed[0])
     given = []
     finished = []
-
-    def experts_of(step, piece, turn):
-        have = [piece]
+    mixture = resid_wide
+    for turn, step in enumerate(order):
+        have = [crossed[turn] if step > 0 else normed]
         for bit in bits + [1]:
             have += [exchange(part, bit) for part in have]
         after = given[turn - 2 : turn - 1] if turn >= 2 else []
         after = after + (finished[turn - 3 : turn - 2] if turn >= 3 else [])
-        return expert_call(
+        kept, sent = expert_call(
             place,
             arrived[step],
             have,
-            gate_up,
-            down_weight,
+            held_gate_up,
+            held_down,
             after,
             ep_count,
             blocks,
             held + tokens,
         )
-
-    kept, sent = experts_of(0, normed, 0)
-    sent, head_pages, *crossed = lax.optimization_barrier(
-        [sent, head_pages] + [across(normed, step) for step in order[1:]]
-    )
-    mixture = resid_wide
-    for turn, step in enumerate(order):
-        if turn > 0:
-            kept, sent = experts_of(step, crossed[turn - 1], turn)
         own, gives = scatter(kept, sent)
         own = own.astype(jnp.bfloat16)
         given.append(gives[0] if gives else own)

time: 121 us -> 116 us (0.959)
  Pallas kernels: 35.8 us -> 17.6 us
  local copies, waits for them, and re-layouts: 11.6 us -> 26.9 us
  other arithmetic: 11.5 us -> 8.52 us
    unnamed x61 -> x29, local copies, waits for them, and re-layouts: 5.24 us -> 22.8 us
    pallas_call x4, Pallas kernels: 29.3 us -> 12.8 us  [expert_call(): pl.pallas_call(lambda *refs: expert_kernel(len(have), ep_count, blocks, w...]
    ppermute x3, waiting for transfers between devices: 11.5 us -> 3.96 us  [local(): lax.ppermute(payload, 'ep', [(i, i ^ step) for i in range(ep_count)])]
    ppermute x6, waiting for transfers between devices: 8.25 us -> 12.7 us  [local(): lax.ppermute(value, 'ep', [(i, i ^ step) for i in range(ep_count)])]
    ppermute x22, waiting for transfers between devices: 14 us -> 17.5 us  [local(): lax.ppermute(value, ('kv', 'tp'), [(i, i ^ bit) for i in range(blocks)])]
    pallas_call x1, Pallas kernels: 6.44 us -> 3.38 us  [attend_call(): pl.pallas_call(lambda *refs: attend_kernel(ep_count, held, tokens, blocks...]
    slice x3, local copies, waits for them, and re-layouts: 2.28 us -> 0.01 us  [local(): block[held:held + tokens]]
    convert_element_type x5, other arithmetic: 2.93 us -> 1.07 us  [scatter(): gives.append(give.astype(jnp.bfloat16))]
  transfers between devices with their start and end apart: 32 -> 32, of which waited for: 12 -> 12; matrix products, arithmetic and copies ran while one was open for 9% -> 6% of each run, Pallas kernels for 24% -> 12%
where the time goes in v6:
time: 116 us; the launch traced here: 115 us
  waiting for transfers between devices  34.2 us (29%)
  local copies, waits for them, and re-layouts  26.9 us (23%)
  starting transfers between devices  26.8 us (23%)
  Pallas kernels  17.6 us (15%)
  other arithmetic  8.52 us (7%)
    unnamed x29, local copies, waits for them, and re-layouts  22.8 us
    ppermute x22, waiting for transfers between devices, local(): lax.ppermute(value, ('kv', 'tp'), [(i, i ^ bit) for i in range(blocks)])  17.5 us
    pallas_call x4, Pallas kernels, expert_call(): pl.pallas_call(lambda *refs: expert_kernel(len(have), ep_count, blocks, w...  12.8 us
    ppermute x6, waiting for transfers between devices, local(): lax.ppermute(value, 'ep', [(i, i ^ step) for i in range(ep_count)])  12.7 us
    ppermute x22, starting transfers between devices, local(): lax.ppermute(value, ('kv', 'tp'), [(i, i ^ bit) for i in range(blocks)])  11.8 us
    ppermute x6, starting transfers between devices, local(): lax.ppermute(value, 'ep', [(i, i ^ step) for i in range(ep_count)])  9.06 us
    ppermute x3, starting transfers between devices, local(): lax.ppermute(payload, 'ep', [(i, i ^ step) for i in range(ep_count)])  5.68 us
    ppermute x3, waiting for transfers between devices, local(): lax.ppermute(payload, 'ep', [(i, i ^ step) for i in range(ep_count)])  3.96 us
  transfers between devices with their start and end apart: 32, of which 12 were waited for; matrix products, arithmetic and copies ran while one was open for 6% of the time, Pallas kernels for 12%

profile of v6, /device:TPU:0, one launch (start us, length us, event | category | flops | bytes accessed | tf_op | source)
XLA Modules:
  0.0 115.0 jit_solution(3062570602305688693)
XLA Ops:
  5.5 3.1 %collective-permute-start = (bf16[336,256]{1,0:T(8,128)(2,1)S(1)}, bf16[336,256]{1,0:T(8,128)(2,1)S(1)}, u32[]{:S(2)}, u32[]{:S(2)}) collective-permute-start(bf16[336,256]{1,0:T(8,128)(2,1)S(1)} %pad_maximum_fusion.refs_1_.refs_4_), channel_id=1, source_target_pairs={{0,4},{4,0},{8,12},{12,8},{1,5},{5,1},{9,13},{13,9},{2,6},{6,2},{1... | collective-permute-start | bytes 516104 | tf_op jit(solution)/shard_map/ppermute | solution.py:302
  8.6 2.6 %collective-permute-start.1 = (bf16[336,256]{1,0:T(8,128)(2,1)S(1)}, bf16[336,256]{1,0:T(8,128)(2,1)S(1)}, u32[]{:S(2)}, u32[]{:S(2)}) collective-permute-start(bf16[336,256]{1,0:T(8,128)(2,1)S(1)} %pad_maximum_fusion.refs_1_.refs_4_), channel_id=1, source_target_pairs={{0,8},{4,12},{8,0},{12,4},{1,9},{5,13},{9,1},{13,5},{2,10},{6,14},... | collective-permute-start | bytes 516104 | tf_op jit(solution)/shard_map/ppermute | solution.py:302
  12.2 3.4 %copy-done.8 = bf16[1024,4096]{1,0:T(8,128)(2,1)S(1)} copy-done((bf16[1024,4096]{1,0:T(8,128)(2,1)S(1)}, bf16[1024,4096]{1,0:T(8,128)(2,1)}, u32[]{:S(2)}) %copy-start.8) | copy-done | bytes 8388632
  16.2 3.3 %copy-done.6 = bf16[1024,4096]{1,0:T(8,128)(2,1)} copy-done((bf16[1024,4096]{1,0:T(8,128)(2,1)}, bf16[1024,4096]{1,0:T(8,128)(2,1)S(1)}, u32[]{:S(2)}) %copy-start.6) | copy-done | bytes 8388632
  20.2 4.0 %collective-permute-done.1.refs_6_.refs_1_ = bf16[336,256]{1,0:T(8,128)(2,1)S(1)} collective-permute-done((bf16[336,256]{1,0:T(8,128)(2,1)S(1)}, bf16[336,256]{1,0:T(8,128)(2,1)S(1)}, u32[]{:S(2)}, u32[]{:S(2)}) %collective-permute-start.1) | collective-permute-done | bytes 172064 | tf_op jit(solution)/shard_map/ppermute | solution.py:302
  24.2 3.4 %copy-done.7 = bf16[1024,4096]{1,0:T(8,128)(2,1)S(1)} copy-done((bf16[1024,4096]{1,0:T(8,128)(2,1)S(1)}, bf16[1024,4096]{1,0:T(8,128)(2,1)}, u32[]{:S(2)}) %copy-start.7) | copy-done | bytes 8388632
  27.5 3.4 %attend.1 = (f32[32,4096]{1,0:T(8,128)S(1)}, bf16[32,4096]{1,0:T(8,128)(2,1)S(1)}) custom-call(s32[4]{0:T(128)S(1)} %copy-done.1, s32[2]{0:T(128)S(1)} %pad_add_fusion.refs_1_.refs_0_, s32[1]{0:T(128)} %constant.90.clone.1.refs_2_, bf16[64,1024]{1,0:T(8,128)(2,1)S(1)} %copy-done.11, bf16[336,256]{1,0:T(8,128)(2,1)S(1)} %pad_maximum_fusion.refs_1_.refs_4_, ...), custom_call_target="tpu_custom_call" | custom-call | flops 872415232 | bytes 8388608 | tf_op jit(solution)/shard_map/attend/pallas_call | solution.py:159
  34.2 4.0 %collective-permute-done.4 = bf16[16,4096]{1,0:T(8,128)(2,1)S(1)} collective-permute-done((bf16[16,4096]{1,0:T(8,128)(2,1)S(1)}, bf16[16,4096]{1,0:T(8,128)(2,1)S(1)}, u32[]{:S(2)}, u32[]{:S(2)}) %collective-permute-start.4) | collective-permute-done | bytes 131104 | tf_op jit(solution)/shard_map/ppermute | solution.py:315
  39.4 2.4 %collective-permute-start.5 = (bf16[16,4096]{1,0:T(8,128)(2,1)S(1)}, bf16[16,4096]{1,0:T(8,128)(2,1)S(1)}, u32[]{:S(2)}, u32[]{:S(2)}) collective-permute-start(bf16[16,4096]{1,0:T(8,128)(2,1)S(1)} %fusion.2.refs_2_), channel_id=1, source_target_pairs={{0,12},{4,8},{8,4},{12,0},{1,13},{5,9},{9,5},{13,1},{2,14},{6,10},... | collective-permute-start | bytes 393224 | tf_op jit(solution)/shard_map/ppermute | solution.py:318
  43.9 2.8 %collective-permute-done.5.refs_2_ = bf16[16,4096]{1,0:T(8,128)(2,1)S(1)} collective-permute-done((bf16[16,4096]{1,0:T(8,128)(2,1)S(1)}, bf16[16,4096]{1,0:T(8,128)(2,1)S(1)}, u32[]{:S(2)}, u32[]{:S(2)}) %collective-permute-start.5) | collective-permute-done | bytes 131104 | tf_op jit(solution)/shard_map/ppermute | solution.py:318
  46.7 7.7 %collective-permute-done.6.refs_2_ = bf16[16,4096]{1,0:T(8,128)(2,1)S(1)} collective-permute-done((bf16[16,4096]{1,0:T(8,128)(2,1)S(1)}, bf16[16,4096]{1,0:T(8,128)(2,1)S(1)}, u32[]{:S(2)}, u32[]{:S(2)}) %collective-permute-start.6) | collective-permute-done | bytes 131104 | tf_op jit(solution)/shard_map/ppermute | solution.py:318
  55.9 3.7 %collective-permute-done.8.refs_3_ = bf16[16,4096]{1,0:T(8,128)(2,1)S(1)} collective-permute-done((bf16[16,4096]{1,0:T(8,128)(2,1)S(1)}, bf16[16,4096]{1,0:T(8,128)(2,1)S(1)}, u32[]{:S(2)}, u32[]{:S(2)}) %collective-permute-start.8) | collective-permute-done | bytes 131104 | tf_op jit(solution)/shard_map/ppermute | solution.py:315
  61.1 2.8 %copy-done.9 = bf16[1,2,384,4096]{3,2,1,0:T(8,128)(2,1)S(1)} copy-done((bf16[1,2,384,4096]{3,2,1,0:T(8,128)(2,1)S(1)}, bf16[1,2,384,4096]{3,2,1,0:T(8,128)(2,1)}, u32[]{:S(2)}) %copy-start.9) | copy-done | bytes 6291480
  66.6 3.2 %experts.4 = (bf16[32,4096]{1,0:T(8,128)(2,1)S(1)}, bf16[32,4096]{1,0:T(8,128)(2,1)S(1)}) custom-call(s32[2]{0:T(128)S(1)} %pad_add_fusion.refs_1_.refs_0_, bf16[336,256]{1,0:T(8,128)(2,1)S(1)} %collective-permute-done.2.refs_7_.refs_1_, bf16[16,4096]{1,0:T(8,128)(2,1)S(1)} %collective-permute-done.5.refs_2_, ...), custom_call_target="tpu_custom_call" | custom-call | flops 603979776 | bytes 9437184 | tf_op jit(solution)/shard_map/experts/pallas_call | solution.py:226
  69.9 2.6 %copy-done.2 = bf16[1,2,384,4096]{3,2,1,0:T(8,128)(2,1)} copy-done((bf16[1,2,384,4096]{3,2,1,0:T(8,128)(2,1)}, bf16[1,2,384,4096]{3,2,1,0:T(8,128)(2,1)S(1)}, u32[]{:S(2)}) %copy-start.2) | copy-done | bytes 6291480
  76.6 2.7 %collective-permute-done.20.refs_3_ = bf16[16,4096]{1,0:T(8,128)(2,1)S(1)} collective-permute-done((bf16[16,4096]{1,0:T(8,128)(2,1)S(1)}, bf16[16,4096]{1,0:T(8,128)(2,1)S(1)}, u32[]{:S(2)}, u32[]{:S(2)}) %collective-permute-start.20) | collective-permute-done | bytes 131104 | tf_op jit(solution)/shard_map/ppermute | solution.py:315
  79.8 2.8 %copy-done.3 = bf16[1,2,384,4096]{3,2,1,0:T(8,128)(2,1)S(1)} copy-done((bf16[1,2,384,4096]{3,2,1,0:T(8,128)(2,1)S(1)}, bf16[1,2,384,4096]{3,2,1,0:T(8,128)(2,1)}, u32[]{:S(2)}) %copy-start.3) | copy-done | bytes 6291480
  84.5 3.2 %experts.5 = (bf16[32,4096]{1,0:T(8,128)(2,1)S(1)}, bf16[32,4096]{1,0:T(8,128)(2,1)S(1)}) custom-call(s32[2]{0:T(128)S(1)} %pad_add_fusion.refs_1_.refs_0_, bf16[336,256]{1,0:T(8,128)(2,1)S(1)} %collective-permute-done.1.refs_6_.refs_1_, bf16[16,4096]{1,0:T(8,128)(2,1)S(1)} %collective-permute-done.6.refs_2_, ...), custom_call_target="tpu_custom_call" | custom-call | flops 603979776 | bytes 9437184 | tf_op jit(solution)/shard_map/experts/pallas_call | solution.py:226
  91.9 3.2 %experts.6 = (bf16[32,4096]{1,0:T(8,128)(2,1)S(1)}, bf16[32,4096]{1,0:T(8,128)(2,1)S(1)}) custom-call(s32[2]{0:T(128)S(1)} %pad_add_fusion.refs_1_.refs_0_, bf16[336,256]{1,0:T(8,128)(2,1)S(1)} %collective-permute-done.refs_5_.refs_1_, bf16[16,4096]{1,0:T(8,128)(2,1)S(1)} %collective-permute-done.7.refs_2_, ...), custom_call_target="tpu_custom_call" | custom-call | flops 603979776 | bytes 9437184 | tf_op jit(solution)/shard_map/experts/pallas_call | solution.py:226
  96.6 2.4 %collective-permute-start.13 = (bf16[16,4096]{1,0:T(8,128)(2,1)S(1)}, bf16[16,4096]{1,0:T(8,128)(2,1)S(1)}, u32[]{:S(2)}, u32[]{:S(2)}) collective-permute-start(bf16[16,4096]{1,0:T(8,128)(2,1)S(1)} %add_convert_fusion.6.refs_9_), channel_id=1, source_target_pairs={{0,12},{4,8},{8,4},{12,0},{1,13},{5,9},{9,5},{13,1},{2,14},{6,10},... | collective-permute-start | bytes 393224 | tf_op jit(solution)/shard_map/ppermute | solution.py:318
  99.0 3.2 %experts.7 = (bf16[32,4096]{1,0:T(8,128)(2,1)S(1)}, bf16[32,4096]{1,0:T(8,128)(2,1)S(1)}) custom-call(s32[2]{0:T(128)S(1)} %pad_add_fusion.refs_1_.refs_0_, bf16[336,256]{1,0:T(8,128)(2,1)S(1)} %pad_maximum_fusion.refs_1_.refs_4_, bf16[16,4096]{1,0:T(8,128)(2,1)S(1)} %fusion.2.refs_2_, bf16[16,4096]{1,0:T(8,128)(2,1)S(1)} %collective-permute-done.26.refs_3_, ...), custom_call_target="tpu_custom_call" | custom-call | flops 603979776 | bytes 9437184 | tf_op jit(solution)/shard_map/experts/pallas_call | solution.py:226
  104.9 4.2 %collective-permute-done.24 = bf16[16,4096]{1,0:T(8,128)(2,1)S(1)} collective-permute-done((bf16[16,4096]{1,0:T(8,128)(2,1)S(1)}, bf16[16,4096]{1,0:T(8,128)(2,1)S(1)}, u32[]{:S(2)}, u32[]{:S(2)}) %collective-permute-start.24) | collective-permute-done | bytes 131104 | tf_op jit(solution)/shard_map/ppermute | solution.py:315
  109.2 2.1 %collective-permute-start.25 = (bf16[16,4096]{1,0:T(8,128)(2,1)S(1)}, bf16[16,4096]{1,0:T(8,128)(2,1)S(1)}, u32[]{:S(2)}, u32[]{:S(2)}) collective-permute-start(bf16[16,4096]{1,0:T(8,128)(2,1)S(1)} %add_convert_fusion.2), channel_id=1, source_target_pairs={{0,4},{4,0},{8,12},{12,8},{1,5},{5,1},{9,13},{13,9},{2,6},{6,2},{1... | collective-permute-start | bytes 393224 | tf_op jit(solution)/shard_map/ppermute | solution.py:318
  112.1 2.1 %collective-permute-done.25 = bf16[16,4096]{1,0:T(8,128)(2,1)S(1)} collective-permute-done((bf16[16,4096]{1,0:T(8,128)(2,1)S(1)}, bf16[16,4096]{1,0:T(8,128)(2,1)S(1)}, u32[]{:S(2)}, u32[]{:S(2)}) %collective-permute-start.25) | collective-permute-done | bytes 131104 | tf_op jit(solution)/shard_map/ppermute | solution.py:318
  (122 shorter events, 35.8 us)
Async XLA Ops:
  5.5 14.7 %collective-permute-start = (bf16[336,256]{1,0:T(8,128)(2,1)S(1)}, bf16[336,256]{1,0:T(8,128)(2,1)S(1)}, u32[]{:S(2)}, u32[]{:S(2)}) collective-permute-start(bf16[336,256]{1,0:T(8,128)(2,1)S(1)} %pad_maximum_fusion.refs_1_.refs_4_), channel_id=1, source_target_pairs={{0,4},{4,0},{8,12},{12,8},{1,5},{5,1},{9,13},{13,9},{2,6},{6,2},{1... | collective-permute-start | bytes 516104 | tf_op jit(solution)/shard_map/ppermute | solution.py:302
  8.6 15.6 %collective-permute-start.1 = (bf16[336,256]{1,0:T(8,128)(2,1)S(1)}, bf16[336,256]{1,0:T(8,128)(2,1)S(1)}, u32[]{:S(2)}, u32[]{:S(2)}) collective-permute-start(bf16[336,256]{1,0:T(8,128)(2,1)S(1)} %pad_maximum_fusion.refs_1_.refs_4_), channel_id=1, source_target_pairs={{0,8},{4,12},{8,0},{12,4},{1,9},{5,13},{9,1},{13,5},{2,10},{6,14},... | collective-permute-start | bytes 516104 | tf_op jit(solution)/shard_map/ppermute | solution.py:302
  11.2 13.0 %collective-permute-start.2 = (bf16[336,256]{1,0:T(8,128)(2,1)S(1)}, bf16[336,256]{1,0:T(8,128)(2,1)S(1)}, u32[]{:S(2)}, u32[]{:S(2)}) collective-permute-start(bf16[336,256]{1,0:T(8,128)(2,1)S(1)} %pad_maximum_fusion.refs_1_.refs_4_), channel_id=1, source_target_pairs={{0,12},{4,8},{8,4},{12,0},{1,13},{5,9},{9,5},{13,1},{2,14},{6,10},... | collective-permute-start | bytes 516104 | tf_op jit(solution)/shard_map/ppermute | solution.py:302
  39.4 7.3 %collective-permute-start.5 = (bf16[16,4096]{1,0:T(8,128)(2,1)S(1)}, bf16[16,4096]{1,0:T(8,128)(2,1)S(1)}, u32[]{:S(2)}, u32[]{:S(2)}) collective-permute-start(bf16[16,4096]{1,0:T(8,128)(2,1)S(1)} %fusion.2.refs_2_), channel_id=1, source_target_pairs={{0,12},{4,8},{8,4},{12,0},{1,13},{5,9},{9,5},{13,1},{2,14},{6,10},... | collective-permute-start | bytes 393224 | tf_op jit(solution)/shard_map/ppermute | solution.py:318
  41.8 12.6 %collective-permute-start.6 = (bf16[16,4096]{1,0:T(8,128)(2,1)S(1)}, bf16[16,4096]{1,0:T(8,128)(2,1)S(1)}, u32[]{:S(2)}, u32[]{:S(2)}) collective-permute-start(bf16[16,4096]{1,0:T(8,128)(2,1)S(1)} %fusion.2.refs_2_), channel_id=1, source_target_pairs={{0,8},{4,12},{8,0},{12,4},{1,9},{5,13},{9,1},{13,5},{2,10},{6,14},... | collective-permute-start | bytes 393224 | tf_op jit(solution)/shard_map/ppermute | solution.py:318
  43.7 10.7 %collective-permute-start.7 = (bf16[16,4096]{1,0:T(8,128)(2,1)S(1)}, bf16[16,4096]{1,0:T(8,128)(2,1)S(1)}, u32[]{:S(2)}, u32[]{:S(2)}) collective-permute-start(bf16[16,4096]{1,0:T(8,128)(2,1)S(1)} %fusion.2.refs_2_), channel_id=1, source_target_pairs={{0,4},{4,0},{8,12},{12,8},{1,5},{5,1},{9,13},{13,9},{2,6},{6,2},{1... | collective-permute-start | bytes 393224 | tf_op jit(solution)/shard_map/ppermute | solution.py:318
  55.9 10.7 %collective-permute-start.9 = (bf16[16,4096]{1,0:T(8,128)(2,1)S(1)}, bf16[16,4096]{1,0:T(8,128)(2,1)S(1)}, u32[]{:S(2)}, u32[]{:S(2)}) collective-permute-start(bf16[16,4096]{1,0:T(8,128)(2,1)S(1)} %collective-permute-done.5.refs_2_), channel_id=1, source_target_pairs={{0,1},{1,0},{2,3},{3,2},{4,5},{5,4},{6,7},{7,6},{8,9},{9,8},{10,11... | collective-permute-start | bytes 393224 | tf_op jit(solution)/shard_map/ppermute | solution.py:315
  59.6 7.0 %collective-permute-start.10 = (bf16[16,4096]{1,0:T(8,128)(2,1)S(1)}, bf16[16,4096]{1,0:T(8,128)(2,1)S(1)}, u32[]{:S(2)}, u32[]{:S(2)}) collective-permute-start(bf16[16,4096]{1,0:T(8,128)(2,1)S(1)} %collective-permute-done.8.refs_3_), channel_id=1, source_target_pairs={{0,1},{1,0},{2,3},{3,2},{4,5},{5,4},{6,7},{7,6},{8,9},{9,8},{10,11... | collective-permute-start | bytes 393224 | tf_op jit(solution)/shard_map/ppermute | solution.py:315
  59.6 13.9 %collective-permute-start.14 = (bf16[16,4096]{1,0:T(8,128)(2,1)S(1)}, bf16[16,4096]{1,0:T(8,128)(2,1)S(1)}, u32[]{:S(2)}, u32[]{:S(2)}) collective-permute-start(bf16[16,4096]{1,0:T(8,128)(2,1)S(1)} %collective-permute-done.6.refs_2_), channel_id=1, source_target_pairs={{0,2},{1,3},{2,0},{3,1},{4,6},{5,7},{6,4},{7,5},{8,10},{9,11},{10,... | collective-permute-start | bytes 393224 | tf_op jit(solution)/shard_map/ppermute | solution.py:315
  72.5 15.2 %collective-permute-start.11 = (bf16[32,4096]{1,0:T(8,128)(2,1)S(1)}, bf16[32,4096]{1,0:T(8,128)(2,1)}, u32[]{:S(2)}, u32[]{:S(2)}) collective-permute-start(bf16[32,4096]{1,0:T(8,128)(2,1)S(1)} %get-tuple-element.26), channel_id=1, source_target_pairs={{0,1},{1,0},{2,3},{3,2},{4,5},{5,4},{6,7},{7,6},{8,9},{9,8},{10,11... | collective-permute-start | bytes 786440 | tf_op jit(solution)/shard_map/ppermute | solution.py:315
  73.0 6.3 %collective-permute-start.20 = (bf16[16,4096]{1,0:T(8,128)(2,1)S(1)}, bf16[16,4096]{1,0:T(8,128)(2,1)S(1)}, u32[]{:S(2)}, u32[]{:S(2)}) collective-permute-start(bf16[16,4096]{1,0:T(8,128)(2,1)S(1)} %collective-permute-done.7.refs_2_), channel_id=1, source_target_pairs={{0,2},{1,3},{2,0},{3,1},{4,6},{5,7},{6,4},{7,5},{8,10},{9,11},{10,... | collective-permute-start | bytes 393224 | tf_op jit(solution)/shard_map/ppermute | solution.py:315
  74.8 14.5 %collective-permute-start.26 = (bf16[16,4096]{1,0:T(8,128)(2,1)S(1)}, bf16[16,4096]{1,0:T(8,128)(2,1)S(1)}, u32[]{:S(2)}, u32[]{:S(2)}) collective-permute-start(bf16[16,4096]{1,0:T(8,128)(2,1)S(1)} %fusion.2.refs_2_), channel_id=1, source_target_pairs={{0,2},{1,3},{2,0},{3,1},{4,6},{5,7},{6,4},{7,5},{8,10},{9,11},{10,... | collective-permute-start | bytes 393224 | tf_op jit(solution)/shard_map/ppermute | solution.py:315
  76.3 20.2 %collective-permute-start.27 = (bf16[16,4096]{1,0:T(8,128)(2,1)S(1)}, bf16[16,4096]{1,0:T(8,128)(2,1)S(1)}, u32[]{:S(2)}, u32[]{:S(2)}) collective-permute-start(bf16[16,4096]{1,0:T(8,128)(2,1)S(1)} %fusion.2.refs_2_), channel_id=1, source_target_pairs={{0,1},{1,0},{2,3},{3,2},{4,5},{5,4},{6,7},{7,6},{8,9},{9,8},{10,11... | collective-permute-start | bytes 393224 | tf_op jit(solution)/shard_map/ppermute | solution.py:315
  79.3 10.3 %collective-permute-start.21 = (bf16[16,4096]{1,0:T(8,128)(2,1)S(1)}, bf16[16,4096]{1,0:T(8,128)(2,1)S(1)}, u32[]{:S(2)}, u32[]{:S(2)}) collective-permute-start(bf16[16,4096]{1,0:T(8,128)(2,1)S(1)} %collective-permute-done.7.refs_2_), channel_id=1, source_target_pairs={{0,1},{1,0},{2,3},{3,2},{4,5},{5,4},{6,7},{7,6},{8,9},{9,8},{10,11... | collective-permute-start | bytes 393224 | tf_op jit(solution)/shard_map/ppermute | solution.py:315
  79.3 10.6 %collective-permute-start.22 = (bf16[16,4096]{1,0:T(8,128)(2,1)S(1)}, bf16[16,4096]{1,0:T(8,128)(2,1)S(1)}, u32[]{:S(2)}, u32[]{:S(2)}) collective-permute-start(bf16[16,4096]{1,0:T(8,128)(2,1)S(1)} %collective-permute-done.20.refs_3_), channel_id=1, source_target_pairs={{0,1},{1,0},{2,3},{3,2},{4,5},{5,4},{6,7},{7,6},{8,9},{9,8},{10,11... | collective-permute-start | bytes 393224 | tf_op jit(solution)/shard_map/ppermute | solution.py:315
  89.3 6.3 %collective-permute-start.12 = (bf16[16,4096]{1,0:T(8,128)(2,1)S(1)}, bf16[16,4096]{1,0:T(8,128)(2,1)S(1)}, u32[]{:S(2)}, u32[]{:S(2)}) collective-permute-start(bf16[16,4096]{1,0:T(8,128)(2,1)S(1)} %add_convert_fusion.7.refs_8_), channel_id=1, source_target_pairs={{0,2},{1,3},{2,0},{3,1},{4,6},{5,7},{6,4},{7,5},{8,10},{9,11},{10,... | collective-permute-start | bytes 393224 | tf_op jit(solution)/shard_map/ppermute | solution.py:315
  89.3 21.9 %collective-permute-start.31 = (bf16[8,16,256]{2,1,0:T(8,128)(2,1)S(1)}, bf16[8,16,256]{2,1,0:T(8,128)(2,1)S(1)}, u32[]{:S(2)}, u32[]{:S(2)}) collective-permute-start(bf16[8,16,256]{2,1,0:T(8,128)(2,1)S(1)} %broadcast_select_fusion), channel_id=1, source_target_pairs={{0,1},{1,0},{2,3},{3,2},{4,5},{5,4},{6,7},{7,6},{8,9},{9,8},{10,11... | collective-permute-start | bytes 196616 | tf_op jit(solution)/shard_map/ppermute | solution.py:406
  89.5 9.5 %collective-permute-start.28 = (bf16[16,4096]{1,0:T(8,128)(2,1)S(1)}, bf16[16,4096]{1,0:T(8,128)(2,1)S(1)}, u32[]{:S(2)}, u32[]{:S(2)}) collective-permute-start(bf16[16,4096]{1,0:T(8,128)(2,1)S(1)} %collective-permute-done.26.refs_3_), channel_id=1, source_target_pairs={{0,1},{1,0},{2,3},{3,2},{4,5},{5,4},{6,7},{7,6},{8,9},{9,8},{10,11... | collective-permute-start | bytes 393224 | tf_op jit(solution)/shard_map/ppermute | solution.py:315
  89.9 12.6 %collective-permute-start.18 = (bf16[16,4096]{1,0:T(8,128)(2,1)S(1)}, bf16[16,4096]{1,0:T(8,128)(2,1)S(1)}, u32[]{:S(2)}, u32[]{:S(2)}) collective-permute-start(bf16[16,4096]{1,0:T(8,128)(2,1)S(1)} %add_convert_fusion.5.refs_8_), channel_id=1, source_target_pairs={{0,2},{1,3},{2,0},{3,1},{4,6},{5,7},{6,4},{7,5},{8,10},{9,11},{10,... | collective-permute-start | bytes 393224 | tf_op jit(solution)/shard_map/ppermute | solution.py:315
  95.6 7.1 %collective-permute-start.23 = (bf16[32,4096]{1,0:T(8,128)(2,1)S(1)}, bf16[32,4096]{1,0:T(8,128)(2,1)S(1)}, u32[]{:S(2)}, u32[]{:S(2)}) collective-permute-start(bf16[32,4096]{1,0:T(8,128)(2,1)S(1)} %get-tuple-element.32), channel_id=1, source_target_pairs={{0,1},{1,0},{2,3},{3,2},{4,5},{5,4},{6,7},{7,6},{8,9},{9,8},{10,11... | collective-permute-start | bytes 786440 | tf_op jit(solution)/shard_map/ppermute | solution.py:315
  96.6 15.5 %collective-permute-start.13 = (bf16[16,4096]{1,0:T(8,128)(2,1)S(1)}, bf16[16,4096]{1,0:T(8,128)(2,1)S(1)}, u32[]{:S(2)}, u32[]{:S(2)}) collective-permute-start(bf16[16,4096]{1,0:T(8,128)(2,1)S(1)} %add_convert_fusion.6.refs_9_), channel_id=1, source_target_pairs={{0,12},{4,8},{8,4},{12,0},{1,13},{5,9},{9,5},{13,1},{2,14},{6,10},... | collective-permute-start | bytes 393224 | tf_op jit(solution)/shard_map/ppermute | solution.py:318
  102.6 9.5 %collective-permute-start.19 = (bf16[16,4096]{1,0:T(8,128)(2,1)S(1)}, bf16[16,4096]{1,0:T(8,128)(2,1)S(1)}, u32[]{:S(2)}, u32[]{:S(2)}) collective-permute-start(bf16[16,4096]{1,0:T(8,128)(2,1)S(1)} %add_convert_fusion.4), channel_id=1, source_target_pairs={{0,8},{4,12},{8,0},{12,4},{1,9},{5,13},{9,1},{13,5},{2,10},{6,14},... | collective-permute-start | bytes 393224 | tf_op jit(solution)/shard_map/ppermute | solution.py:318
  102.7 6.4 %collective-permute-start.24 = (bf16[16,4096]{1,0:T(8,128)(2,1)S(1)}, bf16[16,4096]{1,0:T(8,128)(2,1)S(1)}, u32[]{:S(2)}, u32[]{:S(2)}) collective-permute-start(bf16[16,4096]{1,0:T(8,128)(2,1)S(1)} %add_convert_fusion.3), channel_id=1, source_target_pairs={{0,2},{1,3},{2,0},{3,1},{4,6},{5,7},{6,4},{7,5},{8,10},{9,11},{10,... | collective-permute-start | bytes 393224 | tf_op jit(solution)/shard_map/ppermute | solution.py:315
  103.9 8.2 %collective-permute-start.30 = (bf16[16,4096]{1,0:T(8,128)(2,1)S(1)}, bf16[16,4096]{1,0:T(8,128)(2,1)S(1)}, u32[]{:S(2)}, u32[]{:S(2)}) collective-permute-start(bf16[16,4096]{1,0:T(8,128)(2,1)S(1)} %add_convert_fusion.1), channel_id=1, source_target_pairs={{0,2},{1,3},{2,0},{3,1},{4,6},{5,7},{6,4},{7,5},{8,10},{9,11},{10,... | collective-permute-start | bytes 393224 | tf_op jit(solution)/shard_map/ppermute | solution.py:315
  (21 other events, 89.4 us)

commit v7 on v6

--- a/solution.py
+++ b/solution.py
@@ -43,9 +43,9 @@
 VMEM_LIMIT = 16 * 2**20
 
 
-def hold_kernel(*refs):
-    count = (len(refs) - 2) // 2
-    sources, held, sem = refs[:count], refs[count + 1 : -1], refs[-1]
+def hold_kernel(count, *refs):
+    sources, held, token, sem = refs[:count], refs[-2 - count : -2], refs[-2], refs[-1]
+    token[...] = jnp.zeros_like(token)
     copies = [
         pltpu.make_async_copy(source, target, sem.at[i])
         for i, (source, target) in enumerate(zip(sources, held))
@@ -56,29 +56,54 @@
         copy.wait()
 
 
-def hold_call(arrays, after):
+def hold_call(arrays, *after):
     size = sum(math.prod(array.shape) * 2 for array in arrays)
     return pl.pallas_call(
-        hold_kernel,
-        out_shape=[jax.ShapeDtypeStruct(array.shape, array.dtype) for array in arrays],
-        in_specs=[ANYWHERE] * (len(arrays) + 1),
-        out_specs=[WHOLE] * len(arrays),
+        lambda *refs: hold_kernel(len(arrays), *refs),
+        out_shape=[jax.ShapeDtypeStruct(array.shape, array.dtype) for array in arrays]
+        + [jax.ShapeDtypeStruct((8, 128), jnp.float32)],
+        in_specs=[ANYWHERE] * (len(arrays) + len(after)),
+        out_specs=[WHOLE] * (len(arrays) + 1),
         scratch_shapes=[pltpu.SemaphoreType.DMA((len(arrays),))],
         compiler_params=pltpu.CompilerParams(vmem_limit_bytes=VMEM_LIMIT),
         cost_estimate=pl.CostEstimate(flops=0, bytes_accessed=2 * size, transcendentals=0),
         name="hold",
-    )(*arrays, after)
-
-
-def attend_kernel(ep_count, held, tokens, row_blocks, all_open, lens, place, counts, queries, *refs):
+    )(*arrays, *after)
+
+
+def attend_kernel(ep_count, held, tokens, row_blocks, all_open, lens, place, counts, owners, queries, *refs):
     blocks = refs[:ep_count]
     out_weight = refs[ep_count]
-    kept_ref, sent_ref = refs[ep_count + 1 : ep_count + 3]
-    scores, projected = refs[ep_count + 3 :]
+    kept_ref, sent_ref, pages_ref = refs[ep_count + 1 : ep_count + 4]
+    scores, projected, ranks = refs[ep_count + 4 :]
     heads = queries.shape[1] // HD
     ep_index = place[0]
     block_index = place[1]
     suffix = ep_count * tokens
+
+    page_count = owners.shape[0]
+    pages_here = page_count // ep_count
+    page_size = tokens // pages_here
+
+    def rank_of(page, earlier):
+        ranks[page] = earlier
+        return earlier + (owners[page] == ep_index).astype(jnp.int32)
+
+    lax.fori_loop(0, page_count, rank_of, jnp.int32(0))
+    pages_ref[...] = jnp.zeros_like(pages_ref)
+    for step in range(ep_count):
+        source = ep_index ^ step
+        for k in range(pages_here):
+            page = source * pages_here + k
+
+            @pl.when(owners[page] == ep_index)
+            def _(step=step, source=source, k=k, page=page):
+                first = held + k * page_size
+                entries = blocks[step][first : first + page_size, :]
+                row = lax.broadcasted_iota(jnp.int32, entries.shape, 0) + k * page_size
+                entries = jnp.where(row < lens[source], entries.astype(jnp.float32), 0.0)
+                at = pl.multiple_of(ranks[page] * page_size, page_size)
+                pages_ref[pl.ds(at, page_size), :] = entries.astype(jnp.bfloat16)
 
     own_start = jnp.int32(0)
     for j in range(ep_count):
@@ -150,23 +175,28 @@
         ref[spot * count : (spot + 1) * count, :] = rows.astype(ref.dtype)
 
 
-def attend_call(lens, place, counts, queries, arrived, out_weight, held, blocks, all_open):
+def attend_call(
+    lens, place, counts, owners, queries, arrived, out_weight, held, blocks, own_most, all_open
+):
     tokens = queries.shape[0]
     ep_count = len(arrived)
     model_width = out_weight.shape[1]
     heads = queries.shape[1] // HD
     keys = ep_count * (held + tokens)
+    page_size = tokens * ep_count // owners.shape[0]
     return pl.pallas_call(
         lambda *refs: attend_kernel(ep_count, held, tokens, blocks, all_open, *refs),
         out_shape=[
             jax.ShapeDtypeStruct((tokens // 2, model_width), jnp.float32),
             jax.ShapeDtypeStruct((tokens // 2, model_width), jnp.bfloat16),
+            jax.ShapeDtypeStruct((own_most * page_size, 2 * HD), jnp.bfloat16),
         ],
-        in_specs=[SCALARS] * 3 + [WHOLE] * (ep_count + 2),
-        out_specs=[WHOLE] * 2,
+        in_specs=[SCALARS] * 4 + [WHOLE] * (ep_count + 2),
+        out_specs=[WHOLE] * 3,
         scratch_shapes=[
             pltpu.VMEM((min(ROWS, heads * tokens), ep_count * held), jnp.float32),
             pltpu.VMEM((tokens, model_width), jnp.float32),
+            pltpu.SMEM((owners.shape[0],), jnp.int32),
         ],
         compiler_params=pltpu.CompilerParams(vmem_limit_bytes=VMEM_LIMIT),
         cost_estimate=pl.CostEstimate(
@@ -175,7 +205,7 @@
             transcendentals=heads * tokens * keys,
         ),
         name="attend",
-    )(lens, place, counts, queries, *arrived, out_weight)
+    )(lens, place, counts, owners, queries, *arrived, out_weight)
 
 
 def expert_kernel(count, ep_count, blocks, weight_at, place, payload, *refs):
@@ -303,7 +333,6 @@
         )
     sources = [ep_index ^ step for step in range(ep_count)]
 
-    held_out = hold_call([out_weight], payload)[0]
     all_open = hits == HOLD_MOST * ep_count
     holder = hit_pages // pool_pages
     counts = jnp.sum(
@@ -331,32 +360,25 @@
             got = exchange(gives[-1], bit)
         return kept.astype(jnp.float32) + got.astype(jnp.float32), gives
 
-    heads_out, _ = scatter(
-        *attend_call(
-            span_lengths, place, counts, queries, arrived, held_out, held, blocks, all_open
-        )
-    )
     own_most = 2 * (tokens // page_size)
-    page_count = new_owner.shape[0]
-    pages_here = tokens // page_size
-    owned_pages = new_owner == ep_index
-    page_ids = jnp.arange(page_count, dtype=jnp.int32)
-    owner_rank = jnp.sum(
-        ((page_ids[None, :] < page_ids[:, None]) & owned_pages[None, :]).astype(jnp.int32), axis=1
-    )
-    choose = owned_pages[None, :] & (
-        owner_rank[None, :] == jnp.arange(own_most, dtype=jnp.int32)[:, None]
-    )
-    page_index = jnp.sum(jnp.where(choose, page_ids[None, :], 0), axis=1)
-    has_page = jnp.any(choose, axis=1)
-    suffix = jnp.concatenate([block[held : held + tokens] for block in arrived], axis=0)
-    spot = (ep_index ^ (page_index // pages_here)) * pages_here + page_index % pages_here
-    taken = suffix.reshape(page_count, page_size, 2 * HD).at[spot].get(mode="promise_in_bounds")
-    slot_in_span = (page_index % pages_here)[:, None] * page_size + jnp.arange(page_size)[None, :]
-    kept = has_page[:, None] & (slot_in_span < span_lengths[page_index // pages_here][:, None])
-    head_pages = jnp.where(kept[:, :, None], taken, jnp.zeros((), jnp.bfloat16))
-    heads_out, head_pages = lax.optimization_barrier([heads_out, head_pages])
-
+    own_slots = block_index * row_count + jnp.arange(row_count, dtype=jnp.int32)
+    rows_filled = own_slots < span_lengths[ep_index]
+    held_out = hold_call([out_weight], payload, place, rows_filled.astype(jnp.int32))[0]
+    kept, sent, head_pages = attend_call(
+        span_lengths,
+        place,
+        counts,
+        new_owner,
+        queries,
+        arrived,
+        held_out,
+        held,
+        blocks,
+        own_most,
+        all_open,
+    )
+    head_pages = head_pages.reshape(own_most, page_size, 2 * HD)
+    heads_out, _ = scatter(kept, sent)
     own_hidden = lax.dynamic_slice_in_dim(hidden_in, block_index * row_count, row_count, 0)
     residual = (own_hidden.astype(jnp.float32) + heads_out).astype(jnp.bfloat16)
     resid_wide = residual.astype(jnp.float32)
@@ -367,8 +389,10 @@
     ).astype(jnp.bfloat16)
 
     order = list(range(ep_count - 1, -1, -1))
-    crossed = lax.optimization_barrier([across(normed, step) for step in order[:-1]])
-    held_gate_up, held_down = hold_call([gate_up, down_weight], crossed[0])
+    held_gate_up, held_down, token = hold_call([gate_up, down_weight], normed)
+    token, *crossed = lax.optimization_barrier(
+        [token] + [across(normed, step) for step in order[:-1]]
+    )
     given = []
     finished = []
     mixture = resid_wide
@@ -376,7 +400,7 @@
         have = [crossed[turn] if step > 0 else normed]
         for bit in bits + [1]:
             have += [exchange(part, bit) for part in have]
-        after = given[turn - 2 : turn - 1] if turn >= 2 else []
+        after = given[turn - 2 : turn - 1] if turn >= 2 else [token]
         after = after + (finished[turn - 3 : turn - 2] if turn >= 3 else [])
         kept, sent = expert_call(
             place,
@@ -396,8 +420,6 @@
         if step > 0:
             own = across(own, step)
         mixture = mixture + own.astype(jnp.float32)
-    own_slots = block_index * row_count + jnp.arange(row_count, dtype=jnp.int32)
-    rows_filled = own_slots < span_lengths[ep_index]
     layer_out = jnp.where(rows_filled[:, None], mixture, 0.0).astype(jnp.bfloat16)
 
     if keyval_local == 1:

time: 116 us -> 107 us (0.922)
  local copies, waits for them, and re-layouts: 26.9 us -> 19.9 us
  waiting for transfers between devices: 34.2 us -> 31.5 us
  starting transfers between devices: 26.8 us -> 28.4 us
    unnamed x29 -> x31, local copies, waits for them, and re-layouts: 22.8 us -> 16.3 us
    ppermute x6, waiting for transfers between devices: 12.7 us -> 7.32 us  [local(): lax.ppermute(value, 'ep', [(i, i ^ step) for i in range(ep_count)])]
    ppermute x3, waiting for transfers between devices: 3.96 us -> 6.4 us  [local(): lax.ppermute(payload, 'ep', [(i, i ^ step) for i in range(ep_count)])]
    ppermute x22, starting transfers between devices: 11.8 us -> 13.2 us  [local(): lax.ppermute(value, ('kv', 'tp'), [(i, i ^ bit) for i in range(blocks)])]
    gather x2 -> x0, local copies, waits for them, and re-layouts: 1.19 us -> none  [the longest x1 0.64 us: local(): span_lengths[page_index // pages_here][:, None]]
  transfers between devices with their start and end apart: 32 -> 32, of which waited for: 12 -> 10; matrix products, arithmetic and copies ran while one was open for 6% -> 5% of each run, Pallas kernels for 12% -> 14%
where the time goes in v7:
time: 107 us
  waiting for transfers between devices  31.5 us (29%)
  starting transfers between devices  28.4 us (27%)
  local copies, waits for them, and re-layouts  19.9 us (19%)
  Pallas kernels  18.2 us (17%)
  other arithmetic  7.42 us (7%)
  between operations  1.07 us (1%)
    ppermute x22, waiting for transfers between devices, local(): lax.ppermute(value, ('kv', 'tp'), [(i, i ^ bit) for i in range(blocks)])  17.8 us
    unnamed x31, local copies, waits for them, and re-layouts  16.3 us
    ppermute x22, starting transfers between devices, local(): lax.ppermute(value, ('kv', 'tp'), [(i, i ^ bit) for i in range(blocks)])  13.2 us
    pallas_call x4, Pallas kernels, expert_call(): pl.pallas_call(lambda *refs: expert_kernel(len(have), ep_count, blocks, w...  12.8 us
    ppermute x6, starting transfers between devices, local(): lax.ppermute(value, 'ep', [(i, i ^ step) for i in range(ep_count)])  9.07 us
    ppermute x6, waiting for transfers between devices, local(): lax.ppermute(value, 'ep', [(i, i ^ step) for i in range(ep_count)])  7.32 us
    ppermute x3, waiting for transfers between devices, local(): lax.ppermute(payload, 'ep', [(i, i ^ step) for i in range(ep_count)])  6.4 us
    ppermute x3, starting transfers between devices, local(): lax.ppermute(payload, 'ep', [(i, i ^ step) for i in range(ep_count)])  5.68 us
  transfers between devices with their start and end apart: 32, of which 10 were waited for; matrix products, arithmetic and copies ran while one was open for 5% of the time, Pallas kernels for 14%

profile of v7, /device:TPU:0, one launch (start us, length us, event | category | flops | bytes accessed | tf_op | source)
XLA Modules:
  0.0 106.5 jit_solution(15230825500905842127)
XLA Ops:
  5.5 3.1 %collective-permute-start = (bf16[336,256]{1,0:T(8,128)(2,1)S(1)}, bf16[336,256]{1,0:T(8,128)(2,1)S(1)}, u32[]{:S(2)}, u32[]{:S(2)}) collective-permute-start(bf16[336,256]{1,0:T(8,128)(2,1)S(1)} %pad_maximum_fusion.refs_1_.refs_5_), channel_id=1, source_target_pairs={{0,4},{4,0},{8,12},{12,8},{1,5},{5,1},{9,13},{13,9},{2,6},{6,2},{1... | collective-permute-start | bytes 516104 | tf_op jit(solution)/shard_map/ppermute | solution.py:332
  8.6 2.6 %collective-permute-start.1 = (bf16[336,256]{1,0:T(8,128)(2,1)S(1)}, bf16[336,256]{1,0:T(8,128)(2,1)S(1)}, u32[]{:S(2)}, u32[]{:S(2)}) collective-permute-start(bf16[336,256]{1,0:T(8,128)(2,1)S(1)} %pad_maximum_fusion.refs_1_.refs_5_), channel_id=1, source_target_pairs={{0,8},{4,12},{8,0},{12,4},{1,9},{5,13},{9,1},{13,5},{2,10},{6,14},... | collective-permute-start | bytes 516104 | tf_op jit(solution)/shard_map/ppermute | solution.py:332
  13.2 3.4 %copy-done.5 = bf16[1024,4096]{1,0:T(8,128)(2,1)S(1)} copy-done((bf16[1024,4096]{1,0:T(8,128)(2,1)S(1)}, bf16[1024,4096]{1,0:T(8,128)(2,1)}, u32[]{:S(2)}) %copy-start.5) | copy-done | bytes 8388632
  17.8 6.4 %collective-permute-done.1.refs_7_.refs_1_ = bf16[336,256]{1,0:T(8,128)(2,1)S(1)} collective-permute-done((bf16[336,256]{1,0:T(8,128)(2,1)S(1)}, bf16[336,256]{1,0:T(8,128)(2,1)S(1)}, u32[]{:S(2)}, u32[]{:S(2)}) %collective-permute-start.1) | collective-permute-done | bytes 172064 | tf_op jit(solution)/shard_map/ppermute | solution.py:332
  24.2 3.6 %attend.1 = (f32[32,4096]{1,0:T(8,128)S(1)}, bf16[32,4096]{1,0:T(8,128)(2,1)S(1)}, bf16[128,256]{1,0:T(8,128)(2,1)S(1)}) custom-call(s32[4]{0:T(128)S(1)} %copy-done.9, s32[2]{0:T(128)S(1)} %pad_add_fusion.refs_2_.refs_1_.refs_0_, s32[1]{0:T(128)} %constant.58.clone.1.refs_2_, s32[16]{0:T(128)S(1)} %copy-done.10, bf16[64,1024]{1,0:T(8,128)(2,1)S(1)} %copy-done.8, ...), custom_call_target="tpu_custom_call" | custom-call | flops 872415232 | bytes 8388608 | tf_op jit(solution)/shard_map/attend/pallas_call | solution.py:187
  31.0 4.0 %collective-permute-done.4 = bf16[16,4096]{1,0:T(8,128)(2,1)S(1)} collective-permute-done((bf16[16,4096]{1,0:T(8,128)(2,1)S(1)}, bf16[16,4096]{1,0:T(8,128)(2,1)S(1)}, u32[]{:S(2)}, u32[]{:S(2)}) %collective-permute-start.4) | collective-permute-done | bytes 131104 | tf_op jit(solution)/shard_map/ppermute | solution.py:344
  36.3 2.5 %collective-permute-start.5 = (bf16[16,4096]{1,0:T(8,128)(2,1)S(1)}, bf16[16,4096]{1,0:T(8,128)(2,1)S(1)}, u32[]{:S(2)}, u32[]{:S(2)}) collective-permute-start(bf16[16,4096]{1,0:T(8,128)(2,1)S(1)} %fusion.2.refs_2_), channel_id=1, source_target_pairs={{0,12},{4,8},{8,4},{12,0},{1,13},{5,9},{9,5},{13,1},{2,14},{6,10},... | collective-permute-start | bytes 393224 | tf_op jit(solution)/shard_map/ppermute | solution.py:347
  38.7 1.9 %collective-permute-start.6 = (bf16[16,4096]{1,0:T(8,128)(2,1)S(1)}, bf16[16,4096]{1,0:T(8,128)(2,1)S(1)}, u32[]{:S(2)}, u32[]{:S(2)}) collective-permute-start(bf16[16,4096]{1,0:T(8,128)(2,1)S(1)} %fusion.2.refs_2_), channel_id=1, source_target_pairs={{0,8},{4,12},{8,0},{12,4},{1,9},{5,13},{9,1},{13,5},{2,10},{6,14},... | collective-permute-start | bytes 393224 | tf_op jit(solution)/shard_map/ppermute | solution.py:347
  40.8 2.8 %copy-done.6 = bf16[1,2,384,4096]{3,2,1,0:T(8,128)(2,1)S(1)} copy-done((bf16[1,2,384,4096]{3,2,1,0:T(8,128)(2,1)S(1)}, bf16[1,2,384,4096]{3,2,1,0:T(8,128)(2,1)}, u32[]{:S(2)}) %copy-start.6) | copy-done | bytes 6291480
  43.5 1.9 %copy-done.7 = bf16[1,384,4096]{2,1,0:T(8,128)(2,1)S(1)} copy-done((bf16[1,384,4096]{2,1,0:T(8,128)(2,1)S(1)}, bf16[1,384,4096]{2,1,0:T(8,128)(2,1)}, u32[]{:S(2)}) %copy-start.7) | copy-done | bytes 3145752
  46.1 5.2 %collective-permute-done.6.refs_2_ = bf16[16,4096]{1,0:T(8,128)(2,1)S(1)} collective-permute-done((bf16[16,4096]{1,0:T(8,128)(2,1)S(1)}, bf16[16,4096]{1,0:T(8,128)(2,1)S(1)}, u32[]{:S(2)}, u32[]{:S(2)}) %collective-permute-start.6) | collective-permute-done | bytes 131104 | tf_op jit(solution)/shard_map/ppermute | solution.py:347
  52.8 3.7 %collective-permute-done.8.refs_3_ = bf16[16,4096]{1,0:T(8,128)(2,1)S(1)} collective-permute-done((bf16[16,4096]{1,0:T(8,128)(2,1)S(1)}, bf16[16,4096]{1,0:T(8,128)(2,1)S(1)}, u32[]{:S(2)}, u32[]{:S(2)}) %collective-permute-start.8) | collective-permute-done | bytes 131104 | tf_op jit(solution)/shard_map/ppermute | solution.py:344
  58.0 3.2 %experts.4 = (bf16[32,4096]{1,0:T(8,128)(2,1)S(1)}, bf16[32,4096]{1,0:T(8,128)(2,1)S(1)}) custom-call(s32[2]{0:T(128)S(1)} %pad_add_fusion.refs_2_.refs_1_.refs_0_, bf16[336,256]{1,0:T(8,128)(2,1)S(1)} %collective-permute-done.2.refs_8_.refs_1_, bf16[16,4096]{1,0:T(8,128)(2,1)S(1)} %collective-permute-done.5.refs_2_, ...), custom_call_target="tpu_custom_call" | custom-call | flops 603979776 | bytes 9437184 | tf_op jit(solution)/shard_map/experts/pallas_call | solution.py:256
  61.2 2.7 %copy-done.1 = bf16[1,2,384,4096]{3,2,1,0:T(8,128)(2,1)} copy-done((bf16[1,2,384,4096]{3,2,1,0:T(8,128)(2,1)}, bf16[1,2,384,4096]{3,2,1,0:T(8,128)(2,1)S(1)}, u32[]{:S(2)}) %copy-start.1) | copy-done | bytes 6291480
  67.0 3.8 %collective-permute-done.20.refs_3_ = bf16[16,4096]{1,0:T(8,128)(2,1)S(1)} collective-permute-done((bf16[16,4096]{1,0:T(8,128)(2,1)S(1)}, bf16[16,4096]{1,0:T(8,128)(2,1)S(1)}, u32[]{:S(2)}, u32[]{:S(2)}) %collective-permute-start.20) | collective-permute-done | bytes 131104 | tf_op jit(solution)/shard_map/ppermute | solution.py:344
  71.3 2.8 %copy-done.2 = bf16[1,2,384,4096]{3,2,1,0:T(8,128)(2,1)S(1)} copy-done((bf16[1,2,384,4096]{3,2,1,0:T(8,128)(2,1)S(1)}, bf16[1,2,384,4096]{3,2,1,0:T(8,128)(2,1)}, u32[]{:S(2)}) %copy-start.2) | copy-done | bytes 6291480
  74.0 1.9 %copy-done.4 = bf16[1,384,4096]{2,1,0:T(8,128)(2,1)S(1)} copy-done((bf16[1,384,4096]{2,1,0:T(8,128)(2,1)S(1)}, bf16[1,384,4096]{2,1,0:T(8,128)(2,1)}, u32[]{:S(2)}) %copy-start.4) | copy-done | bytes 3145752
  75.9 3.2 %experts.5 = (bf16[32,4096]{1,0:T(8,128)(2,1)S(1)}, bf16[32,4096]{1,0:T(8,128)(2,1)S(1)}) custom-call(s32[2]{0:T(128)S(1)} %pad_add_fusion.refs_2_.refs_1_.refs_0_, bf16[336,256]{1,0:T(8,128)(2,1)S(1)} %collective-permute-done.1.refs_7_.refs_1_, bf16[16,4096]{1,0:T(8,128)(2,1)S(1)} %collective-permute-done.6.refs_2_, ...), custom_call_target="tpu_custom_call" | custom-call | flops 603979776 | bytes 9437184 | tf_op jit(solution)/shard_map/experts/pallas_call | solution.py:256
  83.4 3.2 %experts.6 = (bf16[32,4096]{1,0:T(8,128)(2,1)S(1)}, bf16[32,4096]{1,0:T(8,128)(2,1)S(1)}) custom-call(s32[2]{0:T(128)S(1)} %pad_add_fusion.refs_2_.refs_1_.refs_0_, bf16[336,256]{1,0:T(8,128)(2,1)S(1)} %collective-permute-done.refs_6_.refs_1_, bf16[16,4096]{1,0:T(8,128)(2,1)S(1)} %collective-permute-done.7.refs_2_, ...), custom_call_target="tpu_custom_call" | custom-call | flops 603979776 | bytes 9437184 | tf_op jit(solution)/shard_map/experts/pallas_call | solution.py:256
  88.1 2.5 %collective-permute-start.13 = (bf16[16,4096]{1,0:T(8,128)(2,1)S(1)}, bf16[16,4096]{1,0:T(8,128)(2,1)S(1)}, u32[]{:S(2)}, u32[]{:S(2)}) collective-permute-start(bf16[16,4096]{1,0:T(8,128)(2,1)S(1)} %add_convert_fusion.6.refs_9_), channel_id=1, source_target_pairs={{0,12},{4,8},{8,4},{12,0},{1,13},{5,9},{9,5},{13,1},{2,14},{6,10},... | collective-permute-start | bytes 393224 | tf_op jit(solution)/shard_map/ppermute | solution.py:347
  90.5 3.2 %experts.7 = (bf16[32,4096]{1,0:T(8,128)(2,1)S(1)}, bf16[32,4096]{1,0:T(8,128)(2,1)S(1)}) custom-call(s32[2]{0:T(128)S(1)} %pad_add_fusion.refs_2_.refs_1_.refs_0_, bf16[336,256]{1,0:T(8,128)(2,1)S(1)} %pad_maximum_fusion.refs_1_.refs_5_, bf16[16,4096]{1,0:T(8,128)(2,1)S(1)} %fusion.2.refs_2_, bf16[16,4096]{1,0:T(8,128)(2,1)S(1)} %collective-permute-done.26.refs_3_, ...), custom_call_target="tpu_custom_call" | custom-call | flops 603979776 | bytes 9437184 | tf_op jit(solution)/shard_map/experts/pallas_call | solution.py:256
  96.8 3.8 %collective-permute-done.24 = bf16[16,4096]{1,0:T(8,128)(2,1)S(1)} collective-permute-done((bf16[16,4096]{1,0:T(8,128)(2,1)S(1)}, bf16[16,4096]{1,0:T(8,128)(2,1)S(1)}, u32[]{:S(2)}, u32[]{:S(2)}) %collective-permute-start.24) | collective-permute-done | bytes 131104 | tf_op jit(solution)/shard_map/ppermute | solution.py:344
  100.7 2.0 %collective-permute-start.25 = (bf16[16,4096]{1,0:T(8,128)(2,1)S(1)}, bf16[16,4096]{1,0:T(8,128)(2,1)S(1)}, u32[]{:S(2)}, u32[]{:S(2)}) collective-permute-start(bf16[16,4096]{1,0:T(8,128)(2,1)S(1)} %add_convert_fusion.2), channel_id=1, source_target_pairs={{0,4},{4,0},{8,12},{12,8},{1,5},{5,1},{9,13},{13,9},{2,6},{6,2},{1... | collective-permute-start | bytes 393224 | tf_op jit(solution)/shard_map/ppermute | solution.py:347
  103.6 2.1 %collective-permute-done.25 = bf16[16,4096]{1,0:T(8,128)(2,1)S(1)} collective-permute-done((bf16[16,4096]{1,0:T(8,128)(2,1)S(1)}, bf16[16,4096]{1,0:T(8,128)(2,1)S(1)}, u32[]{:S(2)}, u32[]{:S(2)}) %collective-permute-start.25) | collective-permute-done | bytes 131104 | tf_op jit(solution)/shard_map/ppermute | solution.py:347
  (109 shorter events, 30.0 us)
Async XLA Ops:
  5.5 12.3 %collective-permute-start = (bf16[336,256]{1,0:T(8,128)(2,1)S(1)}, bf16[336,256]{1,0:T(8,128)(2,1)S(1)}, u32[]{:S(2)}, u32[]{:S(2)}) collective-permute-start(bf16[336,256]{1,0:T(8,128)(2,1)S(1)} %pad_maximum_fusion.refs_1_.refs_5_), channel_id=1, source_target_pairs={{0,4},{4,0},{8,12},{12,8},{1,5},{5,1},{9,13},{13,9},{2,6},{6,2},{1... | collective-permute-start | bytes 516104 | tf_op jit(solution)/shard_map/ppermute | solution.py:332
  8.6 15.6 %collective-permute-start.1 = (bf16[336,256]{1,0:T(8,128)(2,1)S(1)}, bf16[336,256]{1,0:T(8,128)(2,1)S(1)}, u32[]{:S(2)}, u32[]{:S(2)}) collective-permute-start(bf16[336,256]{1,0:T(8,128)(2,1)S(1)} %pad_maximum_fusion.refs_1_.refs_5_), channel_id=1, source_target_pairs={{0,8},{4,12},{8,0},{12,4},{1,9},{5,13},{9,1},{13,5},{2,10},{6,14},... | collective-permute-start | bytes 516104 | tf_op jit(solution)/shard_map/ppermute | solution.py:332
  11.2 13.0 %collective-permute-start.2 = (bf16[336,256]{1,0:T(8,128)(2,1)S(1)}, bf16[336,256]{1,0:T(8,128)(2,1)S(1)}, u32[]{:S(2)}, u32[]{:S(2)}) collective-permute-start(bf16[336,256]{1,0:T(8,128)(2,1)S(1)} %pad_maximum_fusion.refs_1_.refs_5_), channel_id=1, source_target_pairs={{0,12},{4,8},{8,4},{12,0},{1,13},{5,9},{9,5},{13,1},{2,14},{6,10},... | collective-permute-start | bytes 516104 | tf_op jit(solution)/shard_map/ppermute | solution.py:332
  29.4 5.6 %collective-permute-start.4 = (bf16[16,4096]{1,0:T(8,128)(2,1)S(1)}, bf16[16,4096]{1,0:T(8,128)(2,1)S(1)}, u32[]{:S(2)}, u32[]{:S(2)}) collective-permute-start(bf16[16,4096]{1,0:T(8,128)(2,1)S(1)} %add_convert_fusion.9), channel_id=1, source_target_pairs={{0,2},{1,3},{2,0},{3,1},{4,6},{5,7},{6,4},{7,5},{8,10},{9,11},{10,... | collective-permute-start | bytes 393224 | tf_op jit(solution)/shard_map/ppermute | solution.py:344
  36.3 9.8 %collective-permute-start.5 = (bf16[16,4096]{1,0:T(8,128)(2,1)S(1)}, bf16[16,4096]{1,0:T(8,128)(2,1)S(1)}, u32[]{:S(2)}, u32[]{:S(2)}) collective-permute-start(bf16[16,4096]{1,0:T(8,128)(2,1)S(1)} %fusion.2.refs_2_), channel_id=1, source_target_pairs={{0,12},{4,8},{8,4},{12,0},{1,13},{5,9},{9,5},{13,1},{2,14},{6,10},... | collective-permute-start | bytes 393224 | tf_op jit(solution)/shard_map/ppermute | solution.py:347
  38.7 12.5 %collective-permute-start.6 = (bf16[16,4096]{1,0:T(8,128)(2,1)S(1)}, bf16[16,4096]{1,0:T(8,128)(2,1)S(1)}, u32[]{:S(2)}, u32[]{:S(2)}) collective-permute-start(bf16[16,4096]{1,0:T(8,128)(2,1)S(1)} %fusion.2.refs_2_), channel_id=1, source_target_pairs={{0,8},{4,12},{8,0},{12,4},{1,9},{5,13},{9,1},{13,5},{2,10},{6,14},... | collective-permute-start | bytes 393224 | tf_op jit(solution)/shard_map/ppermute | solution.py:347
  40.6 10.6 %collective-permute-start.7 = (bf16[16,4096]{1,0:T(8,128)(2,1)S(1)}, bf16[16,4096]{1,0:T(8,128)(2,1)S(1)}, u32[]{:S(2)}, u32[]{:S(2)}) collective-permute-start(bf16[16,4096]{1,0:T(8,128)(2,1)S(1)} %fusion.2.refs_2_), channel_id=1, source_target_pairs={{0,4},{4,0},{8,12},{12,8},{1,5},{5,1},{9,13},{13,9},{2,6},{6,2},{1... | collective-permute-start | bytes 393224 | tf_op jit(solution)/shard_map/ppermute | solution.py:347
  52.8 5.2 %collective-permute-start.9 = (bf16[16,4096]{1,0:T(8,128)(2,1)S(1)}, bf16[16,4096]{1,0:T(8,128)(2,1)S(1)}, u32[]{:S(2)}, u32[]{:S(2)}) collective-permute-start(bf16[16,4096]{1,0:T(8,128)(2,1)S(1)} %collective-permute-done.5.refs_2_), channel_id=1, source_target_pairs={{0,1},{1,0},{2,3},{3,2},{4,5},{5,4},{6,7},{7,6},{8,9},{9,8},{10,11... | collective-permute-start | bytes 393224 | tf_op jit(solution)/shard_map/ppermute | solution.py:344
  56.5 9.3 %collective-permute-start.14 = (bf16[16,4096]{1,0:T(8,128)(2,1)S(1)}, bf16[16,4096]{1,0:T(8,128)(2,1)S(1)}, u32[]{:S(2)}, u32[]{:S(2)}) collective-permute-start(bf16[16,4096]{1,0:T(8,128)(2,1)S(1)} %collective-permute-done.6.refs_2_), channel_id=1, source_target_pairs={{0,2},{1,3},{2,0},{3,1},{4,6},{5,7},{6,4},{7,5},{8,10},{9,11},{10,... | collective-permute-start | bytes 393224 | tf_op jit(solution)/shard_map/ppermute | solution.py:344
  63.9 15.2 %collective-permute-start.11 = (bf16[32,4096]{1,0:T(8,128)(2,1)S(1)}, bf16[32,4096]{1,0:T(8,128)(2,1)}, u32[]{:S(2)}, u32[]{:S(2)}) collective-permute-start(bf16[32,4096]{1,0:T(8,128)(2,1)S(1)} %get-tuple-element.30), channel_id=1, source_target_pairs={{0,1},{1,0},{2,3},{3,2},{4,5},{5,4},{6,7},{7,6},{8,9},{9,8},{10,11... | collective-permute-start | bytes 786440 | tf_op jit(solution)/shard_map/ppermute | solution.py:344
  64.4 6.3 %collective-permute-start.20 = (bf16[16,4096]{1,0:T(8,128)(2,1)S(1)}, bf16[16,4096]{1,0:T(8,128)(2,1)S(1)}, u32[]{:S(2)}, u32[]{:S(2)}) collective-permute-start(bf16[16,4096]{1,0:T(8,128)(2,1)S(1)} %collective-permute-done.7.refs_2_), channel_id=1, source_target_pairs={{0,2},{1,3},{2,0},{3,1},{4,6},{5,7},{6,4},{7,5},{8,10},{9,11},{10,... | collective-permute-start | bytes 393224 | tf_op jit(solution)/shard_map/ppermute | solution.py:344
  65.8 37.0 %collective-permute-start.31 = (bf16[8,16,256]{2,1,0:T(8,128)(2,1)S(1)}, bf16[8,16,256]{2,1,0:T(8,128)(2,1)S(1)}, u32[]{:S(2)}, u32[]{:S(2)}) collective-permute-start(bf16[8,16,256]{2,1,0:T(8,128)(2,1)S(1)} %bitcast.25), channel_id=1, source_target_pairs={{0,1},{1,0},{2,3},{3,2},{4,5},{5,4},{6,7},{7,6},{8,9},{9,8},{10,11... | collective-permute-start | bytes 196616 | tf_op jit(solution)/shard_map/ppermute | solution.py:428
  66.3 15.9 %collective-permute-start.26 = (bf16[16,4096]{1,0:T(8,128)(2,1)S(1)}, bf16[16,4096]{1,0:T(8,128)(2,1)S(1)}, u32[]{:S(2)}, u32[]{:S(2)}) collective-permute-start(bf16[16,4096]{1,0:T(8,128)(2,1)S(1)} %fusion.2.refs_2_), channel_id=1, source_target_pairs={{0,2},{1,3},{2,0},{3,1},{4,6},{5,7},{6,4},{7,5},{8,10},{9,11},{10,... | collective-permute-start | bytes 393224 | tf_op jit(solution)/shard_map/ppermute | solution.py:344
  70.7 11.5 %collective-permute-start.21 = (bf16[16,4096]{1,0:T(8,128)(2,1)S(1)}, bf16[16,4096]{1,0:T(8,128)(2,1)S(1)}, u32[]{:S(2)}, u32[]{:S(2)}) collective-permute-start(bf16[16,4096]{1,0:T(8,128)(2,1)S(1)} %collective-permute-done.7.refs_2_), channel_id=1, source_target_pairs={{0,1},{1,0},{2,3},{3,2},{4,5},{5,4},{6,7},{7,6},{8,9},{9,8},{10,11... | collective-permute-start | bytes 393224 | tf_op jit(solution)/shard_map/ppermute | solution.py:344
  70.7 12.0 %collective-permute-start.22 = (bf16[16,4096]{1,0:T(8,128)(2,1)S(1)}, bf16[16,4096]{1,0:T(8,128)(2,1)S(1)}, u32[]{:S(2)}, u32[]{:S(2)}) collective-permute-start(bf16[16,4096]{1,0:T(8,128)(2,1)S(1)} %collective-permute-done.20.refs_3_), channel_id=1, source_target_pairs={{0,1},{1,0},{2,3},{3,2},{4,5},{5,4},{6,7},{7,6},{8,9},{9,8},{10,11... | collective-permute-start | bytes 393224 | tf_op jit(solution)/shard_map/ppermute | solution.py:344
  80.8 6.3 %collective-permute-start.12 = (bf16[16,4096]{1,0:T(8,128)(2,1)S(1)}, bf16[16,4096]{1,0:T(8,128)(2,1)S(1)}, u32[]{:S(2)}, u32[]{:S(2)}) collective-permute-start(bf16[16,4096]{1,0:T(8,128)(2,1)S(1)} %add_convert_fusion.7.refs_8_), channel_id=1, source_target_pairs={{0,2},{1,3},{2,0},{3,1},{4,6},{5,7},{6,4},{7,5},{8,10},{9,11},{10,... | collective-permute-start | bytes 393224 | tf_op jit(solution)/shard_map/ppermute | solution.py:344
  82.2 5.9 %collective-permute-start.27 = (bf16[16,4096]{1,0:T(8,128)(2,1)S(1)}, bf16[16,4096]{1,0:T(8,128)(2,1)S(1)}, u32[]{:S(2)}, u32[]{:S(2)}) collective-permute-start(bf16[16,4096]{1,0:T(8,128)(2,1)S(1)} %fusion.2.refs_2_), channel_id=1, source_target_pairs={{0,1},{1,0},{2,3},{3,2},{4,5},{5,4},{6,7},{7,6},{8,9},{9,8},{10,11... | collective-permute-start | bytes 393224 | tf_op jit(solution)/shard_map/ppermute | solution.py:344
  82.3 8.3 %collective-permute-start.28 = (bf16[16,4096]{1,0:T(8,128)(2,1)S(1)}, bf16[16,4096]{1,0:T(8,128)(2,1)S(1)}, u32[]{:S(2)}, u32[]{:S(2)}) collective-permute-start(bf16[16,4096]{1,0:T(8,128)(2,1)S(1)} %collective-permute-done.26.refs_3_), channel_id=1, source_target_pairs={{0,1},{1,0},{2,3},{3,2},{4,5},{5,4},{6,7},{7,6},{8,9},{9,8},{10,11... | collective-permute-start | bytes 393224 | tf_op jit(solution)/shard_map/ppermute | solution.py:344
  82.7 11.3 %collective-permute-start.18 = (bf16[16,4096]{1,0:T(8,128)(2,1)S(1)}, bf16[16,4096]{1,0:T(8,128)(2,1)S(1)}, u32[]{:S(2)}, u32[]{:S(2)}) collective-permute-start(bf16[16,4096]{1,0:T(8,128)(2,1)S(1)} %add_convert_fusion.5.refs_8_), channel_id=1, source_target_pairs={{0,2},{1,3},{2,0},{3,1},{4,6},{5,7},{6,4},{7,5},{8,10},{9,11},{10,... | collective-permute-start | bytes 393224 | tf_op jit(solution)/shard_map/ppermute | solution.py:344
  87.1 7.1 %collective-permute-start.23 = (bf16[32,4096]{1,0:T(8,128)(2,1)S(1)}, bf16[32,4096]{1,0:T(8,128)(2,1)S(1)}, u32[]{:S(2)}, u32[]{:S(2)}) collective-permute-start(bf16[32,4096]{1,0:T(8,128)(2,1)S(1)} %get-tuple-element.36), channel_id=1, source_target_pairs={{0,1},{1,0},{2,3},{3,2},{4,5},{5,4},{6,7},{7,6},{8,9},{9,8},{10,11... | collective-permute-start | bytes 786440 | tf_op jit(solution)/shard_map/ppermute | solution.py:344
  88.1 15.5 %collective-permute-start.13 = (bf16[16,4096]{1,0:T(8,128)(2,1)S(1)}, bf16[16,4096]{1,0:T(8,128)(2,1)S(1)}, u32[]{:S(2)}, u32[]{:S(2)}) collective-permute-start(bf16[16,4096]{1,0:T(8,128)(2,1)S(1)} %add_convert_fusion.6.refs_9_), channel_id=1, source_target_pairs={{0,12},{4,8},{8,4},{12,0},{1,13},{5,9},{9,5},{13,1},{2,14},{6,10},... | collective-permute-start | bytes 393224 | tf_op jit(solution)/shard_map/ppermute | solution.py:347
  94.1 9.5 %collective-permute-start.19 = (bf16[16,4096]{1,0:T(8,128)(2,1)S(1)}, bf16[16,4096]{1,0:T(8,128)(2,1)S(1)}, u32[]{:S(2)}, u32[]{:S(2)}) collective-permute-start(bf16[16,4096]{1,0:T(8,128)(2,1)S(1)} %add_convert_fusion.4), channel_id=1, source_target_pairs={{0,8},{4,12},{8,0},{12,4},{1,9},{5,13},{9,1},{13,5},{2,10},{6,14},... | collective-permute-start | bytes 393224 | tf_op jit(solution)/shard_map/ppermute | solution.py:347
  94.2 6.4 %collective-permute-start.24 = (bf16[16,4096]{1,0:T(8,128)(2,1)S(1)}, bf16[16,4096]{1,0:T(8,128)(2,1)S(1)}, u32[]{:S(2)}, u32[]{:S(2)}) collective-permute-start(bf16[16,4096]{1,0:T(8,128)(2,1)S(1)} %add_convert_fusion.3), channel_id=1, source_target_pairs={{0,2},{1,3},{2,0},{3,1},{4,6},{5,7},{6,4},{7,5},{8,10},{9,11},{10,... | collective-permute-start | bytes 393224 | tf_op jit(solution)/shard_map/ppermute | solution.py:344
  95.7 7.9 %collective-permute-start.30 = (bf16[16,4096]{1,0:T(8,128)(2,1)S(1)}, bf16[16,4096]{1,0:T(8,128)(2,1)S(1)}, u32[]{:S(2)}, u32[]{:S(2)}) collective-permute-start(bf16[16,4096]{1,0:T(8,128)(2,1)S(1)} %add_convert_fusion.1), channel_id=1, source_target_pairs={{0,2},{1,3},{2,0},{3,1},{4,6},{5,7},{6,4},{7,5},{8,10},{9,11},{10,... | collective-permute-start | bytes 393224 | tf_op jit(solution)/shard_map/ppermute | solution.py:344
  (22 other events, 165.1 us)

commit v8 on v7

--- a/solution.py
+++ b/solution.py
@@ -41,6 +41,7 @@
 COLUMNS = 1024
 ROWS = 256
 VMEM_LIMIT = 16 * 2**20
+EXPERT_COST = pl.CostEstimate(flops=1024, bytes_accessed=1024, transcendentals=0)
 
 
 def hold_kernel(count, *refs):
@@ -69,6 +70,22 @@
         cost_estimate=pl.CostEstimate(flops=0, bytes_accessed=2 * size, transcendentals=0),
         name="hold",
     )(*arrays, *after)
+
+
+def first_reader(gate_up, down_weight, after, token):
+    token[...] = (gate_up[0, 0, :16, :128] + down_weight[0, :16, :128]).astype(jnp.float32)
+
+
+def first_reader_call(gate_up, down_weight, after):
+    return pl.pallas_call(
+        first_reader,
+        out_shape=jax.ShapeDtypeStruct((16, 128), jnp.float32),
+        in_specs=[WHOLE, WHOLE, ANYWHERE],
+        out_specs=WHOLE,
+        compiler_params=pltpu.CompilerParams(vmem_limit_bytes=VMEM_LIMIT),
+        cost_estimate=EXPERT_COST,
+        name="first_reader",
+    )(gate_up, down_weight, after)
 
 
 def attend_kernel(ep_count, held, tokens, row_blocks, all_open, lens, place, counts, owners, queries, *refs):
@@ -259,11 +276,7 @@
         in_specs=[SCALARS] + [WHOLE] * (len(have) + 3) + [ANYWHERE] * len(after),
         out_specs=(WHOLE, WHOLE),
         compiler_params=pltpu.CompilerParams(vmem_limit_bytes=VMEM_LIMIT),
-        cost_estimate=pl.CostEstimate(
-            flops=6 * tokens * hidden_units * model_width,
-            bytes_accessed=6 * hidden_units * model_width,
-            transcendentals=tokens * hidden_units,
-        ),
+        cost_estimate=EXPERT_COST,
         name="experts",
     )(place, payload, *have, gate_up, down_weight, *after)
 
@@ -389,25 +402,30 @@
     ).astype(jnp.bfloat16)
 
     order = list(range(ep_count - 1, -1, -1))
-    held_gate_up, held_down, token = hold_call([gate_up, down_weight], normed)
+    token = first_reader_call(gate_up, down_weight, normed)
     token, *crossed = lax.optimization_barrier(
         [token] + [across(normed, step) for step in order[:-1]]
     )
     given = []
     finished = []
     mixture = resid_wide
-    for turn, step in enumerate(order):
-        have = [crossed[turn] if step > 0 else normed]
+    haves = []
+    for piece in crossed + [normed]:
+        have = [piece]
         for bit in bits + [1]:
             have += [exchange(part, bit) for part in have]
+        haves.append(have)
+    for turn, step in enumerate(order):
         after = given[turn - 2 : turn - 1] if turn >= 2 else [token]
+        after = after + ([sent] if turn >= 1 else [])
         after = after + (finished[turn - 3 : turn - 2] if turn >= 3 else [])
+        after = after + [have[1] for have in haves[turn + 1 : turn + 2]]
         kept, sent = expert_call(
             place,
             arrived[step],
-            have,
-            held_gate_up,
-            held_down,
+            haves[turn],
+            gate_up,
+            down_weight,
             after,
             ep_count,
             blocks,

time: 107 us -> 103 us (0.963)
  other arithmetic: 7.42 us -> 5.44 us
  transfers between devices with their start and end apart: 32 -> 32, of which waited for: 10 -> 11; matrix products, arithmetic and copies ran while one was open for 5% -> 3% of each run, Pallas kernels for 14% -> 10%
where the time goes in v8:
time: 103 us
  waiting for transfers between devices  30.7 us (30%)
  starting transfers between devices  28 us (27%)
  local copies, waits for them, and re-layouts  19.9 us (19%)
  Pallas kernels  17.6 us (17%)
  other arithmetic  5.44 us (5%)
  between operations  1.08 us (1%)
    ppermute x22, waiting for transfers between devices, local(): lax.ppermute(value, ('kv', 'tp'), [(i, i ^ bit) for i in range(blocks)])  16.9 us
    unnamed x31, local copies, waits for them, and re-layouts  16.4 us
    ppermute x22, starting transfers between devices, local(): lax.ppermute(value, ('kv', 'tp'), [(i, i ^ bit) for i in range(blocks)])  12.9 us
    pallas_call x4, Pallas kernels, expert_call(): pl.pallas_call(lambda *refs: expert_kernel(len(have), ep_count, blocks, w...  12.8 us
    ppermute x6, starting transfers between devices, local(): lax.ppermute(value, 'ep', [(i, i ^ step) for i in range(ep_count)])  9.23 us
    ppermute x3, waiting for transfers between devices, local(): lax.ppermute(payload, 'ep', [(i, i ^ step) for i in range(ep_count)])  7.43 us
    ppermute x6, waiting for transfers between devices, local(): lax.ppermute(value, 'ep', [(i, i ^ step) for i in range(ep_count)])  6.41 us
    ppermute x3, starting transfers between devices, local(): lax.ppermute(payload, 'ep', [(i, i ^ step) for i in range(ep_count)])  5.76 us
  transfers between devices with their start and end apart: 32, of which 11 were waited for; matrix products, arithmetic and copies ran while one was open for 3% of the time, Pallas kernels for 10%

profile of v8, /device:TPU:0, one launch (start us, length us, event | category | flops | bytes accessed | tf_op | source)
XLA Modules:
  0.0 102.8 jit_solution(7251371679307519968)
XLA Ops:
  5.5 5.1 %collective-permute-start.2 = (bf16[336,256]{1,0:T(8,128)(2,1)S(1)}, bf16[336,256]{1,0:T(8,128)(2,1)S(1)}, u32[]{:S(2)}, u32[]{:S(2)}) collective-permute-start(bf16[336,256]{1,0:T(8,128)(2,1)S(1)} %pad_maximum_fusion.refs_1_.refs_5_), channel_id=1, source_target_pairs={{0,12},{4,8},{8,4},{12,0},{1,13},{5,9},{9,5},{13,1},{2,14},{6,10},... | collective-permute-start | bytes 516104 | tf_op jit(solution)/shard_map/ppermute | solution.py:345
  13.2 3.4 %copy-done.7 = bf16[1024,4096]{1,0:T(8,128)(2,1)S(1)} copy-done((bf16[1024,4096]{1,0:T(8,128)(2,1)S(1)}, bf16[1024,4096]{1,0:T(8,128)(2,1)}, u32[]{:S(2)}) %copy-start.7) | copy-done | bytes 8388632
  17.8 7.4 %collective-permute-done.1.refs_7_.refs_1_ = bf16[336,256]{1,0:T(8,128)(2,1)S(1)} collective-permute-done((bf16[336,256]{1,0:T(8,128)(2,1)S(1)}, bf16[336,256]{1,0:T(8,128)(2,1)S(1)}, u32[]{:S(2)}, u32[]{:S(2)}) %collective-permute-start.1) | collective-permute-done | bytes 172064 | tf_op jit(solution)/shard_map/ppermute | solution.py:345
  25.2 3.6 %attend.1 = (f32[32,4096]{1,0:T(8,128)S(1)}, bf16[32,4096]{1,0:T(8,128)(2,1)S(1)}, bf16[128,256]{1,0:T(8,128)(2,1)S(1)}) custom-call(s32[4]{0:T(128)S(1)} %copy-done.9, s32[2]{0:T(128)S(1)} %pad_add_fusion.refs_2_.refs_1_.refs_0_, s32[1]{0:T(128)} %constant.58.clone.1.refs_2_, s32[16]{0:T(128)S(1)} %copy-done.10, bf16[64,1024]{1,0:T(8,128)(2,1)S(1)} %copy-done.8, ...), custom_call_target="tpu_custom_call" | custom-call | flops 872415232 | bytes 8388608 | tf_op jit(solution)/shard_map/attend/pallas_call | solution.py:204
  29.0 1.5 %collective-permute-done.3 = bf16[32,4096]{1,0:T(8,128)(2,1)S(1)} collective-permute-done((bf16[32,4096]{1,0:T(8,128)(2,1)S(1)}, bf16[32,4096]{1,0:T(8,128)(2,1)S(1)}, u32[]{:S(2)}, u32[]{:S(2)}) %collective-permute-start.3) | collective-permute-done | bytes 262176 | tf_op jit(solution)/shard_map/ppermute | solution.py:357
  30.5 1.6 %collective-permute-start.4 = (bf16[16,4096]{1,0:T(8,128)(2,1)S(1)}, bf16[16,4096]{1,0:T(8,128)(2,1)S(1)}, u32[]{:S(2)}, u32[]{:S(2)}) collective-permute-start(bf16[16,4096]{1,0:T(8,128)(2,1)S(1)} %add_convert_fusion.9), channel_id=1, source_target_pairs={{0,2},{1,3},{2,0},{3,1},{4,6},{5,7},{6,4},{7,5},{8,10},{9,11},{10,... | collective-permute-start | bytes 393224 | tf_op jit(solution)/shard_map/ppermute | solution.py:357
  32.1 4.0 %collective-permute-done.4 = bf16[16,4096]{1,0:T(8,128)(2,1)S(1)} collective-permute-done((bf16[16,4096]{1,0:T(8,128)(2,1)S(1)}, bf16[16,4096]{1,0:T(8,128)(2,1)S(1)}, u32[]{:S(2)}, u32[]{:S(2)}) %collective-permute-start.4) | collective-permute-done | bytes 131104 | tf_op jit(solution)/shard_map/ppermute | solution.py:357
  37.4 3.0 %collective-permute-start.6 = (bf16[16,4096]{1,0:T(8,128)(2,1)S(1)}, bf16[16,4096]{1,0:T(8,128)(2,1)S(1)}, u32[]{:S(2)}, u32[]{:S(2)}) collective-permute-start(bf16[16,4096]{1,0:T(8,128)(2,1)S(1)} %fusion.2.after.refs_2_), channel_id=1, source_target_pairs={{0,8},{4,12},{8,0},{12,4},{1,9},{5,13},{9,1},{13,5},{2,10},{6,14},... | collective-permute-start | bytes 393224 | tf_op jit(solution)/shard_map/ppermute | solution.py:360
  41.8 2.8 %copy-done.1 = bf16[1,2,384,4096]{3,2,1,0:T(8,128)(2,1)S(1)} copy-done((bf16[1,2,384,4096]{3,2,1,0:T(8,128)(2,1)S(1)}, bf16[1,2,384,4096]{3,2,1,0:T(8,128)(2,1)}, u32[]{:S(2)}) %copy-start.1) | copy-done | bytes 6291480
  44.6 1.9 %copy-done.4 = bf16[1,384,4096]{2,1,0:T(8,128)(2,1)S(1)} copy-done((bf16[1,384,4096]{2,1,0:T(8,128)(2,1)S(1)}, bf16[1,384,4096]{2,1,0:T(8,128)(2,1)}, u32[]{:S(2)}) %copy-start.4) | copy-done | bytes 3145752
  46.5 3.7 %collective-permute-done.6.refs_2_ = bf16[16,4096]{1,0:T(8,128)(2,1)S(1)} collective-permute-done((bf16[16,4096]{1,0:T(8,128)(2,1)S(1)}, bf16[16,4096]{1,0:T(8,128)(2,1)S(1)}, u32[]{:S(2)}, u32[]{:S(2)}) %collective-permute-start.6) | collective-permute-done | bytes 131104 | tf_op jit(solution)/shard_map/ppermute | solution.py:360
  50.2 1.5 %collective-permute-start.8 = (bf16[16,4096]{1,0:T(8,128)(2,1)S(1)}, bf16[16,4096]{1,0:T(8,128)(2,1)S(1)}, u32[]{:S(2)}, u32[]{:S(2)}) collective-permute-start(bf16[16,4096]{1,0:T(8,128)(2,1)S(1)} %collective-permute-done.5.refs_2_), channel_id=1, source_target_pairs={{0,2},{1,3},{2,0},{3,1},{4,6},{5,7},{6,4},{7,5},{8,10},{9,11},{10,... | collective-permute-start | bytes 393224 | tf_op jit(solution)/shard_map/ppermute | solution.py:357
  52.2 2.9 %collective-permute-done.8.refs_3_ = bf16[16,4096]{1,0:T(8,128)(2,1)S(1)} collective-permute-done((bf16[16,4096]{1,0:T(8,128)(2,1)S(1)}, bf16[16,4096]{1,0:T(8,128)(2,1)S(1)}, u32[]{:S(2)}, u32[]{:S(2)}) %collective-permute-start.8) | collective-permute-done | bytes 131104 | tf_op jit(solution)/shard_map/ppermute | solution.py:357
  57.2 2.8 %copy-done.2 = bf16[1,2,384,4096]{3,2,1,0:T(8,128)(2,1)S(1)} copy-done((bf16[1,2,384,4096]{3,2,1,0:T(8,128)(2,1)S(1)}, bf16[1,2,384,4096]{3,2,1,0:T(8,128)(2,1)}, u32[]{:S(2)}) %copy-start.2) | copy-done | bytes 6291480
  60.0 3.2 %experts.4 = (bf16[32,4096]{1,0:T(8,128)(2,1)S(1)}, bf16[32,4096]{1,0:T(8,128)(2,1)S(1)}) custom-call(s32[2]{0:T(128)S(1)} %pad_add_fusion.refs_2_.refs_1_.refs_0_, bf16[336,256]{1,0:T(8,128)(2,1)S(1)} %collective-permute-done.2.refs_8_.refs_1_, bf16[16,4096]{1,0:T(8,128)(2,1)S(1)} %collective-permute-done.5.refs_2_, ...), custom_call_target="tpu_custom_call" | custom-call | flops 1024 | bytes 1024 | tf_op jit(solution)/shard_map/experts/pallas_call | solution.py:273
  63.2 3.2 %experts.5 = (bf16[32,4096]{1,0:T(8,128)(2,1)S(1)}, bf16[32,4096]{1,0:T(8,128)(2,1)S(1)}) custom-call(s32[2]{0:T(128)S(1)} %pad_add_fusion.refs_2_.refs_1_.refs_0_, bf16[336,256]{1,0:T(8,128)(2,1)S(1)} %collective-permute-done.1.refs_7_.refs_1_, bf16[16,4096]{1,0:T(8,128)(2,1)S(1)} %collective-permute-done.6.refs_2_, ...), custom_call_target="tpu_custom_call" | custom-call | flops 1024 | bytes 1024 | tf_op jit(solution)/shard_map/experts/pallas_call | solution.py:273
  71.2 1.8 %collective-permute-done.23.refs_10_.refs_3_ = bf16[16,4096]{1,0:T(8,128)(2,1)S(1)} collective-permute-done((bf16[16,4096]{1,0:T(8,128)(2,1)S(1)}, bf16[16,4096]{1,0:T(8,128)(2,1)S(1)}, u32[]{:S(2)}, u32[]{:S(2)}) %collective-permute-start.23) | collective-permute-done | bytes 131104 | tf_op jit(solution)/shard_map/ppermute | solution.py:357
  74.3 2.8 %copy-done.3 = bf16[1,2,384,4096]{3,2,1,0:T(8,128)(2,1)S(1)} copy-done((bf16[1,2,384,4096]{3,2,1,0:T(8,128)(2,1)S(1)}, bf16[1,2,384,4096]{3,2,1,0:T(8,128)(2,1)}, u32[]{:S(2)}) %copy-start.3) | copy-done | bytes 6291480
  77.1 1.9 %copy-done.6 = bf16[1,384,4096]{2,1,0:T(8,128)(2,1)S(1)} copy-done((bf16[1,384,4096]{2,1,0:T(8,128)(2,1)S(1)}, bf16[1,384,4096]{2,1,0:T(8,128)(2,1)}, u32[]{:S(2)}) %copy-start.6) | copy-done | bytes 3145752
  79.0 3.2 %experts.6 = (bf16[32,4096]{1,0:T(8,128)(2,1)S(1)}, bf16[32,4096]{1,0:T(8,128)(2,1)S(1)}) custom-call(s32[2]{0:T(128)S(1)} %pad_add_fusion.refs_2_.refs_1_.refs_0_, bf16[336,256]{1,0:T(8,128)(2,1)S(1)} %collective-permute-done.refs_6_.refs_1_, bf16[16,4096]{1,0:T(8,128)(2,1)S(1)} %collective-permute-done.7.refs_2_, ...), custom_call_target="tpu_custom_call" | custom-call | flops 1024 | bytes 1024 | tf_op jit(solution)/shard_map/experts/pallas_call | solution.py:273
  82.4 3.3 %collective-permute-start.20 = (bf16[16,4096]{1,0:T(8,128)(2,1)S(1)}, bf16[16,4096]{1,0:T(8,128)(2,1)S(1)}, u32[]{:S(2)}, u32[]{:S(2)}) collective-permute-start(bf16[16,4096]{1,0:T(8,128)(2,1)S(1)} %add_convert_fusion.4), channel_id=1, source_target_pairs={{0,8},{4,12},{8,0},{12,4},{1,9},{5,13},{9,1},{13,5},{2,10},{6,14},... | collective-permute-start | bytes 393224 | tf_op jit(solution)/shard_map/ppermute | solution.py:360
  87.2 3.2 %experts.7 = (bf16[32,4096]{1,0:T(8,128)(2,1)S(1)}, bf16[32,4096]{1,0:T(8,128)(2,1)S(1)}) custom-call(s32[2]{0:T(128)S(1)} %pad_add_fusion.refs_2_.refs_1_.refs_0_, bf16[336,256]{1,0:T(8,128)(2,1)S(1)} %pad_maximum_fusion.refs_1_.refs_5_, bf16[16,4096]{1,0:T(8,128)(2,1)S(1)} %fusion.2.after.refs_2_, ...), custom_call_target="tpu_custom_call" | custom-call | flops 1024 | bytes 1024 | tf_op jit(solution)/shard_map/experts/pallas_call | solution.py:273
  93.3 3.6 %collective-permute-done.25 = bf16[16,4096]{1,0:T(8,128)(2,1)S(1)} collective-permute-done((bf16[16,4096]{1,0:T(8,128)(2,1)S(1)}, bf16[16,4096]{1,0:T(8,128)(2,1)S(1)}, u32[]{:S(2)}, u32[]{:S(2)}) %collective-permute-start.25) | collective-permute-done | bytes 131104 | tf_op jit(solution)/shard_map/ppermute | solution.py:357
  99.3 2.7 %collective-permute-done.26 = bf16[16,4096]{1,0:T(8,128)(2,1)S(1)} collective-permute-done((bf16[16,4096]{1,0:T(8,128)(2,1)S(1)}, bf16[16,4096]{1,0:T(8,128)(2,1)S(1)}, u32[]{:S(2)}, u32[]{:S(2)}) %collective-permute-start.26) | collective-permute-done | bytes 131104 | tf_op jit(solution)/shard_map/ppermute | solution.py:360
  (108 shorter events, 27.6 us)
Async XLA Ops:
  5.5 12.3 %collective-permute-start.2 = (bf16[336,256]{1,0:T(8,128)(2,1)S(1)}, bf16[336,256]{1,0:T(8,128)(2,1)S(1)}, u32[]{:S(2)}, u32[]{:S(2)}) collective-permute-start(bf16[336,256]{1,0:T(8,128)(2,1)S(1)} %pad_maximum_fusion.refs_1_.refs_5_), channel_id=1, source_target_pairs={{0,12},{4,8},{8,4},{12,0},{1,13},{5,9},{9,5},{13,1},{2,14},{6,10},... | collective-permute-start | bytes 516104 | tf_op jit(solution)/shard_map/ppermute | solution.py:345
  10.6 14.6 %collective-permute-start.1 = (bf16[336,256]{1,0:T(8,128)(2,1)S(1)}, bf16[336,256]{1,0:T(8,128)(2,1)S(1)}, u32[]{:S(2)}, u32[]{:S(2)}) collective-permute-start(bf16[336,256]{1,0:T(8,128)(2,1)S(1)} %pad_maximum_fusion.refs_1_.refs_5_), channel_id=1, source_target_pairs={{0,8},{4,12},{8,0},{12,4},{1,9},{5,13},{9,1},{13,5},{2,10},{6,14},... | collective-permute-start | bytes 516104 | tf_op jit(solution)/shard_map/ppermute | solution.py:345
  10.6 14.6 %collective-permute-start = (bf16[336,256]{1,0:T(8,128)(2,1)S(1)}, bf16[336,256]{1,0:T(8,128)(2,1)S(1)}, u32[]{:S(2)}, u32[]{:S(2)}) collective-permute-start(bf16[336,256]{1,0:T(8,128)(2,1)S(1)} %pad_maximum_fusion.refs_1_.refs_5_), channel_id=1, source_target_pairs={{0,4},{4,0},{8,12},{12,8},{1,5},{5,1},{9,13},{13,9},{2,6},{6,2},{1... | collective-permute-start | bytes 516104 | tf_op jit(solution)/shard_map/ppermute | solution.py:345
  30.5 5.6 %collective-permute-start.4 = (bf16[16,4096]{1,0:T(8,128)(2,1)S(1)}, bf16[16,4096]{1,0:T(8,128)(2,1)S(1)}, u32[]{:S(2)}, u32[]{:S(2)}) collective-permute-start(bf16[16,4096]{1,0:T(8,128)(2,1)S(1)} %add_convert_fusion.9), channel_id=1, source_target_pairs={{0,2},{1,3},{2,0},{3,1},{4,6},{5,7},{6,4},{7,5},{8,10},{9,11},{10,... | collective-permute-start | bytes 393224 | tf_op jit(solution)/shard_map/ppermute | solution.py:357
  37.3 9.1 %collective-permute-start.7 = (bf16[16,4096]{1,0:T(8,128)(2,1)S(1)}, bf16[16,4096]{1,0:T(8,128)(2,1)S(1)}, u32[]{:S(2)}, u32[]{:S(2)}) collective-permute-start(bf16[16,4096]{1,0:T(8,128)(2,1)S(1)} %fusion.2.after.refs_2_), channel_id=1, source_target_pairs={{0,4},{4,0},{8,12},{12,8},{1,5},{5,1},{9,13},{13,9},{2,6},{6,2},{1... | collective-permute-start | bytes 393224 | tf_op jit(solution)/shard_map/ppermute | solution.py:360
  37.4 12.8 %collective-permute-start.6 = (bf16[16,4096]{1,0:T(8,128)(2,1)S(1)}, bf16[16,4096]{1,0:T(8,128)(2,1)S(1)}, u32[]{:S(2)}, u32[]{:S(2)}) collective-permute-start(bf16[16,4096]{1,0:T(8,128)(2,1)S(1)} %fusion.2.after.refs_2_), channel_id=1, source_target_pairs={{0,8},{4,12},{8,0},{12,4},{1,9},{5,13},{9,1},{13,5},{2,10},{6,14},... | collective-permute-start | bytes 393224 | tf_op jit(solution)/shard_map/ppermute | solution.py:360
  40.5 9.8 %collective-permute-start.5 = (bf16[16,4096]{1,0:T(8,128)(2,1)S(1)}, bf16[16,4096]{1,0:T(8,128)(2,1)S(1)}, u32[]{:S(2)}, u32[]{:S(2)}) collective-permute-start(bf16[16,4096]{1,0:T(8,128)(2,1)S(1)} %fusion.2.after.refs_2_), channel_id=1, source_target_pairs={{0,12},{4,8},{8,4},{12,0},{1,13},{5,9},{9,5},{13,1},{2,14},{6,10},... | collective-permute-start | bytes 393224 | tf_op jit(solution)/shard_map/ppermute | solution.py:360
  51.7 5.5 %collective-permute-start.11 = (bf16[16,4096]{1,0:T(8,128)(2,1)S(1)}, bf16[16,4096]{1,0:T(8,128)(2,1)S(1)}, u32[]{:S(2)}, u32[]{:S(2)}) collective-permute-start(bf16[16,4096]{1,0:T(8,128)(2,1)S(1)} %collective-permute-done.6.refs_2_), channel_id=1, source_target_pairs={{0,2},{1,3},{2,0},{3,1},{4,6},{5,7},{6,4},{7,5},{8,10},{9,11},{10,... | collective-permute-start | bytes 393224 | tf_op jit(solution)/shard_map/ppermute | solution.py:357
  55.2 8.0 %collective-permute-start.15 = (bf16[16,4096]{1,0:T(8,128)(2,1)S(1)}, bf16[16,4096]{1,0:T(8,128)(2,1)S(1)}, u32[]{:S(2)}, u32[]{:S(2)}) collective-permute-start(bf16[16,4096]{1,0:T(8,128)(2,1)S(1)} %collective-permute-done.6.refs_2_), channel_id=1, source_target_pairs={{0,1},{1,0},{2,3},{3,2},{4,5},{5,4},{6,7},{7,6},{8,9},{9,8},{10,11... | collective-permute-start | bytes 393224 | tf_op jit(solution)/shard_map/ppermute | solution.py:357
  55.7 7.5 %collective-permute-start.17 = (bf16[16,4096]{1,0:T(8,128)(2,1)S(1)}, bf16[16,4096]{1,0:T(8,128)(2,1)S(1)}, u32[]{:S(2)}, u32[]{:S(2)}) collective-permute-start(bf16[16,4096]{1,0:T(8,128)(2,1)S(1)} %collective-permute-done.7.refs_2_), channel_id=1, source_target_pairs={{0,2},{1,3},{2,0},{3,1},{4,6},{5,7},{6,4},{7,5},{8,10},{9,11},{10,... | collective-permute-start | bytes 393224 | tf_op jit(solution)/shard_map/ppermute | solution.py:357
  57.2 6.0 %collective-permute-start.16 = (bf16[16,4096]{1,0:T(8,128)(2,1)S(1)}, bf16[16,4096]{1,0:T(8,128)(2,1)S(1)}, u32[]{:S(2)}, u32[]{:S(2)}) collective-permute-start(bf16[16,4096]{1,0:T(8,128)(2,1)S(1)} %collective-permute-done.11.refs_9_.refs_3_), channel_id=1, source_target_pairs={{0,1},{1,0},{2,3},{3,2},{4,5},{5,4},{6,7},{7,6},{8,9},{9,8},{10,11... | collective-permute-start | bytes 393224 | tf_op jit(solution)/shard_map/ppermute | solution.py:357
  67.0 30.0 %collective-permute-start.31 = (bf16[8,16,256]{2,1,0:T(8,128)(2,1)S(1)}, bf16[8,16,256]{2,1,0:T(8,128)(2,1)S(1)}, u32[]{:S(2)}, u32[]{:S(2)}) collective-permute-start(bf16[8,16,256]{2,1,0:T(8,128)(2,1)S(1)} %bitcast.23), channel_id=1, source_target_pairs={{0,1},{1,0},{2,3},{3,2},{4,5},{5,4},{6,7},{7,6},{8,9},{9,8},{10,11... | collective-permute-start | bytes 196616 | tf_op jit(solution)/shard_map/ppermute | solution.py:446
  67.1 5.9 %collective-permute-start.23 = (bf16[16,4096]{1,0:T(8,128)(2,1)S(1)}, bf16[16,4096]{1,0:T(8,128)(2,1)S(1)}, u32[]{:S(2)}, u32[]{:S(2)}) collective-permute-start(bf16[16,4096]{1,0:T(8,128)(2,1)S(1)} %fusion.2.after.refs_2_), channel_id=1, source_target_pairs={{0,2},{1,3},{2,0},{3,1},{4,6},{5,7},{6,4},{7,5},{8,10},{9,11},{10,... | collective-permute-start | bytes 393224 | tf_op jit(solution)/shard_map/ppermute | solution.py:357
  68.1 5.4 %collective-permute-start.22 = (bf16[16,4096]{1,0:T(8,128)(2,1)S(1)}, bf16[16,4096]{1,0:T(8,128)(2,1)S(1)}, u32[]{:S(2)}, u32[]{:S(2)}) collective-permute-start(bf16[16,4096]{1,0:T(8,128)(2,1)S(1)} %collective-permute-done.17.refs_10_.refs_3_), channel_id=1, source_target_pairs={{0,1},{1,0},{2,3},{3,2},{4,5},{5,4},{6,7},{7,6},{8,9},{9,8},{10,11... | collective-permute-start | bytes 393224 | tf_op jit(solution)/shard_map/ppermute | solution.py:357
  70.0 12.2 %collective-permute-start.19 = (bf16[16,4096]{1,0:T(8,128)(2,1)S(1)}, bf16[16,4096]{1,0:T(8,128)(2,1)S(1)}, u32[]{:S(2)}, u32[]{:S(2)}) collective-permute-start(bf16[16,4096]{1,0:T(8,128)(2,1)S(1)} %add_convert_fusion.5.refs_8_), channel_id=1, source_target_pairs={{0,2},{1,3},{2,0},{3,1},{4,6},{5,7},{6,4},{7,5},{8,10},{9,11},{10,... | collective-permute-start | bytes 393224 | tf_op jit(solution)/shard_map/ppermute | solution.py:357
  73.0 12.7 %collective-permute-start.27 = (bf16[16,4096]{1,0:T(8,128)(2,1)S(1)}, bf16[16,4096]{1,0:T(8,128)(2,1)S(1)}, u32[]{:S(2)}, u32[]{:S(2)}) collective-permute-start(bf16[16,4096]{1,0:T(8,128)(2,1)S(1)} %fusion.2.after.refs_2_), channel_id=1, source_target_pairs={{0,1},{1,0},{2,3},{3,2},{4,5},{5,4},{6,7},{7,6},{8,9},{9,8},{10,11... | collective-permute-start | bytes 393224 | tf_op jit(solution)/shard_map/ppermute | solution.py:357
  73.0 14.2 %collective-permute-start.28 = (bf16[16,4096]{1,0:T(8,128)(2,1)S(1)}, bf16[16,4096]{1,0:T(8,128)(2,1)S(1)}, u32[]{:S(2)}, u32[]{:S(2)}) collective-permute-start(bf16[16,4096]{1,0:T(8,128)(2,1)S(1)} %collective-permute-done.23.refs_10_.refs_3_), channel_id=1, source_target_pairs={{0,1},{1,0},{2,3},{3,2},{4,5},{5,4},{6,7},{7,6},{8,9},{9,8},{10,11... | collective-permute-start | bytes 393224 | tf_op jit(solution)/shard_map/ppermute | solution.py:357
  73.5 8.9 %collective-permute-start.13 = (bf16[16,4096]{1,0:T(8,128)(2,1)S(1)}, bf16[16,4096]{1,0:T(8,128)(2,1)S(1)}, u32[]{:S(2)}, u32[]{:S(2)}) collective-permute-start(bf16[16,4096]{1,0:T(8,128)(2,1)S(1)} %add_convert_fusion.7.refs_8_), channel_id=1, source_target_pairs={{0,2},{1,3},{2,0},{3,1},{4,6},{5,7},{6,4},{7,5},{8,10},{9,11},{10,... | collective-permute-start | bytes 393224 | tf_op jit(solution)/shard_map/ppermute | solution.py:357
  82.2 8.2 %collective-permute-start.24 = (bf16[32,4096]{1,0:T(8,128)(2,1)S(1)}, bf16[32,4096]{1,0:T(8,128)(2,1)S(1)}, u32[]{:S(2)}, u32[]{:S(2)}) collective-permute-start(bf16[32,4096]{1,0:T(8,128)(2,1)S(1)} %get-tuple-element.30.refs_9_), channel_id=1, source_target_pairs={{0,1},{1,0},{2,3},{3,2},{4,5},{5,4},{6,7},{7,6},{8,9},{9,8},{10,11... | collective-permute-start | bytes 786440 | tf_op jit(solution)/shard_map/ppermute | solution.py:357
  82.4 15.5 %collective-permute-start.20 = (bf16[16,4096]{1,0:T(8,128)(2,1)S(1)}, bf16[16,4096]{1,0:T(8,128)(2,1)S(1)}, u32[]{:S(2)}, u32[]{:S(2)}) collective-permute-start(bf16[16,4096]{1,0:T(8,128)(2,1)S(1)} %add_convert_fusion.4), channel_id=1, source_target_pairs={{0,8},{4,12},{8,0},{12,4},{1,9},{5,13},{9,1},{13,5},{2,10},{6,14},... | collective-permute-start | bytes 393224 | tf_op jit(solution)/shard_map/ppermute | solution.py:360
  85.7 12.1 %collective-permute-start.14 = (bf16[16,4096]{1,0:T(8,128)(2,1)S(1)}, bf16[16,4096]{1,0:T(8,128)(2,1)S(1)}, u32[]{:S(2)}, u32[]{:S(2)}) collective-permute-start(bf16[16,4096]{1,0:T(8,128)(2,1)S(1)} %add_convert_fusion.6.refs_10_), channel_id=1, source_target_pairs={{0,12},{4,8},{8,4},{12,0},{1,13},{5,9},{9,5},{13,1},{2,14},{6,10},... | collective-permute-start | bytes 393224 | tf_op jit(solution)/shard_map/ppermute | solution.py:360
  90.5 6.4 %collective-permute-start.25 = (bf16[16,4096]{1,0:T(8,128)(2,1)S(1)}, bf16[16,4096]{1,0:T(8,128)(2,1)S(1)}, u32[]{:S(2)}, u32[]{:S(2)}) collective-permute-start(bf16[16,4096]{1,0:T(8,128)(2,1)S(1)} %add_convert_fusion.3), channel_id=1, source_target_pairs={{0,2},{1,3},{2,0},{3,1},{4,6},{5,7},{6,4},{7,5},{8,10},{9,11},{10,... | collective-permute-start | bytes 393224 | tf_op jit(solution)/shard_map/ppermute | solution.py:357
  92.0 7.3 %collective-permute-start.30 = (bf16[16,4096]{1,0:T(8,128)(2,1)S(1)}, bf16[16,4096]{1,0:T(8,128)(2,1)S(1)}, u32[]{:S(2)}, u32[]{:S(2)}) collective-permute-start(bf16[16,4096]{1,0:T(8,128)(2,1)S(1)} %add_convert_fusion.1), channel_id=1, source_target_pairs={{0,2},{1,3},{2,0},{3,1},{4,6},{5,7},{6,4},{7,5},{8,10},{9,11},{10,... | collective-permute-start | bytes 393224 | tf_op jit(solution)/shard_map/ppermute | solution.py:357
  96.9 5.0 %collective-permute-start.26 = (bf16[16,4096]{1,0:T(8,128)(2,1)S(1)}, bf16[16,4096]{1,0:T(8,128)(2,1)S(1)}, u32[]{:S(2)}, u32[]{:S(2)}) collective-permute-start(bf16[16,4096]{1,0:T(8,128)(2,1)S(1)} %add_convert_fusion.2), channel_id=1, source_target_pairs={{0,4},{4,0},{8,12},{12,8},{1,5},{5,1},{9,13},{13,9},{2,6},{6,2},{1... | collective-permute-start | bytes 393224 | tf_op jit(solution)/shard_map/ppermute | solution.py:360
  (22 other events, 156.1 us)

commit v9 on v8

--- a/solution.py
+++ b/solution.py
@@ -376,7 +376,9 @@
     own_most = 2 * (tokens // page_size)
     own_slots = block_index * row_count + jnp.arange(row_count, dtype=jnp.int32)
     rows_filled = own_slots < span_lengths[ep_index]
-    held_out = hold_call([out_weight], payload, place, rows_filled.astype(jnp.int32))[0]
+    core = jnp.broadcast_to(tp_index.astype(jnp.int32), (1, 1, 2 * HD))
+    core, row_mask = lax.optimization_barrier((core, rows_filled.astype(jnp.int32)))
+    held_out, _ = hold_call([out_weight], payload, place, row_mask, core)
     kept, sent, head_pages = attend_call(
         span_lengths,
         place,
@@ -401,29 +403,19 @@
         * norm_gain
     ).astype(jnp.bfloat16)
 
-    order = list(range(ep_count - 1, -1, -1))
-    token = first_reader_call(gate_up, down_weight, normed)
-    token, *crossed = lax.optimization_barrier(
-        [token] + [across(normed, step) for step in order[:-1]]
-    )
-    given = []
-    finished = []
-    mixture = resid_wide
-    haves = []
-    for piece in crossed + [normed]:
+    order = [0] + list(range(ep_count - 1, 0, -1))
+
+    def group_rows(piece):
         have = [piece]
         for bit in bits + [1]:
             have += [exchange(part, bit) for part in have]
-        haves.append(have)
-    for turn, step in enumerate(order):
-        after = given[turn - 2 : turn - 1] if turn >= 2 else [token]
-        after = after + ([sent] if turn >= 1 else [])
-        after = after + (finished[turn - 3 : turn - 2] if turn >= 3 else [])
-        after = after + [have[1] for have in haves[turn + 1 : turn + 2]]
-        kept, sent = expert_call(
+        return have
+
+    def experts_of(step, have, after):
+        return expert_call(
             place,
             arrived[step],
-            haves[turn],
+            have,
             gate_up,
             down_weight,
             after,
@@ -431,6 +423,25 @@
             blocks,
             held + tokens,
         )
+
+    token = first_reader_call(gate_up, down_weight, normed)
+    early = [exchange(normed, bit) for bit in bits + [1]]
+    token, *crossed = lax.optimization_barrier(
+        [token] + early + [across(normed, step) for step in order[1:]]
+    )
+    own_have = [normed]
+    for bit, piece in zip(bits + [1], crossed):
+        own_have += [piece] + [exchange(part, bit) for part in own_have[1:]]
+    haves = [own_have] + [group_rows(piece) for piece in crossed[len(early) :]]
+    given = []
+    finished = []
+    mixture = resid_wide
+    for turn, step in enumerate(order):
+        after = [sent] if turn >= 1 else [token]
+        after = after + (given[turn - 2 : turn - 1] if turn >= 2 else [])
+        after = after + (finished[turn - 3 : turn - 2] if turn >= 3 else [])
+        after = after + [have[1] for have in haves[turn + 1 : turn + 2] if turn >= 1]
+        kept, sent = experts_of(step, haves[turn], after)
         own, gives = scatter(kept, sent)
         own = own.astype(jnp.bfloat16)
         given.append(gives[0] if gives else own)
@@ -438,13 +449,13 @@
         if step > 0:
             own = across(own, step)
         mixture = mixture + own.astype(jnp.float32)
-    layer_out = jnp.where(rows_filled[:, None], mixture, 0.0).astype(jnp.bfloat16)
+    layer_out = jnp.where(row_mask[:, None] > 0, mixture, 0.0).astype(jnp.bfloat16)
 
     if keyval_local == 1:
         decode_pages = head_pages[:, :, None, :]
     else:
         other = lax.ppermute(head_pages, "tp", [(i, i ^ 1) for i in range(tp_count)])
-        first = tp_index == 0
+        first = core == 0
         decode_pages = jnp.stack(
             [jnp.where(first, head_pages, other), jnp.where(first, other, head_pages)], axis=2
         )

time: 103 us -> 95.3 us (0.925)
  local copies, waits for them, and re-layouts: 19.9 us -> 15.3 us
  waiting for transfers between devices: 30.7 us -> 26.4 us
    ppermute x22, waiting for transfers between devices: 16.9 us -> 11.8 us  [local(): lax.ppermute(value, ('kv', 'tp'), [(i, i ^ bit) for i in range(blocks)])]
    unnamed x31 -> x23, local copies, waits for them, and re-layouts: 16.4 us -> 11.7 us
    ppermute x22, starting transfers between devices: 12.9 us -> 14.1 us  [local(): lax.ppermute(value, ('kv', 'tp'), [(i, i ^ bit) for i in range(blocks)])]
  transfers between devices with their start and end apart: 32 -> 32, of which waited for: 11 -> 10; matrix products, arithmetic and copies ran while one was open for 3% -> 3% of each run, Pallas kernels for 10% -> 15%
where the time goes in v9:
time: 95.3 us; the launch traced here: 94.9 us
  starting transfers between devices  29 us (30%)
  waiting for transfers between devices  26.4 us (28%)
  Pallas kernels  17.6 us (18%)
  local copies, waits for them, and re-layouts  15.3 us (16%)
  other arithmetic  5.56 us (6%)
  between operations  1.01 us (1%)
    ppermute x22, starting transfers between devices, local(): lax.ppermute(value, ('kv', 'tp'), [(i, i ^ bit) for i in range(blocks)])  14.1 us
    pallas_call x4, Pallas kernels, expert_call(): pl.pallas_call(lambda *refs: expert_kernel(len(have), ep_count, blocks, w...  12.8 us
    ppermute x22, waiting for transfers between devices, local(): lax.ppermute(value, ('kv', 'tp'), [(i, i ^ bit) for i in range(blocks)])  11.8 us
    unnamed x23, local copies, waits for them, and re-layouts  11.7 us
    ppermute x6, starting transfers between devices, local(): lax.ppermute(value, 'ep', [(i, i ^ step) for i in range(ep_count)])  9 us
    ppermute x3, waiting for transfers between devices, local(): lax.ppermute(payload, 'ep', [(i, i ^ step) for i in range(ep_count)])  7.31 us
    ppermute x6, waiting for transfers between devices, local(): lax.ppermute(value, 'ep', [(i, i ^ step) for i in range(ep_count)])  7.3 us
    ppermute x3, starting transfers between devices, local(): lax.ppermute(payload, 'ep', [(i, i ^ step) for i in range(ep_count)])  5.76 us
  transfers between devices with their start and end apart: 32, of which 10 were waited for; matrix products, arithmetic and copies ran while one was open for 3% of the time, Pallas kernels for 15%

profile of v9, /device:TPU:0, one launch (start us, length us, event | category | flops | bytes accessed | tf_op | source)
XLA Modules:
  0.0 94.9 jit_solution(1971364188927913977)
XLA Ops:
  5.5 5.1 %collective-permute-start.2 = (bf16[336,256]{1,0:T(8,128)(2,1)S(1)}, bf16[336,256]{1,0:T(8,128)(2,1)S(1)}, u32[]{:S(2)}, u32[]{:S(2)}) collective-permute-start(bf16[336,256]{1,0:T(8,128)(2,1)S(1)} %pad_maximum_fusion.refs_1_.refs_5_), channel_id=1, source_target_pairs={{0,12},{4,8},{8,4},{12,0},{1,13},{5,9},{9,5},{13,1},{2,14},{6,10},... | collective-permute-start | bytes 516104 | tf_op jit(solution)/shard_map/ppermute | solution.py:345
  13.3 3.4 %copy-done.5 = bf16[1024,4096]{1,0:T(8,128)(2,1)S(1)} copy-done((bf16[1024,4096]{1,0:T(8,128)(2,1)S(1)}, bf16[1024,4096]{1,0:T(8,128)(2,1)}, u32[]{:S(2)}) %copy-start.5) | copy-done | bytes 8388632
  17.9 7.3 %collective-permute-done.1.refs_7_.refs_1_ = bf16[336,256]{1,0:T(8,128)(2,1)S(1)} collective-permute-done((bf16[336,256]{1,0:T(8,128)(2,1)S(1)}, bf16[336,256]{1,0:T(8,128)(2,1)S(1)}, u32[]{:S(2)}, u32[]{:S(2)}) %collective-permute-start.1) | collective-permute-done | bytes 172064 | tf_op jit(solution)/shard_map/ppermute | solution.py:345
  25.2 3.7 %attend.1 = (f32[32,4096]{1,0:T(8,128)S(1)}, bf16[32,4096]{1,0:T(8,128)(2,1)S(1)}, bf16[128,256]{1,0:T(8,128)(2,1)S(1)}) custom-call(s32[4]{0:T(128)S(1)} %copy-done.7, s32[2]{0:T(128)S(1)} %pad_add_fusion.refs_2_.refs_1_.refs_0_, s32[1]{0:T(128)} %constant.60.clone.1.refs_2_, s32[16]{0:T(128)S(1)} %copy-done.8, bf16[64,1024]{1,0:T(8,128)(2,1)S(1)} %copy-done.6, ...), custom_call_target="tpu_custom_call" | custom-call | flops 872415232 | bytes 8388608 | tf_op jit(solution)/shard_map/attend/pallas_call | solution.py:204
  29.0 1.5 %collective-permute-done.3 = bf16[32,4096]{1,0:T(8,128)(2,1)S(1)} collective-permute-done((bf16[32,4096]{1,0:T(8,128)(2,1)S(1)}, bf16[32,4096]{1,0:T(8,128)(2,1)S(1)}, u32[]{:S(2)}, u32[]{:S(2)}) %collective-permute-start.3) | collective-permute-done | bytes 262176 | tf_op jit(solution)/shard_map/ppermute | solution.py:357
  30.5 1.6 %collective-permute-start.4 = (bf16[16,4096]{1,0:T(8,128)(2,1)S(1)}, bf16[16,4096]{1,0:T(8,128)(2,1)S(1)}, u32[]{:S(2)}, u32[]{:S(2)}) collective-permute-start(bf16[16,4096]{1,0:T(8,128)(2,1)S(1)} %add_convert_fusion.9), channel_id=1, source_target_pairs={{0,2},{1,3},{2,0},{3,1},{4,6},{5,7},{6,4},{7,5},{8,10},{9,11},{10,... | collective-permute-start | bytes 393224 | tf_op jit(solution)/shard_map/ppermute | solution.py:357
  32.1 4.0 %collective-permute-done.4 = bf16[16,4096]{1,0:T(8,128)(2,1)S(1)} collective-permute-done((bf16[16,4096]{1,0:T(8,128)(2,1)S(1)}, bf16[16,4096]{1,0:T(8,128)(2,1)S(1)}, u32[]{:S(2)}, u32[]{:S(2)}) %collective-permute-start.4) | collective-permute-done | bytes 131104 | tf_op jit(solution)/shard_map/ppermute | solution.py:357
  37.4 3.0 %collective-permute-start.8 = (bf16[16,4096]{1,0:T(8,128)(2,1)S(1)}, bf16[16,4096]{1,0:T(8,128)(2,1)S(1)}, u32[]{:S(2)}, u32[]{:S(2)}) collective-permute-start(bf16[16,4096]{1,0:T(8,128)(2,1)S(1)} %fusion.2.after.refs_2_), channel_id=1, source_target_pairs={{0,8},{4,12},{8,0},{12,4},{1,9},{5,13},{9,1},{13,5},{2,10},{6,14},... | collective-permute-start | bytes 393224 | tf_op jit(solution)/shard_map/ppermute | solution.py:360
  41.8 1.5 %collective-permute-start.5 = (bf16[16,4096]{1,0:T(8,128)(2,1)S(1)}, bf16[16,4096]{1,0:T(8,128)(2,1)S(1)}, u32[]{:S(2)}, u32[]{:S(2)}) collective-permute-start(bf16[16,4096]{1,0:T(8,128)(2,1)S(1)} %fusion.2.after.refs_2_), channel_id=1, source_target_pairs={{0,2},{1,3},{2,0},{3,1},{4,6},{5,7},{6,4},{7,5},{8,10},{9,11},{10,... | collective-permute-start | bytes 393224 | tf_op jit(solution)/shard_map/ppermute | solution.py:357
  43.3 2.8 %copy-done.1 = bf16[1,2,384,4096]{3,2,1,0:T(8,128)(2,1)S(1)} copy-done((bf16[1,2,384,4096]{3,2,1,0:T(8,128)(2,1)S(1)}, bf16[1,2,384,4096]{3,2,1,0:T(8,128)(2,1)}, u32[]{:S(2)}) %copy-start.1) | copy-done | bytes 6291480
  46.1 1.9 %copy-done.3 = bf16[1,384,4096]{2,1,0:T(8,128)(2,1)S(1)} copy-done((bf16[1,384,4096]{2,1,0:T(8,128)(2,1)S(1)}, bf16[1,384,4096]{2,1,0:T(8,128)(2,1)}, u32[]{:S(2)}) %copy-start.3) | copy-done | bytes 3145752
  48.0 2.2 %collective-permute-done.8.refs_2_ = bf16[16,4096]{1,0:T(8,128)(2,1)S(1)} collective-permute-done((bf16[16,4096]{1,0:T(8,128)(2,1)S(1)}, bf16[16,4096]{1,0:T(8,128)(2,1)S(1)}, u32[]{:S(2)}, u32[]{:S(2)}) %collective-permute-start.8) | collective-permute-done | bytes 131104 | tf_op jit(solution)/shard_map/ppermute | solution.py:360
  50.3 1.6 %collective-permute-start.13 = (bf16[16,4096]{1,0:T(8,128)(2,1)S(1)}, bf16[16,4096]{1,0:T(8,128)(2,1)S(1)}, u32[]{:S(2)}, u32[]{:S(2)}) collective-permute-start(bf16[16,4096]{1,0:T(8,128)(2,1)S(1)} %collective-permute-done.7.refs_2_), channel_id=1, source_target_pairs={{0,2},{1,3},{2,0},{3,1},{4,6},{5,7},{6,4},{7,5},{8,10},{9,11},{10,... | collective-permute-start | bytes 393224 | tf_op jit(solution)/shard_map/ppermute | solution.py:357
  52.5 2.8 %copy-done.2 = bf16[1,2,384,4096]{3,2,1,0:T(8,128)(2,1)S(1)} copy-done((bf16[1,2,384,4096]{3,2,1,0:T(8,128)(2,1)S(1)}, bf16[1,2,384,4096]{3,2,1,0:T(8,128)(2,1)}, u32[]{:S(2)}) %copy-start.2) | copy-done | bytes 6291480
  55.3 3.2 %experts.4 = (bf16[32,4096]{1,0:T(8,128)(2,1)S(1)}, bf16[32,4096]{1,0:T(8,128)(2,1)S(1)}) custom-call(s32[2]{0:T(128)S(1)} %pad_add_fusion.refs_2_.refs_1_.refs_0_, bf16[336,256]{1,0:T(8,128)(2,1)S(1)} %pad_maximum_fusion.refs_1_.refs_5_, bf16[16,4096]{1,0:T(8,128)(2,1)S(1)} %fusion.2.after.refs_2_, bf16[16,4096]{1,0:T(8,128)(2,1)S(1)} %collective-permute-done.5.refs_3_, ...), custom_call_target="tpu_custom_call" | custom-call | flops 1024 | bytes 1024 | tf_op jit(solution)/shard_map/experts/pallas_call | solution.py:273
  59.7 1.5 %collective-permute-start.22 = (bf16[16,4096]{1,0:T(8,128)(2,1)S(1)}, bf16[16,4096]{1,0:T(8,128)(2,1)S(1)}, u32[]{:S(2)}, u32[]{:S(2)}) collective-permute-start(bf16[16,4096]{1,0:T(8,128)(2,1)S(1)} %collective-permute-done.9.refs_2_), channel_id=1, source_target_pairs={{0,2},{1,3},{2,0},{3,1},{4,6},{5,7},{6,4},{7,5},{8,10},{9,11},{10,... | collective-permute-start | bytes 393224 | tf_op jit(solution)/shard_map/ppermute | solution.py:357
  61.2 3.2 %experts.5 = (bf16[32,4096]{1,0:T(8,128)(2,1)S(1)}, bf16[32,4096]{1,0:T(8,128)(2,1)S(1)}) custom-call(s32[2]{0:T(128)S(1)} %pad_add_fusion.refs_2_.refs_1_.refs_0_, bf16[336,256]{1,0:T(8,128)(2,1)S(1)} %collective-permute-done.2.refs_8_.refs_1_, bf16[16,4096]{1,0:T(8,128)(2,1)S(1)} %collective-permute-done.7.refs_2_, ...), custom_call_target="tpu_custom_call" | custom-call | flops 1024 | bytes 1024 | tf_op jit(solution)/shard_map/experts/pallas_call | solution.py:273
  66.7 3.2 %experts.6 = (bf16[32,4096]{1,0:T(8,128)(2,1)S(1)}, bf16[32,4096]{1,0:T(8,128)(2,1)S(1)}) custom-call(s32[2]{0:T(128)S(1)} %pad_add_fusion.refs_2_.refs_1_.refs_0_, bf16[336,256]{1,0:T(8,128)(2,1)S(1)} %collective-permute-done.1.refs_7_.refs_1_, bf16[16,4096]{1,0:T(8,128)(2,1)S(1)} %collective-permute-done.8.refs_2_, ...), custom_call_target="tpu_custom_call" | custom-call | flops 1024 | bytes 1024 | tf_op jit(solution)/shard_map/experts/pallas_call | solution.py:273
  71.1 1.5 %collective-permute-start.18 = (bf16[16,4096]{1,0:T(8,128)(2,1)S(1)}, bf16[16,4096]{1,0:T(8,128)(2,1)S(1)}, u32[]{:S(2)}, u32[]{:S(2)}) collective-permute-start(bf16[16,4096]{1,0:T(8,128)(2,1)S(1)} %add_convert_fusion.5.refs_9_), channel_id=1, source_target_pairs={{0,2},{1,3},{2,0},{3,1},{4,6},{5,7},{6,4},{7,5},{8,10},{9,11},{10,... | collective-permute-start | bytes 393224 | tf_op jit(solution)/shard_map/ppermute | solution.py:357
  72.7 3.2 %experts.7 = (bf16[32,4096]{1,0:T(8,128)(2,1)S(1)}, bf16[32,4096]{1,0:T(8,128)(2,1)S(1)}) custom-call(s32[2]{0:T(128)S(1)} %pad_add_fusion.refs_2_.refs_1_.refs_0_, bf16[336,256]{1,0:T(8,128)(2,1)S(1)} %collective-permute-done.refs_6_.refs_1_, bf16[16,4096]{1,0:T(8,128)(2,1)S(1)} %collective-permute-done.9.refs_2_, ...), custom_call_target="tpu_custom_call" | custom-call | flops 1024 | bytes 1024 | tf_op jit(solution)/shard_map/experts/pallas_call | solution.py:273
  76.2 2.5 %collective-permute-start.19 = (bf16[16,4096]{1,0:T(8,128)(2,1)S(1)}, bf16[16,4096]{1,0:T(8,128)(2,1)S(1)}, u32[]{:S(2)}, u32[]{:S(2)}) collective-permute-start(bf16[16,4096]{1,0:T(8,128)(2,1)S(1)} %add_convert_fusion.4), channel_id=1, source_target_pairs={{0,12},{4,8},{8,4},{12,0},{1,13},{5,9},{9,5},{13,1},{2,14},{6,10},... | collective-permute-start | bytes 393224 | tf_op jit(solution)/shard_map/ppermute | solution.py:360
  78.7 1.7 %collective-permute-start.24 = (bf16[16,4096]{1,0:T(8,128)(2,1)S(1)}, bf16[16,4096]{1,0:T(8,128)(2,1)S(1)}, u32[]{:S(2)}, u32[]{:S(2)}) collective-permute-start(bf16[16,4096]{1,0:T(8,128)(2,1)S(1)} %add_convert_fusion.3), channel_id=1, source_target_pairs={{0,2},{1,3},{2,0},{3,1},{4,6},{5,7},{6,4},{7,5},{8,10},{9,11},{10,... | collective-permute-start | bytes 393224 | tf_op jit(solution)/shard_map/ppermute | solution.py:357
  80.9 4.2 %collective-permute-done.24 = bf16[16,4096]{1,0:T(8,128)(2,1)S(1)} collective-permute-done((bf16[16,4096]{1,0:T(8,128)(2,1)S(1)}, bf16[16,4096]{1,0:T(8,128)(2,1)S(1)}, u32[]{:S(2)}, u32[]{:S(2)}) %collective-permute-start.24) | collective-permute-done | bytes 131104 | tf_op jit(solution)/shard_map/ppermute | solution.py:357
  89.1 3.9 %collective-permute-done.25 = bf16[16,4096]{1,0:T(8,128)(2,1)S(1)} collective-permute-done((bf16[16,4096]{1,0:T(8,128)(2,1)S(1)}, bf16[16,4096]{1,0:T(8,128)(2,1)S(1)}, u32[]{:S(2)}, u32[]{:S(2)}) %collective-permute-start.25) | collective-permute-done | bytes 131104 | tf_op jit(solution)/shard_map/ppermute | solution.py:360
  (104 shorter events, 23.5 us)
Async XLA Ops:
  5.5 12.4 %collective-permute-start.2 = (bf16[336,256]{1,0:T(8,128)(2,1)S(1)}, bf16[336,256]{1,0:T(8,128)(2,1)S(1)}, u32[]{:S(2)}, u32[]{:S(2)}) collective-permute-start(bf16[336,256]{1,0:T(8,128)(2,1)S(1)} %pad_maximum_fusion.refs_1_.refs_5_), channel_id=1, source_target_pairs={{0,12},{4,8},{8,4},{12,0},{1,13},{5,9},{9,5},{13,1},{2,14},{6,10},... | collective-permute-start | bytes 516104 | tf_op jit(solution)/shard_map/ppermute | solution.py:345
  10.6 14.6 %collective-permute-start.1 = (bf16[336,256]{1,0:T(8,128)(2,1)S(1)}, bf16[336,256]{1,0:T(8,128)(2,1)S(1)}, u32[]{:S(2)}, u32[]{:S(2)}) collective-permute-start(bf16[336,256]{1,0:T(8,128)(2,1)S(1)} %pad_maximum_fusion.refs_1_.refs_5_), channel_id=1, source_target_pairs={{0,8},{4,12},{8,0},{12,4},{1,9},{5,13},{9,1},{13,5},{2,10},{6,14},... | collective-permute-start | bytes 516104 | tf_op jit(solution)/shard_map/ppermute | solution.py:345
  10.6 14.6 %collective-permute-start = (bf16[336,256]{1,0:T(8,128)(2,1)S(1)}, bf16[336,256]{1,0:T(8,128)(2,1)S(1)}, u32[]{:S(2)}, u32[]{:S(2)}) collective-permute-start(bf16[336,256]{1,0:T(8,128)(2,1)S(1)} %pad_maximum_fusion.refs_1_.refs_5_), channel_id=1, source_target_pairs={{0,4},{4,0},{8,12},{12,8},{1,5},{5,1},{9,13},{13,9},{2,6},{6,2},{1... | collective-permute-start | bytes 516104 | tf_op jit(solution)/shard_map/ppermute | solution.py:345
  30.5 5.6 %collective-permute-start.4 = (bf16[16,4096]{1,0:T(8,128)(2,1)S(1)}, bf16[16,4096]{1,0:T(8,128)(2,1)S(1)}, u32[]{:S(2)}, u32[]{:S(2)}) collective-permute-start(bf16[16,4096]{1,0:T(8,128)(2,1)S(1)} %add_convert_fusion.9), channel_id=1, source_target_pairs={{0,2},{1,3},{2,0},{3,1},{4,6},{5,7},{6,4},{7,5},{8,10},{9,11},{10,... | collective-permute-start | bytes 393224 | tf_op jit(solution)/shard_map/ppermute | solution.py:357
  37.4 10.6 %collective-permute-start.9 = (bf16[16,4096]{1,0:T(8,128)(2,1)S(1)}, bf16[16,4096]{1,0:T(8,128)(2,1)S(1)}, u32[]{:S(2)}, u32[]{:S(2)}) collective-permute-start(bf16[16,4096]{1,0:T(8,128)(2,1)S(1)} %fusion.2.after.refs_2_), channel_id=1, source_target_pairs={{0,4},{4,0},{8,12},{12,8},{1,5},{5,1},{9,13},{13,9},{2,6},{6,2},{1... | collective-permute-start | bytes 393224 | tf_op jit(solution)/shard_map/ppermute | solution.py:360
  37.4 12.8 %collective-permute-start.8 = (bf16[16,4096]{1,0:T(8,128)(2,1)S(1)}, bf16[16,4096]{1,0:T(8,128)(2,1)S(1)}, u32[]{:S(2)}, u32[]{:S(2)}) collective-permute-start(bf16[16,4096]{1,0:T(8,128)(2,1)S(1)} %fusion.2.after.refs_2_), channel_id=1, source_target_pairs={{0,8},{4,12},{8,0},{12,4},{1,9},{5,13},{9,1},{13,5},{2,10},{6,14},... | collective-permute-start | bytes 393224 | tf_op jit(solution)/shard_map/ppermute | solution.py:360
  40.4 9.8 %collective-permute-start.7 = (bf16[16,4096]{1,0:T(8,128)(2,1)S(1)}, bf16[16,4096]{1,0:T(8,128)(2,1)S(1)}, u32[]{:S(2)}, u32[]{:S(2)}) collective-permute-start(bf16[16,4096]{1,0:T(8,128)(2,1)S(1)} %fusion.2.after.refs_2_), channel_id=1, source_target_pairs={{0,12},{4,8},{8,4},{12,0},{1,13},{5,9},{9,5},{13,1},{2,14},{6,10},... | collective-permute-start | bytes 393224 | tf_op jit(solution)/shard_map/ppermute | solution.py:360
  41.8 8.4 %collective-permute-start.6 = (bf16[16,4096]{1,0:T(8,128)(2,1)S(1)}, bf16[16,4096]{1,0:T(8,128)(2,1)S(1)}, u32[]{:S(2)}, u32[]{:S(2)}) collective-permute-start(bf16[16,4096]{1,0:T(8,128)(2,1)S(1)} %fusion.2.after.refs_2_), channel_id=1, source_target_pairs={{0,1},{1,0},{2,3},{3,2},{4,5},{5,4},{6,7},{7,6},{8,9},{9,8},{10,11... | collective-permute-start | bytes 393224 | tf_op jit(solution)/shard_map/ppermute | solution.py:357
  41.8 8.4 %collective-permute-start.5 = (bf16[16,4096]{1,0:T(8,128)(2,1)S(1)}, bf16[16,4096]{1,0:T(8,128)(2,1)S(1)}, u32[]{:S(2)}, u32[]{:S(2)}) collective-permute-start(bf16[16,4096]{1,0:T(8,128)(2,1)S(1)} %fusion.2.after.refs_2_), channel_id=1, source_target_pairs={{0,2},{1,3},{2,0},{3,1},{4,6},{5,7},{6,4},{7,5},{8,10},{9,11},{10,... | collective-permute-start | bytes 393224 | tf_op jit(solution)/shard_map/ppermute | solution.py:357
  50.3 8.4 %collective-permute-start.13 = (bf16[16,4096]{1,0:T(8,128)(2,1)S(1)}, bf16[16,4096]{1,0:T(8,128)(2,1)S(1)}, u32[]{:S(2)}, u32[]{:S(2)}) collective-permute-start(bf16[16,4096]{1,0:T(8,128)(2,1)S(1)} %collective-permute-done.7.refs_2_), channel_id=1, source_target_pairs={{0,2},{1,3},{2,0},{3,1},{4,6},{5,7},{6,4},{7,5},{8,10},{9,11},{10,... | collective-permute-start | bytes 393224 | tf_op jit(solution)/shard_map/ppermute | solution.py:357
  51.8 7.4 %collective-permute-start.14 = (bf16[16,4096]{1,0:T(8,128)(2,1)S(1)}, bf16[16,4096]{1,0:T(8,128)(2,1)S(1)}, u32[]{:S(2)}, u32[]{:S(2)}) collective-permute-start(bf16[16,4096]{1,0:T(8,128)(2,1)S(1)} %collective-permute-done.7.refs_2_), channel_id=1, source_target_pairs={{0,1},{1,0},{2,3},{3,2},{4,5},{5,4},{6,7},{7,6},{8,9},{9,8},{10,11... | collective-permute-start | bytes 393224 | tf_op jit(solution)/shard_map/ppermute | solution.py:357
  52.0 7.7 %collective-permute-start.16 = (bf16[16,4096]{1,0:T(8,128)(2,1)S(1)}, bf16[16,4096]{1,0:T(8,128)(2,1)S(1)}, u32[]{:S(2)}, u32[]{:S(2)}) collective-permute-start(bf16[16,4096]{1,0:T(8,128)(2,1)S(1)} %collective-permute-done.8.refs_2_), channel_id=1, source_target_pairs={{0,2},{1,3},{2,0},{3,1},{4,6},{5,7},{6,4},{7,5},{8,10},{9,11},{10,... | collective-permute-start | bytes 393224 | tf_op jit(solution)/shard_map/ppermute | solution.py:357
  58.5 5.9 %collective-permute-start.11 = (bf16[32,4096]{1,0:T(8,128)(2,1)S(1)}, bf16[32,4096]{1,0:T(8,128)(2,1)S(1)}, u32[]{:S(2)}, u32[]{:S(2)}) collective-permute-start(bf16[32,4096]{1,0:T(8,128)(2,1)S(1)} %get-tuple-element.31.refs_8_), channel_id=1, source_target_pairs={{0,1},{1,0},{2,3},{3,2},{4,5},{5,4},{6,7},{7,6},{8,9},{9,8},{10,11... | collective-permute-start | bytes 786440 | tf_op jit(solution)/shard_map/ppermute | solution.py:357
  59.1 29.1 %collective-permute-start.31 = (bf16[8,16,256]{2,1,0:T(8,128)(2,1)S(1)}, bf16[8,16,256]{2,1,0:T(8,128)(2,1)S(1)}, u32[]{:S(2)}, u32[]{:S(2)}) collective-permute-start(bf16[8,16,256]{2,1,0:T(8,128)(2,1)S(1)} %bitcast.23), channel_id=1, source_target_pairs={{0,1},{1,0},{2,3},{3,2},{4,5},{5,4},{6,7},{7,6},{8,9},{9,8},{10,11... | collective-permute-start | bytes 196616 | tf_op jit(solution)/shard_map/ppermute | solution.py:457
  59.3 5.8 %collective-permute-start.20 = (bf16[16,4096]{1,0:T(8,128)(2,1)S(1)}, bf16[16,4096]{1,0:T(8,128)(2,1)S(1)}, u32[]{:S(2)}, u32[]{:S(2)}) collective-permute-start(bf16[16,4096]{1,0:T(8,128)(2,1)S(1)} %collective-permute-done.8.refs_2_), channel_id=1, source_target_pairs={{0,1},{1,0},{2,3},{3,2},{4,5},{5,4},{6,7},{7,6},{8,9},{9,8},{10,11... | collective-permute-start | bytes 393224 | tf_op jit(solution)/shard_map/ppermute | solution.py:357
  59.7 5.5 %collective-permute-start.22 = (bf16[16,4096]{1,0:T(8,128)(2,1)S(1)}, bf16[16,4096]{1,0:T(8,128)(2,1)S(1)}, u32[]{:S(2)}, u32[]{:S(2)}) collective-permute-start(bf16[16,4096]{1,0:T(8,128)(2,1)S(1)} %collective-permute-done.9.refs_2_), channel_id=1, source_target_pairs={{0,2},{1,3},{2,0},{3,1},{4,6},{5,7},{6,4},{7,5},{8,10},{9,11},{10,... | collective-permute-start | bytes 393224 | tf_op jit(solution)/shard_map/ppermute | solution.py:357
  65.1 7.6 %collective-permute-start.26 = (bf16[16,4096]{1,0:T(8,128)(2,1)S(1)}, bf16[16,4096]{1,0:T(8,128)(2,1)S(1)}, u32[]{:S(2)}, u32[]{:S(2)}) collective-permute-start(bf16[16,4096]{1,0:T(8,128)(2,1)S(1)} %collective-permute-done.9.refs_2_), channel_id=1, source_target_pairs={{0,1},{1,0},{2,3},{3,2},{4,5},{5,4},{6,7},{7,6},{8,9},{9,8},{10,11... | collective-permute-start | bytes 393224 | tf_op jit(solution)/shard_map/ppermute | solution.py:357
  65.2 7.5 %collective-permute-start.27 = (bf16[16,4096]{1,0:T(8,128)(2,1)S(1)}, bf16[16,4096]{1,0:T(8,128)(2,1)S(1)}, u32[]{:S(2)}, u32[]{:S(2)}) collective-permute-start(bf16[16,4096]{1,0:T(8,128)(2,1)S(1)} %collective-permute-done.22.refs_10_.refs_3_), channel_id=1, source_target_pairs={{0,1},{1,0},{2,3},{3,2},{4,5},{5,4},{6,7},{7,6},{8,9},{9,8},{10,11... | collective-permute-start | bytes 393224 | tf_op jit(solution)/shard_map/ppermute | solution.py:357
  69.9 8.8 %collective-permute-start.23 = (bf16[32,4096]{1,0:T(8,128)(2,1)S(1)}, bf16[32,4096]{1,0:T(8,128)(2,1)S(1)}, u32[]{:S(2)}, u32[]{:S(2)}) collective-permute-start(bf16[32,4096]{1,0:T(8,128)(2,1)S(1)} %get-tuple-element.38.refs_8_), channel_id=1, source_target_pairs={{0,1},{1,0},{2,3},{3,2},{4,5},{5,4},{6,7},{7,6},{8,9},{9,8},{10,11... | collective-permute-start | bytes 786440 | tf_op jit(solution)/shard_map/ppermute | solution.py:357
  76.2 12.9 %collective-permute-start.19 = (bf16[16,4096]{1,0:T(8,128)(2,1)S(1)}, bf16[16,4096]{1,0:T(8,128)(2,1)S(1)}, u32[]{:S(2)}, u32[]{:S(2)}) collective-permute-start(bf16[16,4096]{1,0:T(8,128)(2,1)S(1)} %add_convert_fusion.4), channel_id=1, source_target_pairs={{0,12},{4,8},{8,4},{12,0},{1,13},{5,9},{9,5},{13,1},{2,14},{6,10},... | collective-permute-start | bytes 393224 | tf_op jit(solution)/shard_map/ppermute | solution.py:360
  78.7 6.4 %collective-permute-start.24 = (bf16[16,4096]{1,0:T(8,128)(2,1)S(1)}, bf16[16,4096]{1,0:T(8,128)(2,1)S(1)}, u32[]{:S(2)}, u32[]{:S(2)}) collective-permute-start(bf16[16,4096]{1,0:T(8,128)(2,1)S(1)} %add_convert_fusion.3), channel_id=1, source_target_pairs={{0,2},{1,3},{2,0},{3,1},{4,6},{5,7},{6,4},{7,5},{8,10},{9,11},{10,... | collective-permute-start | bytes 393224 | tf_op jit(solution)/shard_map/ppermute | solution.py:357
  80.5 6.6 %collective-permute-start.29 = (bf16[16,4096]{1,0:T(8,128)(2,1)S(1)}, bf16[16,4096]{1,0:T(8,128)(2,1)S(1)}, u32[]{:S(2)}, u32[]{:S(2)}) collective-permute-start(bf16[16,4096]{1,0:T(8,128)(2,1)S(1)} %add_convert_fusion.1), channel_id=1, source_target_pairs={{0,2},{1,3},{2,0},{3,1},{4,6},{5,7},{6,4},{7,5},{8,10},{9,11},{10,... | collective-permute-start | bytes 393224 | tf_op jit(solution)/shard_map/ppermute | solution.py:357
  85.2 7.7 %collective-permute-start.25 = (bf16[16,4096]{1,0:T(8,128)(2,1)S(1)}, bf16[16,4096]{1,0:T(8,128)(2,1)S(1)}, u32[]{:S(2)}, u32[]{:S(2)}) collective-permute-start(bf16[16,4096]{1,0:T(8,128)(2,1)S(1)} %add_convert_fusion.2), channel_id=1, source_target_pairs={{0,8},{4,12},{8,0},{12,4},{1,9},{5,13},{9,1},{13,5},{2,10},{6,14},... | collective-permute-start | bytes 393224 | tf_op jit(solution)/shard_map/ppermute | solution.py:360
  87.2 7.0 %collective-permute-start.30 = (bf16[16,4096]{1,0:T(8,128)(2,1)S(1)}, bf16[16,4096]{1,0:T(8,128)(2,1)S(1)}, u32[]{:S(2)}, u32[]{:S(2)}) collective-permute-start(bf16[16,4096]{1,0:T(8,128)(2,1)S(1)} %add_convert_fusion), channel_id=1, source_target_pairs={{0,4},{4,0},{8,12},{12,8},{1,5},{5,1},{9,13},{13,9},{2,6},{6,2},{1... | collective-permute-start | bytes 393224 | tf_op jit(solution)/shard_map/ppermute | solution.py:360
  (18 other events, 144.4 us)

commit v10 on v9

--- a/solution.py
+++ b/solution.py
@@ -72,20 +72,51 @@
     )(*arrays, *after)
 
 
-def first_reader(gate_up, down_weight, after, token):
-    token[...] = (gate_up[0, 0, :16, :128] + down_weight[0, :16, :128]).astype(jnp.float32)
-
-
-def first_reader_call(gate_up, down_weight, after):
+def prepare_kernel(ep_count, blocks, weight_at, place, *refs):
+    payloads = refs[:ep_count]
+    gate_up_from, down_from, _, gate_up, down_weight, row_weights, sem = refs[ep_count:]
+    copies = [
+        pltpu.make_async_copy(gate_up_from, gate_up, sem.at[0]),
+        pltpu.make_async_copy(down_from, down_weight, sem.at[1]),
+    ]
+    for copy in copies:
+        copy.start()
+
+    tokens = row_weights.shape[0] // ep_count
+    row_count = tokens // blocks
+    wide = (tokens, payloads[0].shape[1])
+    row = lax.broadcasted_iota(jnp.int32, wide, 0)
+    token = row % row_count
+    for spot, piece in enumerate(piece_order(blocks)):
+        token = token + jnp.where(row // row_count == spot, (place[1] ^ piece) * row_count, 0)
+    here = lax.broadcasted_iota(jnp.int32, wide, 1) == token
+    for step, payload in enumerate(payloads):
+        parts = payload[weight_at:, :].astype(jnp.float32)
+        part_row = lax.broadcasted_iota(jnp.int32, parts.shape, 0)
+        chosen = (part_row % ep_count == place[0]) & (part_row < 3 * ep_count)
+        by_token = jnp.sum(jnp.where(chosen, parts, 0.0), axis=0, keepdims=True)
+        column = jnp.sum(jnp.where(here, by_token, 0.0), axis=1, keepdims=True)
+        row_weights[step * tokens : (step + 1) * tokens, :] = jnp.broadcast_to(column, (tokens, HD))
+    for copy in copies:
+        copy.wait()
+
+
+def prepare_call(place, arrived, gate_up, down_weight, after, blocks, tokens, weight_at):
+    ep_count = len(arrived)
     return pl.pallas_call(
-        first_reader,
-        out_shape=jax.ShapeDtypeStruct((16, 128), jnp.float32),
-        in_specs=[WHOLE, WHOLE, ANYWHERE],
-        out_specs=WHOLE,
+        lambda *refs: prepare_kernel(ep_count, blocks, weight_at, *refs),
+        out_shape=[
+            jax.ShapeDtypeStruct(gate_up.shape, gate_up.dtype),
+            jax.ShapeDtypeStruct(down_weight.shape, down_weight.dtype),
+            jax.ShapeDtypeStruct((ep_count * tokens, HD), jnp.float32),
+        ],
+        in_specs=[SCALARS] + [WHOLE] * ep_count + [ANYWHERE] * 3,
+        out_specs=[WHOLE] * 3,
+        scratch_shapes=[pltpu.SemaphoreType.DMA((2,))],
         compiler_params=pltpu.CompilerParams(vmem_limit_bytes=VMEM_LIMIT),
         cost_estimate=EXPERT_COST,
-        name="first_reader",
-    )(gate_up, down_weight, after)
+        name="prepare",
+    )(place, *arrived, gate_up, down_weight, after)
 
 
 def attend_kernel(ep_count, held, tokens, row_blocks, all_open, lens, place, counts, owners, queries, *refs):
@@ -225,24 +256,12 @@
     )(lens, place, counts, owners, queries, *arrived, out_weight)
 
 
-def expert_kernel(count, ep_count, blocks, weight_at, place, payload, *refs):
+def expert_kernel(count, step, row_weights, *refs):
     row_refs = refs[:count]
     gate_up, down_weight = refs[count : count + 2]
     kept_ref, sent_ref = refs[-2:]
     tokens = 2 * kept_ref.shape[0]
-    row_count = tokens // blocks
-
-    parts = payload[weight_at:, :].astype(jnp.float32)
-    part_row = lax.broadcasted_iota(jnp.int32, parts.shape, 0)
-    chosen = (part_row % ep_count == place[0]) & (part_row < 3 * ep_count)
-    by_token = jnp.sum(jnp.where(chosen, parts, 0.0), axis=0, keepdims=True)
-    row = lax.broadcasted_iota(jnp.int32, (tokens, parts.shape[1]), 0)
-    token = row % row_count
-    for spot, piece in enumerate(piece_order(blocks)):
-        token = token + jnp.where(row // row_count == spot, (place[1] ^ piece) * row_count, 0)
-    here = lax.broadcasted_iota(jnp.int32, (tokens, parts.shape[1]), 1) == token
-    row_weight = jnp.sum(jnp.where(here, by_token, 0.0), axis=1, keepdims=True)
-
+    row_weight = row_weights[step * tokens : (step + 1) * tokens, :1]
     gate_part = up_part = 0.0
     for at in range(0, kept_ref.shape[1], COLUMNS):
         rows = jnp.concatenate([ref[:, at : at + COLUMNS] for ref in row_refs], axis=0)
@@ -263,7 +282,7 @@
         sent_ref[:, at : at + COLUMNS] = out[half:]
 
 
-def expert_call(place, payload, have, gate_up, down_weight, after, ep_count, blocks, weight_at):
+def expert_call(step, row_weights, have, gate_up, down_weight, after):
     if have[0].shape[0] % 16:
         have = [jnp.concatenate(have, axis=0)]
     tokens = sum(piece.shape[0] for piece in have)
@@ -271,14 +290,14 @@
     hidden_units = down_weight.shape[1]
     half = jax.ShapeDtypeStruct((tokens // 2, model_width), jnp.bfloat16)
     return pl.pallas_call(
-        lambda *refs: expert_kernel(len(have), ep_count, blocks, weight_at, *refs),
+        lambda *refs: expert_kernel(len(have), step, *refs),
         out_shape=(half, half),
-        in_specs=[SCALARS] + [WHOLE] * (len(have) + 3) + [ANYWHERE] * len(after),
+        in_specs=[WHOLE] * (len(have) + 3) + [ANYWHERE] * len(after),
         out_specs=(WHOLE, WHOLE),
         compiler_params=pltpu.CompilerParams(vmem_limit_bytes=VMEM_LIMIT),
         cost_estimate=EXPERT_COST,
         name="experts",
-    )(place, payload, *have, gate_up, down_weight, *after)
+    )(row_weights, *have, gate_up, down_weight, *after)
 
 
 def local(
@@ -403,7 +422,7 @@
         * norm_gain
     ).astype(jnp.bfloat16)
 
-    order = [0] + list(range(ep_count - 1, 0, -1))
+    order = list(range(ep_count - 1, -1, -1))
 
     def group_rows(piece):
         have = [piece]
@@ -411,37 +430,29 @@
             have += [exchange(part, bit) for part in have]
         return have
 
-    def experts_of(step, have, after):
-        return expert_call(
-            place,
-            arrived[step],
-            have,
-            gate_up,
-            down_weight,
-            after,
-            ep_count,
-            blocks,
-            held + tokens,
-        )
-
-    token = first_reader_call(gate_up, down_weight, normed)
+    held_gate_up, held_down, row_weights = prepare_call(
+        place, arrived, gate_up, down_weight, normed, blocks, tokens, held + tokens
+    )
+    crossed = [across(normed, step) for step in order[:-1]]
     early = [exchange(normed, bit) for bit in bits + [1]]
-    token, *crossed = lax.optimization_barrier(
-        [token] + early + [across(normed, step) for step in order[1:]]
-    )
+    row_weights, *crossed = lax.optimization_barrier([row_weights] + crossed + early)
+    early = crossed[len(order) - 1 :]
     own_have = [normed]
-    for bit, piece in zip(bits + [1], crossed):
+    for bit, piece in zip(bits + [1], early):
         own_have += [piece] + [exchange(part, bit) for part in own_have[1:]]
-    haves = [own_have] + [group_rows(piece) for piece in crossed[len(early) :]]
+    haves = [group_rows(piece) for piece in crossed[: len(order) - 1]] + [own_have]
     given = []
     finished = []
     mixture = resid_wide
     for turn, step in enumerate(order):
-        after = [sent] if turn >= 1 else [token]
-        after = after + (given[turn - 2 : turn - 1] if turn >= 2 else [])
-        after = after + (finished[turn - 3 : turn - 2] if turn >= 3 else [])
-        after = after + [have[1] for have in haves[turn + 1 : turn + 2] if turn >= 1]
-        kept, sent = experts_of(step, haves[turn], after)
+        after = [sent] if turn >= 1 else []
+        after += given[turn - 2 : turn - 1] if turn >= 2 else []
+        after += [have[1] for have in haves[turn + 1 : turn + 2]]
+        if step == 0:
+            after += given[turn - 1 : turn] + finished[max(turn - 3, 0) : turn - 1]
+        kept, sent = expert_call(
+            step, row_weights, haves[turn], held_gate_up, held_down, after
+        )
         own, gives = scatter(kept, sent)
         own = own.astype(jnp.bfloat16)
         given.append(gives[0] if gives else own)

time: 95.3 us -> 91.3 us (0.958)
  local copies, waits for them, and re-layouts: 15.3 us -> 12.4 us
  starting transfers between devices: 29 us -> 27.5 us
  waiting for transfers between devices: 26.4 us -> 27.8 us
    unnamed x23 -> x19, local copies, waits for them, and re-layouts: 11.7 us -> 8.91 us
    ppermute x22, waiting for transfers between devices: 11.8 us -> 13.5 us  [local(): lax.ppermute(value, ('kv', 'tp'), [(i, i ^ bit) for i in range(blocks)])]
  transfers between devices with their start and end apart: 32 -> 32, of which waited for: 10 -> 11; matrix products, arithmetic and copies ran while one was open for 3% -> 3% of each run, Pallas kernels for 15% -> 14%
where the time goes in v10:
time: 91.3 us; the launch traced here: 90.9 us
  waiting for transfers between devices  27.8 us (30%)
  starting transfers between devices  27.5 us (30%)
  Pallas kernels  16.8 us (18%)
  local copies, waits for them, and re-layouts  12.4 us (14%)
  other arithmetic  5.42 us (6%)
  between operations  1.01 us (1%)
    ppermute x22, waiting for transfers between devices, local(): lax.ppermute(value, ('kv', 'tp'), [(i, i ^ bit) for i in range(blocks)])  13.5 us
    ppermute x22, starting transfers between devices, local(): lax.ppermute(value, ('kv', 'tp'), [(i, i ^ bit) for i in range(blocks)])  13.3 us
    pallas_call x4, Pallas kernels, expert_call(): pl.pallas_call(lambda *refs: expert_kernel(len(have), step, *refs), out_s...  10.6 us
    unnamed x19, local copies, waits for them, and re-layouts  8.91 us
    ppermute x6, starting transfers between devices, local(): lax.ppermute(value, 'ep', [(i, i ^ step) for i in range(ep_count)])  8.45 us
    ppermute x6, waiting for transfers between devices, local(): lax.ppermute(value, 'ep', [(i, i ^ step) for i in range(ep_count)])  7.76 us
    ppermute x3, waiting for transfers between devices, local(): lax.ppermute(payload, 'ep', [(i, i ^ step) for i in range(ep_count)])  6.53 us
    ppermute x3, starting transfers between devices, local(): lax.ppermute(payload, 'ep', [(i, i ^ step) for i in range(ep_count)])  5.68 us
  transfers between devices with their start and end apart: 32, of which 11 were waited for; matrix products, arithmetic and copies ran while one was open for 3% of the time, Pallas kernels for 14%

profile of v10, /device:TPU:0, one launch (start us, length us, event | category | flops | bytes accessed | tf_op | source)
XLA Modules:
  0.0 90.9 jit_solution(12571654637779955497)
XLA Ops:
  5.5 3.1 %collective-permute-start = (bf16[336,256]{1,0:T(8,128)(2,1)S(1)}, bf16[336,256]{1,0:T(8,128)(2,1)S(1)}, u32[]{:S(2)}, u32[]{:S(2)}) collective-permute-start(bf16[336,256]{1,0:T(8,128)(2,1)S(1)} %pad_maximum_fusion.refs_1_.refs_5_), channel_id=1, source_target_pairs={{0,4},{4,0},{8,12},{12,8},{1,5},{5,1},{9,13},{13,9},{2,6},{6,2},{1... | collective-permute-start | bytes 516104 | tf_op jit(solution)/shard_map/ppermute | solution.py:364
  8.6 2.6 %collective-permute-start.1 = (bf16[336,256]{1,0:T(8,128)(2,1)S(1)}, bf16[336,256]{1,0:T(8,128)(2,1)S(1)}, u32[]{:S(2)}, u32[]{:S(2)}) collective-permute-start(bf16[336,256]{1,0:T(8,128)(2,1)S(1)} %pad_maximum_fusion.refs_1_.refs_5_), channel_id=1, source_target_pairs={{0,8},{4,12},{8,0},{12,4},{1,9},{5,13},{9,1},{13,5},{2,10},{6,14},... | collective-permute-start | bytes 516104 | tf_op jit(solution)/shard_map/ppermute | solution.py:364
  13.1 3.4 %copy-done.1 = bf16[1024,4096]{1,0:T(8,128)(2,1)S(1)} copy-done((bf16[1024,4096]{1,0:T(8,128)(2,1)S(1)}, bf16[1024,4096]{1,0:T(8,128)(2,1)}, u32[]{:S(2)}) %copy-start.1) | copy-done | bytes 8388632
  17.6 6.5 %collective-permute-done.1.refs_7_.refs_3_ = bf16[336,256]{1,0:T(8,128)(2,1)S(1)} collective-permute-done((bf16[336,256]{1,0:T(8,128)(2,1)S(1)}, bf16[336,256]{1,0:T(8,128)(2,1)S(1)}, u32[]{:S(2)}, u32[]{:S(2)}) %collective-permute-start.1) | collective-permute-done | bytes 172064 | tf_op jit(solution)/shard_map/ppermute | solution.py:364
  24.2 3.7 %attend.1 = (f32[32,4096]{1,0:T(8,128)S(1)}, bf16[32,4096]{1,0:T(8,128)(2,1)S(1)}, bf16[128,256]{1,0:T(8,128)(2,1)S(1)}) custom-call(s32[4]{0:T(128)S(1)} %copy-done.5, s32[2]{0:T(128)S(1)} %pad_add_fusion.refs_2_.refs_1_.refs_0_, s32[1]{0:T(128)} %constant.60.clone.1.refs_2_, s32[16]{0:T(128)S(1)} %copy-done.6, bf16[64,1024]{1,0:T(8,128)(2,1)S(1)} %copy-done.4, ...), custom_call_target="tpu_custom_call" | custom-call | flops 872415232 | bytes 8388608 | tf_op jit(solution)/shard_map/attend/pallas_call | solution.py:235
  27.9 1.5 %collective-permute-done.3 = bf16[32,4096]{1,0:T(8,128)(2,1)S(1)} collective-permute-done((bf16[32,4096]{1,0:T(8,128)(2,1)S(1)}, bf16[32,4096]{1,0:T(8,128)(2,1)S(1)}, u32[]{:S(2)}, u32[]{:S(2)}) %collective-permute-start.3) | collective-permute-done | bytes 262176 | tf_op jit(solution)/shard_map/ppermute | solution.py:376
  29.5 1.6 %collective-permute-start.4 = (bf16[16,4096]{1,0:T(8,128)(2,1)S(1)}, bf16[16,4096]{1,0:T(8,128)(2,1)S(1)}, u32[]{:S(2)}, u32[]{:S(2)}) collective-permute-start(bf16[16,4096]{1,0:T(8,128)(2,1)S(1)} %add_convert_fusion.9), channel_id=1, source_target_pairs={{0,2},{1,3},{2,0},{3,1},{4,6},{5,7},{6,4},{7,5},{8,10},{9,11},{10,... | collective-permute-start | bytes 393224 | tf_op jit(solution)/shard_map/ppermute | solution.py:376
  31.1 4.0 %collective-permute-done.4 = bf16[16,4096]{1,0:T(8,128)(2,1)S(1)} collective-permute-done((bf16[16,4096]{1,0:T(8,128)(2,1)S(1)}, bf16[16,4096]{1,0:T(8,128)(2,1)S(1)}, u32[]{:S(2)}, u32[]{:S(2)}) %collective-permute-start.4) | collective-permute-done | bytes 131104 | tf_op jit(solution)/shard_map/ppermute | solution.py:376
  36.3 2.4 %collective-permute-start.5 = (bf16[16,4096]{1,0:T(8,128)(2,1)S(1)}, bf16[16,4096]{1,0:T(8,128)(2,1)S(1)}, u32[]{:S(2)}, u32[]{:S(2)}) collective-permute-start(bf16[16,4096]{1,0:T(8,128)(2,1)S(1)} %fusion.2.refs_7_.refs_1_), channel_id=1, source_target_pairs={{0,12},{4,8},{8,4},{12,0},{1,13},{5,9},{9,5},{13,1},{2,14},{6,10},... | collective-permute-start | bytes 393224 | tf_op jit(solution)/shard_map/ppermute | solution.py:379
  38.8 1.9 %collective-permute-start.6 = (bf16[16,4096]{1,0:T(8,128)(2,1)S(1)}, bf16[16,4096]{1,0:T(8,128)(2,1)S(1)}, u32[]{:S(2)}, u32[]{:S(2)}) collective-permute-start(bf16[16,4096]{1,0:T(8,128)(2,1)S(1)} %fusion.2.refs_7_.refs_1_), channel_id=1, source_target_pairs={{0,8},{4,12},{8,0},{12,4},{1,9},{5,13},{9,1},{13,5},{2,10},{6,14},... | collective-permute-start | bytes 393224 | tf_op jit(solution)/shard_map/ppermute | solution.py:379
  42.3 2.8 %copy-done.2 = bf16[1,2,384,4096]{3,2,1,0:T(8,128)(2,1)S(1)} copy-done((bf16[1,2,384,4096]{3,2,1,0:T(8,128)(2,1)S(1)}, bf16[1,2,384,4096]{3,2,1,0:T(8,128)(2,1)}, u32[]{:S(2)}) %copy-start.2) | copy-done | bytes 6291480
  45.1 1.9 %copy-done.3 = bf16[1,384,4096]{2,1,0:T(8,128)(2,1)S(1)} copy-done((bf16[1,384,4096]{2,1,0:T(8,128)(2,1)S(1)}, bf16[1,384,4096]{2,1,0:T(8,128)(2,1)}, u32[]{:S(2)}) %copy-start.3) | copy-done | bytes 3145752
  48.3 3.0 %collective-permute-done.6.refs_1_ = bf16[16,4096]{1,0:T(8,128)(2,1)S(1)} collective-permute-done((bf16[16,4096]{1,0:T(8,128)(2,1)S(1)}, bf16[16,4096]{1,0:T(8,128)(2,1)S(1)}, u32[]{:S(2)}, u32[]{:S(2)}) %collective-permute-start.6) | collective-permute-done | bytes 131104 | tf_op jit(solution)/shard_map/ppermute | solution.py:379
  51.3 1.6 %collective-permute-start.10 = (bf16[16,4096]{1,0:T(8,128)(2,1)S(1)}, bf16[16,4096]{1,0:T(8,128)(2,1)S(1)}, u32[]{:S(2)}, u32[]{:S(2)}) collective-permute-start(bf16[16,4096]{1,0:T(8,128)(2,1)S(1)} %collective-permute-done.5.refs_1_), channel_id=1, source_target_pairs={{0,2},{1,3},{2,0},{3,1},{4,6},{5,7},{6,4},{7,5},{8,10},{9,11},{10,... | collective-permute-start | bytes 393224 | tf_op jit(solution)/shard_map/ppermute | solution.py:376
  53.4 4.4 %collective-permute-done.10.refs_2_ = bf16[16,4096]{1,0:T(8,128)(2,1)S(1)} collective-permute-done((bf16[16,4096]{1,0:T(8,128)(2,1)S(1)}, bf16[16,4096]{1,0:T(8,128)(2,1)S(1)}, u32[]{:S(2)}, u32[]{:S(2)}) %collective-permute-start.10) | collective-permute-done | bytes 131104 | tf_op jit(solution)/shard_map/ppermute | solution.py:376
  59.8 2.7 %experts.4 = (bf16[32,4096]{1,0:T(8,128)(2,1)S(1)}, bf16[32,4096]{1,0:T(8,128)(2,1)S(1)}) custom-call(f32[256,128]{1,0:T(8,128)S(1)} %get-tuple-element.31.refs_0_, bf16[16,4096]{1,0:T(8,128)(2,1)S(1)} %collective-permute-done.5.refs_1_, bf16[16,4096]{1,0:T(8,128)(2,1)S(1)} %collective-permute-done.10.refs_2_, ...), custom_call_target="tpu_custom_call" | custom-call | flops 1024 | bytes 1024 | tf_op jit(solution)/shard_map/experts/pallas_call | solution.py:292
  64.2 2.7 %experts.5 = (bf16[32,4096]{1,0:T(8,128)(2,1)S(1)}, bf16[32,4096]{1,0:T(8,128)(2,1)S(1)}) custom-call(f32[256,128]{1,0:T(8,128)S(1)} %get-tuple-element.31.refs_0_, bf16[16,4096]{1,0:T(8,128)(2,1)S(1)} %collective-permute-done.6.refs_1_, bf16[16,4096]{1,0:T(8,128)(2,1)S(1)} %collective-permute-done.13.refs_7_.refs_2_, ...), custom_call_target="tpu_custom_call" | custom-call | flops 1024 | bytes 1024 | tf_op jit(solution)/shard_map/experts/pallas_call | solution.py:292
  70.6 2.7 %experts.6 = (bf16[32,4096]{1,0:T(8,128)(2,1)S(1)}, bf16[32,4096]{1,0:T(8,128)(2,1)S(1)}) custom-call(f32[256,128]{1,0:T(8,128)S(1)} %get-tuple-element.31.refs_0_, bf16[16,4096]{1,0:T(8,128)(2,1)S(1)} %collective-permute-done.7.refs_1_, bf16[16,4096]{1,0:T(8,128)(2,1)S(1)} %collective-permute-done.19.refs_8_.refs_2_, ...), custom_call_target="tpu_custom_call" | custom-call | flops 1024 | bytes 1024 | tf_op jit(solution)/shard_map/experts/pallas_call | solution.py:292
  74.9 2.4 %collective-permute-start.16 = (bf16[16,4096]{1,0:T(8,128)(2,1)S(1)}, bf16[16,4096]{1,0:T(8,128)(2,1)S(1)}, u32[]{:S(2)}, u32[]{:S(2)}) collective-permute-start(bf16[16,4096]{1,0:T(8,128)(2,1)S(1)} %add_convert_fusion.6.refs_10_), channel_id=1, source_target_pairs={{0,12},{4,8},{8,4},{12,0},{1,13},{5,9},{9,5},{13,1},{2,14},{6,10},... | collective-permute-start | bytes 393224 | tf_op jit(solution)/shard_map/ppermute | solution.py:379
  77.4 1.5 %collective-permute-start.26 = (bf16[16,4096]{1,0:T(8,128)(2,1)S(1)}, bf16[16,4096]{1,0:T(8,128)(2,1)S(1)}, u32[]{:S(2)}, u32[]{:S(2)}) collective-permute-start(bf16[16,4096]{1,0:T(8,128)(2,1)S(1)} %add_convert_fusion.3.refs_9_), channel_id=1, source_target_pairs={{0,2},{1,3},{2,0},{3,1},{4,6},{5,7},{6,4},{7,5},{8,10},{9,11},{10,... | collective-permute-start | bytes 393224 | tf_op jit(solution)/shard_map/ppermute | solution.py:376
  79.1 2.7 %experts.7 = (bf16[32,4096]{1,0:T(8,128)(2,1)S(1)}, bf16[32,4096]{1,0:T(8,128)(2,1)S(1)}) custom-call(f32[256,128]{1,0:T(8,128)S(1)} %get-tuple-element.31.refs_0_, bf16[16,4096]{1,0:T(8,128)(2,1)S(1)} %fusion.2.refs_7_.refs_1_, bf16[16,4096]{1,0:T(8,128)(2,1)S(1)} %collective-permute-done.8.refs_9_.refs_2_, ...), custom_call_target="tpu_custom_call" | custom-call | flops 1024 | bytes 1024 | tf_op jit(solution)/shard_map/experts/pallas_call | solution.py:292
  82.5 1.5 %collective-permute-start.27 = (bf16[16,4096]{1,0:T(8,128)(2,1)S(1)}, bf16[16,4096]{1,0:T(8,128)(2,1)S(1)}, u32[]{:S(2)}, u32[]{:S(2)}) collective-permute-start(bf16[16,4096]{1,0:T(8,128)(2,1)S(1)} %add_convert_fusion.2), channel_id=1, source_target_pairs={{0,4},{4,0},{8,12},{12,8},{1,5},{5,1},{9,13},{13,9},{2,6},{6,2},{1... | collective-permute-start | bytes 393224 | tf_op jit(solution)/shard_map/ppermute | solution.py:379
  85.4 2.0 %collective-permute-done.22 = bf16[16,4096]{1,0:T(8,128)(2,1)S(1)} collective-permute-done((bf16[16,4096]{1,0:T(8,128)(2,1)S(1)}, bf16[16,4096]{1,0:T(8,128)(2,1)S(1)}, u32[]{:S(2)}, u32[]{:S(2)}) %collective-permute-start.22) | collective-permute-done | bytes 131104 | tf_op jit(solution)/shard_map/ppermute | solution.py:379
  87.4 2.7 %collective-permute-done.27 = bf16[16,4096]{1,0:T(8,128)(2,1)S(1)} collective-permute-done((bf16[16,4096]{1,0:T(8,128)(2,1)S(1)}, bf16[16,4096]{1,0:T(8,128)(2,1)S(1)}, u32[]{:S(2)}, u32[]{:S(2)}) %collective-permute-start.27) | collective-permute-done | bytes 131104 | tf_op jit(solution)/shard_map/ppermute | solution.py:379
  (99 shorter events, 24.8 us)
Async XLA Ops:
  5.5 12.1 %collective-permute-start = (bf16[336,256]{1,0:T(8,128)(2,1)S(1)}, bf16[336,256]{1,0:T(8,128)(2,1)S(1)}, u32[]{:S(2)}, u32[]{:S(2)}) collective-permute-start(bf16[336,256]{1,0:T(8,128)(2,1)S(1)} %pad_maximum_fusion.refs_1_.refs_5_), channel_id=1, source_target_pairs={{0,4},{4,0},{8,12},{12,8},{1,5},{5,1},{9,13},{13,9},{2,6},{6,2},{1... | collective-permute-start | bytes 516104 | tf_op jit(solution)/shard_map/ppermute | solution.py:364
  8.6 15.6 %collective-permute-start.1 = (bf16[336,256]{1,0:T(8,128)(2,1)S(1)}, bf16[336,256]{1,0:T(8,128)(2,1)S(1)}, u32[]{:S(2)}, u32[]{:S(2)}) collective-permute-start(bf16[336,256]{1,0:T(8,128)(2,1)S(1)} %pad_maximum_fusion.refs_1_.refs_5_), channel_id=1, source_target_pairs={{0,8},{4,12},{8,0},{12,4},{1,9},{5,13},{9,1},{13,5},{2,10},{6,14},... | collective-permute-start | bytes 516104 | tf_op jit(solution)/shard_map/ppermute | solution.py:364
  11.2 13.0 %collective-permute-start.2 = (bf16[336,256]{1,0:T(8,128)(2,1)S(1)}, bf16[336,256]{1,0:T(8,128)(2,1)S(1)}, u32[]{:S(2)}, u32[]{:S(2)}) collective-permute-start(bf16[336,256]{1,0:T(8,128)(2,1)S(1)} %pad_maximum_fusion.refs_1_.refs_5_), channel_id=1, source_target_pairs={{0,12},{4,8},{8,4},{12,0},{1,13},{5,9},{9,5},{13,1},{2,14},{6,10},... | collective-permute-start | bytes 516104 | tf_op jit(solution)/shard_map/ppermute | solution.py:364
  29.5 5.6 %collective-permute-start.4 = (bf16[16,4096]{1,0:T(8,128)(2,1)S(1)}, bf16[16,4096]{1,0:T(8,128)(2,1)S(1)}, u32[]{:S(2)}, u32[]{:S(2)}) collective-permute-start(bf16[16,4096]{1,0:T(8,128)(2,1)S(1)} %add_convert_fusion.9), channel_id=1, source_target_pairs={{0,2},{1,3},{2,0},{3,1},{4,6},{5,7},{6,4},{7,5},{8,10},{9,11},{10,... | collective-permute-start | bytes 393224 | tf_op jit(solution)/shard_map/ppermute | solution.py:376
  36.3 12.0 %collective-permute-start.5 = (bf16[16,4096]{1,0:T(8,128)(2,1)S(1)}, bf16[16,4096]{1,0:T(8,128)(2,1)S(1)}, u32[]{:S(2)}, u32[]{:S(2)}) collective-permute-start(bf16[16,4096]{1,0:T(8,128)(2,1)S(1)} %fusion.2.refs_7_.refs_1_), channel_id=1, source_target_pairs={{0,12},{4,8},{8,4},{12,0},{1,13},{5,9},{9,5},{13,1},{2,14},{6,10},... | collective-permute-start | bytes 393224 | tf_op jit(solution)/shard_map/ppermute | solution.py:379
  38.8 12.6 %collective-permute-start.6 = (bf16[16,4096]{1,0:T(8,128)(2,1)S(1)}, bf16[16,4096]{1,0:T(8,128)(2,1)S(1)}, u32[]{:S(2)}, u32[]{:S(2)}) collective-permute-start(bf16[16,4096]{1,0:T(8,128)(2,1)S(1)} %fusion.2.refs_7_.refs_1_), channel_id=1, source_target_pairs={{0,8},{4,12},{8,0},{12,4},{1,9},{5,13},{9,1},{13,5},{2,10},{6,14},... | collective-permute-start | bytes 393224 | tf_op jit(solution)/shard_map/ppermute | solution.py:379
  40.7 10.7 %collective-permute-start.7 = (bf16[16,4096]{1,0:T(8,128)(2,1)S(1)}, bf16[16,4096]{1,0:T(8,128)(2,1)S(1)}, u32[]{:S(2)}, u32[]{:S(2)}) collective-permute-start(bf16[16,4096]{1,0:T(8,128)(2,1)S(1)} %fusion.2.refs_7_.refs_1_), channel_id=1, source_target_pairs={{0,4},{4,0},{8,12},{12,8},{1,5},{5,1},{9,13},{13,9},{2,6},{6,2},{1... | collective-permute-start | bytes 393224 | tf_op jit(solution)/shard_map/ppermute | solution.py:379
  40.8 10.6 %collective-permute-start.8 = (bf16[16,4096]{1,0:T(8,128)(2,1)S(1)}, bf16[16,4096]{1,0:T(8,128)(2,1)S(1)}, u32[]{:S(2)}, u32[]{:S(2)}) collective-permute-start(bf16[16,4096]{1,0:T(8,128)(2,1)S(1)} %fusion.2.refs_7_.refs_1_), channel_id=1, source_target_pairs={{0,2},{1,3},{2,0},{3,1},{4,6},{5,7},{6,4},{7,5},{8,10},{9,11},{10,... | collective-permute-start | bytes 393224 | tf_op jit(solution)/shard_map/ppermute | solution.py:376
  42.3 9.1 %collective-permute-start.9 = (bf16[16,4096]{1,0:T(8,128)(2,1)S(1)}, bf16[16,4096]{1,0:T(8,128)(2,1)S(1)}, u32[]{:S(2)}, u32[]{:S(2)}) collective-permute-start(bf16[16,4096]{1,0:T(8,128)(2,1)S(1)} %fusion.2.refs_7_.refs_1_), channel_id=1, source_target_pairs={{0,1},{1,0},{2,3},{3,2},{4,5},{5,4},{6,7},{7,6},{8,9},{9,8},{10,11... | collective-permute-start | bytes 393224 | tf_op jit(solution)/shard_map/ppermute | solution.py:376
  51.3 6.5 %collective-permute-start.10 = (bf16[16,4096]{1,0:T(8,128)(2,1)S(1)}, bf16[16,4096]{1,0:T(8,128)(2,1)S(1)}, u32[]{:S(2)}, u32[]{:S(2)}) collective-permute-start(bf16[16,4096]{1,0:T(8,128)(2,1)S(1)} %collective-permute-done.5.refs_1_), channel_id=1, source_target_pairs={{0,2},{1,3},{2,0},{3,1},{4,6},{5,7},{6,4},{7,5},{8,10},{9,11},{10,... | collective-permute-start | bytes 393224 | tf_op jit(solution)/shard_map/ppermute | solution.py:376
  52.9 6.9 %collective-permute-start.13 = (bf16[16,4096]{1,0:T(8,128)(2,1)S(1)}, bf16[16,4096]{1,0:T(8,128)(2,1)S(1)}, u32[]{:S(2)}, u32[]{:S(2)}) collective-permute-start(bf16[16,4096]{1,0:T(8,128)(2,1)S(1)} %collective-permute-done.6.refs_1_), channel_id=1, source_target_pairs={{0,2},{1,3},{2,0},{3,1},{4,6},{5,7},{6,4},{7,5},{8,10},{9,11},{10,... | collective-permute-start | bytes 393224 | tf_op jit(solution)/shard_map/ppermute | solution.py:376
  53.4 6.4 %collective-permute-start.11 = (bf16[16,4096]{1,0:T(8,128)(2,1)S(1)}, bf16[16,4096]{1,0:T(8,128)(2,1)S(1)}, u32[]{:S(2)}, u32[]{:S(2)}) collective-permute-start(bf16[16,4096]{1,0:T(8,128)(2,1)S(1)} %collective-permute-done.5.refs_1_), channel_id=1, source_target_pairs={{0,1},{1,0},{2,3},{3,2},{4,5},{5,4},{6,7},{7,6},{8,9},{9,8},{10,11... | collective-permute-start | bytes 393224 | tf_op jit(solution)/shard_map/ppermute | solution.py:376
  57.8 5.4 %collective-permute-start.17 = (bf16[16,4096]{1,0:T(8,128)(2,1)S(1)}, bf16[16,4096]{1,0:T(8,128)(2,1)S(1)}, u32[]{:S(2)}, u32[]{:S(2)}) collective-permute-start(bf16[16,4096]{1,0:T(8,128)(2,1)S(1)} %collective-permute-done.6.refs_1_), channel_id=1, source_target_pairs={{0,1},{1,0},{2,3},{3,2},{4,5},{5,4},{6,7},{7,6},{8,9},{9,8},{10,11... | collective-permute-start | bytes 393224 | tf_op jit(solution)/shard_map/ppermute | solution.py:376
  58.3 5.4 %collective-permute-start.19 = (bf16[16,4096]{1,0:T(8,128)(2,1)S(1)}, bf16[16,4096]{1,0:T(8,128)(2,1)S(1)}, u32[]{:S(2)}, u32[]{:S(2)}) collective-permute-start(bf16[16,4096]{1,0:T(8,128)(2,1)S(1)} %collective-permute-done.7.refs_1_), channel_id=1, source_target_pairs={{0,2},{1,3},{2,0},{3,1},{4,6},{5,7},{6,4},{7,5},{8,10},{9,11},{10,... | collective-permute-start | bytes 393224 | tf_op jit(solution)/shard_map/ppermute | solution.py:376
  63.1 21.5 %collective-permute-start.31 = (bf16[8,16,256]{2,1,0:T(8,128)(2,1)S(1)}, bf16[8,16,256]{2,1,0:T(8,128)(2,1)S(1)}, u32[]{:S(2)}, u32[]{:S(2)}) collective-permute-start(bf16[8,16,256]{2,1,0:T(8,128)(2,1)S(1)} %bitcast.23), channel_id=1, source_target_pairs={{0,1},{1,0},{2,3},{3,2},{4,5},{5,4},{6,7},{7,6},{8,9},{9,8},{10,11... | collective-permute-start | bytes 196616 | tf_op jit(solution)/shard_map/ppermute | solution.py:468
  63.2 6.9 %collective-permute-start.23 = (bf16[16,4096]{1,0:T(8,128)(2,1)S(1)}, bf16[16,4096]{1,0:T(8,128)(2,1)S(1)}, u32[]{:S(2)}, u32[]{:S(2)}) collective-permute-start(bf16[16,4096]{1,0:T(8,128)(2,1)S(1)} %collective-permute-done.7.refs_1_), channel_id=1, source_target_pairs={{0,1},{1,0},{2,3},{3,2},{4,5},{5,4},{6,7},{7,6},{8,9},{9,8},{10,11... | collective-permute-start | bytes 393224 | tf_op jit(solution)/shard_map/ppermute | solution.py:376
  63.7 15.3 %collective-permute-start.28 = (bf16[16,4096]{1,0:T(8,128)(2,1)S(1)}, bf16[16,4096]{1,0:T(8,128)(2,1)S(1)}, u32[]{:S(2)}, u32[]{:S(2)}) collective-permute-start(bf16[16,4096]{1,0:T(8,128)(2,1)S(1)} %collective-permute-done.8.refs_9_.refs_2_), channel_id=1, source_target_pairs={{0,1},{1,0},{2,3},{3,2},{4,5},{5,4},{6,7},{7,6},{8,9},{9,8},{10,11... | collective-permute-start | bytes 393224 | tf_op jit(solution)/shard_map/ppermute | solution.py:376
  63.7 6.9 %collective-permute-start.24 = (bf16[16,4096]{1,0:T(8,128)(2,1)S(1)}, bf16[16,4096]{1,0:T(8,128)(2,1)S(1)}, u32[]{:S(2)}, u32[]{:S(2)}) collective-permute-start(bf16[16,4096]{1,0:T(8,128)(2,1)S(1)} %collective-permute-done.19.refs_8_.refs_2_), channel_id=1, source_target_pairs={{0,1},{1,0},{2,3},{3,2},{4,5},{5,4},{6,7},{7,6},{8,9},{9,8},{10,11... | collective-permute-start | bytes 393224 | tf_op jit(solution)/shard_map/ppermute | solution.py:376
  68.5 6.3 %collective-permute-start.15 = (bf16[16,4096]{1,0:T(8,128)(2,1)S(1)}, bf16[16,4096]{1,0:T(8,128)(2,1)S(1)}, u32[]{:S(2)}, u32[]{:S(2)}) collective-permute-start(bf16[16,4096]{1,0:T(8,128)(2,1)S(1)} %add_convert_fusion.7.refs_8_), channel_id=1, source_target_pairs={{0,2},{1,3},{2,0},{3,1},{4,6},{5,7},{6,4},{7,5},{8,10},{9,11},{10,... | collective-permute-start | bytes 393224 | tf_op jit(solution)/shard_map/ppermute | solution.py:376
  70.0 8.9 %collective-permute-start.21 = (bf16[16,4096]{1,0:T(8,128)(2,1)S(1)}, bf16[16,4096]{1,0:T(8,128)(2,1)S(1)}, u32[]{:S(2)}, u32[]{:S(2)}) collective-permute-start(bf16[16,4096]{1,0:T(8,128)(2,1)S(1)} %add_convert_fusion.5.refs_8_), channel_id=1, source_target_pairs={{0,2},{1,3},{2,0},{3,1},{4,6},{5,7},{6,4},{7,5},{8,10},{9,11},{10,... | collective-permute-start | bytes 393224 | tf_op jit(solution)/shard_map/ppermute | solution.py:376
  74.9 10.5 %collective-permute-start.16 = (bf16[16,4096]{1,0:T(8,128)(2,1)S(1)}, bf16[16,4096]{1,0:T(8,128)(2,1)S(1)}, u32[]{:S(2)}, u32[]{:S(2)}) collective-permute-start(bf16[16,4096]{1,0:T(8,128)(2,1)S(1)} %add_convert_fusion.6.refs_10_), channel_id=1, source_target_pairs={{0,12},{4,8},{8,4},{12,0},{1,13},{5,9},{9,5},{13,1},{2,14},{6,10},... | collective-permute-start | bytes 393224 | tf_op jit(solution)/shard_map/ppermute | solution.py:379
  79.0 8.5 %collective-permute-start.22 = (bf16[16,4096]{1,0:T(8,128)(2,1)S(1)}, bf16[16,4096]{1,0:T(8,128)(2,1)S(1)}, u32[]{:S(2)}, u32[]{:S(2)}) collective-permute-start(bf16[16,4096]{1,0:T(8,128)(2,1)S(1)} %add_convert_fusion.4.refs_11_), channel_id=1, source_target_pairs={{0,8},{4,12},{8,0},{12,4},{1,9},{5,13},{9,1},{13,5},{2,10},{6,14},... | collective-permute-start | bytes 393224 | tf_op jit(solution)/shard_map/ppermute | solution.py:379
  82.5 7.7 %collective-permute-start.27 = (bf16[16,4096]{1,0:T(8,128)(2,1)S(1)}, bf16[16,4096]{1,0:T(8,128)(2,1)S(1)}, u32[]{:S(2)}, u32[]{:S(2)}) collective-permute-start(bf16[16,4096]{1,0:T(8,128)(2,1)S(1)} %add_convert_fusion.2), channel_id=1, source_target_pairs={{0,4},{4,0},{8,12},{12,8},{1,5},{5,1},{9,13},{13,9},{2,6},{6,2},{1... | collective-permute-start | bytes 393224 | tf_op jit(solution)/shard_map/ppermute | solution.py:379
  84.0 6.2 %collective-permute-start.30 = (bf16[16,4096]{1,0:T(8,128)(2,1)S(1)}, bf16[16,4096]{1,0:T(8,128)(2,1)S(1)}, u32[]{:S(2)}, u32[]{:S(2)}) collective-permute-start(bf16[16,4096]{1,0:T(8,128)(2,1)S(1)} %add_convert_fusion.1), channel_id=1, source_target_pairs={{0,2},{1,3},{2,0},{3,1},{4,6},{5,7},{6,4},{7,5},{8,10},{9,11},{10,... | collective-permute-start | bytes 393224 | tf_op jit(solution)/shard_map/ppermute | solution.py:376
  (16 other events, 123.8 us)

commit v11 on v10

--- a/solution.py
+++ b/solution.py
@@ -74,14 +74,7 @@
 
 def prepare_kernel(ep_count, blocks, weight_at, place, *refs):
     payloads = refs[:ep_count]
-    gate_up_from, down_from, _, gate_up, down_weight, row_weights, sem = refs[ep_count:]
-    copies = [
-        pltpu.make_async_copy(gate_up_from, gate_up, sem.at[0]),
-        pltpu.make_async_copy(down_from, down_weight, sem.at[1]),
-    ]
-    for copy in copies:
-        copy.start()
-
+    row_weights = refs[-1]
     tokens = row_weights.shape[0] // ep_count
     row_count = tokens // blocks
     wide = (tokens, payloads[0].shape[1])
@@ -97,26 +90,19 @@
         by_token = jnp.sum(jnp.where(chosen, parts, 0.0), axis=0, keepdims=True)
         column = jnp.sum(jnp.where(here, by_token, 0.0), axis=1, keepdims=True)
         row_weights[step * tokens : (step + 1) * tokens, :] = jnp.broadcast_to(column, (tokens, HD))
-    for copy in copies:
-        copy.wait()
-
-
-def prepare_call(place, arrived, gate_up, down_weight, after, blocks, tokens, weight_at):
+
+
+def prepare_call(place, arrived, after, blocks, tokens, weight_at):
     ep_count = len(arrived)
     return pl.pallas_call(
         lambda *refs: prepare_kernel(ep_count, blocks, weight_at, *refs),
-        out_shape=[
-            jax.ShapeDtypeStruct(gate_up.shape, gate_up.dtype),
-            jax.ShapeDtypeStruct(down_weight.shape, down_weight.dtype),
-            jax.ShapeDtypeStruct((ep_count * tokens, HD), jnp.float32),
-        ],
-        in_specs=[SCALARS] + [WHOLE] * ep_count + [ANYWHERE] * 3,
-        out_specs=[WHOLE] * 3,
-        scratch_shapes=[pltpu.SemaphoreType.DMA((2,))],
+        out_shape=jax.ShapeDtypeStruct((ep_count * tokens, HD), jnp.float32),
+        in_specs=[SCALARS] + [WHOLE] * ep_count + [ANYWHERE],
+        out_specs=WHOLE,
         compiler_params=pltpu.CompilerParams(vmem_limit_bytes=VMEM_LIMIT),
         cost_estimate=EXPERT_COST,
         name="prepare",
-    )(place, *arrived, gate_up, down_weight, after)
+    )(place, *arrived, after)
 
 
 def attend_kernel(ep_count, held, tokens, row_blocks, all_open, lens, place, counts, owners, queries, *refs):
@@ -256,12 +242,20 @@
     )(lens, place, counts, owners, queries, *arrived, out_weight)
 
 
-def expert_kernel(count, step, row_weights, *refs):
+def expert_kernel(count, steps, blocks, row_weights, *refs):
     row_refs = refs[:count]
     gate_up, down_weight = refs[count : count + 2]
     kept_ref, sent_ref = refs[-2:]
-    tokens = 2 * kept_ref.shape[0]
-    row_weight = row_weights[step * tokens : (step + 1) * tokens, :1]
+    tokens = 2 * kept_ref.shape[0] // len(steps)
+    row_count = tokens // blocks
+    row_weight = jnp.concatenate(
+        [
+            row_weights[step * tokens + spot * row_count : step * tokens + (spot + 1) * row_count, :1]
+            for spot in range(blocks)
+            for step in steps
+        ],
+        axis=0,
+    )
     gate_part = up_part = 0.0
     for at in range(0, kept_ref.shape[1], COLUMNS):
         rows = jnp.concatenate([ref[:, at : at + COLUMNS] for ref in row_refs], axis=0)
@@ -282,7 +276,7 @@
         sent_ref[:, at : at + COLUMNS] = out[half:]
 
 
-def expert_call(step, row_weights, have, gate_up, down_weight, after):
+def expert_call(steps, blocks, row_weights, have, gate_up, down_weight, after):
     if have[0].shape[0] % 16:
         have = [jnp.concatenate(have, axis=0)]
     tokens = sum(piece.shape[0] for piece in have)
@@ -290,7 +284,7 @@
     hidden_units = down_weight.shape[1]
     half = jax.ShapeDtypeStruct((tokens // 2, model_width), jnp.bfloat16)
     return pl.pallas_call(
-        lambda *refs: expert_kernel(len(have), step, *refs),
+        lambda *refs: expert_kernel(len(have), steps, blocks, *refs),
         out_shape=(half, half),
         in_specs=[WHOLE] * (len(have) + 3) + [ANYWHERE] * len(after),
         out_specs=(WHOLE, WHOLE),
@@ -397,7 +391,10 @@
     rows_filled = own_slots < span_lengths[ep_index]
     core = jnp.broadcast_to(tp_index.astype(jnp.int32), (1, 1, 2 * HD))
     core, row_mask = lax.optimization_barrier((core, rows_filled.astype(jnp.int32)))
-    held_out, _ = hold_call([out_weight], payload, place, row_mask, core)
+    own_hidden = lax.dynamic_slice_in_dim(hidden_in, block_index * row_count, row_count, 0)
+    held_out, held_gate_up, held_down, _ = hold_call(
+        [out_weight, gate_up, down_weight], payload, place, row_mask, core, own_hidden
+    )
     kept, sent, head_pages = attend_call(
         span_lengths,
         place,
@@ -413,7 +410,6 @@
     )
     head_pages = head_pages.reshape(own_most, page_size, 2 * HD)
     heads_out, _ = scatter(kept, sent)
-    own_hidden = lax.dynamic_slice_in_dim(hidden_in, block_index * row_count, row_count, 0)
     residual = (own_hidden.astype(jnp.float32) + heads_out).astype(jnp.bfloat16)
     resid_wide = residual.astype(jnp.float32)
     normed = (
@@ -422,44 +418,55 @@
         * norm_gain
     ).astype(jnp.bfloat16)
 
-    order = list(range(ep_count - 1, -1, -1))
-
-    def group_rows(piece):
+    def group_rows(piece, before=None):
         have = [piece]
         for bit in bits + [1]:
             have += [exchange(part, bit) for part in have]
+            if before is not None and len(have) == 2:
+                have[1], before = lax.optimization_barrier([have[1], before])
         return have
 
-    held_gate_up, held_down, row_weights = prepare_call(
-        place, arrived, gate_up, down_weight, normed, blocks, tokens, held + tokens
-    )
-    crossed = [across(normed, step) for step in order[:-1]]
+    row_weights = prepare_call(place, arrived, normed, blocks, tokens, held + tokens)
+    ep_bits = [1 << place for place in reversed(range(ep_count.bit_length() - 1))]
     early = [exchange(normed, bit) for bit in bits + [1]]
-    row_weights, *crossed = lax.optimization_barrier([row_weights] + crossed + early)
-    early = crossed[len(order) - 1 :]
+    direct = [across(normed, bit) for bit in ep_bits]
+    row_weights, *tied = lax.optimization_barrier([row_weights] + early + direct)
+    early, direct = tied[: len(early)], dict(zip(ep_bits, tied[len(early) :]))
+    crossed = {0: normed}
+    for bit in ep_bits:
+        for step in list(crossed):
+            crossed[step ^ bit] = across(crossed[step], bit) if step else direct[bit]
     own_have = [normed]
     for bit, piece in zip(bits + [1], early):
         own_have += [piece] + [exchange(part, bit) for part in own_have[1:]]
-    haves = [group_rows(piece) for piece in crossed[: len(order) - 1]] + [own_have]
-    given = []
-    finished = []
-    mixture = resid_wide
-    for turn, step in enumerate(order):
+
+    groups = [[step] for step in [ep_count // 2] + [step for step in reversed(range(1, ep_count)) if step != ep_count // 2] + [0]]
+    sums = {}
+    sent, given, finished = None, [], []
+    for turn, group in enumerate(groups):
         after = [sent] if turn >= 1 else []
         after += given[turn - 2 : turn - 1] if turn >= 2 else []
-        after += [have[1] for have in haves[turn + 1 : turn + 2]]
-        if step == 0:
-            after += given[turn - 1 : turn] + finished[max(turn - 3, 0) : turn - 1]
+        if turn == len(groups) - 1:
+            after += given[turn - 1 :] + finished[: turn - 1]
+        haves = {
+            step: group_rows(crossed[step], sent if turn == 1 else None) if step else own_have
+            for step in group
+        }
+        have = [haves[step][spot] for spot in range(blocks) for step in group]
         kept, sent = expert_call(
-            step, row_weights, haves[turn], held_gate_up, held_down, after
+            tuple(group), blocks, row_weights, have, held_gate_up, held_down, after
         )
         own, gives = scatter(kept, sent)
-        own = own.astype(jnp.bfloat16)
-        given.append(gives[0] if gives else own)
-        finished.append(own)
-        if step > 0:
-            own = across(own, step)
-        mixture = mixture + own.astype(jnp.float32)
+        given.append(gives[0] if gives else own.astype(jnp.bfloat16))
+        finished.append(own.astype(jnp.bfloat16))
+        for spot, step in enumerate(group):
+            sums[step] = own[spot * row_count : (spot + 1) * row_count]
+    for bit in reversed(ep_bits):
+        for step in [step for step in sums if step & bit]:
+            sums[step ^ bit] = sums[step ^ bit] + across(
+                sums.pop(step).astype(jnp.bfloat16), bit
+            ).astype(jnp.float32)
+    mixture = resid_wide + sums[0]
     layer_out = jnp.where(row_mask[:, None] > 0, mixture, 0.0).astype(jnp.bfloat16)
 
     if keyval_local == 1:

time: 91.3 us -> 89.4 us (0.979)
  starting transfers between devices: 27.5 us -> 24.2 us
    ppermute x3, waiting for transfers between devices: 6.53 us -> 1.24 us  [local(): lax.ppermute(payload, 'ep', [(i, i ^ step) for i in range(ep_count)])]
    ppermute x22, waiting for transfers between devices: 13.5 us -> 17.2 us  [local(): lax.ppermute(value, ('kv', 'tp'), [(i, i ^ bit) for i in range(blocks)])]
    ppermute x6, starting transfers between devices: 8.45 us -> 6.23 us  [local(): lax.ppermute(value, 'ep', [(i, i ^ step) for i in range(ep_count)])]
    ppermute x6, waiting for transfers between devices: 7.76 us -> 9.84 us  [local(): lax.ppermute(value, 'ep', [(i, i ^ step) for i in range(ep_count)])]
    ppermute x22, starting transfers between devices: 13.3 us -> 11.8 us  [local(): lax.ppermute(value, ('kv', 'tp'), [(i, i ^ bit) for i in range(blocks)])]
  transfers between devices with their start and end apart: 32 -> 32, of which waited for: 11 -> 17; matrix products, arithmetic and copies ran while one was open for 3% -> 4% of each run, Pallas kernels for 14% -> 15%
where the time goes in v11:
time: 89.4 us; the launch traced here: 89 us
  waiting for transfers between devices  28.3 us (32%)
  starting transfers between devices  24.2 us (27%)
  Pallas kernels  16.7 us (19%)
  local copies, waits for them, and re-layouts  13.3 us (15%)
  other arithmetic  5.41 us (6%)
  between operations  0.97 us (1%)
    ppermute x22, waiting for transfers between devices, local(): lax.ppermute(value, ('kv', 'tp'), [(i, i ^ bit) for i in range(blocks)])  17.2 us
    ppermute x22, starting transfers between devices, local(): lax.ppermute(value, ('kv', 'tp'), [(i, i ^ bit) for i in range(blocks)])  11.8 us
    pallas_call x4, Pallas kernels, expert_call(): pl.pallas_call(lambda *refs: expert_kernel(len(have), steps, blocks, *ref...  10.6 us
    ppermute x6, waiting for transfers between devices, local(): lax.ppermute(value, 'ep', [(i, i ^ step) for i in range(ep_count)])  9.84 us
    unnamed x19, local copies, waits for them, and re-layouts  8.9 us
    ppermute x6, starting transfers between devices, local(): lax.ppermute(value, 'ep', [(i, i ^ step) for i in range(ep_count)])  6.23 us
    ppermute x3, starting transfers between devices, local(): lax.ppermute(payload, 'ep', [(i, i ^ step) for i in range(ep_count)])  5.76 us
    pallas_call x1, Pallas kernels, attend_call(): pl.pallas_call(lambda *refs: attend_kernel(ep_count, held, tokens, blocks...  3.66 us
  transfers between devices with their start and end apart: 32, of which 17 were waited for; matrix products, arithmetic and copies ran while one was open for 4% of the time, Pallas kernels for 15%

profile of v11, /device:TPU:0, one launch (start us, length us, event | category | flops | bytes accessed | tf_op | source)
XLA Modules:
  0.0 89.0 jit_solution(11730047167292291399)
XLA Ops:
  5.5 5.1 %collective-permute-start.2 = (bf16[336,256]{1,0:T(8,128)(2,1)S(1)}, bf16[336,256]{1,0:T(8,128)(2,1)S(1)}, u32[]{:S(2)}, u32[]{:S(2)}) collective-permute-start(bf16[336,256]{1,0:T(8,128)(2,1)S(1)} %pad_maximum_fusion.refs_3_.refs_5_.refs_1_), channel_id=1, source_target_pairs={{0,12},{4,8},{8,4},{12,0},{1,13},{5,9},{9,5},{13,1},{2,14},{6,10},... | collective-permute-start | bytes 516104 | tf_op jit(solution)/shard_map/ppermute | solution.py:358
  14.0 3.4 %copy-done.1 = bf16[1024,4096]{1,0:T(8,128)(2,1)S(1)} copy-done((bf16[1024,4096]{1,0:T(8,128)(2,1)S(1)}, bf16[1024,4096]{1,0:T(8,128)(2,1)}, u32[]{:S(2)}) %copy-start.1) | copy-done | bytes 8388632
  17.4 2.8 %copy-done.2 = bf16[1,2,384,4096]{3,2,1,0:T(8,128)(2,1)S(1)} copy-done((bf16[1,2,384,4096]{3,2,1,0:T(8,128)(2,1)S(1)}, bf16[1,2,384,4096]{3,2,1,0:T(8,128)(2,1)}, u32[]{:S(2)}) %copy-start.2) | copy-done | bytes 6291480
  20.2 1.9 %copy-done.3 = bf16[1,384,4096]{2,1,0:T(8,128)(2,1)S(1)} copy-done((bf16[1,384,4096]{2,1,0:T(8,128)(2,1)S(1)}, bf16[1,384,4096]{2,1,0:T(8,128)(2,1)}, u32[]{:S(2)}) %copy-start.3) | copy-done | bytes 3145752
  22.1 1.8 %hold.1 = (bf16[1024,4096]{1,0:T(8,128)(2,1)S(1)}, bf16[1,2,384,4096]{3,2,1,0:T(8,128)(2,1)S(1)}, bf16[1,384,4096]{2,1,0:T(8,128)(2,1)S(1)}, f32[8,128]{1,0:T(8,128)}) custom-call(bf16[1024,4096]{1,0:T(8,128)(2,1)S(1)} %copy-done.1, bf16[1,2,384,4096]{3,2,1,0:T(8,128)(2,1)S(1)} %copy-done.2, bf16[1,384,4096]{2,1,0:T(8,128)(2,1)S(1)} %copy-done.3, ...), custom_call_target="tpu_custom_call" | custom-call | bytes 35651584 | tf_op jit(solution)/shard_map/hold/pallas_call | solution.py:62
  25.2 3.7 %attend.1 = (f32[32,4096]{1,0:T(8,128)S(1)}, bf16[32,4096]{1,0:T(8,128)(2,1)S(1)}, bf16[128,256]{1,0:T(8,128)(2,1)S(1)}) custom-call(s32[4]{0:T(128)S(1)} %copy-done.5, s32[2]{0:T(128)S(1)} %pad_add_fusion.refs_4_.refs_1_.refs_0_, s32[1]{0:T(128)} %constant.60.clone.1.refs_2_, s32[16]{0:T(128)S(1)} %copy-done.6, bf16[64,1024]{1,0:T(8,128)(2,1)S(1)} %copy-done.4, ...), custom_call_target="tpu_custom_call" | custom-call | flops 872415232 | bytes 8388608 | tf_op jit(solution)/shard_map/attend/pallas_call | solution.py:221
  28.9 1.5 %collective-permute-done.3 = bf16[32,4096]{1,0:T(8,128)(2,1)S(1)} collective-permute-done((bf16[32,4096]{1,0:T(8,128)(2,1)S(1)}, bf16[32,4096]{1,0:T(8,128)(2,1)S(1)}, u32[]{:S(2)}, u32[]{:S(2)}) %collective-permute-start.3) | collective-permute-done | bytes 262176 | tf_op jit(solution)/shard_map/ppermute | solution.py:370
  30.5 1.6 %collective-permute-start.4 = (bf16[16,4096]{1,0:T(8,128)(2,1)S(1)}, bf16[16,4096]{1,0:T(8,128)(2,1)S(1)}, u32[]{:S(2)}, u32[]{:S(2)}) collective-permute-start(bf16[16,4096]{1,0:T(8,128)(2,1)S(1)} %add_convert_fusion.8), channel_id=1, source_target_pairs={{0,2},{1,3},{2,0},{3,1},{4,6},{5,7},{6,4},{7,5},{8,10},{9,11},{10,... | collective-permute-start | bytes 393224 | tf_op jit(solution)/shard_map/ppermute | solution.py:370
  32.0 4.0 %collective-permute-done.4 = bf16[16,4096]{1,0:T(8,128)(2,1)S(1)} collective-permute-done((bf16[16,4096]{1,0:T(8,128)(2,1)S(1)}, bf16[16,4096]{1,0:T(8,128)(2,1)S(1)}, u32[]{:S(2)}, u32[]{:S(2)}) %collective-permute-start.4) | collective-permute-done | bytes 131104 | tf_op jit(solution)/shard_map/ppermute | solution.py:370
  37.6 2.9 %collective-permute-start.7 = (bf16[16,4096]{1,0:T(8,128)(2,1)S(1)}, bf16[16,4096]{1,0:T(8,128)(2,1)S(1)}, u32[]{:S(2)}, u32[]{:S(2)}) collective-permute-start(bf16[16,4096]{1,0:T(8,128)(2,1)S(1)} %fusion.2.refs_5_.refs_1_), channel_id=1, source_target_pairs={{0,8},{4,12},{8,0},{12,4},{1,9},{5,13},{9,1},{13,5},{2,10},{6,14},... | collective-permute-start | bytes 393224 | tf_op jit(solution)/shard_map/ppermute | solution.py:373
  40.5 1.5 %collective-permute-start.5 = (bf16[16,4096]{1,0:T(8,128)(2,1)S(1)}, bf16[16,4096]{1,0:T(8,128)(2,1)S(1)}, u32[]{:S(2)}, u32[]{:S(2)}) collective-permute-start(bf16[16,4096]{1,0:T(8,128)(2,1)S(1)} %fusion.2.refs_5_.refs_1_), channel_id=1, source_target_pairs={{0,2},{1,3},{2,0},{3,1},{4,6},{5,7},{6,4},{7,5},{8,10},{9,11},{10,... | collective-permute-start | bytes 393224 | tf_op jit(solution)/shard_map/ppermute | solution.py:370
  42.6 2.0 %collective-permute-done.8.refs_1_ = bf16[16,4096]{1,0:T(8,128)(2,1)S(1)} collective-permute-done((bf16[16,4096]{1,0:T(8,128)(2,1)S(1)}, bf16[16,4096]{1,0:T(8,128)(2,1)S(1)}, u32[]{:S(2)}, u32[]{:S(2)}) %collective-permute-start.8) | collective-permute-done | bytes 131104 | tf_op jit(solution)/shard_map/ppermute | solution.py:373
  44.6 1.4 %collective-permute-done.7.refs_1_ = bf16[16,4096]{1,0:T(8,128)(2,1)S(1)} collective-permute-done((bf16[16,4096]{1,0:T(8,128)(2,1)S(1)}, bf16[16,4096]{1,0:T(8,128)(2,1)S(1)}, u32[]{:S(2)}, u32[]{:S(2)}) %collective-permute-start.7) | collective-permute-done | bytes 131104 | tf_op jit(solution)/shard_map/ppermute | solution.py:373
  46.4 1.5 %collective-permute-start.15 = (bf16[16,4096]{1,0:T(8,128)(2,1)S(1)}, bf16[16,4096]{1,0:T(8,128)(2,1)S(1)}, u32[]{:S(2)}, u32[]{:S(2)}) collective-permute-start(bf16[16,4096]{1,0:T(8,128)(2,1)S(1)} %collective-permute-done.7.refs_1_), channel_id=1, source_target_pairs={{0,2},{1,3},{2,0},{3,1},{4,6},{5,7},{6,4},{7,5},{8,10},{9,11},{10,... | collective-permute-start | bytes 393224 | tf_op jit(solution)/shard_map/ppermute | solution.py:370
  47.9 3.6 %collective-permute-done.15.refs_2_ = bf16[16,4096]{1,0:T(8,128)(2,1)S(1)} collective-permute-done((bf16[16,4096]{1,0:T(8,128)(2,1)S(1)}, bf16[16,4096]{1,0:T(8,128)(2,1)S(1)}, u32[]{:S(2)}, u32[]{:S(2)}) %collective-permute-start.15) | collective-permute-done | bytes 131104 | tf_op jit(solution)/shard_map/ppermute | solution.py:370
  53.4 2.6 %experts.4 = (bf16[32,4096]{1,0:T(8,128)(2,1)S(1)}, bf16[32,4096]{1,0:T(8,128)(2,1)S(1)}) custom-call(f32[256,128]{1,0:T(8,128)S(1)} %prepare.1.refs_0_, bf16[16,4096]{1,0:T(8,128)(2,1)S(1)} %collective-permute-done.7.refs_1_, bf16[16,4096]{1,0:T(8,128)(2,1)S(1)} %collective-permute-done.15.refs_2_, bf16[16,4096]{1,0:T(8,128)(2,1)S(1)} %collective-permute-done.16.refs_3_, ...), custom_call_target="tpu_custom_call" | custom-call | flops 1024 | bytes 1024 | tf_op jit(solution)/shard_map/experts/pallas_call | solution.py:286
  56.0 1.8 %collective-permute-done.14.refs_2_ = bf16[16,4096]{1,0:T(8,128)(2,1)S(1)} collective-permute-done((bf16[16,4096]{1,0:T(8,128)(2,1)S(1)}, bf16[16,4096]{1,0:T(8,128)(2,1)S(1)}, u32[]{:S(2)}, u32[]{:S(2)}) %collective-permute-start.14) | collective-permute-done | bytes 131104 | tf_op jit(solution)/shard_map/ppermute | solution.py:370
  59.2 2.7 %experts.5 = (bf16[32,4096]{1,0:T(8,128)(2,1)S(1)}, bf16[32,4096]{1,0:T(8,128)(2,1)S(1)}) custom-call(f32[256,128]{1,0:T(8,128)S(1)} %prepare.1.refs_0_, bf16[16,4096]{1,0:T(8,128)(2,1)S(1)} %collective-permute-done.13.refs_1_, bf16[16,4096]{1,0:T(8,128)(2,1)S(1)} %collective-permute-done.14.refs_2_, bf16[16,4096]{1,0:T(8,128)(2,1)S(1)} %collective-permute-done.18.refs_3_, ...), custom_call_target="tpu_custom_call" | custom-call | flops 1024 | bytes 1024 | tf_op jit(solution)/shard_map/experts/pallas_call | solution.py:286
  67.6 2.7 %experts.6 = (bf16[32,4096]{1,0:T(8,128)(2,1)S(1)}, bf16[32,4096]{1,0:T(8,128)(2,1)S(1)}) custom-call(f32[256,128]{1,0:T(8,128)S(1)} %prepare.1.refs_0_, bf16[16,4096]{1,0:T(8,128)(2,1)S(1)} %collective-permute-done.8.refs_1_, bf16[16,4096]{1,0:T(8,128)(2,1)S(1)} %collective-permute-done.10.refs_2_, bf16[16,4096]{1,0:T(8,128)(2,1)S(1)} %collective-permute-done.11.refs_3_, ...), custom_call_target="tpu_custom_call" | custom-call | flops 1024 | bytes 1024 | tf_op jit(solution)/shard_map/experts/pallas_call | solution.py:286
  74.0 2.9 %collective-permute-done.29 = bf16[16,4096]{1,0:T(8,128)(2,1)S(1)} collective-permute-done((bf16[16,4096]{1,0:T(8,128)(2,1)S(1)}, bf16[16,4096]{1,0:T(8,128)(2,1)S(1)}, u32[]{:S(2)}, u32[]{:S(2)}) %collective-permute-start.29) | collective-permute-done | bytes 131104 | tf_op jit(solution)/shard_map/ppermute | solution.py:373
  77.6 2.7 %experts.7 = (bf16[32,4096]{1,0:T(8,128)(2,1)S(1)}, bf16[32,4096]{1,0:T(8,128)(2,1)S(1)}) custom-call(f32[256,128]{1,0:T(8,128)S(1)} %prepare.1.refs_0_, bf16[16,4096]{1,0:T(8,128)(2,1)S(1)} %fusion.2.refs_5_.refs_1_, bf16[16,4096]{1,0:T(8,128)(2,1)S(1)} %collective-permute-done.5.refs_2_, bf16[16,4096]{1,0:T(8,128)(2,1)S(1)} %collective-permute-done.6.refs_3_, ...), custom_call_target="tpu_custom_call" | custom-call | flops 1024 | bytes 1024 | tf_op jit(solution)/shard_map/experts/pallas_call | solution.py:286
  80.4 2.1 %collective-permute-start.28 = (bf16[16,4096]{1,0:T(8,128)(2,1)S(1)}, bf16[16,4096]{1,0:T(8,128)(2,1)S(1)}, u32[]{:S(2)}, u32[]{:S(2)}) collective-permute-start(bf16[16,4096]{1,0:T(8,128)(2,1)S(1)} %add_convert_fusion.1), channel_id=1, source_target_pairs={{0,4},{4,0},{8,12},{12,8},{1,5},{5,1},{9,13},{13,9},{2,6},{6,2},{1... | collective-permute-start | bytes 393224 | tf_op jit(solution)/shard_map/ppermute | solution.py:373
  84.4 2.2 %collective-permute-done.28 = bf16[16,4096]{1,0:T(8,128)(2,1)S(1)} collective-permute-done((bf16[16,4096]{1,0:T(8,128)(2,1)S(1)}, bf16[16,4096]{1,0:T(8,128)(2,1)S(1)}, u32[]{:S(2)}, u32[]{:S(2)}) %collective-permute-start.28) | collective-permute-done | bytes 131104 | tf_op jit(solution)/shard_map/ppermute | solution.py:373
  86.7 1.6 %collective-permute-done.26 = bf16[16,4096]{1,0:T(8,128)(2,1)S(1)} collective-permute-done((bf16[16,4096]{1,0:T(8,128)(2,1)S(1)}, bf16[16,4096]{1,0:T(8,128)(2,1)S(1)}, u32[]{:S(2)}, u32[]{:S(2)}) %collective-permute-start.26) | collective-permute-done | bytes 131104 | tf_op jit(solution)/shard_map/ppermute | solution.py:370
  (100 shorter events, 28.3 us)
Async XLA Ops:
  5.5 18.5 %collective-permute-start.2 = (bf16[336,256]{1,0:T(8,128)(2,1)S(1)}, bf16[336,256]{1,0:T(8,128)(2,1)S(1)}, u32[]{:S(2)}, u32[]{:S(2)}) collective-permute-start(bf16[336,256]{1,0:T(8,128)(2,1)S(1)} %pad_maximum_fusion.refs_3_.refs_5_.refs_1_), channel_id=1, source_target_pairs={{0,12},{4,8},{8,4},{12,0},{1,13},{5,9},{9,5},{13,1},{2,14},{6,10},... | collective-permute-start | bytes 516104 | tf_op jit(solution)/shard_map/ppermute | solution.py:358
  10.6 14.6 %collective-permute-start.1 = (bf16[336,256]{1,0:T(8,128)(2,1)S(1)}, bf16[336,256]{1,0:T(8,128)(2,1)S(1)}, u32[]{:S(2)}, u32[]{:S(2)}) collective-permute-start(bf16[336,256]{1,0:T(8,128)(2,1)S(1)} %pad_maximum_fusion.refs_3_.refs_5_.refs_1_), channel_id=1, source_target_pairs={{0,8},{4,12},{8,0},{12,4},{1,9},{5,13},{9,1},{13,5},{2,10},{6,14},... | collective-permute-start | bytes 516104 | tf_op jit(solution)/shard_map/ppermute | solution.py:358
  10.6 14.6 %collective-permute-start = (bf16[336,256]{1,0:T(8,128)(2,1)S(1)}, bf16[336,256]{1,0:T(8,128)(2,1)S(1)}, u32[]{:S(2)}, u32[]{:S(2)}) collective-permute-start(bf16[336,256]{1,0:T(8,128)(2,1)S(1)} %pad_maximum_fusion.refs_3_.refs_5_.refs_1_), channel_id=1, source_target_pairs={{0,4},{4,0},{8,12},{12,8},{1,5},{5,1},{9,13},{13,9},{2,6},{6,2},{1... | collective-permute-start | bytes 516104 | tf_op jit(solution)/shard_map/ppermute | solution.py:358
  30.5 5.6 %collective-permute-start.4 = (bf16[16,4096]{1,0:T(8,128)(2,1)S(1)}, bf16[16,4096]{1,0:T(8,128)(2,1)S(1)}, u32[]{:S(2)}, u32[]{:S(2)}) collective-permute-start(bf16[16,4096]{1,0:T(8,128)(2,1)S(1)} %add_convert_fusion.8), channel_id=1, source_target_pairs={{0,2},{1,3},{2,0},{3,1},{4,6},{5,7},{6,4},{7,5},{8,10},{9,11},{10,... | collective-permute-start | bytes 393224 | tf_op jit(solution)/shard_map/ppermute | solution.py:370
  37.3 7.3 %collective-permute-start.8 = (bf16[16,4096]{1,0:T(8,128)(2,1)S(1)}, bf16[16,4096]{1,0:T(8,128)(2,1)S(1)}, u32[]{:S(2)}, u32[]{:S(2)}) collective-permute-start(bf16[16,4096]{1,0:T(8,128)(2,1)S(1)} %fusion.2.refs_5_.refs_1_), channel_id=1, source_target_pairs={{0,4},{4,0},{8,12},{12,8},{1,5},{5,1},{9,13},{13,9},{2,6},{6,2},{1... | collective-permute-start | bytes 393224 | tf_op jit(solution)/shard_map/ppermute | solution.py:373
  37.6 8.5 %collective-permute-start.7 = (bf16[16,4096]{1,0:T(8,128)(2,1)S(1)}, bf16[16,4096]{1,0:T(8,128)(2,1)S(1)}, u32[]{:S(2)}, u32[]{:S(2)}) collective-permute-start(bf16[16,4096]{1,0:T(8,128)(2,1)S(1)} %fusion.2.refs_5_.refs_1_), channel_id=1, source_target_pairs={{0,8},{4,12},{8,0},{12,4},{1,9},{5,13},{9,1},{13,5},{2,10},{6,14},... | collective-permute-start | bytes 393224 | tf_op jit(solution)/shard_map/ppermute | solution.py:373
  40.5 5.5 %collective-permute-start.6 = (bf16[16,4096]{1,0:T(8,128)(2,1)S(1)}, bf16[16,4096]{1,0:T(8,128)(2,1)S(1)}, u32[]{:S(2)}, u32[]{:S(2)}) collective-permute-start(bf16[16,4096]{1,0:T(8,128)(2,1)S(1)} %fusion.2.refs_5_.refs_1_), channel_id=1, source_target_pairs={{0,1},{1,0},{2,3},{3,2},{4,5},{5,4},{6,7},{7,6},{8,9},{9,8},{10,11... | collective-permute-start | bytes 393224 | tf_op jit(solution)/shard_map/ppermute | solution.py:370
  40.5 5.9 %collective-permute-start.5 = (bf16[16,4096]{1,0:T(8,128)(2,1)S(1)}, bf16[16,4096]{1,0:T(8,128)(2,1)S(1)}, u32[]{:S(2)}, u32[]{:S(2)}) collective-permute-start(bf16[16,4096]{1,0:T(8,128)(2,1)S(1)} %fusion.2.refs_5_.refs_1_), channel_id=1, source_target_pairs={{0,2},{1,3},{2,0},{3,1},{4,6},{5,7},{6,4},{7,5},{8,10},{9,11},{10,... | collective-permute-start | bytes 393224 | tf_op jit(solution)/shard_map/ppermute | solution.py:370
  46.4 5.1 %collective-permute-start.15 = (bf16[16,4096]{1,0:T(8,128)(2,1)S(1)}, bf16[16,4096]{1,0:T(8,128)(2,1)S(1)}, u32[]{:S(2)}, u32[]{:S(2)}) collective-permute-start(bf16[16,4096]{1,0:T(8,128)(2,1)S(1)} %collective-permute-done.7.refs_1_), channel_id=1, source_target_pairs={{0,2},{1,3},{2,0},{3,1},{4,6},{5,7},{6,4},{7,5},{8,10},{9,11},{10,... | collective-permute-start | bytes 393224 | tf_op jit(solution)/shard_map/ppermute | solution.py:370
  47.9 5.0 %collective-permute-start.13 = (bf16[16,4096]{1,0:T(8,128)(2,1)S(1)}, bf16[16,4096]{1,0:T(8,128)(2,1)S(1)}, u32[]{:S(2)}, u32[]{:S(2)}) collective-permute-start(bf16[16,4096]{1,0:T(8,128)(2,1)S(1)} %collective-permute-done.7.refs_1_), channel_id=1, source_target_pairs={{0,4},{4,0},{8,12},{12,8},{1,5},{5,1},{9,13},{13,9},{2,6},{6,2},{1... | collective-permute-start | bytes 393224 | tf_op jit(solution)/shard_map/ppermute | solution.py:373
  47.9 5.4 %collective-permute-start.16 = (bf16[16,4096]{1,0:T(8,128)(2,1)S(1)}, bf16[16,4096]{1,0:T(8,128)(2,1)S(1)}, u32[]{:S(2)}, u32[]{:S(2)}) collective-permute-start(bf16[16,4096]{1,0:T(8,128)(2,1)S(1)} %collective-permute-done.7.refs_1_), channel_id=1, source_target_pairs={{0,1},{1,0},{2,3},{3,2},{4,5},{5,4},{6,7},{7,6},{8,9},{9,8},{10,11... | collective-permute-start | bytes 393224 | tf_op jit(solution)/shard_map/ppermute | solution.py:370
  52.8 5.0 %collective-permute-start.14 = (bf16[16,4096]{1,0:T(8,128)(2,1)S(1)}, bf16[16,4096]{1,0:T(8,128)(2,1)S(1)}, u32[]{:S(2)}, u32[]{:S(2)}) collective-permute-start(bf16[16,4096]{1,0:T(8,128)(2,1)S(1)} %collective-permute-done.13.refs_1_), channel_id=1, source_target_pairs={{0,2},{1,3},{2,0},{3,1},{4,6},{5,7},{6,4},{7,5},{8,10},{9,11},{10,... | collective-permute-start | bytes 393224 | tf_op jit(solution)/shard_map/ppermute | solution.py:370
  53.4 5.5 %collective-permute-start.18 = (bf16[16,4096]{1,0:T(8,128)(2,1)S(1)}, bf16[16,4096]{1,0:T(8,128)(2,1)S(1)}, u32[]{:S(2)}, u32[]{:S(2)}) collective-permute-start(bf16[16,4096]{1,0:T(8,128)(2,1)S(1)} %collective-permute-done.13.refs_1_), channel_id=1, source_target_pairs={{0,1},{1,0},{2,3},{3,2},{4,5},{5,4},{6,7},{7,6},{8,9},{9,8},{10,11... | collective-permute-start | bytes 393224 | tf_op jit(solution)/shard_map/ppermute | solution.py:370
  57.8 5.9 %collective-permute-start.10 = (bf16[16,4096]{1,0:T(8,128)(2,1)S(1)}, bf16[16,4096]{1,0:T(8,128)(2,1)S(1)}, u32[]{:S(2)}, u32[]{:S(2)}) collective-permute-start(bf16[16,4096]{1,0:T(8,128)(2,1)S(1)} %collective-permute-done.8.refs_1_), channel_id=1, source_target_pairs={{0,2},{1,3},{2,0},{3,1},{4,6},{5,7},{6,4},{7,5},{8,10},{9,11},{10,... | collective-permute-start | bytes 393224 | tf_op jit(solution)/shard_map/ppermute | solution.py:370
  62.1 21.5 %collective-permute-start.31 = (bf16[8,16,256]{2,1,0:T(8,128)(2,1)S(1)}, bf16[8,16,256]{2,1,0:T(8,128)(2,1)S(1)}, u32[]{:S(2)}, u32[]{:S(2)}) collective-permute-start(bf16[8,16,256]{2,1,0:T(8,128)(2,1)S(1)} %bitcast.23), channel_id=1, source_target_pairs={{0,1},{1,0},{2,3},{3,2},{4,5},{5,4},{6,7},{7,6},{8,9},{9,8},{10,11... | collective-permute-start | bytes 196616 | tf_op jit(solution)/shard_map/ppermute | solution.py:475
  62.5 4.1 %collective-permute-start.11 = (bf16[16,4096]{1,0:T(8,128)(2,1)S(1)}, bf16[16,4096]{1,0:T(8,128)(2,1)S(1)}, u32[]{:S(2)}, u32[]{:S(2)}) collective-permute-start(bf16[16,4096]{1,0:T(8,128)(2,1)S(1)} %collective-permute-done.8.refs_1_), channel_id=1, source_target_pairs={{0,1},{1,0},{2,3},{3,2},{4,5},{5,4},{6,7},{7,6},{8,9},{9,8},{10,11... | collective-permute-start | bytes 393224 | tf_op jit(solution)/shard_map/ppermute | solution.py:370
  62.6 15.0 %collective-permute-start.9 = (bf16[16,4096]{1,0:T(8,128)(2,1)S(1)}, bf16[16,4096]{1,0:T(8,128)(2,1)S(1)}, u32[]{:S(2)}, u32[]{:S(2)}) collective-permute-start(bf16[16,4096]{1,0:T(8,128)(2,1)S(1)} %collective-permute-done.5.refs_2_), channel_id=1, source_target_pairs={{0,1},{1,0},{2,3},{3,2},{4,5},{5,4},{6,7},{7,6},{8,9},{9,8},{10,11... | collective-permute-start | bytes 393224 | tf_op jit(solution)/shard_map/ppermute | solution.py:370
  65.4 6.3 %collective-permute-start.24 = (bf16[16,4096]{1,0:T(8,128)(2,1)S(1)}, bf16[16,4096]{1,0:T(8,128)(2,1)S(1)}, u32[]{:S(2)}, u32[]{:S(2)}) collective-permute-start(bf16[16,4096]{1,0:T(8,128)(2,1)S(1)} %add_convert_fusion.5.refs_8_), channel_id=1, source_target_pairs={{0,2},{1,3},{2,0},{3,1},{4,6},{5,7},{6,4},{7,5},{8,10},{9,11},{10,... | collective-permute-start | bytes 393224 | tf_op jit(solution)/shard_map/ppermute | solution.py:370
  66.6 7.4 %collective-permute-start.23 = (bf16[16,4096]{1,0:T(8,128)(2,1)S(1)}, bf16[16,4096]{1,0:T(8,128)(2,1)S(1)}, u32[]{:S(2)}, u32[]{:S(2)}) collective-permute-start(bf16[16,4096]{1,0:T(8,128)(2,1)S(1)} %add_convert_fusion.6.refs_8_), channel_id=1, source_target_pairs={{0,2},{1,3},{2,0},{3,1},{4,6},{5,7},{6,4},{7,5},{8,10},{9,11},{10,... | collective-permute-start | bytes 393224 | tf_op jit(solution)/shard_map/ppermute | solution.py:370
  71.8 5.0 %collective-permute-start.29 = (bf16[16,4096]{1,0:T(8,128)(2,1)S(1)}, bf16[16,4096]{1,0:T(8,128)(2,1)S(1)}, u32[]{:S(2)}, u32[]{:S(2)}) collective-permute-start(bf16[16,4096]{1,0:T(8,128)(2,1)S(1)} %add_convert_fusion.3.refs_11_), channel_id=1, source_target_pairs={{0,4},{4,0},{8,12},{12,8},{1,5},{5,1},{9,13},{13,9},{2,6},{6,2},{1... | collective-permute-start | bytes 393224 | tf_op jit(solution)/shard_map/ppermute | solution.py:373
  72.1 8.3 %collective-permute-start.27 = (bf16[16,4096]{1,0:T(8,128)(2,1)S(1)}, bf16[16,4096]{1,0:T(8,128)(2,1)S(1)}, u32[]{:S(2)}, u32[]{:S(2)}) collective-permute-start(bf16[16,4096]{1,0:T(8,128)(2,1)S(1)} %add_convert_fusion.4.refs_9_), channel_id=1, source_target_pairs={{0,2},{1,3},{2,0},{3,1},{4,6},{5,7},{6,4},{7,5},{8,10},{9,11},{10,... | collective-permute-start | bytes 393224 | tf_op jit(solution)/shard_map/ppermute | solution.py:370
  76.9 7.5 %collective-permute-start.30 = (bf16[16,4096]{1,0:T(8,128)(2,1)S(1)}, bf16[16,4096]{1,0:T(8,128)(2,1)S(1)}, u32[]{:S(2)}, u32[]{:S(2)}) collective-permute-start(bf16[16,4096]{1,0:T(8,128)(2,1)S(1)} %get-tuple-element.55), channel_id=1, source_target_pairs={{0,8},{4,12},{8,0},{12,4},{1,9},{5,13},{9,1},{13,5},{2,10},{6,14},... | collective-permute-start | bytes 393224 | tf_op jit(solution)/shard_map/ppermute | solution.py:373
  80.4 6.2 %collective-permute-start.28 = (bf16[16,4096]{1,0:T(8,128)(2,1)S(1)}, bf16[16,4096]{1,0:T(8,128)(2,1)S(1)}, u32[]{:S(2)}, u32[]{:S(2)}) collective-permute-start(bf16[16,4096]{1,0:T(8,128)(2,1)S(1)} %add_convert_fusion.1), channel_id=1, source_target_pairs={{0,4},{4,0},{8,12},{12,8},{1,5},{5,1},{9,13},{13,9},{2,6},{6,2},{1... | collective-permute-start | bytes 393224 | tf_op jit(solution)/shard_map/ppermute | solution.py:373
  82.6 5.7 %collective-permute-start.26 = (bf16[16,4096]{1,0:T(8,128)(2,1)S(1)}, bf16[16,4096]{1,0:T(8,128)(2,1)S(1)}, u32[]{:S(2)}, u32[]{:S(2)}) collective-permute-start(bf16[16,4096]{1,0:T(8,128)(2,1)S(1)} %add_convert_fusion.2), channel_id=1, source_target_pairs={{0,2},{1,3},{2,0},{3,1},{4,6},{5,7},{6,4},{7,5},{8,10},{9,11},{10,... | collective-permute-start | bytes 393224 | tf_op jit(solution)/shard_map/ppermute | solution.py:370
  (16 other events, 50.3 us)

commit v12 on v11

--- a/solution.py
+++ b/solution.py
@@ -375,16 +375,19 @@
     )
     bits = [1 << place for place in range(1, blocks.bit_length() - 1)]
 
-    def scatter(kept, sent):
+    def scatter(kept, sent, before=None):
         got = exchange(sent, 1)
         gives = []
         for bit in reversed(bits):
             half = kept.shape[0] // 2
             give = kept[half:].astype(jnp.float32) + got[half:].astype(jnp.float32)
-            gives.append(give.astype(jnp.bfloat16))
+            give = give.astype(jnp.bfloat16)
+            if before is not None and not gives:
+                give, before = lax.optimization_barrier((give, before))
+            gives.append(give)
             kept = kept[:half].astype(jnp.float32) + got[:half].astype(jnp.float32)
-            got = exchange(gives[-1], bit)
-        return kept.astype(jnp.float32) + got.astype(jnp.float32), gives
+            got = exchange(give, bit)
+        return kept.astype(jnp.float32) + got.astype(jnp.float32), gives, got
 
     own_most = 2 * (tokens // page_size)
     own_slots = block_index * row_count + jnp.arange(row_count, dtype=jnp.int32)
@@ -409,7 +412,7 @@
         all_open,
     )
     head_pages = head_pages.reshape(own_most, page_size, 2 * HD)
-    heads_out, _ = scatter(kept, sent)
+    heads_out, _, _ = scatter(kept, sent)
     residual = (own_hidden.astype(jnp.float32) + heads_out).astype(jnp.bfloat16)
     resid_wide = residual.astype(jnp.float32)
     normed = (
@@ -418,13 +421,16 @@
         * norm_gain
     ).astype(jnp.bfloat16)
 
-    def group_rows(piece, before=None):
-        have = [piece]
-        for bit in bits + [1]:
-            have += [exchange(part, bit) for part in have]
-            if before is not None and len(have) == 2:
-                have[1], before = lax.optimization_barrier([have[1], before])
+    def group_rows(have, bits):
+        for bit in bits:
+            have = have + [exchange(part, bit) for part in have]
         return have
+
+    def experts(group, haves, after):
+        have = [haves[step][spot] for spot in range(blocks) for step in group]
+        return expert_call(
+            tuple(group), blocks, row_weights, have, held_gate_up, held_down, after
+        )
 
     row_weights = prepare_call(place, arrived, normed, blocks, tokens, held + tokens)
     ep_bits = [1 << place for place in reversed(range(ep_count.bit_length() - 1))]
@@ -432,35 +438,36 @@
     direct = [across(normed, bit) for bit in ep_bits]
     row_weights, *tied = lax.optimization_barrier([row_weights] + early + direct)
     early, direct = tied[: len(early)], dict(zip(ep_bits, tied[len(early) :]))
+
+    own_have = [normed]
+    for bit, piece in zip(bits + [1], early):
+        own_have += [piece] + [exchange(part, bit) for part in own_have[1:]]
+    kept, sent = experts([0], {0: own_have}, [])
     crossed = {0: normed}
     for bit in ep_bits:
         for step in list(crossed):
             crossed[step ^ bit] = across(crossed[step], bit) if step else direct[bit]
-    own_have = [normed]
-    for bit, piece in zip(bits + [1], early):
-        own_have += [piece] + [exchange(part, bit) for part in own_have[1:]]
-
-    groups = [[step] for step in [ep_count // 2] + [step for step in reversed(range(1, ep_count)) if step != ep_count // 2] + [0]]
+    forwarded = [step for step in crossed if step & (step - 1)]
+    leading = ep_bits[0]
+    halves = [group_rows([direct[bit]], bits[:1]) for bit in ep_bits]
+    sent, halves, ahead = lax.optimization_barrier(
+        (sent, halves, [crossed[step] for step in forwarded])
+    )
+    haves = {bit: group_rows(half, bits[1:] + [1]) for bit, half in zip(ep_bits, halves)}
+    haves.update({step: group_rows([piece], bits + [1]) for step, piece in zip(forwarded, ahead)})
+
+    order = [0, leading] + [step for step in reversed(range(1, ep_count)) if step != leading]
     sums = {}
-    sent, given, finished = None, [], []
-    for turn, group in enumerate(groups):
-        after = [sent] if turn >= 1 else []
-        after += given[turn - 2 : turn - 1] if turn >= 2 else []
-        if turn == len(groups) - 1:
-            after += given[turn - 1 :] + finished[: turn - 1]
-        haves = {
-            step: group_rows(crossed[step], sent if turn == 1 else None) if step else own_have
-            for step in group
-        }
-        have = [haves[step][spot] for spot in range(blocks) for step in group]
-        kept, sent = expert_call(
-            tuple(group), blocks, row_weights, have, held_gate_up, held_down, after
-        )
-        own, gives = scatter(kept, sent)
-        given.append(gives[0] if gives else own.astype(jnp.bfloat16))
-        finished.append(own.astype(jnp.bfloat16))
-        for spot, step in enumerate(group):
-            sums[step] = own[spot * row_count : (spot + 1) * row_count]
+    given, finished = [], []
+    for turn, step in enumerate(order):
+        if turn >= 1:
+            after = [sent]
+            after += given[:2] if turn == 2 else []
+            kept, sent = experts([step], haves, after)
+        last = turn >= 3 and turn == len(order) - 1
+        sums[step], gives, received = scatter(kept, sent, received if last else None)
+        finished.append(sums[step].astype(jnp.bfloat16))
+        given.append(gives[0] if gives else finished[-1])
     for bit in reversed(ep_bits):
         for step in [step for step in sums if step & bit]:
             sums[step ^ bit] = sums[step ^ bit] + across(

time: 89.4 us -> 93.5 us (1.046)
  waiting for transfers between devices: 28.3 us -> 31.5 us
    ppermute x22, waiting for transfers between devices: 17.2 us -> 19.4 us  [local(): lax.ppermute(value, ('kv', 'tp'), [(i, i ^ bit) for i in range(blocks)])]
    ppermute x22, starting transfers between devices: 11.8 us -> 13.8 us  [local(): lax.ppermute(value, ('kv', 'tp'), [(i, i ^ bit) for i in range(blocks)])]
    ppermute x6, starting transfers between devices: 6.23 us -> 5.12 us  [local(): lax.ppermute(value, 'ep', [(i, i ^ step) for i in range(ep_count)])]
    ppermute x6, waiting for transfers between devices: 9.84 us -> 10.9 us  [local(): lax.ppermute(value, 'ep', [(i, i ^ step) for i in range(ep_count)])]
  transfers between devices with their start and end apart: 32 -> 32, of which waited for: 17 -> 17; matrix products, arithmetic and copies ran while one was open for 4% -> 4% of each run, Pallas kernels for 15% -> 14%
where the time goes in v12:
time: 93.5 us; the launch traced here: 93.1 us
  waiting for transfers between devices  31.5 us (34%)
  starting transfers between devices  25.1 us (27%)
  Pallas kernels  16.7 us (18%)
  local copies, waits for them, and re-layouts  13.4 us (14%)
  other arithmetic  5.47 us (6%)
  between operations  0.95 us (1%)
    ppermute x22, waiting for transfers between devices, local(): lax.ppermute(value, ('kv', 'tp'), [(i, i ^ bit) for i in range(blocks)])  19.4 us
    ppermute x22, starting transfers between devices, local(): lax.ppermute(value, ('kv', 'tp'), [(i, i ^ bit) for i in range(blocks)])  13.8 us
    ppermute x6, waiting for transfers between devices, local(): lax.ppermute(value, 'ep', [(i, i ^ step) for i in range(ep_count)])  10.9 us
    pallas_call x4, Pallas kernels, expert_call(): pl.pallas_call(lambda *refs: expert_kernel(len(have), steps, blocks, *ref...  10.6 us
    unnamed x19, local copies, waits for them, and re-layouts  8.9 us
    ppermute x3, starting transfers between devices, local(): lax.ppermute(payload, 'ep', [(i, i ^ step) for i in range(ep_count)])  5.76 us
    ppermute x6, starting transfers between devices, local(): lax.ppermute(value, 'ep', [(i, i ^ step) for i in range(ep_count)])  5.12 us
    pallas_call x1, Pallas kernels, attend_call(): pl.pallas_call(lambda *refs: attend_kernel(ep_count, held, tokens, blocks...  3.66 us
  transfers between devices with their start and end apart: 32, of which 17 were waited for; matrix products, arithmetic and copies ran while one was open for 4% of the time, Pallas kernels for 14%

profile of v12, /device:TPU:0, one launch (start us, length us, event | category | flops | bytes accessed | tf_op | source)
XLA Modules:
  0.0 93.1 jit_solution(9945544992139909602)
XLA Ops:
  5.5 5.1 %collective-permute-start.2 = (bf16[336,256]{1,0:T(8,128)(2,1)S(1)}, bf16[336,256]{1,0:T(8,128)(2,1)S(1)}, u32[]{:S(2)}, u32[]{:S(2)}) collective-permute-start(bf16[336,256]{1,0:T(8,128)(2,1)S(1)} %pad_maximum_fusion.refs_3_.refs_5_.refs_1_), channel_id=1, source_target_pairs={{0,12},{4,8},{8,4},{12,0},{1,13},{5,9},{9,5},{13,1},{2,14},{6,10},... | collective-permute-start | bytes 516104 | tf_op jit(solution)/shard_map/ppermute | solution.py:358
  14.1 3.4 %copy-done.1 = bf16[1024,4096]{1,0:T(8,128)(2,1)S(1)} copy-done((bf16[1024,4096]{1,0:T(8,128)(2,1)S(1)}, bf16[1024,4096]{1,0:T(8,128)(2,1)}, u32[]{:S(2)}) %copy-start.1) | copy-done | bytes 8388632
  17.5 2.8 %copy-done.2 = bf16[1,2,384,4096]{3,2,1,0:T(8,128)(2,1)S(1)} copy-done((bf16[1,2,384,4096]{3,2,1,0:T(8,128)(2,1)S(1)}, bf16[1,2,384,4096]{3,2,1,0:T(8,128)(2,1)}, u32[]{:S(2)}) %copy-start.2) | copy-done | bytes 6291480
  20.3 1.9 %copy-done.3 = bf16[1,384,4096]{2,1,0:T(8,128)(2,1)S(1)} copy-done((bf16[1,384,4096]{2,1,0:T(8,128)(2,1)S(1)}, bf16[1,384,4096]{2,1,0:T(8,128)(2,1)}, u32[]{:S(2)}) %copy-start.3) | copy-done | bytes 3145752
  22.2 1.8 %hold.1 = (bf16[1024,4096]{1,0:T(8,128)(2,1)S(1)}, bf16[1,2,384,4096]{3,2,1,0:T(8,128)(2,1)S(1)}, bf16[1,384,4096]{2,1,0:T(8,128)(2,1)S(1)}, f32[8,128]{1,0:T(8,128)}) custom-call(bf16[1024,4096]{1,0:T(8,128)(2,1)S(1)} %copy-done.1, bf16[1,2,384,4096]{3,2,1,0:T(8,128)(2,1)S(1)} %copy-done.2, bf16[1,384,4096]{2,1,0:T(8,128)(2,1)S(1)} %copy-done.3, ...), custom_call_target="tpu_custom_call" | custom-call | bytes 35651584 | tf_op jit(solution)/shard_map/hold/pallas_call | solution.py:62
  25.2 3.7 %attend.1 = (f32[32,4096]{1,0:T(8,128)S(1)}, bf16[32,4096]{1,0:T(8,128)(2,1)S(1)}, bf16[128,256]{1,0:T(8,128)(2,1)S(1)}) custom-call(s32[4]{0:T(128)S(1)} %copy-done.5, s32[2]{0:T(128)S(1)} %pad_add_fusion.refs_4_.refs_1_.refs_0_, s32[1]{0:T(128)} %constant.60.clone.1.refs_2_, s32[16]{0:T(128)S(1)} %copy-done.6, bf16[64,1024]{1,0:T(8,128)(2,1)S(1)} %copy-done.4, ...), custom_call_target="tpu_custom_call" | custom-call | flops 872415232 | bytes 8388608 | tf_op jit(solution)/shard_map/attend/pallas_call | solution.py:221
  28.9 1.5 %collective-permute-done.3 = bf16[32,4096]{1,0:T(8,128)(2,1)S(1)} collective-permute-done((bf16[32,4096]{1,0:T(8,128)(2,1)S(1)}, bf16[32,4096]{1,0:T(8,128)(2,1)S(1)}, u32[]{:S(2)}, u32[]{:S(2)}) %collective-permute-start.3) | collective-permute-done | bytes 262176 | tf_op jit(solution)/shard_map/ppermute | solution.py:370
  30.5 1.6 %collective-permute-start.4 = (bf16[16,4096]{1,0:T(8,128)(2,1)S(1)}, bf16[16,4096]{1,0:T(8,128)(2,1)S(1)}, u32[]{:S(2)}, u32[]{:S(2)}) collective-permute-start(bf16[16,4096]{1,0:T(8,128)(2,1)S(1)} %add_convert_fusion.8), channel_id=1, source_target_pairs={{0,2},{1,3},{2,0},{3,1},{4,6},{5,7},{6,4},{7,5},{8,10},{9,11},{10,... | collective-permute-start | bytes 393224 | tf_op jit(solution)/shard_map/ppermute | solution.py:370
  32.1 4.0 %collective-permute-done.4 = bf16[16,4096]{1,0:T(8,128)(2,1)S(1)} collective-permute-done((bf16[16,4096]{1,0:T(8,128)(2,1)S(1)}, bf16[16,4096]{1,0:T(8,128)(2,1)S(1)}, u32[]{:S(2)}, u32[]{:S(2)}) %collective-permute-start.4) | collective-permute-done | bytes 131104 | tf_op jit(solution)/shard_map/ppermute | solution.py:370
  37.7 2.9 %collective-permute-start.7 = (bf16[16,4096]{1,0:T(8,128)(2,1)S(1)}, bf16[16,4096]{1,0:T(8,128)(2,1)S(1)}, u32[]{:S(2)}, u32[]{:S(2)}) collective-permute-start(bf16[16,4096]{1,0:T(8,128)(2,1)S(1)} %fusion.2.refs_5_.refs_1_), channel_id=1, source_target_pairs={{0,8},{4,12},{8,0},{12,4},{1,9},{5,13},{9,1},{13,5},{2,10},{6,14},... | collective-permute-start | bytes 393224 | tf_op jit(solution)/shard_map/ppermute | solution.py:373
  42.7 1.9 %collective-permute-done.8.refs_1_ = bf16[16,4096]{1,0:T(8,128)(2,1)S(1)} collective-permute-done((bf16[16,4096]{1,0:T(8,128)(2,1)S(1)}, bf16[16,4096]{1,0:T(8,128)(2,1)S(1)}, u32[]{:S(2)}, u32[]{:S(2)}) %collective-permute-start.8) | collective-permute-done | bytes 131104 | tf_op jit(solution)/shard_map/ppermute | solution.py:373
  44.6 1.5 %collective-permute-done.7.refs_1_ = bf16[16,4096]{1,0:T(8,128)(2,1)S(1)} collective-permute-done((bf16[16,4096]{1,0:T(8,128)(2,1)S(1)}, bf16[16,4096]{1,0:T(8,128)(2,1)S(1)}, u32[]{:S(2)}, u32[]{:S(2)}) %collective-permute-start.7) | collective-permute-done | bytes 131104 | tf_op jit(solution)/shard_map/ppermute | solution.py:373
  48.6 2.7 %experts.4 = (bf16[32,4096]{1,0:T(8,128)(2,1)S(1)}, bf16[32,4096]{1,0:T(8,128)(2,1)S(1)}) custom-call(f32[256,128]{1,0:T(8,128)S(1)} %prepare.1.refs_0_, bf16[16,4096]{1,0:T(8,128)(2,1)S(1)} %fusion.2.refs_5_.refs_1_, bf16[16,4096]{1,0:T(8,128)(2,1)S(1)} %collective-permute-done.5.refs_2_, bf16[16,4096]{1,0:T(8,128)(2,1)S(1)} %collective-permute-done.6.refs_3_, ...), custom_call_target="tpu_custom_call" | custom-call | flops 1024 | bytes 1024 | tf_op jit(solution)/shard_map/experts/pallas_call | solution.py:286
  51.3 1.5 %collective-permute-done.11.refs_2_ = bf16[16,4096]{1,0:T(8,128)(2,1)S(1)} collective-permute-done((bf16[16,4096]{1,0:T(8,128)(2,1)S(1)}, bf16[16,4096]{1,0:T(8,128)(2,1)S(1)}, u32[]{:S(2)}, u32[]{:S(2)}) %collective-permute-start.11) | collective-permute-done | bytes 131104 | tf_op jit(solution)/shard_map/ppermute | solution.py:370
  53.6 1.6 %collective-permute-done.10.refs_2_ = bf16[16,4096]{1,0:T(8,128)(2,1)S(1)} collective-permute-done((bf16[16,4096]{1,0:T(8,128)(2,1)S(1)}, bf16[16,4096]{1,0:T(8,128)(2,1)S(1)}, u32[]{:S(2)}, u32[]{:S(2)}) %collective-permute-start.10) | collective-permute-done | bytes 131104 | tf_op jit(solution)/shard_map/ppermute | solution.py:370
  58.0 2.6 %experts.5 = (bf16[32,4096]{1,0:T(8,128)(2,1)S(1)}, bf16[32,4096]{1,0:T(8,128)(2,1)S(1)}) custom-call(f32[256,128]{1,0:T(8,128)S(1)} %prepare.1.refs_0_, bf16[16,4096]{1,0:T(8,128)(2,1)S(1)} %collective-permute-done.7.refs_1_, bf16[16,4096]{1,0:T(8,128)(2,1)S(1)} %collective-permute-done.10.refs_2_, bf16[16,4096]{1,0:T(8,128)(2,1)S(1)} %collective-permute-done.20.refs_3_, ...), custom_call_target="tpu_custom_call" | custom-call | flops 1024 | bytes 1024 | tf_op jit(solution)/shard_map/experts/pallas_call | solution.py:286
  63.3 2.7 %experts.6 = (bf16[32,4096]{1,0:T(8,128)(2,1)S(1)}, bf16[32,4096]{1,0:T(8,128)(2,1)S(1)}) custom-call(f32[256,128]{1,0:T(8,128)S(1)} %prepare.1.refs_0_, bf16[16,4096]{1,0:T(8,128)(2,1)S(1)} %collective-permute-done.12.refs_1_, bf16[16,4096]{1,0:T(8,128)(2,1)S(1)} %collective-permute-done.17.refs_2_, bf16[16,4096]{1,0:T(8,128)(2,1)S(1)} %collective-permute-done.18.refs_3_, ...), custom_call_target="tpu_custom_call" | custom-call | flops 1024 | bytes 1024 | tf_op jit(solution)/shard_map/experts/pallas_call | solution.py:286
  66.7 1.5 %collective-permute-start.14 = (bf16[16,4096]{1,0:T(8,128)(2,1)S(1)}, bf16[16,4096]{1,0:T(8,128)(2,1)S(1)}, u32[]{:S(2)}, u32[]{:S(2)}) collective-permute-start(bf16[16,4096]{1,0:T(8,128)(2,1)S(1)} %add_convert_fusion.6.refs_8_), channel_id=1, source_target_pairs={{0,2},{1,3},{2,0},{3,1},{4,6},{5,7},{6,4},{7,5},{8,10},{9,11},{10,... | collective-permute-start | bytes 393224 | tf_op jit(solution)/shard_map/ppermute | solution.py:370
  68.7 2.7 %experts.7 = (bf16[32,4096]{1,0:T(8,128)(2,1)S(1)}, bf16[32,4096]{1,0:T(8,128)(2,1)S(1)}) custom-call(f32[256,128]{1,0:T(8,128)S(1)} %prepare.1.refs_0_, bf16[16,4096]{1,0:T(8,128)(2,1)S(1)} %collective-permute-done.8.refs_1_, bf16[16,4096]{1,0:T(8,128)(2,1)S(1)} %collective-permute-done.11.refs_2_, bf16[16,4096]{1,0:T(8,128)(2,1)S(1)} %collective-permute-done.15.refs_3_, ...), custom_call_target="tpu_custom_call" | custom-call | flops 1024 | bytes 1024 | tf_op jit(solution)/shard_map/experts/pallas_call | solution.py:286
  71.5 1.6 %collective-permute-start.25 = (bf16[16,4096]{1,0:T(8,128)(2,1)S(1)}, bf16[16,4096]{1,0:T(8,128)(2,1)S(1)}, u32[]{:S(2)}, u32[]{:S(2)}) collective-permute-start(bf16[16,4096]{1,0:T(8,128)(2,1)S(1)} %add_convert_fusion.3), channel_id=1, source_target_pairs={{0,2},{1,3},{2,0},{3,1},{4,6},{5,7},{6,4},{7,5},{8,10},{9,11},{10,... | collective-permute-start | bytes 393224 | tf_op jit(solution)/shard_map/ppermute | solution.py:370
  73.1 4.7 %collective-permute-done.25 = bf16[16,4096]{1,0:T(8,128)(2,1)S(1)} collective-permute-done((bf16[16,4096]{1,0:T(8,128)(2,1)S(1)}, bf16[16,4096]{1,0:T(8,128)(2,1)S(1)}, u32[]{:S(2)}, u32[]{:S(2)}) %collective-permute-start.25) | collective-permute-done | bytes 131104 | tf_op jit(solution)/shard_map/ppermute | solution.py:370
  79.5 3.5 %collective-permute-done.26 = bf16[16,4096]{1,0:T(8,128)(2,1)S(1)} collective-permute-done((bf16[16,4096]{1,0:T(8,128)(2,1)S(1)}, bf16[16,4096]{1,0:T(8,128)(2,1)S(1)}, u32[]{:S(2)}, u32[]{:S(2)}) %collective-permute-start.26) | collective-permute-done | bytes 131104 | tf_op jit(solution)/shard_map/ppermute | solution.py:370
  86.8 2.9 %collective-permute-done.27 = bf16[16,4096]{1,0:T(8,128)(2,1)S(1)} collective-permute-done((bf16[16,4096]{1,0:T(8,128)(2,1)S(1)}, bf16[16,4096]{1,0:T(8,128)(2,1)S(1)}, u32[]{:S(2)}, u32[]{:S(2)}) %collective-permute-start.27) | collective-permute-done | bytes 131104 | tf_op jit(solution)/shard_map/ppermute | solution.py:373
  89.7 2.7 %collective-permute-done.30 = bf16[16,4096]{1,0:T(8,128)(2,1)S(1)} collective-permute-done((bf16[16,4096]{1,0:T(8,128)(2,1)S(1)}, bf16[16,4096]{1,0:T(8,128)(2,1)S(1)}, u32[]{:S(2)}, u32[]{:S(2)}) %collective-permute-start.30) | collective-permute-done | bytes 131104 | tf_op jit(solution)/shard_map/ppermute | solution.py:373
  (100 shorter events, 29.5 us)
Async XLA Ops:
  5.5 18.5 %collective-permute-start.2 = (bf16[336,256]{1,0:T(8,128)(2,1)S(1)}, bf16[336,256]{1,0:T(8,128)(2,1)S(1)}, u32[]{:S(2)}, u32[]{:S(2)}) collective-permute-start(bf16[336,256]{1,0:T(8,128)(2,1)S(1)} %pad_maximum_fusion.refs_3_.refs_5_.refs_1_), channel_id=1, source_target_pairs={{0,12},{4,8},{8,4},{12,0},{1,13},{5,9},{9,5},{13,1},{2,14},{6,10},... | collective-permute-start | bytes 516104 | tf_op jit(solution)/shard_map/ppermute | solution.py:358
  10.6 14.6 %collective-permute-start.1 = (bf16[336,256]{1,0:T(8,128)(2,1)S(1)}, bf16[336,256]{1,0:T(8,128)(2,1)S(1)}, u32[]{:S(2)}, u32[]{:S(2)}) collective-permute-start(bf16[336,256]{1,0:T(8,128)(2,1)S(1)} %pad_maximum_fusion.refs_3_.refs_5_.refs_1_), channel_id=1, source_target_pairs={{0,8},{4,12},{8,0},{12,4},{1,9},{5,13},{9,1},{13,5},{2,10},{6,14},... | collective-permute-start | bytes 516104 | tf_op jit(solution)/shard_map/ppermute | solution.py:358
  10.6 14.6 %collective-permute-start = (bf16[336,256]{1,0:T(8,128)(2,1)S(1)}, bf16[336,256]{1,0:T(8,128)(2,1)S(1)}, u32[]{:S(2)}, u32[]{:S(2)}) collective-permute-start(bf16[336,256]{1,0:T(8,128)(2,1)S(1)} %pad_maximum_fusion.refs_3_.refs_5_.refs_1_), channel_id=1, source_target_pairs={{0,4},{4,0},{8,12},{12,8},{1,5},{5,1},{9,13},{13,9},{2,6},{6,2},{1... | collective-permute-start | bytes 516104 | tf_op jit(solution)/shard_map/ppermute | solution.py:358
  30.5 5.6 %collective-permute-start.4 = (bf16[16,4096]{1,0:T(8,128)(2,1)S(1)}, bf16[16,4096]{1,0:T(8,128)(2,1)S(1)}, u32[]{:S(2)}, u32[]{:S(2)}) collective-permute-start(bf16[16,4096]{1,0:T(8,128)(2,1)S(1)} %add_convert_fusion.8), channel_id=1, source_target_pairs={{0,2},{1,3},{2,0},{3,1},{4,6},{5,7},{6,4},{7,5},{8,10},{9,11},{10,... | collective-permute-start | bytes 393224 | tf_op jit(solution)/shard_map/ppermute | solution.py:370
  37.3 7.3 %collective-permute-start.8 = (bf16[16,4096]{1,0:T(8,128)(2,1)S(1)}, bf16[16,4096]{1,0:T(8,128)(2,1)S(1)}, u32[]{:S(2)}, u32[]{:S(2)}) collective-permute-start(bf16[16,4096]{1,0:T(8,128)(2,1)S(1)} %fusion.2.refs_5_.refs_1_), channel_id=1, source_target_pairs={{0,4},{4,0},{8,12},{12,8},{1,5},{5,1},{9,13},{13,9},{2,6},{6,2},{1... | collective-permute-start | bytes 393224 | tf_op jit(solution)/shard_map/ppermute | solution.py:373
  37.7 8.5 %collective-permute-start.7 = (bf16[16,4096]{1,0:T(8,128)(2,1)S(1)}, bf16[16,4096]{1,0:T(8,128)(2,1)S(1)}, u32[]{:S(2)}, u32[]{:S(2)}) collective-permute-start(bf16[16,4096]{1,0:T(8,128)(2,1)S(1)} %fusion.2.refs_5_.refs_1_), channel_id=1, source_target_pairs={{0,8},{4,12},{8,0},{12,4},{1,9},{5,13},{9,1},{13,5},{2,10},{6,14},... | collective-permute-start | bytes 393224 | tf_op jit(solution)/shard_map/ppermute | solution.py:373
  40.6 5.5 %collective-permute-start.6 = (bf16[16,4096]{1,0:T(8,128)(2,1)S(1)}, bf16[16,4096]{1,0:T(8,128)(2,1)S(1)}, u32[]{:S(2)}, u32[]{:S(2)}) collective-permute-start(bf16[16,4096]{1,0:T(8,128)(2,1)S(1)} %fusion.2.refs_5_.refs_1_), channel_id=1, source_target_pairs={{0,1},{1,0},{2,3},{3,2},{4,5},{5,4},{6,7},{7,6},{8,9},{9,8},{10,11... | collective-permute-start | bytes 393224 | tf_op jit(solution)/shard_map/ppermute | solution.py:370
  40.6 5.9 %collective-permute-start.5 = (bf16[16,4096]{1,0:T(8,128)(2,1)S(1)}, bf16[16,4096]{1,0:T(8,128)(2,1)S(1)}, u32[]{:S(2)}, u32[]{:S(2)}) collective-permute-start(bf16[16,4096]{1,0:T(8,128)(2,1)S(1)} %fusion.2.refs_5_.refs_1_), channel_id=1, source_target_pairs={{0,2},{1,3},{2,0},{3,1},{4,6},{5,7},{6,4},{7,5},{8,10},{9,11},{10,... | collective-permute-start | bytes 393224 | tf_op jit(solution)/shard_map/ppermute | solution.py:370
  46.5 6.3 %collective-permute-start.11 = (bf16[16,4096]{1,0:T(8,128)(2,1)S(1)}, bf16[16,4096]{1,0:T(8,128)(2,1)S(1)}, u32[]{:S(2)}, u32[]{:S(2)}) collective-permute-start(bf16[16,4096]{1,0:T(8,128)(2,1)S(1)} %collective-permute-done.8.refs_1_), channel_id=1, source_target_pairs={{0,2},{1,3},{2,0},{3,1},{4,6},{5,7},{6,4},{7,5},{8,10},{9,11},{10,... | collective-permute-start | bytes 393224 | tf_op jit(solution)/shard_map/ppermute | solution.py:370
  48.0 5.6 %collective-permute-start.12 = (bf16[16,4096]{1,0:T(8,128)(2,1)S(1)}, bf16[16,4096]{1,0:T(8,128)(2,1)S(1)}, u32[]{:S(2)}, u32[]{:S(2)}) collective-permute-start(bf16[16,4096]{1,0:T(8,128)(2,1)S(1)} %collective-permute-done.7.refs_1_), channel_id=1, source_target_pairs={{0,4},{4,0},{8,12},{12,8},{1,5},{5,1},{9,13},{13,9},{2,6},{6,2},{1... | collective-permute-start | bytes 393224 | tf_op jit(solution)/shard_map/ppermute | solution.py:373
  48.1 7.1 %collective-permute-start.10 = (bf16[16,4096]{1,0:T(8,128)(2,1)S(1)}, bf16[16,4096]{1,0:T(8,128)(2,1)S(1)}, u32[]{:S(2)}, u32[]{:S(2)}) collective-permute-start(bf16[16,4096]{1,0:T(8,128)(2,1)S(1)} %collective-permute-done.7.refs_1_), channel_id=1, source_target_pairs={{0,2},{1,3},{2,0},{3,1},{4,6},{5,7},{6,4},{7,5},{8,10},{9,11},{10,... | collective-permute-start | bytes 393224 | tf_op jit(solution)/shard_map/ppermute | solution.py:370
  55.2 6.4 %collective-permute-start.13 = (bf16[32,4096]{1,0:T(8,128)(2,1)S(1)}, bf16[32,4096]{1,0:T(8,128)(2,1)S(1)}, u32[]{:S(2)}, u32[]{:S(2)}) collective-permute-start(bf16[32,4096]{1,0:T(8,128)(2,1)S(1)} %get-tuple-element.44.refs_7_), channel_id=1, source_target_pairs={{0,1},{1,0},{2,3},{3,2},{4,5},{5,4},{6,7},{7,6},{8,9},{9,8},{10,11... | collective-permute-start | bytes 786440 | tf_op jit(solution)/shard_map/ppermute | solution.py:370
  55.7 5.9 %collective-permute-start.17 = (bf16[16,4096]{1,0:T(8,128)(2,1)S(1)}, bf16[16,4096]{1,0:T(8,128)(2,1)S(1)}, u32[]{:S(2)}, u32[]{:S(2)}) collective-permute-start(bf16[16,4096]{1,0:T(8,128)(2,1)S(1)} %collective-permute-done.12.refs_1_), channel_id=1, source_target_pairs={{0,2},{1,3},{2,0},{3,1},{4,6},{5,7},{6,4},{7,5},{8,10},{9,11},{10,... | collective-permute-start | bytes 393224 | tf_op jit(solution)/shard_map/ppermute | solution.py:370
  57.2 6.0 %collective-permute-start.18 = (bf16[16,4096]{1,0:T(8,128)(2,1)S(1)}, bf16[16,4096]{1,0:T(8,128)(2,1)S(1)}, u32[]{:S(2)}, u32[]{:S(2)}) collective-permute-start(bf16[16,4096]{1,0:T(8,128)(2,1)S(1)} %collective-permute-done.12.refs_1_), channel_id=1, source_target_pairs={{0,1},{1,0},{2,3},{3,2},{4,5},{5,4},{6,7},{7,6},{8,9},{9,8},{10,11... | collective-permute-start | bytes 393224 | tf_op jit(solution)/shard_map/ppermute | solution.py:370
  57.4 10.8 %collective-permute-start.15 = (bf16[16,4096]{1,0:T(8,128)(2,1)S(1)}, bf16[16,4096]{1,0:T(8,128)(2,1)S(1)}, u32[]{:S(2)}, u32[]{:S(2)}) collective-permute-start(bf16[16,4096]{1,0:T(8,128)(2,1)S(1)} %collective-permute-done.8.refs_1_), channel_id=1, source_target_pairs={{0,1},{1,0},{2,3},{3,2},{4,5},{5,4},{6,7},{7,6},{8,9},{9,8},{10,11... | collective-permute-start | bytes 393224 | tf_op jit(solution)/shard_map/ppermute | solution.py:370
  57.7 11.0 %collective-permute-start.16 = (bf16[16,4096]{1,0:T(8,128)(2,1)S(1)}, bf16[16,4096]{1,0:T(8,128)(2,1)S(1)}, u32[]{:S(2)}, u32[]{:S(2)}) collective-permute-start(bf16[16,4096]{1,0:T(8,128)(2,1)S(1)} %collective-permute-done.11.refs_2_), channel_id=1, source_target_pairs={{0,1},{1,0},{2,3},{3,2},{4,5},{5,4},{6,7},{7,6},{8,9},{9,8},{10,11... | collective-permute-start | bytes 393224 | tf_op jit(solution)/shard_map/ppermute | solution.py:370
  66.0 5.4 %collective-permute-start.24 = (bf16[32,4096]{1,0:T(8,128)(2,1)S(1)}, bf16[32,4096]{1,0:T(8,128)(2,1)S(1)}, u32[]{:S(2)}, u32[]{:S(2)}) collective-permute-start(bf16[32,4096]{1,0:T(8,128)(2,1)S(1)} %get-tuple-element.52.refs_7_), channel_id=1, source_target_pairs={{0,1},{1,0},{2,3},{3,2},{4,5},{5,4},{6,7},{7,6},{8,9},{9,8},{10,11... | collective-permute-start | bytes 786440 | tf_op jit(solution)/shard_map/ppermute | solution.py:370
  66.2 19.7 %collective-permute-start.31 = (bf16[8,16,256]{2,1,0:T(8,128)(2,1)S(1)}, bf16[8,16,256]{2,1,0:T(8,128)(2,1)S(1)}, u32[]{:S(2)}, u32[]{:S(2)}) collective-permute-start(bf16[8,16,256]{2,1,0:T(8,128)(2,1)S(1)} %bitcast.23), channel_id=1, source_target_pairs={{0,1},{1,0},{2,3},{3,2},{4,5},{5,4},{6,7},{7,6},{8,9},{9,8},{10,11... | collective-permute-start | bytes 196616 | tf_op jit(solution)/shard_map/ppermute | solution.py:482
  66.7 20.1 %collective-permute-start.14 = (bf16[16,4096]{1,0:T(8,128)(2,1)S(1)}, bf16[16,4096]{1,0:T(8,128)(2,1)S(1)}, u32[]{:S(2)}, u32[]{:S(2)}) collective-permute-start(bf16[16,4096]{1,0:T(8,128)(2,1)S(1)} %add_convert_fusion.6.refs_8_), channel_id=1, source_target_pairs={{0,2},{1,3},{2,0},{3,1},{4,6},{5,7},{6,4},{7,5},{8,10},{9,11},{10,... | collective-permute-start | bytes 393224 | tf_op jit(solution)/shard_map/ppermute | solution.py:370
  68.2 15.1 %collective-permute-start.28 = (bf16[16,4096]{1,0:T(8,128)(2,1)S(1)}, bf16[16,4096]{1,0:T(8,128)(2,1)S(1)}, u32[]{:S(2)}, u32[]{:S(2)}) collective-permute-start(bf16[16,4096]{1,0:T(8,128)(2,1)S(1)} %add_convert_fusion.5.refs_9_), channel_id=1, source_target_pairs={{0,2},{1,3},{2,0},{3,1},{4,6},{5,7},{6,4},{7,5},{8,10},{9,11},{10,... | collective-permute-start | bytes 393224 | tf_op jit(solution)/shard_map/ppermute | solution.py:370
  71.5 6.3 %collective-permute-start.25 = (bf16[16,4096]{1,0:T(8,128)(2,1)S(1)}, bf16[16,4096]{1,0:T(8,128)(2,1)S(1)}, u32[]{:S(2)}, u32[]{:S(2)}) collective-permute-start(bf16[16,4096]{1,0:T(8,128)(2,1)S(1)} %add_convert_fusion.3), channel_id=1, source_target_pairs={{0,2},{1,3},{2,0},{3,1},{4,6},{5,7},{6,4},{7,5},{8,10},{9,11},{10,... | collective-permute-start | bytes 393224 | tf_op jit(solution)/shard_map/ppermute | solution.py:370
  77.8 5.2 %collective-permute-start.26 = (bf16[16,4096]{1,0:T(8,128)(2,1)S(1)}, bf16[16,4096]{1,0:T(8,128)(2,1)S(1)}, u32[]{:S(2)}, u32[]{:S(2)}) collective-permute-start(bf16[16,4096]{1,0:T(8,128)(2,1)S(1)} %add_convert_fusion.4), channel_id=1, source_target_pairs={{0,2},{1,3},{2,0},{3,1},{4,6},{5,7},{6,4},{7,5},{8,10},{9,11},{10,... | collective-permute-start | bytes 393224 | tf_op jit(solution)/shard_map/ppermute | solution.py:370
  83.1 6.6 %collective-permute-start.27 = (bf16[16,4096]{1,0:T(8,128)(2,1)S(1)}, bf16[16,4096]{1,0:T(8,128)(2,1)S(1)}, u32[]{:S(2)}, u32[]{:S(2)}) collective-permute-start(bf16[16,4096]{1,0:T(8,128)(2,1)S(1)} %add_convert_fusion.2), channel_id=1, source_target_pairs={{0,4},{4,0},{8,12},{12,8},{1,5},{5,1},{9,13},{13,9},{2,6},{6,2},{1... | collective-permute-start | bytes 393224 | tf_op jit(solution)/shard_map/ppermute | solution.py:373
  84.5 7.9 %collective-permute-start.30 = (bf16[16,4096]{1,0:T(8,128)(2,1)S(1)}, bf16[16,4096]{1,0:T(8,128)(2,1)S(1)}, u32[]{:S(2)}, u32[]{:S(2)}) collective-permute-start(bf16[16,4096]{1,0:T(8,128)(2,1)S(1)} %add_convert_fusion), channel_id=1, source_target_pairs={{0,8},{4,12},{8,0},{12,4},{1,9},{5,13},{9,1},{13,5},{2,10},{6,14},... | collective-permute-start | bytes 393224 | tf_op jit(solution)/shard_map/ppermute | solution.py:373
  (16 other events, 51.6 us)

commit v13 on v11

--- a/solution.py
+++ b/solution.py
@@ -418,10 +418,9 @@
         * norm_gain
     ).astype(jnp.bfloat16)
 
-    def group_rows(piece, before=None):
-        have = [piece]
-        for bit in bits + [1]:
-            have += [exchange(part, bit) for part in have]
+    def group_rows(have, bits, before=None):
+        for bit in bits:
+            have = have + [exchange(part, bit) for part in have]
             if before is not None and len(have) == 2:
                 have[1], before = lax.optimization_barrier([have[1], before])
         return have
@@ -436,6 +435,14 @@
     for bit in ep_bits:
         for step in list(crossed):
             crossed[step ^ bit] = across(crossed[step], bit) if step else direct[bit]
+    leading = ep_bits[0]
+    forwarded = [step for step in crossed if step & (step - 1)]
+    lead_have = group_rows([crossed[leading]], bits[:1])
+    lead_have[1:], ahead = lax.optimization_barrier(
+        (lead_have[1:], [crossed[step] for step in forwarded])
+    )
+    crossed.update(zip(forwarded, ahead))
+    lead_have = group_rows(lead_have, bits[1:] + [1])
     own_have = [normed]
     for bit, piece in zip(bits + [1], early):
         own_have += [piece] + [exchange(part, bit) for part in own_have[1:]]
@@ -445,13 +452,17 @@
     sent, given, finished = None, [], []
     for turn, group in enumerate(groups):
         after = [sent] if turn >= 1 else []
-        after += given[turn - 2 : turn - 1] if turn >= 2 else []
+        after += given[turn - 2 : turn] if turn >= 2 else []
         if turn == len(groups) - 1:
-            after += given[turn - 1 :] + finished[: turn - 1]
-        haves = {
-            step: group_rows(crossed[step], sent if turn == 1 else None) if step else own_have
-            for step in group
-        }
+            after += finished[: turn - 1]
+        haves = {0: own_have, leading: lead_have}
+        for step in group:
+            if step not in haves:
+                piece = crossed[step]
+                if turn > 1 and bits:
+                    piece, reached = lax.optimization_barrier((piece, reached))
+                haves[step] = group_rows([piece], bits + [1], sent if turn == 1 else None)
+                reached = haves[step][1]
         have = [haves[step][spot] for spot in range(blocks) for step in group]
         kept, sent = expert_call(
             tuple(group), blocks, row_weights, have, held_gate_up, held_down, after
@@ -461,12 +472,11 @@
         finished.append(own.astype(jnp.bfloat16))
         for spot, step in enumerate(group):
             sums[step] = own[spot * row_count : (spot + 1) * row_count]
-    for bit in reversed(ep_bits):
-        for step in [step for step in sums if step & bit]:
-            sums[step ^ bit] = sums[step ^ bit] + across(
-                sums.pop(step).astype(jnp.bfloat16), bit
-            ).astype(jnp.float32)
-    mixture = resid_wide + sums[0]
+    mixture = resid_wide
+    for step, own in sums.items():
+        if step:
+            own = across(own.astype(jnp.bfloat16), step).astype(jnp.float32)
+        mixture = mixture + own
     layer_out = jnp.where(row_mask[:, None] > 0, mixture, 0.0).astype(jnp.bfloat16)
 
     if keyval_local == 1:

time: 89.4 us -> 88.5 us (0.990)
  waiting for transfers between devices: 28.3 us -> 24.1 us
  starting transfers between devices: 24.2 us -> 27.4 us
    ppermute x22, waiting for transfers between devices: 17.2 us -> 12.8 us  [local(): lax.ppermute(value, ('kv', 'tp'), [(i, i ^ bit) for i in range(blocks)])]
    ppermute x22, starting transfers between devices: 11.8 us -> 13.6 us  [local(): lax.ppermute(value, ('kv', 'tp'), [(i, i ^ bit) for i in range(blocks)])]
    ppermute x6, starting transfers between devices: 6.23 us -> 7.77 us  [local(): lax.ppermute(value, 'ep', [(i, i ^ step) for i in range(ep_count)])]
  transfers between devices with their start and end apart: 32 -> 32, of which waited for: 17 -> 15; matrix products, arithmetic and copies ran while one was open for 4% -> 5% of each run, Pallas kernels for 15% -> 15%
where the time goes in v13:
time: 88.5 us; the launch traced here: 88.1 us
  starting transfers between devices  27.4 us (31%)
  waiting for transfers between devices  24.1 us (27%)
  Pallas kernels  16.7 us (19%)
  local copies, waits for them, and re-layouts  13.4 us (15%)
  other arithmetic  5.45 us (6%)
  between operations  0.98 us (1%)
    ppermute x22, starting transfers between devices, local(): lax.ppermute(value, ('kv', 'tp'), [(i, i ^ bit) for i in range(blocks)])  13.6 us
    ppermute x22, waiting for transfers between devices, local(): lax.ppermute(value, ('kv', 'tp'), [(i, i ^ bit) for i in range(blocks)])  12.8 us
    pallas_call x4, Pallas kernels, expert_call(): pl.pallas_call(lambda *refs: expert_kernel(len(have), steps, blocks, *ref...  10.6 us
    ppermute x6, waiting for transfers between devices, local(): lax.ppermute(value, 'ep', [(i, i ^ step) for i in range(ep_count)])  10.2 us
    unnamed x19, local copies, waits for them, and re-layouts  8.9 us
    ppermute x6, starting transfers between devices, local(): lax.ppermute(value, 'ep', [(i, i ^ step) for i in range(ep_count)])  7.77 us
    ppermute x3, starting transfers between devices, local(): lax.ppermute(payload, 'ep', [(i, i ^ step) for i in range(ep_count)])  5.76 us
    pallas_call x1, Pallas kernels, attend_call(): pl.pallas_call(lambda *refs: attend_kernel(ep_count, held, tokens, blocks...  3.66 us
  transfers between devices with their start and end apart: 32, of which 15 were waited for; matrix products, arithmetic and copies ran while one was open for 5% of the time, Pallas kernels for 15%

profile of v13, /device:TPU:0, one launch (start us, length us, event | category | flops | bytes accessed | tf_op | source)
XLA Modules:
  0.0 88.1 jit_solution(6183619288977311358)
XLA Ops:
  5.5 5.1 %collective-permute-start.2 = (bf16[336,256]{1,0:T(8,128)(2,1)S(1)}, bf16[336,256]{1,0:T(8,128)(2,1)S(1)}, u32[]{:S(2)}, u32[]{:S(2)}) collective-permute-start(bf16[336,256]{1,0:T(8,128)(2,1)S(1)} %pad_maximum_fusion.refs_3_.refs_5_.refs_1_), channel_id=1, source_target_pairs={{0,12},{4,8},{8,4},{12,0},{1,13},{5,9},{9,5},{13,1},{2,14},{6,10},... | collective-permute-start | bytes 516104 | tf_op jit(solution)/shard_map/ppermute | solution.py:358
  14.1 3.4 %copy-done.1 = bf16[1024,4096]{1,0:T(8,128)(2,1)S(1)} copy-done((bf16[1024,4096]{1,0:T(8,128)(2,1)S(1)}, bf16[1024,4096]{1,0:T(8,128)(2,1)}, u32[]{:S(2)}) %copy-start.1) | copy-done | bytes 8388632
  17.5 2.8 %copy-done.2 = bf16[1,2,384,4096]{3,2,1,0:T(8,128)(2,1)S(1)} copy-done((bf16[1,2,384,4096]{3,2,1,0:T(8,128)(2,1)S(1)}, bf16[1,2,384,4096]{3,2,1,0:T(8,128)(2,1)}, u32[]{:S(2)}) %copy-start.2) | copy-done | bytes 6291480
  20.3 1.9 %copy-done.3 = bf16[1,384,4096]{2,1,0:T(8,128)(2,1)S(1)} copy-done((bf16[1,384,4096]{2,1,0:T(8,128)(2,1)S(1)}, bf16[1,384,4096]{2,1,0:T(8,128)(2,1)}, u32[]{:S(2)}) %copy-start.3) | copy-done | bytes 3145752
  22.2 1.8 %hold.1 = (bf16[1024,4096]{1,0:T(8,128)(2,1)S(1)}, bf16[1,2,384,4096]{3,2,1,0:T(8,128)(2,1)S(1)}, bf16[1,384,4096]{2,1,0:T(8,128)(2,1)S(1)}, f32[8,128]{1,0:T(8,128)}) custom-call(bf16[1024,4096]{1,0:T(8,128)(2,1)S(1)} %copy-done.1, bf16[1,2,384,4096]{3,2,1,0:T(8,128)(2,1)S(1)} %copy-done.2, bf16[1,384,4096]{2,1,0:T(8,128)(2,1)S(1)} %copy-done.3, ...), custom_call_target="tpu_custom_call" | custom-call | bytes 35651584 | tf_op jit(solution)/shard_map/hold/pallas_call | solution.py:62
  25.2 3.7 %attend.1 = (f32[32,4096]{1,0:T(8,128)S(1)}, bf16[32,4096]{1,0:T(8,128)(2,1)S(1)}, bf16[128,256]{1,0:T(8,128)(2,1)S(1)}) custom-call(s32[4]{0:T(128)S(1)} %copy-done.5, s32[2]{0:T(128)S(1)} %pad_add_fusion.refs_4_.refs_1_.refs_0_, s32[1]{0:T(128)} %constant.60.clone.1.refs_2_, s32[16]{0:T(128)S(1)} %copy-done.6, bf16[64,1024]{1,0:T(8,128)(2,1)S(1)} %copy-done.4, ...), custom_call_target="tpu_custom_call" | custom-call | flops 872415232 | bytes 8388608 | tf_op jit(solution)/shard_map/attend/pallas_call | solution.py:221
  28.9 1.5 %collective-permute-done.3 = bf16[32,4096]{1,0:T(8,128)(2,1)S(1)} collective-permute-done((bf16[32,4096]{1,0:T(8,128)(2,1)S(1)}, bf16[32,4096]{1,0:T(8,128)(2,1)S(1)}, u32[]{:S(2)}, u32[]{:S(2)}) %collective-permute-start.3) | collective-permute-done | bytes 262176 | tf_op jit(solution)/shard_map/ppermute | solution.py:370
  30.5 1.6 %collective-permute-start.4 = (bf16[16,4096]{1,0:T(8,128)(2,1)S(1)}, bf16[16,4096]{1,0:T(8,128)(2,1)S(1)}, u32[]{:S(2)}, u32[]{:S(2)}) collective-permute-start(bf16[16,4096]{1,0:T(8,128)(2,1)S(1)} %add_convert_fusion.8), channel_id=1, source_target_pairs={{0,2},{1,3},{2,0},{3,1},{4,6},{5,7},{6,4},{7,5},{8,10},{9,11},{10,... | collective-permute-start | bytes 393224 | tf_op jit(solution)/shard_map/ppermute | solution.py:370
  32.0 4.0 %collective-permute-done.4 = bf16[16,4096]{1,0:T(8,128)(2,1)S(1)} collective-permute-done((bf16[16,4096]{1,0:T(8,128)(2,1)S(1)}, bf16[16,4096]{1,0:T(8,128)(2,1)S(1)}, u32[]{:S(2)}, u32[]{:S(2)}) %collective-permute-start.4) | collective-permute-done | bytes 131104 | tf_op jit(solution)/shard_map/ppermute | solution.py:370
  37.6 2.9 %collective-permute-start.7 = (bf16[16,4096]{1,0:T(8,128)(2,1)S(1)}, bf16[16,4096]{1,0:T(8,128)(2,1)S(1)}, u32[]{:S(2)}, u32[]{:S(2)}) collective-permute-start(bf16[16,4096]{1,0:T(8,128)(2,1)S(1)} %fusion.2.refs_5_.refs_1_), channel_id=1, source_target_pairs={{0,8},{4,12},{8,0},{12,4},{1,9},{5,13},{9,1},{13,5},{2,10},{6,14},... | collective-permute-start | bytes 393224 | tf_op jit(solution)/shard_map/ppermute | solution.py:373
  40.6 1.5 %collective-permute-start.5 = (bf16[16,4096]{1,0:T(8,128)(2,1)S(1)}, bf16[16,4096]{1,0:T(8,128)(2,1)S(1)}, u32[]{:S(2)}, u32[]{:S(2)}) collective-permute-start(bf16[16,4096]{1,0:T(8,128)(2,1)S(1)} %fusion.2.refs_5_.refs_1_), channel_id=1, source_target_pairs={{0,2},{1,3},{2,0},{3,1},{4,6},{5,7},{6,4},{7,5},{8,10},{9,11},{10,... | collective-permute-start | bytes 393224 | tf_op jit(solution)/shard_map/ppermute | solution.py:370
  42.7 1.8 %collective-permute-done.8.refs_1_ = bf16[16,4096]{1,0:T(8,128)(2,1)S(1)} collective-permute-done((bf16[16,4096]{1,0:T(8,128)(2,1)S(1)}, bf16[16,4096]{1,0:T(8,128)(2,1)S(1)}, u32[]{:S(2)}, u32[]{:S(2)}) %collective-permute-start.8) | collective-permute-done | bytes 131104 | tf_op jit(solution)/shard_map/ppermute | solution.py:373
  44.6 1.5 %collective-permute-done.7.refs_1_ = bf16[16,4096]{1,0:T(8,128)(2,1)S(1)} collective-permute-done((bf16[16,4096]{1,0:T(8,128)(2,1)S(1)}, bf16[16,4096]{1,0:T(8,128)(2,1)S(1)}, u32[]{:S(2)}, u32[]{:S(2)}) %collective-permute-start.7) | collective-permute-done | bytes 131104 | tf_op jit(solution)/shard_map/ppermute | solution.py:373
  48.1 3.6 %collective-permute-done.10.refs_1_ = bf16[16,4096]{1,0:T(8,128)(2,1)S(1)} collective-permute-done((bf16[16,4096]{1,0:T(8,128)(2,1)S(1)}, bf16[16,4096]{1,0:T(8,128)(2,1)S(1)}, u32[]{:S(2)}, u32[]{:S(2)}) %collective-permute-start.10) | collective-permute-done | bytes 131104 | tf_op jit(solution)/shard_map/ppermute | solution.py:373
  51.6 1.5 %collective-permute-start.16 = (bf16[16,4096]{1,0:T(8,128)(2,1)S(1)}, bf16[16,4096]{1,0:T(8,128)(2,1)S(1)}, u32[]{:S(2)}, u32[]{:S(2)}) collective-permute-start(bf16[16,4096]{1,0:T(8,128)(2,1)S(1)} %collective-permute-done.10.refs_1_), channel_id=1, source_target_pairs={{0,2},{1,3},{2,0},{3,1},{4,6},{5,7},{6,4},{7,5},{8,10},{9,11},{10,... | collective-permute-start | bytes 393224 | tf_op jit(solution)/shard_map/ppermute | solution.py:370
  53.3 2.7 %experts.4 = (bf16[32,4096]{1,0:T(8,128)(2,1)S(1)}, bf16[32,4096]{1,0:T(8,128)(2,1)S(1)}) custom-call(f32[256,128]{1,0:T(8,128)S(1)} %prepare.1.refs_0_, bf16[16,4096]{1,0:T(8,128)(2,1)S(1)} %collective-permute-done.7.refs_1_, bf16[16,4096]{1,0:T(8,128)(2,1)S(1)} %collective-permute-done.9.refs_2_, bf16[16,4096]{1,0:T(8,128)(2,1)S(1)} %collective-permute-done.11.refs_3_, ...), custom_call_target="tpu_custom_call" | custom-call | flops 1024 | bytes 1024 | tf_op jit(solution)/shard_map/experts/pallas_call | solution.py:286
  57.5 1.5 %collective-permute-start.22 = (bf16[16,4096]{1,0:T(8,128)(2,1)S(1)}, bf16[16,4096]{1,0:T(8,128)(2,1)S(1)}, u32[]{:S(2)}, u32[]{:S(2)}) collective-permute-start(bf16[16,4096]{1,0:T(8,128)(2,1)S(1)} %collective-permute-done.8.refs_1_), channel_id=1, source_target_pairs={{0,2},{1,3},{2,0},{3,1},{4,6},{5,7},{6,4},{7,5},{8,10},{9,11},{10,... | collective-permute-start | bytes 393224 | tf_op jit(solution)/shard_map/ppermute | solution.py:370
  59.9 2.7 %experts.5 = (bf16[32,4096]{1,0:T(8,128)(2,1)S(1)}, bf16[32,4096]{1,0:T(8,128)(2,1)S(1)}) custom-call(f32[256,128]{1,0:T(8,128)S(1)} %prepare.1.refs_0_, bf16[16,4096]{1,0:T(8,128)(2,1)S(1)} %collective-permute-done.10.refs_1_, bf16[16,4096]{1,0:T(8,128)(2,1)S(1)} %collective-permute-done.16.refs_2_, bf16[16,4096]{1,0:T(8,128)(2,1)S(1)} %collective-permute-done.17.refs_3_, ...), custom_call_target="tpu_custom_call" | custom-call | flops 1024 | bytes 1024 | tf_op jit(solution)/shard_map/experts/pallas_call | solution.py:286
  67.1 2.7 %experts.6 = (bf16[32,4096]{1,0:T(8,128)(2,1)S(1)}, bf16[32,4096]{1,0:T(8,128)(2,1)S(1)}) custom-call(f32[256,128]{1,0:T(8,128)S(1)} %prepare.1.refs_0_, bf16[16,4096]{1,0:T(8,128)(2,1)S(1)} %collective-permute-done.8.refs_1_, bf16[16,4096]{1,0:T(8,128)(2,1)S(1)} %collective-permute-done.22.refs_2_, bf16[16,4096]{1,0:T(8,128)(2,1)S(1)} %collective-permute-done.23.refs_3_, ...), custom_call_target="tpu_custom_call" | custom-call | flops 1024 | bytes 1024 | tf_op jit(solution)/shard_map/experts/pallas_call | solution.py:286
  71.4 2.5 %collective-permute-start.15 = (bf16[16,4096]{1,0:T(8,128)(2,1)S(1)}, bf16[16,4096]{1,0:T(8,128)(2,1)S(1)}, u32[]{:S(2)}, u32[]{:S(2)}) collective-permute-start(bf16[16,4096]{1,0:T(8,128)(2,1)S(1)} %add_convert_fusion.5.refs_10_), channel_id=1, source_target_pairs={{0,8},{4,12},{8,0},{12,4},{1,9},{5,13},{9,1},{13,5},{2,10},{6,14},... | collective-permute-start | bytes 393224 | tf_op jit(solution)/shard_map/ppermute | solution.py:373
  74.0 1.6 %collective-permute-start.26 = (bf16[16,4096]{1,0:T(8,128)(2,1)S(1)}, bf16[16,4096]{1,0:T(8,128)(2,1)S(1)}, u32[]{:S(2)}, u32[]{:S(2)}) collective-permute-start(bf16[16,4096]{1,0:T(8,128)(2,1)S(1)} %add_convert_fusion.2.refs_9_), channel_id=1, source_target_pairs={{0,2},{1,3},{2,0},{3,1},{4,6},{5,7},{6,4},{7,5},{8,10},{9,11},{10,... | collective-permute-start | bytes 393224 | tf_op jit(solution)/shard_map/ppermute | solution.py:370
  75.6 1.8 %collective-permute-start.21 = (bf16[16,4096]{1,0:T(8,128)(2,1)S(1)}, bf16[16,4096]{1,0:T(8,128)(2,1)S(1)}, u32[]{:S(2)}, u32[]{:S(2)}) collective-permute-start(bf16[16,4096]{1,0:T(8,128)(2,1)S(1)} %add_convert_fusion.3.refs_11_), channel_id=1, source_target_pairs={{0,12},{4,8},{8,4},{12,0},{1,13},{5,9},{9,5},{13,1},{2,14},{6,10},... | collective-permute-start | bytes 393224 | tf_op jit(solution)/shard_map/ppermute | solution.py:373
  77.4 2.7 %experts.7 = (bf16[32,4096]{1,0:T(8,128)(2,1)S(1)}, bf16[32,4096]{1,0:T(8,128)(2,1)S(1)}) custom-call(f32[256,128]{1,0:T(8,128)S(1)} %prepare.1.refs_0_, bf16[16,4096]{1,0:T(8,128)(2,1)S(1)} %fusion.2.refs_5_.refs_1_, bf16[16,4096]{1,0:T(8,128)(2,1)S(1)} %collective-permute-done.5.refs_2_, bf16[16,4096]{1,0:T(8,128)(2,1)S(1)} %collective-permute-done.6.refs_3_, ...), custom_call_target="tpu_custom_call" | custom-call | flops 1024 | bytes 1024 | tf_op jit(solution)/shard_map/experts/pallas_call | solution.py:286
  83.8 2.6 %collective-permute-done.27 = bf16[16,4096]{1,0:T(8,128)(2,1)S(1)} collective-permute-done((bf16[16,4096]{1,0:T(8,128)(2,1)S(1)}, bf16[16,4096]{1,0:T(8,128)(2,1)S(1)}, u32[]{:S(2)}, u32[]{:S(2)}) %collective-permute-start.27) | collective-permute-done | bytes 131104 | tf_op jit(solution)/shard_map/ppermute | solution.py:373
  (100 shorter events, 27.9 us)
Async XLA Ops:
  5.5 18.5 %collective-permute-start.2 = (bf16[336,256]{1,0:T(8,128)(2,1)S(1)}, bf16[336,256]{1,0:T(8,128)(2,1)S(1)}, u32[]{:S(2)}, u32[]{:S(2)}) collective-permute-start(bf16[336,256]{1,0:T(8,128)(2,1)S(1)} %pad_maximum_fusion.refs_3_.refs_5_.refs_1_), channel_id=1, source_target_pairs={{0,12},{4,8},{8,4},{12,0},{1,13},{5,9},{9,5},{13,1},{2,14},{6,10},... | collective-permute-start | bytes 516104 | tf_op jit(solution)/shard_map/ppermute | solution.py:358
  10.6 14.6 %collective-permute-start.1 = (bf16[336,256]{1,0:T(8,128)(2,1)S(1)}, bf16[336,256]{1,0:T(8,128)(2,1)S(1)}, u32[]{:S(2)}, u32[]{:S(2)}) collective-permute-start(bf16[336,256]{1,0:T(8,128)(2,1)S(1)} %pad_maximum_fusion.refs_3_.refs_5_.refs_1_), channel_id=1, source_target_pairs={{0,8},{4,12},{8,0},{12,4},{1,9},{5,13},{9,1},{13,5},{2,10},{6,14},... | collective-permute-start | bytes 516104 | tf_op jit(solution)/shard_map/ppermute | solution.py:358
  10.6 14.6 %collective-permute-start = (bf16[336,256]{1,0:T(8,128)(2,1)S(1)}, bf16[336,256]{1,0:T(8,128)(2,1)S(1)}, u32[]{:S(2)}, u32[]{:S(2)}) collective-permute-start(bf16[336,256]{1,0:T(8,128)(2,1)S(1)} %pad_maximum_fusion.refs_3_.refs_5_.refs_1_), channel_id=1, source_target_pairs={{0,4},{4,0},{8,12},{12,8},{1,5},{5,1},{9,13},{13,9},{2,6},{6,2},{1... | collective-permute-start | bytes 516104 | tf_op jit(solution)/shard_map/ppermute | solution.py:358
  30.5 5.6 %collective-permute-start.4 = (bf16[16,4096]{1,0:T(8,128)(2,1)S(1)}, bf16[16,4096]{1,0:T(8,128)(2,1)S(1)}, u32[]{:S(2)}, u32[]{:S(2)}) collective-permute-start(bf16[16,4096]{1,0:T(8,128)(2,1)S(1)} %add_convert_fusion.8), channel_id=1, source_target_pairs={{0,2},{1,3},{2,0},{3,1},{4,6},{5,7},{6,4},{7,5},{8,10},{9,11},{10,... | collective-permute-start | bytes 393224 | tf_op jit(solution)/shard_map/ppermute | solution.py:370
  37.3 7.3 %collective-permute-start.8 = (bf16[16,4096]{1,0:T(8,128)(2,1)S(1)}, bf16[16,4096]{1,0:T(8,128)(2,1)S(1)}, u32[]{:S(2)}, u32[]{:S(2)}) collective-permute-start(bf16[16,4096]{1,0:T(8,128)(2,1)S(1)} %fusion.2.refs_5_.refs_1_), channel_id=1, source_target_pairs={{0,4},{4,0},{8,12},{12,8},{1,5},{5,1},{9,13},{13,9},{2,6},{6,2},{1... | collective-permute-start | bytes 393224 | tf_op jit(solution)/shard_map/ppermute | solution.py:373
  37.6 8.5 %collective-permute-start.7 = (bf16[16,4096]{1,0:T(8,128)(2,1)S(1)}, bf16[16,4096]{1,0:T(8,128)(2,1)S(1)}, u32[]{:S(2)}, u32[]{:S(2)}) collective-permute-start(bf16[16,4096]{1,0:T(8,128)(2,1)S(1)} %fusion.2.refs_5_.refs_1_), channel_id=1, source_target_pairs={{0,8},{4,12},{8,0},{12,4},{1,9},{5,13},{9,1},{13,5},{2,10},{6,14},... | collective-permute-start | bytes 393224 | tf_op jit(solution)/shard_map/ppermute | solution.py:373
  40.6 5.5 %collective-permute-start.6 = (bf16[16,4096]{1,0:T(8,128)(2,1)S(1)}, bf16[16,4096]{1,0:T(8,128)(2,1)S(1)}, u32[]{:S(2)}, u32[]{:S(2)}) collective-permute-start(bf16[16,4096]{1,0:T(8,128)(2,1)S(1)} %fusion.2.refs_5_.refs_1_), channel_id=1, source_target_pairs={{0,1},{1,0},{2,3},{3,2},{4,5},{5,4},{6,7},{7,6},{8,9},{9,8},{10,11... | collective-permute-start | bytes 393224 | tf_op jit(solution)/shard_map/ppermute | solution.py:370
  40.6 5.9 %collective-permute-start.5 = (bf16[16,4096]{1,0:T(8,128)(2,1)S(1)}, bf16[16,4096]{1,0:T(8,128)(2,1)S(1)}, u32[]{:S(2)}, u32[]{:S(2)}) collective-permute-start(bf16[16,4096]{1,0:T(8,128)(2,1)S(1)} %fusion.2.refs_5_.refs_1_), channel_id=1, source_target_pairs={{0,2},{1,3},{2,0},{3,1},{4,6},{5,7},{6,4},{7,5},{8,10},{9,11},{10,... | collective-permute-start | bytes 393224 | tf_op jit(solution)/shard_map/ppermute | solution.py:370
  46.5 5.1 %collective-permute-start.10 = (bf16[16,4096]{1,0:T(8,128)(2,1)S(1)}, bf16[16,4096]{1,0:T(8,128)(2,1)S(1)}, u32[]{:S(2)}, u32[]{:S(2)}) collective-permute-start(bf16[16,4096]{1,0:T(8,128)(2,1)S(1)} %collective-permute-done.7.refs_1_), channel_id=1, source_target_pairs={{0,4},{4,0},{8,12},{12,8},{1,5},{5,1},{9,13},{13,9},{2,6},{6,2},{1... | collective-permute-start | bytes 393224 | tf_op jit(solution)/shard_map/ppermute | solution.py:373
  48.1 5.3 %collective-permute-start.11 = (bf16[16,4096]{1,0:T(8,128)(2,1)S(1)}, bf16[16,4096]{1,0:T(8,128)(2,1)S(1)}, u32[]{:S(2)}, u32[]{:S(2)}) collective-permute-start(bf16[16,4096]{1,0:T(8,128)(2,1)S(1)} %collective-permute-done.7.refs_1_), channel_id=1, source_target_pairs={{0,1},{1,0},{2,3},{3,2},{4,5},{5,4},{6,7},{7,6},{8,9},{9,8},{10,11... | collective-permute-start | bytes 393224 | tf_op jit(solution)/shard_map/ppermute | solution.py:370
  51.6 5.9 %collective-permute-start.16 = (bf16[16,4096]{1,0:T(8,128)(2,1)S(1)}, bf16[16,4096]{1,0:T(8,128)(2,1)S(1)}, u32[]{:S(2)}, u32[]{:S(2)}) collective-permute-start(bf16[16,4096]{1,0:T(8,128)(2,1)S(1)} %collective-permute-done.10.refs_1_), channel_id=1, source_target_pairs={{0,2},{1,3},{2,0},{3,1},{4,6},{5,7},{6,4},{7,5},{8,10},{9,11},{10,... | collective-permute-start | bytes 393224 | tf_op jit(solution)/shard_map/ppermute | solution.py:370
  53.1 6.2 %collective-permute-start.17 = (bf16[16,4096]{1,0:T(8,128)(2,1)S(1)}, bf16[16,4096]{1,0:T(8,128)(2,1)S(1)}, u32[]{:S(2)}, u32[]{:S(2)}) collective-permute-start(bf16[16,4096]{1,0:T(8,128)(2,1)S(1)} %collective-permute-done.10.refs_1_), channel_id=1, source_target_pairs={{0,1},{1,0},{2,3},{3,2},{4,5},{5,4},{6,7},{7,6},{8,9},{9,8},{10,11... | collective-permute-start | bytes 393224 | tf_op jit(solution)/shard_map/ppermute | solution.py:370
  56.0 7.4 %collective-permute-start.13 = (bf16[32,4096]{1,0:T(8,128)(2,1)S(1)}, bf16[32,4096]{1,0:T(8,128)(2,1)S(1)}, u32[]{:S(2)}, u32[]{:S(2)}) collective-permute-start(bf16[32,4096]{1,0:T(8,128)(2,1)S(1)} %get-tuple-element.38.refs_7_), channel_id=1, source_target_pairs={{0,1},{1,0},{2,3},{3,2},{4,5},{5,4},{6,7},{7,6},{8,9},{9,8},{10,11... | collective-permute-start | bytes 786440 | tf_op jit(solution)/shard_map/ppermute | solution.py:370
  57.5 5.9 %collective-permute-start.22 = (bf16[16,4096]{1,0:T(8,128)(2,1)S(1)}, bf16[16,4096]{1,0:T(8,128)(2,1)S(1)}, u32[]{:S(2)}, u32[]{:S(2)}) collective-permute-start(bf16[16,4096]{1,0:T(8,128)(2,1)S(1)} %collective-permute-done.8.refs_1_), channel_id=1, source_target_pairs={{0,2},{1,3},{2,0},{3,1},{4,6},{5,7},{6,4},{7,5},{8,10},{9,11},{10,... | collective-permute-start | bytes 393224 | tf_op jit(solution)/shard_map/ppermute | solution.py:370
  59.1 23.3 %collective-permute-start.31 = (bf16[8,16,256]{2,1,0:T(8,128)(2,1)S(1)}, bf16[8,16,256]{2,1,0:T(8,128)(2,1)S(1)}, u32[]{:S(2)}, u32[]{:S(2)}) collective-permute-start(bf16[8,16,256]{2,1,0:T(8,128)(2,1)S(1)} %bitcast.23), channel_id=1, source_target_pairs={{0,1},{1,0},{2,3},{3,2},{4,5},{5,4},{6,7},{7,6},{8,9},{9,8},{10,11... | collective-permute-start | bytes 196616 | tf_op jit(solution)/shard_map/ppermute | solution.py:485
  59.3 18.0 %collective-permute-start.28 = (bf16[16,4096]{1,0:T(8,128)(2,1)S(1)}, bf16[16,4096]{1,0:T(8,128)(2,1)S(1)}, u32[]{:S(2)}, u32[]{:S(2)}) collective-permute-start(bf16[16,4096]{1,0:T(8,128)(2,1)S(1)} %collective-permute-done.5.refs_2_), channel_id=1, source_target_pairs={{0,1},{1,0},{2,3},{3,2},{4,5},{5,4},{6,7},{7,6},{8,9},{9,8},{10,11... | collective-permute-start | bytes 393224 | tf_op jit(solution)/shard_map/ppermute | solution.py:370
  59.6 6.9 %collective-permute-start.23 = (bf16[16,4096]{1,0:T(8,128)(2,1)S(1)}, bf16[16,4096]{1,0:T(8,128)(2,1)S(1)}, u32[]{:S(2)}, u32[]{:S(2)}) collective-permute-start(bf16[16,4096]{1,0:T(8,128)(2,1)S(1)} %collective-permute-done.8.refs_1_), channel_id=1, source_target_pairs={{0,1},{1,0},{2,3},{3,2},{4,5},{5,4},{6,7},{7,6},{8,9},{9,8},{10,11... | collective-permute-start | bytes 393224 | tf_op jit(solution)/shard_map/ppermute | solution.py:370
  65.0 6.3 %collective-permute-start.14 = (bf16[16,4096]{1,0:T(8,128)(2,1)S(1)}, bf16[16,4096]{1,0:T(8,128)(2,1)S(1)}, u32[]{:S(2)}, u32[]{:S(2)}) collective-permute-start(bf16[16,4096]{1,0:T(8,128)(2,1)S(1)} %add_convert_fusion.6.refs_8_), channel_id=1, source_target_pairs={{0,2},{1,3},{2,0},{3,1},{4,6},{5,7},{6,4},{7,5},{8,10},{9,11},{10,... | collective-permute-start | bytes 393224 | tf_op jit(solution)/shard_map/ppermute | solution.py:370
  66.5 9.0 %collective-permute-start.20 = (bf16[16,4096]{1,0:T(8,128)(2,1)S(1)}, bf16[16,4096]{1,0:T(8,128)(2,1)S(1)}, u32[]{:S(2)}, u32[]{:S(2)}) collective-permute-start(bf16[16,4096]{1,0:T(8,128)(2,1)S(1)} %add_convert_fusion.4.refs_9_.refs_8_), channel_id=1, source_target_pairs={{0,2},{1,3},{2,0},{3,1},{4,6},{5,7},{6,4},{7,5},{8,10},{9,11},{10,... | collective-permute-start | bytes 393224 | tf_op jit(solution)/shard_map/ppermute | solution.py:370
  71.4 12.4 %collective-permute-start.15 = (bf16[16,4096]{1,0:T(8,128)(2,1)S(1)}, bf16[16,4096]{1,0:T(8,128)(2,1)S(1)}, u32[]{:S(2)}, u32[]{:S(2)}) collective-permute-start(bf16[16,4096]{1,0:T(8,128)(2,1)S(1)} %add_convert_fusion.5.refs_10_), channel_id=1, source_target_pairs={{0,8},{4,12},{8,0},{12,4},{1,9},{5,13},{9,1},{13,5},{2,10},{6,14},... | collective-permute-start | bytes 393224 | tf_op jit(solution)/shard_map/ppermute | solution.py:373
  74.0 6.2 %collective-permute-start.26 = (bf16[16,4096]{1,0:T(8,128)(2,1)S(1)}, bf16[16,4096]{1,0:T(8,128)(2,1)S(1)}, u32[]{:S(2)}, u32[]{:S(2)}) collective-permute-start(bf16[16,4096]{1,0:T(8,128)(2,1)S(1)} %add_convert_fusion.2.refs_9_), channel_id=1, source_target_pairs={{0,2},{1,3},{2,0},{3,1},{4,6},{5,7},{6,4},{7,5},{8,10},{9,11},{10,... | collective-permute-start | bytes 393224 | tf_op jit(solution)/shard_map/ppermute | solution.py:370
  75.6 8.2 %collective-permute-start.21 = (bf16[16,4096]{1,0:T(8,128)(2,1)S(1)}, bf16[16,4096]{1,0:T(8,128)(2,1)S(1)}, u32[]{:S(2)}, u32[]{:S(2)}) collective-permute-start(bf16[16,4096]{1,0:T(8,128)(2,1)S(1)} %add_convert_fusion.3.refs_11_), channel_id=1, source_target_pairs={{0,12},{4,8},{8,4},{12,0},{1,13},{5,9},{9,5},{13,1},{2,14},{6,10},... | collective-permute-start | bytes 393224 | tf_op jit(solution)/shard_map/ppermute | solution.py:373
  80.2 6.2 %collective-permute-start.27 = (bf16[16,4096]{1,0:T(8,128)(2,1)S(1)}, bf16[16,4096]{1,0:T(8,128)(2,1)S(1)}, u32[]{:S(2)}, u32[]{:S(2)}) collective-permute-start(bf16[16,4096]{1,0:T(8,128)(2,1)S(1)} %add_convert_fusion.1), channel_id=1, source_target_pairs={{0,4},{4,0},{8,12},{12,8},{1,5},{5,1},{9,13},{13,9},{2,6},{6,2},{1... | collective-permute-start | bytes 393224 | tf_op jit(solution)/shard_map/ppermute | solution.py:373
  81.7 5.6 %collective-permute-start.30 = (bf16[16,4096]{1,0:T(8,128)(2,1)S(1)}, bf16[16,4096]{1,0:T(8,128)(2,1)S(1)}, u32[]{:S(2)}, u32[]{:S(2)}) collective-permute-start(bf16[16,4096]{1,0:T(8,128)(2,1)S(1)} %add_convert_fusion), channel_id=1, source_target_pairs={{0,2},{1,3},{2,0},{3,1},{4,6},{5,7},{6,4},{7,5},{8,10},{9,11},{10,... | collective-permute-start | bytes 393224 | tf_op jit(solution)/shard_map/ppermute | solution.py:370
  (16 other events, 55.0 us)

commit v14 on v13

--- a/solution.py
+++ b/solution.py
@@ -327,13 +327,14 @@
     held = HOLD_MOST * page_size
 
     hits = hit_pages.shape[0]
-    owned_hits = hit_pages // pool_pages == ep_index
+    here_page = lax.optimization_barrier(hit_pages - ep_index * pool_pages)
+    owned_hits = (here_page >= 0) & (here_page < pool_pages)
     earlier = jnp.arange(hits)[None, :] < jnp.arange(hits)[:, None]
     hit_rank = jnp.sum((earlier & owned_hits[None, :]).astype(jnp.int32), axis=1)
     hit_pick = owned_hits[None, :] & (
         hit_rank[None, :] == jnp.arange(HOLD_MOST, dtype=jnp.int32)[:, None]
     )
-    local_page = jnp.sum(jnp.where(hit_pick, hit_pages[None, :] - ep_index * pool_pages, 0), axis=1)
+    local_page = jnp.sum(jnp.where(hit_pick, here_page[None, :], 0), axis=1)
     chosen = cache_pool.at[local_page].get(mode="promise_in_bounds")
     own_pages = lax.dynamic_index_in_dim(chosen, keyval_pick, 2, keepdims=False).reshape(held, 2 * HD)
     own_suffix = lax.dynamic_index_in_dim(new_kv, keyval_pick, 1, keepdims=False)
@@ -376,7 +377,7 @@
     bits = [1 << place for place in range(1, blocks.bit_length() - 1)]
 
     def scatter(kept, sent):
-        got = exchange(sent, 1)
+        got = received = exchange(sent, 1)
         gives = []
         for bit in reversed(bits):
             half = kept.shape[0] // 2
@@ -384,7 +385,7 @@
             gives.append(give.astype(jnp.bfloat16))
             kept = kept[:half].astype(jnp.float32) + got[:half].astype(jnp.float32)
             got = exchange(gives[-1], bit)
-        return kept.astype(jnp.float32) + got.astype(jnp.float32), gives
+        return kept.astype(jnp.float32) + got.astype(jnp.float32), gives, received
 
     own_most = 2 * (tokens // page_size)
     own_slots = block_index * row_count + jnp.arange(row_count, dtype=jnp.int32)
@@ -409,7 +410,7 @@
         all_open,
     )
     head_pages = head_pages.reshape(own_most, page_size, 2 * HD)
-    heads_out, _ = scatter(kept, sent)
+    heads_out, _, _ = scatter(kept, sent)
     residual = (own_hidden.astype(jnp.float32) + heads_out).astype(jnp.bfloat16)
     resid_wide = residual.astype(jnp.float32)
     normed = (
@@ -461,13 +462,13 @@
                 piece = crossed[step]
                 if turn > 1 and bits:
                     piece, reached = lax.optimization_barrier((piece, reached))
-                haves[step] = group_rows([piece], bits + [1], sent if turn == 1 else None)
+                haves[step] = group_rows([piece], bits + [1], sent if turn == 1 else received)
                 reached = haves[step][1]
         have = [haves[step][spot] for spot in range(blocks) for step in group]
         kept, sent = expert_call(
             tuple(group), blocks, row_weights, have, held_gate_up, held_down, after
         )
-        own, gives = scatter(kept, sent)
+        own, gives, received = scatter(kept, sent)
         given.append(gives[0] if gives else own.astype(jnp.bfloat16))
         finished.append(own.astype(jnp.bfloat16))
         for spot, step in enumerate(group):

time: 88.5 us -> 87.1 us (0.984)
    ppermute x22, waiting for transfers between devices: 12.8 us -> 11.6 us  [local(): lax.ppermute(value, ('kv', 'tp'), [(i, i ^ bit) for i in range(blocks)])]
where the time goes in v14:
time: 87.1 us; the launch traced here: 86.7 us
  starting transfers between devices  27.4 us (31%)
  waiting for transfers between devices  23.4 us (27%)
  Pallas kernels  16.7 us (19%)
  local copies, waits for them, and re-layouts  13.4 us (15%)
  other arithmetic  4.8 us (6%)
  between operations  0.99 us (1%)
    ppermute x22, starting transfers between devices, local(): lax.ppermute(value, ('kv', 'tp'), [(i, i ^ bit) for i in range(blocks)])  13.3 us
    ppermute x22, waiting for transfers between devices, local(): lax.ppermute(value, ('kv', 'tp'), [(i, i ^ bit) for i in range(blocks)])  11.6 us
    ppermute x6, waiting for transfers between devices, local(): lax.ppermute(value, 'ep', [(i, i ^ step) for i in range(ep_count)])  10.6 us
    pallas_call x4, Pallas kernels, expert_call(): pl.pallas_call(lambda *refs: expert_kernel(len(have), steps, blocks, *ref...  10.6 us
    unnamed x19, local copies, waits for them, and re-layouts  8.9 us
    ppermute x6, starting transfers between devices, local(): lax.ppermute(value, 'ep', [(i, i ^ step) for i in range(ep_count)])  7.77 us
    ppermute x3, starting transfers between devices, local(): lax.ppermute(payload, 'ep', [(i, i ^ step) for i in range(ep_count)])  5.76 us
    pallas_call x1, Pallas kernels, attend_call(): pl.pallas_call(lambda *refs: attend_kernel(ep_count, held, tokens, blocks...  3.66 us
  transfers between devices with their start and end apart: 32, of which 15 were waited for; matrix products, arithmetic and copies ran while one was open for 5% of the time, Pallas kernels for 15%

profile of v14, /device:TPU:0, one launch (start us, length us, event | category | flops | bytes accessed | tf_op | source)
XLA Modules:
  0.0 86.7 jit_solution(12879824629927135518)
XLA Ops:
  4.8 5.1 %collective-permute-start.2 = (bf16[336,256]{1,0:T(8,128)(2,1)S(1)}, bf16[336,256]{1,0:T(8,128)(2,1)S(1)}, u32[]{:S(2)}, u32[]{:S(2)}) collective-permute-start(bf16[336,256]{1,0:T(8,128)(2,1)S(1)} %pad_maximum_fusion.refs_3_.refs_5_.refs_1_), channel_id=1, source_target_pairs={{0,12},{4,8},{8,4},{12,0},{1,13},{5,9},{9,5},{13,1},{2,14},{6,10},... | collective-permute-start | bytes 516104 | tf_op jit(solution)/shard_map/ppermute | solution.py:359
  13.5 3.4 %copy-done.1 = bf16[1024,4096]{1,0:T(8,128)(2,1)S(1)} copy-done((bf16[1024,4096]{1,0:T(8,128)(2,1)S(1)}, bf16[1024,4096]{1,0:T(8,128)(2,1)}, u32[]{:S(2)}) %copy-start.1) | copy-done | bytes 8388632
  16.9 2.8 %copy-done.2 = bf16[1,2,384,4096]{3,2,1,0:T(8,128)(2,1)S(1)} copy-done((bf16[1,2,384,4096]{3,2,1,0:T(8,128)(2,1)S(1)}, bf16[1,2,384,4096]{3,2,1,0:T(8,128)(2,1)}, u32[]{:S(2)}) %copy-start.2) | copy-done | bytes 6291480
  19.6 1.9 %copy-done.3 = bf16[1,384,4096]{2,1,0:T(8,128)(2,1)S(1)} copy-done((bf16[1,384,4096]{2,1,0:T(8,128)(2,1)S(1)}, bf16[1,384,4096]{2,1,0:T(8,128)(2,1)}, u32[]{:S(2)}) %copy-start.3) | copy-done | bytes 3145752
  21.5 1.8 %hold.1 = (bf16[1024,4096]{1,0:T(8,128)(2,1)S(1)}, bf16[1,2,384,4096]{3,2,1,0:T(8,128)(2,1)S(1)}, bf16[1,384,4096]{2,1,0:T(8,128)(2,1)S(1)}, f32[8,128]{1,0:T(8,128)}) custom-call(bf16[1024,4096]{1,0:T(8,128)(2,1)S(1)} %copy-done.1, bf16[1,2,384,4096]{3,2,1,0:T(8,128)(2,1)S(1)} %copy-done.2, bf16[1,384,4096]{2,1,0:T(8,128)(2,1)S(1)} %copy-done.3, ...), custom_call_target="tpu_custom_call" | custom-call | bytes 35651584 | tf_op jit(solution)/shard_map/hold/pallas_call | solution.py:62
  24.5 3.7 %attend.1 = (f32[32,4096]{1,0:T(8,128)S(1)}, bf16[32,4096]{1,0:T(8,128)(2,1)S(1)}, bf16[128,256]{1,0:T(8,128)(2,1)S(1)}) custom-call(s32[4]{0:T(128)S(1)} %copy-done.5, s32[2]{0:T(128)S(1)} %pad_add_fusion.refs_4_.refs_1_.refs_0_, s32[1]{0:T(128)} %constant.52.clone.1.refs_2_, s32[16]{0:T(128)S(1)} %copy-done.6, bf16[64,1024]{1,0:T(8,128)(2,1)S(1)} %copy-done.4, ...), custom_call_target="tpu_custom_call" | custom-call | flops 872415232 | bytes 8388608 | tf_op jit(solution)/shard_map/attend/pallas_call | solution.py:221
  28.3 1.5 %collective-permute-done.3 = bf16[32,4096]{1,0:T(8,128)(2,1)S(1)} collective-permute-done((bf16[32,4096]{1,0:T(8,128)(2,1)S(1)}, bf16[32,4096]{1,0:T(8,128)(2,1)S(1)}, u32[]{:S(2)}, u32[]{:S(2)}) %collective-permute-start.3) | collective-permute-done | bytes 262176 | tf_op jit(solution)/shard_map/ppermute | solution.py:371
  29.8 1.6 %collective-permute-start.4 = (bf16[16,4096]{1,0:T(8,128)(2,1)S(1)}, bf16[16,4096]{1,0:T(8,128)(2,1)S(1)}, u32[]{:S(2)}, u32[]{:S(2)}) collective-permute-start(bf16[16,4096]{1,0:T(8,128)(2,1)S(1)} %add_convert_fusion.8), channel_id=1, source_target_pairs={{0,2},{1,3},{2,0},{3,1},{4,6},{5,7},{6,4},{7,5},{8,10},{9,11},{10,... | collective-permute-start | bytes 393224 | tf_op jit(solution)/shard_map/ppermute | solution.py:371
  31.4 4.0 %collective-permute-done.4 = bf16[16,4096]{1,0:T(8,128)(2,1)S(1)} collective-permute-done((bf16[16,4096]{1,0:T(8,128)(2,1)S(1)}, bf16[16,4096]{1,0:T(8,128)(2,1)S(1)}, u32[]{:S(2)}, u32[]{:S(2)}) %collective-permute-start.4) | collective-permute-done | bytes 131104 | tf_op jit(solution)/shard_map/ppermute | solution.py:371
  37.0 2.9 %collective-permute-start.7 = (bf16[16,4096]{1,0:T(8,128)(2,1)S(1)}, bf16[16,4096]{1,0:T(8,128)(2,1)S(1)}, u32[]{:S(2)}, u32[]{:S(2)}) collective-permute-start(bf16[16,4096]{1,0:T(8,128)(2,1)S(1)} %fusion.2.refs_5_.refs_1_), channel_id=1, source_target_pairs={{0,8},{4,12},{8,0},{12,4},{1,9},{5,13},{9,1},{13,5},{2,10},{6,14},... | collective-permute-start | bytes 393224 | tf_op jit(solution)/shard_map/ppermute | solution.py:374
  39.9 1.5 %collective-permute-start.5 = (bf16[16,4096]{1,0:T(8,128)(2,1)S(1)}, bf16[16,4096]{1,0:T(8,128)(2,1)S(1)}, u32[]{:S(2)}, u32[]{:S(2)}) collective-permute-start(bf16[16,4096]{1,0:T(8,128)(2,1)S(1)} %fusion.2.refs_5_.refs_1_), channel_id=1, source_target_pairs={{0,2},{1,3},{2,0},{3,1},{4,6},{5,7},{6,4},{7,5},{8,10},{9,11},{10,... | collective-permute-start | bytes 393224 | tf_op jit(solution)/shard_map/ppermute | solution.py:371
  42.1 1.9 %collective-permute-done.8.refs_1_ = bf16[16,4096]{1,0:T(8,128)(2,1)S(1)} collective-permute-done((bf16[16,4096]{1,0:T(8,128)(2,1)S(1)}, bf16[16,4096]{1,0:T(8,128)(2,1)S(1)}, u32[]{:S(2)}, u32[]{:S(2)}) %collective-permute-start.8) | collective-permute-done | bytes 131104 | tf_op jit(solution)/shard_map/ppermute | solution.py:374
  43.9 1.5 %collective-permute-done.7.refs_1_ = bf16[16,4096]{1,0:T(8,128)(2,1)S(1)} collective-permute-done((bf16[16,4096]{1,0:T(8,128)(2,1)S(1)}, bf16[16,4096]{1,0:T(8,128)(2,1)S(1)}, u32[]{:S(2)}, u32[]{:S(2)}) %collective-permute-start.7) | collective-permute-done | bytes 131104 | tf_op jit(solution)/shard_map/ppermute | solution.py:374
  47.4 3.6 %collective-permute-done.10.refs_1_ = bf16[16,4096]{1,0:T(8,128)(2,1)S(1)} collective-permute-done((bf16[16,4096]{1,0:T(8,128)(2,1)S(1)}, bf16[16,4096]{1,0:T(8,128)(2,1)S(1)}, u32[]{:S(2)}, u32[]{:S(2)}) %collective-permute-start.10) | collective-permute-done | bytes 131104 | tf_op jit(solution)/shard_map/ppermute | solution.py:374
  51.0 1.5 %collective-permute-start.16 = (bf16[16,4096]{1,0:T(8,128)(2,1)S(1)}, bf16[16,4096]{1,0:T(8,128)(2,1)S(1)}, u32[]{:S(2)}, u32[]{:S(2)}) collective-permute-start(bf16[16,4096]{1,0:T(8,128)(2,1)S(1)} %collective-permute-done.10.refs_1_), channel_id=1, source_target_pairs={{0,2},{1,3},{2,0},{3,1},{4,6},{5,7},{6,4},{7,5},{8,10},{9,11},{10,... | collective-permute-start | bytes 393224 | tf_op jit(solution)/shard_map/ppermute | solution.py:371
  52.7 2.7 %experts.4 = (bf16[32,4096]{1,0:T(8,128)(2,1)S(1)}, bf16[32,4096]{1,0:T(8,128)(2,1)S(1)}) custom-call(f32[256,128]{1,0:T(8,128)S(1)} %prepare.1.refs_0_, bf16[16,4096]{1,0:T(8,128)(2,1)S(1)} %collective-permute-done.7.refs_1_, bf16[16,4096]{1,0:T(8,128)(2,1)S(1)} %collective-permute-done.9.refs_2_, bf16[16,4096]{1,0:T(8,128)(2,1)S(1)} %collective-permute-done.11.refs_3_, ...), custom_call_target="tpu_custom_call" | custom-call | flops 1024 | bytes 1024 | tf_op jit(solution)/shard_map/experts/pallas_call | solution.py:286
  58.2 1.5 %collective-permute-start.22 = (bf16[16,4096]{1,0:T(8,128)(2,1)S(1)}, bf16[16,4096]{1,0:T(8,128)(2,1)S(1)}, u32[]{:S(2)}, u32[]{:S(2)}) collective-permute-start(bf16[16,4096]{1,0:T(8,128)(2,1)S(1)} %collective-permute-done.8.refs_1_), channel_id=1, source_target_pairs={{0,2},{1,3},{2,0},{3,1},{4,6},{5,7},{6,4},{7,5},{8,10},{9,11},{10,... | collective-permute-start | bytes 393224 | tf_op jit(solution)/shard_map/ppermute | solution.py:371
  59.7 2.7 %experts.5 = (bf16[32,4096]{1,0:T(8,128)(2,1)S(1)}, bf16[32,4096]{1,0:T(8,128)(2,1)S(1)}) custom-call(f32[256,128]{1,0:T(8,128)S(1)} %prepare.1.refs_0_, bf16[16,4096]{1,0:T(8,128)(2,1)S(1)} %collective-permute-done.10.refs_1_, bf16[16,4096]{1,0:T(8,128)(2,1)S(1)} %collective-permute-done.16.refs_2_, bf16[16,4096]{1,0:T(8,128)(2,1)S(1)} %collective-permute-done.17.refs_3_, ...), custom_call_target="tpu_custom_call" | custom-call | flops 1024 | bytes 1024 | tf_op jit(solution)/shard_map/experts/pallas_call | solution.py:286
  66.6 2.7 %experts.6 = (bf16[32,4096]{1,0:T(8,128)(2,1)S(1)}, bf16[32,4096]{1,0:T(8,128)(2,1)S(1)}) custom-call(f32[256,128]{1,0:T(8,128)S(1)} %prepare.1.refs_0_, bf16[16,4096]{1,0:T(8,128)(2,1)S(1)} %collective-permute-done.8.refs_1_, bf16[16,4096]{1,0:T(8,128)(2,1)S(1)} %collective-permute-done.22.refs_2_, bf16[16,4096]{1,0:T(8,128)(2,1)S(1)} %collective-permute-done.23.refs_3_, ...), custom_call_target="tpu_custom_call" | custom-call | flops 1024 | bytes 1024 | tf_op jit(solution)/shard_map/experts/pallas_call | solution.py:286
  69.5 2.6 %collective-permute-start.15 = (bf16[16,4096]{1,0:T(8,128)(2,1)S(1)}, bf16[16,4096]{1,0:T(8,128)(2,1)S(1)}, u32[]{:S(2)}, u32[]{:S(2)}) collective-permute-start(bf16[16,4096]{1,0:T(8,128)(2,1)S(1)} %add_convert_fusion.5.refs_10_), channel_id=1, source_target_pairs={{0,8},{4,12},{8,0},{12,4},{1,9},{5,13},{9,1},{13,5},{2,10},{6,14},... | collective-permute-start | bytes 393224 | tf_op jit(solution)/shard_map/ppermute | solution.py:374
  72.1 2.0 %collective-permute-start.26 = (bf16[16,4096]{1,0:T(8,128)(2,1)S(1)}, bf16[16,4096]{1,0:T(8,128)(2,1)S(1)}, u32[]{:S(2)}, u32[]{:S(2)}) collective-permute-start(bf16[16,4096]{1,0:T(8,128)(2,1)S(1)} %add_convert_fusion.2.refs_9_), channel_id=1, source_target_pairs={{0,2},{1,3},{2,0},{3,1},{4,6},{5,7},{6,4},{7,5},{8,10},{9,11},{10,... | collective-permute-start | bytes 393224 | tf_op jit(solution)/shard_map/ppermute | solution.py:371
  74.2 1.8 %collective-permute-start.21 = (bf16[16,4096]{1,0:T(8,128)(2,1)S(1)}, bf16[16,4096]{1,0:T(8,128)(2,1)S(1)}, u32[]{:S(2)}, u32[]{:S(2)}) collective-permute-start(bf16[16,4096]{1,0:T(8,128)(2,1)S(1)} %add_convert_fusion.3.refs_11_), channel_id=1, source_target_pairs={{0,12},{4,8},{8,4},{12,0},{1,13},{5,9},{9,5},{13,1},{2,14},{6,10},... | collective-permute-start | bytes 393224 | tf_op jit(solution)/shard_map/ppermute | solution.py:374
  76.0 2.7 %experts.7 = (bf16[32,4096]{1,0:T(8,128)(2,1)S(1)}, bf16[32,4096]{1,0:T(8,128)(2,1)S(1)}) custom-call(f32[256,128]{1,0:T(8,128)S(1)} %prepare.1.refs_0_, bf16[16,4096]{1,0:T(8,128)(2,1)S(1)} %fusion.2.refs_5_.refs_1_, bf16[16,4096]{1,0:T(8,128)(2,1)S(1)} %collective-permute-done.5.refs_2_, bf16[16,4096]{1,0:T(8,128)(2,1)S(1)} %collective-permute-done.6.refs_3_, ...), custom_call_target="tpu_custom_call" | custom-call | flops 1024 | bytes 1024 | tf_op jit(solution)/shard_map/experts/pallas_call | solution.py:286
  82.5 2.6 %collective-permute-done.27 = bf16[16,4096]{1,0:T(8,128)(2,1)S(1)} collective-permute-done((bf16[16,4096]{1,0:T(8,128)(2,1)S(1)}, bf16[16,4096]{1,0:T(8,128)(2,1)S(1)}, u32[]{:S(2)}, u32[]{:S(2)}) %collective-permute-start.27) | collective-permute-done | bytes 131104 | tf_op jit(solution)/shard_map/ppermute | solution.py:374
  (100 shorter events, 26.1 us)
Async XLA Ops:
  4.8 18.5 %collective-permute-start.2 = (bf16[336,256]{1,0:T(8,128)(2,1)S(1)}, bf16[336,256]{1,0:T(8,128)(2,1)S(1)}, u32[]{:S(2)}, u32[]{:S(2)}) collective-permute-start(bf16[336,256]{1,0:T(8,128)(2,1)S(1)} %pad_maximum_fusion.refs_3_.refs_5_.refs_1_), channel_id=1, source_target_pairs={{0,12},{4,8},{8,4},{12,0},{1,13},{5,9},{9,5},{13,1},{2,14},{6,10},... | collective-permute-start | bytes 516104 | tf_op jit(solution)/shard_map/ppermute | solution.py:359
  9.9 14.6 %collective-permute-start.1 = (bf16[336,256]{1,0:T(8,128)(2,1)S(1)}, bf16[336,256]{1,0:T(8,128)(2,1)S(1)}, u32[]{:S(2)}, u32[]{:S(2)}) collective-permute-start(bf16[336,256]{1,0:T(8,128)(2,1)S(1)} %pad_maximum_fusion.refs_3_.refs_5_.refs_1_), channel_id=1, source_target_pairs={{0,8},{4,12},{8,0},{12,4},{1,9},{5,13},{9,1},{13,5},{2,10},{6,14},... | collective-permute-start | bytes 516104 | tf_op jit(solution)/shard_map/ppermute | solution.py:359
  9.9 14.6 %collective-permute-start = (bf16[336,256]{1,0:T(8,128)(2,1)S(1)}, bf16[336,256]{1,0:T(8,128)(2,1)S(1)}, u32[]{:S(2)}, u32[]{:S(2)}) collective-permute-start(bf16[336,256]{1,0:T(8,128)(2,1)S(1)} %pad_maximum_fusion.refs_3_.refs_5_.refs_1_), channel_id=1, source_target_pairs={{0,4},{4,0},{8,12},{12,8},{1,5},{5,1},{9,13},{13,9},{2,6},{6,2},{1... | collective-permute-start | bytes 516104 | tf_op jit(solution)/shard_map/ppermute | solution.py:359
  29.8 5.6 %collective-permute-start.4 = (bf16[16,4096]{1,0:T(8,128)(2,1)S(1)}, bf16[16,4096]{1,0:T(8,128)(2,1)S(1)}, u32[]{:S(2)}, u32[]{:S(2)}) collective-permute-start(bf16[16,4096]{1,0:T(8,128)(2,1)S(1)} %add_convert_fusion.8), channel_id=1, source_target_pairs={{0,2},{1,3},{2,0},{3,1},{4,6},{5,7},{6,4},{7,5},{8,10},{9,11},{10,... | collective-permute-start | bytes 393224 | tf_op jit(solution)/shard_map/ppermute | solution.py:371
  36.7 7.3 %collective-permute-start.8 = (bf16[16,4096]{1,0:T(8,128)(2,1)S(1)}, bf16[16,4096]{1,0:T(8,128)(2,1)S(1)}, u32[]{:S(2)}, u32[]{:S(2)}) collective-permute-start(bf16[16,4096]{1,0:T(8,128)(2,1)S(1)} %fusion.2.refs_5_.refs_1_), channel_id=1, source_target_pairs={{0,4},{4,0},{8,12},{12,8},{1,5},{5,1},{9,13},{13,9},{2,6},{6,2},{1... | collective-permute-start | bytes 393224 | tf_op jit(solution)/shard_map/ppermute | solution.py:374
  37.0 8.5 %collective-permute-start.7 = (bf16[16,4096]{1,0:T(8,128)(2,1)S(1)}, bf16[16,4096]{1,0:T(8,128)(2,1)S(1)}, u32[]{:S(2)}, u32[]{:S(2)}) collective-permute-start(bf16[16,4096]{1,0:T(8,128)(2,1)S(1)} %fusion.2.refs_5_.refs_1_), channel_id=1, source_target_pairs={{0,8},{4,12},{8,0},{12,4},{1,9},{5,13},{9,1},{13,5},{2,10},{6,14},... | collective-permute-start | bytes 393224 | tf_op jit(solution)/shard_map/ppermute | solution.py:374
  39.9 5.5 %collective-permute-start.6 = (bf16[16,4096]{1,0:T(8,128)(2,1)S(1)}, bf16[16,4096]{1,0:T(8,128)(2,1)S(1)}, u32[]{:S(2)}, u32[]{:S(2)}) collective-permute-start(bf16[16,4096]{1,0:T(8,128)(2,1)S(1)} %fusion.2.refs_5_.refs_1_), channel_id=1, source_target_pairs={{0,1},{1,0},{2,3},{3,2},{4,5},{5,4},{6,7},{7,6},{8,9},{9,8},{10,11... | collective-permute-start | bytes 393224 | tf_op jit(solution)/shard_map/ppermute | solution.py:371
  39.9 5.9 %collective-permute-start.5 = (bf16[16,4096]{1,0:T(8,128)(2,1)S(1)}, bf16[16,4096]{1,0:T(8,128)(2,1)S(1)}, u32[]{:S(2)}, u32[]{:S(2)}) collective-permute-start(bf16[16,4096]{1,0:T(8,128)(2,1)S(1)} %fusion.2.refs_5_.refs_1_), channel_id=1, source_target_pairs={{0,2},{1,3},{2,0},{3,1},{4,6},{5,7},{6,4},{7,5},{8,10},{9,11},{10,... | collective-permute-start | bytes 393224 | tf_op jit(solution)/shard_map/ppermute | solution.py:371
  45.8 5.1 %collective-permute-start.10 = (bf16[16,4096]{1,0:T(8,128)(2,1)S(1)}, bf16[16,4096]{1,0:T(8,128)(2,1)S(1)}, u32[]{:S(2)}, u32[]{:S(2)}) collective-permute-start(bf16[16,4096]{1,0:T(8,128)(2,1)S(1)} %collective-permute-done.7.refs_1_), channel_id=1, source_target_pairs={{0,4},{4,0},{8,12},{12,8},{1,5},{5,1},{9,13},{13,9},{2,6},{6,2},{1... | collective-permute-start | bytes 393224 | tf_op jit(solution)/shard_map/ppermute | solution.py:374
  47.4 5.3 %collective-permute-start.11 = (bf16[16,4096]{1,0:T(8,128)(2,1)S(1)}, bf16[16,4096]{1,0:T(8,128)(2,1)S(1)}, u32[]{:S(2)}, u32[]{:S(2)}) collective-permute-start(bf16[16,4096]{1,0:T(8,128)(2,1)S(1)} %collective-permute-done.7.refs_1_), channel_id=1, source_target_pairs={{0,1},{1,0},{2,3},{3,2},{4,5},{5,4},{6,7},{7,6},{8,9},{9,8},{10,11... | collective-permute-start | bytes 393224 | tf_op jit(solution)/shard_map/ppermute | solution.py:371
  51.0 5.9 %collective-permute-start.16 = (bf16[16,4096]{1,0:T(8,128)(2,1)S(1)}, bf16[16,4096]{1,0:T(8,128)(2,1)S(1)}, u32[]{:S(2)}, u32[]{:S(2)}) collective-permute-start(bf16[16,4096]{1,0:T(8,128)(2,1)S(1)} %collective-permute-done.10.refs_1_), channel_id=1, source_target_pairs={{0,2},{1,3},{2,0},{3,1},{4,6},{5,7},{6,4},{7,5},{8,10},{9,11},{10,... | collective-permute-start | bytes 393224 | tf_op jit(solution)/shard_map/ppermute | solution.py:371
  52.4 5.1 %collective-permute-start.17 = (bf16[16,4096]{1,0:T(8,128)(2,1)S(1)}, bf16[16,4096]{1,0:T(8,128)(2,1)S(1)}, u32[]{:S(2)}, u32[]{:S(2)}) collective-permute-start(bf16[16,4096]{1,0:T(8,128)(2,1)S(1)} %collective-permute-done.10.refs_1_), channel_id=1, source_target_pairs={{0,1},{1,0},{2,3},{3,2},{4,5},{5,4},{6,7},{7,6},{8,9},{9,8},{10,11... | collective-permute-start | bytes 393224 | tf_op jit(solution)/shard_map/ppermute | solution.py:371
  55.3 7.0 %collective-permute-start.13 = (bf16[32,4096]{1,0:T(8,128)(2,1)S(1)}, bf16[32,4096]{1,0:T(8,128)(2,1)S(1)}, u32[]{:S(2)}, u32[]{:S(2)}) collective-permute-start(bf16[32,4096]{1,0:T(8,128)(2,1)S(1)} %get-tuple-element.39.refs_7_), channel_id=1, source_target_pairs={{0,1},{1,0},{2,3},{3,2},{4,5},{5,4},{6,7},{7,6},{8,9},{9,8},{10,11... | collective-permute-start | bytes 786440 | tf_op jit(solution)/shard_map/ppermute | solution.py:371
  56.9 23.6 %collective-permute-start.31 = (bf16[8,16,256]{2,1,0:T(8,128)(2,1)S(1)}, bf16[8,16,256]{2,1,0:T(8,128)(2,1)S(1)}, u32[]{:S(2)}, u32[]{:S(2)}) collective-permute-start(bf16[8,16,256]{2,1,0:T(8,128)(2,1)S(1)} %bitcast.23), channel_id=1, source_target_pairs={{0,1},{1,0},{2,3},{3,2},{4,5},{5,4},{6,7},{7,6},{8,9},{9,8},{10,11... | collective-permute-start | bytes 196616 | tf_op jit(solution)/shard_map/ppermute | solution.py:486
  57.5 18.5 %collective-permute-start.28 = (bf16[16,4096]{1,0:T(8,128)(2,1)S(1)}, bf16[16,4096]{1,0:T(8,128)(2,1)S(1)}, u32[]{:S(2)}, u32[]{:S(2)}) collective-permute-start(bf16[16,4096]{1,0:T(8,128)(2,1)S(1)} %collective-permute-done.5.refs_2_), channel_id=1, source_target_pairs={{0,1},{1,0},{2,3},{3,2},{4,5},{5,4},{6,7},{7,6},{8,9},{9,8},{10,11... | collective-permute-start | bytes 393224 | tf_op jit(solution)/shard_map/ppermute | solution.py:371
  57.5 7.8 %collective-permute-start.23 = (bf16[16,4096]{1,0:T(8,128)(2,1)S(1)}, bf16[16,4096]{1,0:T(8,128)(2,1)S(1)}, u32[]{:S(2)}, u32[]{:S(2)}) collective-permute-start(bf16[16,4096]{1,0:T(8,128)(2,1)S(1)} %collective-permute-done.8.refs_1_), channel_id=1, source_target_pairs={{0,1},{1,0},{2,3},{3,2},{4,5},{5,4},{6,7},{7,6},{8,9},{9,8},{10,11... | collective-permute-start | bytes 393224 | tf_op jit(solution)/shard_map/ppermute | solution.py:371
  58.2 5.6 %collective-permute-start.22 = (bf16[16,4096]{1,0:T(8,128)(2,1)S(1)}, bf16[16,4096]{1,0:T(8,128)(2,1)S(1)}, u32[]{:S(2)}, u32[]{:S(2)}) collective-permute-start(bf16[16,4096]{1,0:T(8,128)(2,1)S(1)} %collective-permute-done.8.refs_1_), channel_id=1, source_target_pairs={{0,2},{1,3},{2,0},{3,1},{4,6},{5,7},{6,4},{7,5},{8,10},{9,11},{10,... | collective-permute-start | bytes 393224 | tf_op jit(solution)/shard_map/ppermute | solution.py:371
  63.8 5.7 %collective-permute-start.14 = (bf16[16,4096]{1,0:T(8,128)(2,1)S(1)}, bf16[16,4096]{1,0:T(8,128)(2,1)S(1)}, u32[]{:S(2)}, u32[]{:S(2)}) collective-permute-start(bf16[16,4096]{1,0:T(8,128)(2,1)S(1)} %add_convert_fusion.6.refs_8_), channel_id=1, source_target_pairs={{0,2},{1,3},{2,0},{3,1},{4,6},{5,7},{6,4},{7,5},{8,10},{9,11},{10,... | collective-permute-start | bytes 393224 | tf_op jit(solution)/shard_map/ppermute | solution.py:371
  65.3 8.8 %collective-permute-start.20 = (bf16[16,4096]{1,0:T(8,128)(2,1)S(1)}, bf16[16,4096]{1,0:T(8,128)(2,1)S(1)}, u32[]{:S(2)}, u32[]{:S(2)}) collective-permute-start(bf16[16,4096]{1,0:T(8,128)(2,1)S(1)} %add_convert_fusion.4.refs_9_.refs_8_), channel_id=1, source_target_pairs={{0,2},{1,3},{2,0},{3,1},{4,6},{5,7},{6,4},{7,5},{8,10},{9,11},{10,... | collective-permute-start | bytes 393224 | tf_op jit(solution)/shard_map/ppermute | solution.py:371
  69.5 12.9 %collective-permute-start.15 = (bf16[16,4096]{1,0:T(8,128)(2,1)S(1)}, bf16[16,4096]{1,0:T(8,128)(2,1)S(1)}, u32[]{:S(2)}, u32[]{:S(2)}) collective-permute-start(bf16[16,4096]{1,0:T(8,128)(2,1)S(1)} %add_convert_fusion.5.refs_10_), channel_id=1, source_target_pairs={{0,8},{4,12},{8,0},{12,4},{1,9},{5,13},{9,1},{13,5},{2,10},{6,14},... | collective-permute-start | bytes 393224 | tf_op jit(solution)/shard_map/ppermute | solution.py:374
  72.1 6.6 %collective-permute-start.26 = (bf16[16,4096]{1,0:T(8,128)(2,1)S(1)}, bf16[16,4096]{1,0:T(8,128)(2,1)S(1)}, u32[]{:S(2)}, u32[]{:S(2)}) collective-permute-start(bf16[16,4096]{1,0:T(8,128)(2,1)S(1)} %add_convert_fusion.2.refs_9_), channel_id=1, source_target_pairs={{0,2},{1,3},{2,0},{3,1},{4,6},{5,7},{6,4},{7,5},{8,10},{9,11},{10,... | collective-permute-start | bytes 393224 | tf_op jit(solution)/shard_map/ppermute | solution.py:371
  74.2 8.3 %collective-permute-start.21 = (bf16[16,4096]{1,0:T(8,128)(2,1)S(1)}, bf16[16,4096]{1,0:T(8,128)(2,1)S(1)}, u32[]{:S(2)}, u32[]{:S(2)}) collective-permute-start(bf16[16,4096]{1,0:T(8,128)(2,1)S(1)} %add_convert_fusion.3.refs_11_), channel_id=1, source_target_pairs={{0,12},{4,8},{8,4},{12,0},{1,13},{5,9},{9,5},{13,1},{2,14},{6,10},... | collective-permute-start | bytes 393224 | tf_op jit(solution)/shard_map/ppermute | solution.py:374
  78.8 6.2 %collective-permute-start.27 = (bf16[16,4096]{1,0:T(8,128)(2,1)S(1)}, bf16[16,4096]{1,0:T(8,128)(2,1)S(1)}, u32[]{:S(2)}, u32[]{:S(2)}) collective-permute-start(bf16[16,4096]{1,0:T(8,128)(2,1)S(1)} %add_convert_fusion.1), channel_id=1, source_target_pairs={{0,4},{4,0},{8,12},{12,8},{1,5},{5,1},{9,13},{13,9},{2,6},{6,2},{1... | collective-permute-start | bytes 393224 | tf_op jit(solution)/shard_map/ppermute | solution.py:374
  80.3 5.6 %collective-permute-start.30 = (bf16[16,4096]{1,0:T(8,128)(2,1)S(1)}, bf16[16,4096]{1,0:T(8,128)(2,1)S(1)}, u32[]{:S(2)}, u32[]{:S(2)}) collective-permute-start(bf16[16,4096]{1,0:T(8,128)(2,1)S(1)} %add_convert_fusion), channel_id=1, source_target_pairs={{0,2},{1,3},{2,0},{3,1},{4,6},{5,7},{6,4},{7,5},{8,10},{9,11},{10,... | collective-permute-start | bytes 393224 | tf_op jit(solution)/shard_map/ppermute | solution.py:371
  (16 other events, 51.4 us)

commit v15 on v14

--- a/solution.py
+++ b/solution.py
@@ -72,9 +72,30 @@
     )(*arrays, *after)
 
 
-def prepare_kernel(ep_count, blocks, weight_at, place, *refs):
+def normalize_kernel(kept, got, hidden, gain, residual, normed):
+    wide = hidden[...].astype(jnp.float32) + (kept[...] + got[...].astype(jnp.float32))
+    residual[...] = wide.astype(jnp.bfloat16)
+    wide = residual[...].astype(jnp.float32)
+    square = jnp.mean(wide * wide, axis=1, keepdims=True)
+    normed[...] = (wide * lax.rsqrt(square + EPSILON) * gain[...]).astype(jnp.bfloat16)
+
+
+def normalize_call(kept, got, hidden, gain):
+    rows = jax.ShapeDtypeStruct(hidden.shape, jnp.bfloat16)
+    return pl.pallas_call(
+        normalize_kernel,
+        out_shape=[rows, rows],
+        in_specs=[WHOLE] * 4,
+        out_specs=[WHOLE] * 2,
+        compiler_params=pltpu.CompilerParams(vmem_limit_bytes=VMEM_LIMIT),
+        cost_estimate=EXPERT_COST,
+        name="normalize",
+    )(kept, got, hidden, gain)
+
+
+def prepare_kernel(ep_count, blocks, weight_at, lens, owners, place, *refs):
     payloads = refs[:ep_count]
-    row_weights = refs[-1]
+    row_weights, pages_ref, ranks = refs[-3:]
     tokens = row_weights.shape[0] // ep_count
     row_count = tokens // blocks
     wide = (tokens, payloads[0].shape[1])
@@ -91,30 +112,7 @@
         column = jnp.sum(jnp.where(here, by_token, 0.0), axis=1, keepdims=True)
         row_weights[step * tokens : (step + 1) * tokens, :] = jnp.broadcast_to(column, (tokens, HD))
 
-
-def prepare_call(place, arrived, after, blocks, tokens, weight_at):
-    ep_count = len(arrived)
-    return pl.pallas_call(
-        lambda *refs: prepare_kernel(ep_count, blocks, weight_at, *refs),
-        out_shape=jax.ShapeDtypeStruct((ep_count * tokens, HD), jnp.float32),
-        in_specs=[SCALARS] + [WHOLE] * ep_count + [ANYWHERE],
-        out_specs=WHOLE,
-        compiler_params=pltpu.CompilerParams(vmem_limit_bytes=VMEM_LIMIT),
-        cost_estimate=EXPERT_COST,
-        name="prepare",
-    )(place, *arrived, after)
-
-
-def attend_kernel(ep_count, held, tokens, row_blocks, all_open, lens, place, counts, owners, queries, *refs):
-    blocks = refs[:ep_count]
-    out_weight = refs[ep_count]
-    kept_ref, sent_ref, pages_ref = refs[ep_count + 1 : ep_count + 4]
-    scores, projected, ranks = refs[ep_count + 4 :]
-    heads = queries.shape[1] // HD
     ep_index = place[0]
-    block_index = place[1]
-    suffix = ep_count * tokens
-
     page_count = owners.shape[0]
     pages_here = page_count // ep_count
     page_size = tokens // pages_here
@@ -132,12 +130,41 @@
 
             @pl.when(owners[page] == ep_index)
             def _(step=step, source=source, k=k, page=page):
-                first = held + k * page_size
-                entries = blocks[step][first : first + page_size, :]
+                first = weight_at - tokens + k * page_size
+                entries = payloads[step][first : first + page_size, :]
                 row = lax.broadcasted_iota(jnp.int32, entries.shape, 0) + k * page_size
                 entries = jnp.where(row < lens[source], entries.astype(jnp.float32), 0.0)
                 at = pl.multiple_of(ranks[page] * page_size, page_size)
                 pages_ref[pl.ds(at, page_size), :] = entries.astype(jnp.bfloat16)
+
+
+def prepare_call(lens, owners, place, arrived, after, blocks, tokens, weight_at, own_most):
+    ep_count = len(arrived)
+    page_size = tokens * ep_count // owners.shape[0]
+    return pl.pallas_call(
+        lambda *refs: prepare_kernel(ep_count, blocks, weight_at, *refs),
+        out_shape=[
+            jax.ShapeDtypeStruct((ep_count * tokens, HD), jnp.float32),
+            jax.ShapeDtypeStruct((own_most * page_size, 2 * HD), jnp.bfloat16),
+        ],
+        in_specs=[SCALARS] * 3 + [WHOLE] * ep_count + [ANYWHERE],
+        out_specs=[WHOLE] * 2,
+        scratch_shapes=[pltpu.SMEM((owners.shape[0],), jnp.int32)],
+        compiler_params=pltpu.CompilerParams(vmem_limit_bytes=VMEM_LIMIT),
+        cost_estimate=EXPERT_COST,
+        name="prepare",
+    )(lens, owners, place, *arrived, after)
+
+
+def attend_kernel(ep_count, held, tokens, row_blocks, all_open, lens, place, counts, queries, *refs):
+    blocks = refs[:ep_count]
+    out_weight = refs[ep_count]
+    kept_ref, sent_ref = refs[ep_count + 1 : ep_count + 3]
+    scores, projected = refs[ep_count + 3 :]
+    heads = queries.shape[1] // HD
+    ep_index = place[0]
+    block_index = place[1]
+    suffix = ep_count * tokens
 
     own_start = jnp.int32(0)
     for j in range(ep_count):
@@ -210,27 +237,24 @@
 
 
 def attend_call(
-    lens, place, counts, owners, queries, arrived, out_weight, held, blocks, own_most, all_open
+    lens, place, counts, queries, arrived, out_weight, held, blocks, all_open
 ):
     tokens = queries.shape[0]
     ep_count = len(arrived)
     model_width = out_weight.shape[1]
     heads = queries.shape[1] // HD
     keys = ep_count * (held + tokens)
-    page_size = tokens * ep_count // owners.shape[0]
     return pl.pallas_call(
         lambda *refs: attend_kernel(ep_count, held, tokens, blocks, all_open, *refs),
         out_shape=[
             jax.ShapeDtypeStruct((tokens // 2, model_width), jnp.float32),
             jax.ShapeDtypeStruct((tokens // 2, model_width), jnp.bfloat16),
-            jax.ShapeDtypeStruct((own_most * page_size, 2 * HD), jnp.bfloat16),
         ],
-        in_specs=[SCALARS] * 4 + [WHOLE] * (ep_count + 2),
-        out_specs=[WHOLE] * 3,
+        in_specs=[SCALARS] * 3 + [WHOLE] * (ep_count + 2),
+        out_specs=[WHOLE] * 2,
         scratch_shapes=[
             pltpu.VMEM((min(ROWS, heads * tokens), ep_count * held), jnp.float32),
             pltpu.VMEM((tokens, model_width), jnp.float32),
-            pltpu.SMEM((owners.shape[0],), jnp.int32),
         ],
         compiler_params=pltpu.CompilerParams(vmem_limit_bytes=VMEM_LIMIT),
         cost_estimate=pl.CostEstimate(
@@ -239,7 +263,7 @@
             transcendentals=heads * tokens * keys,
         ),
         name="attend",
-    )(lens, place, counts, owners, queries, *arrived, out_weight)
+    )(lens, place, counts, queries, *arrived, out_weight)
 
 
 def expert_kernel(count, steps, blocks, row_weights, *refs):
@@ -385,39 +409,31 @@
             gives.append(give.astype(jnp.bfloat16))
             kept = kept[:half].astype(jnp.float32) + got[:half].astype(jnp.float32)
             got = exchange(gives[-1], bit)
-        return kept.astype(jnp.float32) + got.astype(jnp.float32), gives, received
+        return kept.astype(jnp.float32), got, gives, received
 
     own_most = 2 * (tokens // page_size)
     own_slots = block_index * row_count + jnp.arange(row_count, dtype=jnp.int32)
     rows_filled = own_slots < span_lengths[ep_index]
     core = jnp.broadcast_to(tp_index.astype(jnp.int32), (1, 1, 2 * HD))
     core, row_mask = lax.optimization_barrier((core, rows_filled.astype(jnp.int32)))
+    wide_gain = norm_gain[None, :]
     own_hidden = lax.dynamic_slice_in_dim(hidden_in, block_index * row_count, row_count, 0)
     held_out, held_gate_up, held_down, _ = hold_call(
-        [out_weight, gate_up, down_weight], payload, place, row_mask, core, own_hidden
-    )
-    kept, sent, head_pages = attend_call(
+        [out_weight, gate_up, down_weight], payload, place, row_mask, core, own_hidden, wide_gain
+    )
+    kept, sent = attend_call(
         span_lengths,
         place,
         counts,
-        new_owner,
         queries,
         arrived,
         held_out,
         held,
         blocks,
-        own_most,
         all_open,
     )
-    head_pages = head_pages.reshape(own_most, page_size, 2 * HD)
-    heads_out, _, _ = scatter(kept, sent)
-    residual = (own_hidden.astype(jnp.float32) + heads_out).astype(jnp.bfloat16)
+    residual, normed = normalize_call(*scatter(kept, sent)[:2], own_hidden, wide_gain)
     resid_wide = residual.astype(jnp.float32)
-    normed = (
-        resid_wide
-        * lax.rsqrt(jnp.mean(resid_wide * resid_wide, axis=1, keepdims=True) + EPSILON)
-        * norm_gain
-    ).astype(jnp.bfloat16)
 
     def group_rows(have, bits, before=None):
         for bit in bits:
@@ -426,7 +442,18 @@
                 have[1], before = lax.optimization_barrier([have[1], before])
         return have
 
-    row_weights = prepare_call(place, arrived, normed, blocks, tokens, held + tokens)
+    row_weights, head_pages = prepare_call(
+        span_lengths,
+        new_owner,
+        place,
+        arrived,
+        normed,
+        blocks,
+        tokens,
+        held + tokens,
+        own_most,
+    )
+    head_pages = head_pages.reshape(own_most, page_size, 2 * HD)
     ep_bits = [1 << place for place in reversed(range(ep_count.bit_length() - 1))]
     early = [exchange(normed, bit) for bit in bits + [1]]
     direct = [across(normed, bit) for bit in ep_bits]
@@ -453,22 +480,24 @@
     sent, given, finished = None, [], []
     for turn, group in enumerate(groups):
         after = [sent] if turn >= 1 else []
-        after += given[turn - 2 : turn] if turn >= 2 else []
-        if turn == len(groups) - 1:
-            after += finished[: turn - 1]
+        if turn == 1:
+            after += []
+        elif turn == len(groups) - 1:
+            after += given[turn - 1 : turn]
+        elif turn >= 2:
+            after += given[turn - 2 : turn]
         haves = {0: own_have, leading: lead_have}
         for step in group:
             if step not in haves:
                 piece = crossed[step]
-                if turn > 1 and bits:
-                    piece, reached = lax.optimization_barrier((piece, reached))
                 haves[step] = group_rows([piece], bits + [1], sent if turn == 1 else received)
                 reached = haves[step][1]
         have = [haves[step][spot] for spot in range(blocks) for step in group]
         kept, sent = expert_call(
             tuple(group), blocks, row_weights, have, held_gate_up, held_down, after
         )
-        own, gives, received = scatter(kept, sent)
+        own, got, gives, received = scatter(kept, sent)
+        own = own + got.astype(jnp.float32)
         given.append(gives[0] if gives else own.astype(jnp.bfloat16))
         finished.append(own.astype(jnp.bfloat16))
         for spot, step in enumerate(group):

time: 87.1 us -> 86.4 us (level)
  waiting for transfers between devices: 23.4 us -> 21.9 us
  other arithmetic: 4.8 us -> 3.63 us
  starting transfers between devices: 27.4 us -> 28.3 us
    reduce_sum x1 -> x0, other arithmetic: 1.09 us -> none  [local(): jnp.mean(resid_wide * resid_wide, axis=1, keepdims=True) + EPSILON]
    unnamed x19 -> x21, local copies, waits for them, and re-layouts: 8.9 us -> 9.62 us
  transfers between devices with their start and end apart: 32 -> 32, of which waited for: 15 -> 14; matrix products, arithmetic and copies ran while one was open for 5% -> 5% of each run, Pallas kernels for 15% -> 16%
where the time goes in v15:
time: 86.4 us; the launch traced here: 86 us
  starting transfers between devices  28.3 us (33%)
  waiting for transfers between devices  21.9 us (25%)
  Pallas kernels  17.1 us (20%)
  local copies, waits for them, and re-layouts  14.1 us (16%)
  other arithmetic  3.63 us (4%)
  between operations  0.99 us (1%)
    ppermute x22, starting transfers between devices, local(): lax.ppermute(value, ('kv', 'tp'), [(i, i ^ bit) for i in range(blocks)])  13.5 us
    ppermute x22, waiting for transfers between devices, local(): lax.ppermute(value, ('kv', 'tp'), [(i, i ^ bit) for i in range(blocks)])  11.3 us
    pallas_call x4, Pallas kernels, expert_call(): pl.pallas_call(lambda *refs: expert_kernel(len(have), steps, blocks, *ref...  10.7 us
    ppermute x6, waiting for transfers between devices, local(): lax.ppermute(value, 'ep', [(i, i ^ step) for i in range(ep_count)])  10.2 us
    unnamed x21, local copies, waits for them, and re-layouts  9.62 us
    ppermute x6, starting transfers between devices, local(): lax.ppermute(value, 'ep', [(i, i ^ step) for i in range(ep_count)])  8.52 us
    ppermute x3, starting transfers between devices, local(): lax.ppermute(payload, 'ep', [(i, i ^ step) for i in range(ep_count)])  5.76 us
    pallas_call x1, Pallas kernels, attend_call(): pl.pallas_call(lambda *refs: attend_kernel(ep_count, held, tokens, blocks...  3.4 us
  transfers between devices with their start and end apart: 32, of which 14 were waited for; matrix products, arithmetic and copies ran while one was open for 5% of the time, Pallas kernels for 16%

profile of v15, /device:TPU:0, one launch (start us, length us, event | category | flops | bytes accessed | tf_op | source)
XLA Modules:
  0.0 86.0 jit_solution(10204012482030205080)
XLA Ops:
  4.8 5.1 %collective-permute-start.2 = (bf16[336,256]{1,0:T(8,128)(2,1)S(1)}, bf16[336,256]{1,0:T(8,128)(2,1)S(1)}, u32[]{:S(2)}, u32[]{:S(2)}) collective-permute-start(bf16[336,256]{1,0:T(8,128)(2,1)S(1)} %pad_maximum_fusion.refs_3_.refs_4_), channel_id=1, source_target_pairs={{0,12},{4,8},{8,4},{12,0},{1,13},{5,9},{9,5},{13,1},{2,14},{6,10},... | collective-permute-start | bytes 516104 | tf_op jit(solution)/shard_map/ppermute | solution.py:383
  13.5 3.4 %copy-done.1 = bf16[1024,4096]{1,0:T(8,128)(2,1)S(1)} copy-done((bf16[1024,4096]{1,0:T(8,128)(2,1)S(1)}, bf16[1024,4096]{1,0:T(8,128)(2,1)}, u32[]{:S(2)}) %copy-start.1) | copy-done | bytes 8388632
  16.9 2.8 %copy-done.2 = bf16[1,2,384,4096]{3,2,1,0:T(8,128)(2,1)S(1)} copy-done((bf16[1,2,384,4096]{3,2,1,0:T(8,128)(2,1)S(1)}, bf16[1,2,384,4096]{3,2,1,0:T(8,128)(2,1)}, u32[]{:S(2)}) %copy-start.2) | copy-done | bytes 6291480
  19.7 1.9 %copy-done.3 = bf16[1,384,4096]{2,1,0:T(8,128)(2,1)S(1)} copy-done((bf16[1,384,4096]{2,1,0:T(8,128)(2,1)S(1)}, bf16[1,384,4096]{2,1,0:T(8,128)(2,1)}, u32[]{:S(2)}) %copy-start.3) | copy-done | bytes 3145752
  22.3 1.8 %hold.1 = (bf16[1024,4096]{1,0:T(8,128)(2,1)S(1)}, bf16[1,2,384,4096]{3,2,1,0:T(8,128)(2,1)S(1)}, bf16[1,384,4096]{2,1,0:T(8,128)(2,1)S(1)}, f32[8,128]{1,0:T(8,128)}) custom-call(bf16[1024,4096]{1,0:T(8,128)(2,1)S(1)} %copy-done.1, bf16[1,2,384,4096]{3,2,1,0:T(8,128)(2,1)S(1)} %copy-done.2, bf16[1,384,4096]{2,1,0:T(8,128)(2,1)S(1)} %copy-done.3, ...), custom_call_target="tpu_custom_call" | custom-call | bytes 35651584 | tf_op jit(solution)/shard_map/hold/pallas_call | solution.py:62
  24.5 3.4 %attend.1 = (f32[32,4096]{1,0:T(8,128)S(1)}, bf16[32,4096]{1,0:T(8,128)(2,1)S(1)}) custom-call(s32[4]{0:T(128)S(1)} %copy-done.7, s32[2]{0:T(128)S(1)} %pad_add_fusion.refs_4_.refs_1_.refs_2_, s32[1]{0:T(128)} %constant.48.clone.1.refs_2_, bf16[64,1024]{1,0:T(8,128)(2,1)S(1)} %copy-done.4, bf16[336,256]{1,0:T(8,128)(2,1)S(1)} %pad_maximum_fusion.refs_3_.refs_4_, ...), custom_call_target="tpu_custom_call" | custom-call | flops 872415232 | bytes 8388608 | tf_op jit(solution)/shard_map/attend/pallas_call | solution.py:247
  28.0 1.5 %collective-permute-done.3 = bf16[32,4096]{1,0:T(8,128)(2,1)S(1)} collective-permute-done((bf16[32,4096]{1,0:T(8,128)(2,1)S(1)}, bf16[32,4096]{1,0:T(8,128)(2,1)S(1)}, u32[]{:S(2)}, u32[]{:S(2)}) %collective-permute-start.3) | collective-permute-done | bytes 262176 | tf_op jit(solution)/shard_map/ppermute | solution.py:395
  29.6 1.6 %collective-permute-start.4 = (bf16[16,4096]{1,0:T(8,128)(2,1)S(1)}, bf16[16,4096]{1,0:T(8,128)(2,1)S(1)}, u32[]{:S(2)}, u32[]{:S(2)}) collective-permute-start(bf16[16,4096]{1,0:T(8,128)(2,1)S(1)} %get-tuple-element.64), channel_id=1, source_target_pairs={{0,2},{1,3},{2,0},{3,1},{4,6},{5,7},{6,4},{7,5},{8,10},{9,11},{10,... | collective-permute-start | bytes 393224 | tf_op jit(solution)/shard_map/ppermute | solution.py:395
  31.1 4.1 %collective-permute-done.4.got = bf16[16,4096]{1,0:T(8,128)(2,1)S(1)} collective-permute-done((bf16[16,4096]{1,0:T(8,128)(2,1)S(1)}, bf16[16,4096]{1,0:T(8,128)(2,1)S(1)}, u32[]{:S(2)}, u32[]{:S(2)}) %collective-permute-start.4) | collective-permute-done | bytes 131104 | tf_op jit(solution)/shard_map/ppermute | solution.py:395
  36.5 2.9 %collective-permute-start.7 = (bf16[16,4096]{1,0:T(8,128)(2,1)S(1)}, bf16[16,4096]{1,0:T(8,128)(2,1)S(1)}, u32[]{:S(2)}, u32[]{:S(2)}) collective-permute-start(bf16[16,4096]{1,0:T(8,128)(2,1)S(1)} %get-tuple-element.36.refs_7_.refs_1_), channel_id=1, source_target_pairs={{0,8},{4,12},{8,0},{12,4},{1,9},{5,13},{9,1},{13,5},{2,10},{6,14},... | collective-permute-start | bytes 393224 | tf_op jit(solution)/shard_map/ppermute | solution.py:398
  39.4 1.5 %collective-permute-start.5 = (bf16[16,4096]{1,0:T(8,128)(2,1)S(1)}, bf16[16,4096]{1,0:T(8,128)(2,1)S(1)}, u32[]{:S(2)}, u32[]{:S(2)}) collective-permute-start(bf16[16,4096]{1,0:T(8,128)(2,1)S(1)} %get-tuple-element.36.refs_7_.refs_1_), channel_id=1, source_target_pairs={{0,2},{1,3},{2,0},{3,1},{4,6},{5,7},{6,4},{7,5},{8,10},{9,11},{10,... | collective-permute-start | bytes 393224 | tf_op jit(solution)/shard_map/ppermute | solution.py:395
  42.6 2.4 %collective-permute-done.7.refs_1_ = bf16[16,4096]{1,0:T(8,128)(2,1)S(1)} collective-permute-done((bf16[16,4096]{1,0:T(8,128)(2,1)S(1)}, bf16[16,4096]{1,0:T(8,128)(2,1)S(1)}, u32[]{:S(2)}, u32[]{:S(2)}) %collective-permute-start.7) | collective-permute-done | bytes 131104 | tf_op jit(solution)/shard_map/ppermute | solution.py:398
  45.4 1.5 %collective-permute-start.9 = (bf16[16,4096]{1,0:T(8,128)(2,1)S(1)}, bf16[16,4096]{1,0:T(8,128)(2,1)S(1)}, u32[]{:S(2)}, u32[]{:S(2)}) collective-permute-start(bf16[16,4096]{1,0:T(8,128)(2,1)S(1)} %collective-permute-done.7.refs_1_), channel_id=1, source_target_pairs={{0,2},{1,3},{2,0},{3,1},{4,6},{5,7},{6,4},{7,5},{8,10},{9,11},{10,... | collective-permute-start | bytes 393224 | tf_op jit(solution)/shard_map/ppermute | solution.py:395
  46.9 3.6 %collective-permute-done.10.refs_1_ = bf16[16,4096]{1,0:T(8,128)(2,1)S(1)} collective-permute-done((bf16[16,4096]{1,0:T(8,128)(2,1)S(1)}, bf16[16,4096]{1,0:T(8,128)(2,1)S(1)}, u32[]{:S(2)}, u32[]{:S(2)}) %collective-permute-start.10) | collective-permute-done | bytes 131104 | tf_op jit(solution)/shard_map/ppermute | solution.py:398
  50.5 1.5 %collective-permute-start.16 = (bf16[16,4096]{1,0:T(8,128)(2,1)S(1)}, bf16[16,4096]{1,0:T(8,128)(2,1)S(1)}, u32[]{:S(2)}, u32[]{:S(2)}) collective-permute-start(bf16[16,4096]{1,0:T(8,128)(2,1)S(1)} %collective-permute-done.10.refs_1_), channel_id=1, source_target_pairs={{0,2},{1,3},{2,0},{3,1},{4,6},{5,7},{6,4},{7,5},{8,10},{9,11},{10,... | collective-permute-start | bytes 393224 | tf_op jit(solution)/shard_map/ppermute | solution.py:395
  52.2 2.7 %experts.4 = (bf16[32,4096]{1,0:T(8,128)(2,1)S(1)}, bf16[32,4096]{1,0:T(8,128)(2,1)S(1)}) custom-call(f32[256,128]{1,0:T(8,128)S(1)} %get-tuple-element.38.refs_0_, bf16[16,4096]{1,0:T(8,128)(2,1)S(1)} %collective-permute-done.7.refs_1_, bf16[16,4096]{1,0:T(8,128)(2,1)S(1)} %collective-permute-done.9.refs_2_, ...), custom_call_target="tpu_custom_call" | custom-call | flops 1024 | bytes 1024 | tf_op jit(solution)/shard_map/experts/pallas_call | solution.py:310
  57.0 1.5 %collective-permute-start.22 = (bf16[16,4096]{1,0:T(8,128)(2,1)S(1)}, bf16[16,4096]{1,0:T(8,128)(2,1)S(1)}, u32[]{:S(2)}, u32[]{:S(2)}) collective-permute-start(bf16[16,4096]{1,0:T(8,128)(2,1)S(1)} %collective-permute-done.8.refs_1_), channel_id=1, source_target_pairs={{0,2},{1,3},{2,0},{3,1},{4,6},{5,7},{6,4},{7,5},{8,10},{9,11},{10,... | collective-permute-start | bytes 393224 | tf_op jit(solution)/shard_map/ppermute | solution.py:395
  58.7 2.7 %experts.5 = (bf16[32,4096]{1,0:T(8,128)(2,1)S(1)}, bf16[32,4096]{1,0:T(8,128)(2,1)S(1)}) custom-call(f32[256,128]{1,0:T(8,128)S(1)} %get-tuple-element.38.refs_0_, bf16[16,4096]{1,0:T(8,128)(2,1)S(1)} %collective-permute-done.10.refs_1_, bf16[16,4096]{1,0:T(8,128)(2,1)S(1)} %collective-permute-done.16.refs_2_, ...), custom_call_target="tpu_custom_call" | custom-call | flops 1024 | bytes 1024 | tf_op jit(solution)/shard_map/experts/pallas_call | solution.py:310
  65.7 2.7 %experts.6 = (bf16[32,4096]{1,0:T(8,128)(2,1)S(1)}, bf16[32,4096]{1,0:T(8,128)(2,1)S(1)}) custom-call(f32[256,128]{1,0:T(8,128)S(1)} %get-tuple-element.38.refs_0_, bf16[16,4096]{1,0:T(8,128)(2,1)S(1)} %collective-permute-done.8.refs_1_, bf16[16,4096]{1,0:T(8,128)(2,1)S(1)} %collective-permute-done.22.refs_2_, ...), custom_call_target="tpu_custom_call" | custom-call | flops 1024 | bytes 1024 | tf_op jit(solution)/shard_map/experts/pallas_call | solution.py:310
  68.7 2.5 %collective-permute-start.15 = (bf16[16,4096]{1,0:T(8,128)(2,1)S(1)}, bf16[16,4096]{1,0:T(8,128)(2,1)S(1)}, u32[]{:S(2)}, u32[]{:S(2)}) collective-permute-start(bf16[16,4096]{1,0:T(8,128)(2,1)S(1)} %add_convert_fusion.5), channel_id=1, source_target_pairs={{0,8},{4,12},{8,0},{12,4},{1,9},{5,13},{9,1},{13,5},{2,10},{6,14},... | collective-permute-start | bytes 393224 | tf_op jit(solution)/shard_map/ppermute | solution.py:398
  71.3 2.2 %collective-permute-start.26 = (bf16[16,4096]{1,0:T(8,128)(2,1)S(1)}, bf16[16,4096]{1,0:T(8,128)(2,1)S(1)}, u32[]{:S(2)}, u32[]{:S(2)}) collective-permute-start(bf16[16,4096]{1,0:T(8,128)(2,1)S(1)} %add_convert_fusion.2.refs_8_), channel_id=1, source_target_pairs={{0,2},{1,3},{2,0},{3,1},{4,6},{5,7},{6,4},{7,5},{8,10},{9,11},{10,... | collective-permute-start | bytes 393224 | tf_op jit(solution)/shard_map/ppermute | solution.py:395
  73.5 1.8 %collective-permute-start.21 = (bf16[16,4096]{1,0:T(8,128)(2,1)S(1)}, bf16[16,4096]{1,0:T(8,128)(2,1)S(1)}, u32[]{:S(2)}, u32[]{:S(2)}) collective-permute-start(bf16[16,4096]{1,0:T(8,128)(2,1)S(1)} %add_convert_fusion.3), channel_id=1, source_target_pairs={{0,12},{4,8},{8,4},{12,0},{1,13},{5,9},{9,5},{13,1},{2,14},{6,10},... | collective-permute-start | bytes 393224 | tf_op jit(solution)/shard_map/ppermute | solution.py:398
  75.3 2.7 %experts.7 = (bf16[32,4096]{1,0:T(8,128)(2,1)S(1)}, bf16[32,4096]{1,0:T(8,128)(2,1)S(1)}) custom-call(f32[256,128]{1,0:T(8,128)S(1)} %get-tuple-element.38.refs_0_, bf16[16,4096]{1,0:T(8,128)(2,1)S(1)} %get-tuple-element.36.refs_7_.refs_1_, bf16[16,4096]{1,0:T(8,128)(2,1)S(1)} %collective-permute-done.5.refs_2_, ...), custom_call_target="tpu_custom_call" | custom-call | flops 1024 | bytes 1024 | tf_op jit(solution)/shard_map/experts/pallas_call | solution.py:310
  81.6 2.7 %collective-permute-done.27 = bf16[16,4096]{1,0:T(8,128)(2,1)S(1)} collective-permute-done((bf16[16,4096]{1,0:T(8,128)(2,1)S(1)}, bf16[16,4096]{1,0:T(8,128)(2,1)S(1)}, u32[]{:S(2)}, u32[]{:S(2)}) %collective-permute-start.27) | collective-permute-done | bytes 131104 | tf_op jit(solution)/shard_map/ppermute | solution.py:398
  (100 shorter events, 24.9 us)
Async XLA Ops:
  4.8 19.3 %collective-permute-start.2 = (bf16[336,256]{1,0:T(8,128)(2,1)S(1)}, bf16[336,256]{1,0:T(8,128)(2,1)S(1)}, u32[]{:S(2)}, u32[]{:S(2)}) collective-permute-start(bf16[336,256]{1,0:T(8,128)(2,1)S(1)} %pad_maximum_fusion.refs_3_.refs_4_), channel_id=1, source_target_pairs={{0,12},{4,8},{8,4},{12,0},{1,13},{5,9},{9,5},{13,1},{2,14},{6,10},... | collective-permute-start | bytes 516104 | tf_op jit(solution)/shard_map/ppermute | solution.py:383
  9.9 14.6 %collective-permute-start.1 = (bf16[336,256]{1,0:T(8,128)(2,1)S(1)}, bf16[336,256]{1,0:T(8,128)(2,1)S(1)}, u32[]{:S(2)}, u32[]{:S(2)}) collective-permute-start(bf16[336,256]{1,0:T(8,128)(2,1)S(1)} %pad_maximum_fusion.refs_3_.refs_4_), channel_id=1, source_target_pairs={{0,8},{4,12},{8,0},{12,4},{1,9},{5,13},{9,1},{13,5},{2,10},{6,14},... | collective-permute-start | bytes 516104 | tf_op jit(solution)/shard_map/ppermute | solution.py:383
  9.9 14.6 %collective-permute-start = (bf16[336,256]{1,0:T(8,128)(2,1)S(1)}, bf16[336,256]{1,0:T(8,128)(2,1)S(1)}, u32[]{:S(2)}, u32[]{:S(2)}) collective-permute-start(bf16[336,256]{1,0:T(8,128)(2,1)S(1)} %pad_maximum_fusion.refs_3_.refs_4_), channel_id=1, source_target_pairs={{0,4},{4,0},{8,12},{12,8},{1,5},{5,1},{9,13},{13,9},{2,6},{6,2},{1... | collective-permute-start | bytes 516104 | tf_op jit(solution)/shard_map/ppermute | solution.py:383
  29.6 5.6 %collective-permute-start.4 = (bf16[16,4096]{1,0:T(8,128)(2,1)S(1)}, bf16[16,4096]{1,0:T(8,128)(2,1)S(1)}, u32[]{:S(2)}, u32[]{:S(2)}) collective-permute-start(bf16[16,4096]{1,0:T(8,128)(2,1)S(1)} %get-tuple-element.64), channel_id=1, source_target_pairs={{0,2},{1,3},{2,0},{3,1},{4,6},{5,7},{6,4},{7,5},{8,10},{9,11},{10,... | collective-permute-start | bytes 393224 | tf_op jit(solution)/shard_map/ppermute | solution.py:395
  35.4 7.2 %collective-permute-start.8 = (bf16[16,4096]{1,0:T(8,128)(2,1)S(1)}, bf16[16,4096]{1,0:T(8,128)(2,1)S(1)}, u32[]{:S(2)}, u32[]{:S(2)}) collective-permute-start(bf16[16,4096]{1,0:T(8,128)(2,1)S(1)} %get-tuple-element.36.refs_7_.refs_1_), channel_id=1, source_target_pairs={{0,4},{4,0},{8,12},{12,8},{1,5},{5,1},{9,13},{13,9},{2,6},{6,2},{1... | collective-permute-start | bytes 393224 | tf_op jit(solution)/shard_map/ppermute | solution.py:398
  36.5 8.5 %collective-permute-start.7 = (bf16[16,4096]{1,0:T(8,128)(2,1)S(1)}, bf16[16,4096]{1,0:T(8,128)(2,1)S(1)}, u32[]{:S(2)}, u32[]{:S(2)}) collective-permute-start(bf16[16,4096]{1,0:T(8,128)(2,1)S(1)} %get-tuple-element.36.refs_7_.refs_1_), channel_id=1, source_target_pairs={{0,8},{4,12},{8,0},{12,4},{1,9},{5,13},{9,1},{13,5},{2,10},{6,14},... | collective-permute-start | bytes 393224 | tf_op jit(solution)/shard_map/ppermute | solution.py:398
  39.4 5.5 %collective-permute-start.6 = (bf16[16,4096]{1,0:T(8,128)(2,1)S(1)}, bf16[16,4096]{1,0:T(8,128)(2,1)S(1)}, u32[]{:S(2)}, u32[]{:S(2)}) collective-permute-start(bf16[16,4096]{1,0:T(8,128)(2,1)S(1)} %get-tuple-element.36.refs_7_.refs_1_), channel_id=1, source_target_pairs={{0,1},{1,0},{2,3},{3,2},{4,5},{5,4},{6,7},{7,6},{8,9},{9,8},{10,11... | collective-permute-start | bytes 393224 | tf_op jit(solution)/shard_map/ppermute | solution.py:395
  39.4 5.9 %collective-permute-start.5 = (bf16[16,4096]{1,0:T(8,128)(2,1)S(1)}, bf16[16,4096]{1,0:T(8,128)(2,1)S(1)}, u32[]{:S(2)}, u32[]{:S(2)}) collective-permute-start(bf16[16,4096]{1,0:T(8,128)(2,1)S(1)} %get-tuple-element.36.refs_7_.refs_1_), channel_id=1, source_target_pairs={{0,2},{1,3},{2,0},{3,1},{4,6},{5,7},{6,4},{7,5},{8,10},{9,11},{10,... | collective-permute-start | bytes 393224 | tf_op jit(solution)/shard_map/ppermute | solution.py:395
  45.3 5.1 %collective-permute-start.10 = (bf16[16,4096]{1,0:T(8,128)(2,1)S(1)}, bf16[16,4096]{1,0:T(8,128)(2,1)S(1)}, u32[]{:S(2)}, u32[]{:S(2)}) collective-permute-start(bf16[16,4096]{1,0:T(8,128)(2,1)S(1)} %collective-permute-done.7.refs_1_), channel_id=1, source_target_pairs={{0,4},{4,0},{8,12},{12,8},{1,5},{5,1},{9,13},{13,9},{2,6},{6,2},{1... | collective-permute-start | bytes 393224 | tf_op jit(solution)/shard_map/ppermute | solution.py:398
  46.9 5.3 %collective-permute-start.11 = (bf16[16,4096]{1,0:T(8,128)(2,1)S(1)}, bf16[16,4096]{1,0:T(8,128)(2,1)S(1)}, u32[]{:S(2)}, u32[]{:S(2)}) collective-permute-start(bf16[16,4096]{1,0:T(8,128)(2,1)S(1)} %collective-permute-done.7.refs_1_), channel_id=1, source_target_pairs={{0,1},{1,0},{2,3},{3,2},{4,5},{5,4},{6,7},{7,6},{8,9},{9,8},{10,11... | collective-permute-start | bytes 393224 | tf_op jit(solution)/shard_map/ppermute | solution.py:395
  50.5 5.9 %collective-permute-start.16 = (bf16[16,4096]{1,0:T(8,128)(2,1)S(1)}, bf16[16,4096]{1,0:T(8,128)(2,1)S(1)}, u32[]{:S(2)}, u32[]{:S(2)}) collective-permute-start(bf16[16,4096]{1,0:T(8,128)(2,1)S(1)} %collective-permute-done.10.refs_1_), channel_id=1, source_target_pairs={{0,2},{1,3},{2,0},{3,1},{4,6},{5,7},{6,4},{7,5},{8,10},{9,11},{10,... | collective-permute-start | bytes 393224 | tf_op jit(solution)/shard_map/ppermute | solution.py:395
  52.0 5.1 %collective-permute-start.17 = (bf16[16,4096]{1,0:T(8,128)(2,1)S(1)}, bf16[16,4096]{1,0:T(8,128)(2,1)S(1)}, u32[]{:S(2)}, u32[]{:S(2)}) collective-permute-start(bf16[16,4096]{1,0:T(8,128)(2,1)S(1)} %collective-permute-done.10.refs_1_), channel_id=1, source_target_pairs={{0,1},{1,0},{2,3},{3,2},{4,5},{5,4},{6,7},{7,6},{8,9},{9,8},{10,11... | collective-permute-start | bytes 393224 | tf_op jit(solution)/shard_map/ppermute | solution.py:395
  54.9 6.5 %collective-permute-start.13 = (bf16[32,4096]{1,0:T(8,128)(2,1)S(1)}, bf16[32,4096]{1,0:T(8,128)(2,1)S(1)}, u32[]{:S(2)}, u32[]{:S(2)}) collective-permute-start(bf16[32,4096]{1,0:T(8,128)(2,1)S(1)} %get-tuple-element.44.refs_7_), channel_id=1, source_target_pairs={{0,1},{1,0},{2,3},{3,2},{4,5},{5,4},{6,7},{7,6},{8,9},{9,8},{10,11... | collective-permute-start | bytes 786440 | tf_op jit(solution)/shard_map/ppermute | solution.py:395
  56.4 23.3 %collective-permute-start.31 = (bf16[8,16,256]{2,1,0:T(8,128)(2,1)S(1)}, bf16[8,16,256]{2,1,0:T(8,128)(2,1)S(1)}, u32[]{:S(2)}, u32[]{:S(2)}) collective-permute-start(bf16[8,16,256]{2,1,0:T(8,128)(2,1)S(1)} %bitcast.26), channel_id=1, source_target_pairs={{0,1},{1,0},{2,3},{3,2},{4,5},{5,4},{6,7},{7,6},{8,9},{9,8},{10,11... | collective-permute-start | bytes 196616 | tf_op jit(solution)/shard_map/ppermute | solution.py:515
  57.0 7.5 %collective-permute-start.23 = (bf16[16,4096]{1,0:T(8,128)(2,1)S(1)}, bf16[16,4096]{1,0:T(8,128)(2,1)S(1)}, u32[]{:S(2)}, u32[]{:S(2)}) collective-permute-start(bf16[16,4096]{1,0:T(8,128)(2,1)S(1)} %collective-permute-done.8.refs_1_), channel_id=1, source_target_pairs={{0,1},{1,0},{2,3},{3,2},{4,5},{5,4},{6,7},{7,6},{8,9},{9,8},{10,11... | collective-permute-start | bytes 393224 | tf_op jit(solution)/shard_map/ppermute | solution.py:395
  57.0 5.8 %collective-permute-start.22 = (bf16[16,4096]{1,0:T(8,128)(2,1)S(1)}, bf16[16,4096]{1,0:T(8,128)(2,1)S(1)}, u32[]{:S(2)}, u32[]{:S(2)}) collective-permute-start(bf16[16,4096]{1,0:T(8,128)(2,1)S(1)} %collective-permute-done.8.refs_1_), channel_id=1, source_target_pairs={{0,2},{1,3},{2,0},{3,1},{4,6},{5,7},{6,4},{7,5},{8,10},{9,11},{10,... | collective-permute-start | bytes 393224 | tf_op jit(solution)/shard_map/ppermute | solution.py:395
  58.5 16.8 %collective-permute-start.28 = (bf16[16,4096]{1,0:T(8,128)(2,1)S(1)}, bf16[16,4096]{1,0:T(8,128)(2,1)S(1)}, u32[]{:S(2)}, u32[]{:S(2)}) collective-permute-start(bf16[16,4096]{1,0:T(8,128)(2,1)S(1)} %collective-permute-done.5.refs_2_), channel_id=1, source_target_pairs={{0,1},{1,0},{2,3},{3,2},{4,5},{5,4},{6,7},{7,6},{8,9},{9,8},{10,11... | collective-permute-start | bytes 393224 | tf_op jit(solution)/shard_map/ppermute | solution.py:395
  62.9 5.7 %collective-permute-start.14 = (bf16[16,4096]{1,0:T(8,128)(2,1)S(1)}, bf16[16,4096]{1,0:T(8,128)(2,1)S(1)}, u32[]{:S(2)}, u32[]{:S(2)}) collective-permute-start(bf16[16,4096]{1,0:T(8,128)(2,1)S(1)} %add_convert_fusion.6.refs_8_), channel_id=1, source_target_pairs={{0,2},{1,3},{2,0},{3,1},{4,6},{5,7},{6,4},{7,5},{8,10},{9,11},{10,... | collective-permute-start | bytes 393224 | tf_op jit(solution)/shard_map/ppermute | solution.py:395
  64.4 9.0 %collective-permute-start.20 = (bf16[16,4096]{1,0:T(8,128)(2,1)S(1)}, bf16[16,4096]{1,0:T(8,128)(2,1)S(1)}, u32[]{:S(2)}, u32[]{:S(2)}) collective-permute-start(bf16[16,4096]{1,0:T(8,128)(2,1)S(1)} %add_convert_fusion.4.refs_9_), channel_id=1, source_target_pairs={{0,2},{1,3},{2,0},{3,1},{4,6},{5,7},{6,4},{7,5},{8,10},{9,11},{10,... | collective-permute-start | bytes 393224 | tf_op jit(solution)/shard_map/ppermute | solution.py:395
  68.7 12.9 %collective-permute-start.15 = (bf16[16,4096]{1,0:T(8,128)(2,1)S(1)}, bf16[16,4096]{1,0:T(8,128)(2,1)S(1)}, u32[]{:S(2)}, u32[]{:S(2)}) collective-permute-start(bf16[16,4096]{1,0:T(8,128)(2,1)S(1)} %add_convert_fusion.5), channel_id=1, source_target_pairs={{0,8},{4,12},{8,0},{12,4},{1,9},{5,13},{9,1},{13,5},{2,10},{6,14},... | collective-permute-start | bytes 393224 | tf_op jit(solution)/shard_map/ppermute | solution.py:398
  71.3 6.8 %collective-permute-start.26 = (bf16[16,4096]{1,0:T(8,128)(2,1)S(1)}, bf16[16,4096]{1,0:T(8,128)(2,1)S(1)}, u32[]{:S(2)}, u32[]{:S(2)}) collective-permute-start(bf16[16,4096]{1,0:T(8,128)(2,1)S(1)} %add_convert_fusion.2.refs_8_), channel_id=1, source_target_pairs={{0,2},{1,3},{2,0},{3,1},{4,6},{5,7},{6,4},{7,5},{8,10},{9,11},{10,... | collective-permute-start | bytes 393224 | tf_op jit(solution)/shard_map/ppermute | solution.py:395
  73.5 8.1 %collective-permute-start.21 = (bf16[16,4096]{1,0:T(8,128)(2,1)S(1)}, bf16[16,4096]{1,0:T(8,128)(2,1)S(1)}, u32[]{:S(2)}, u32[]{:S(2)}) collective-permute-start(bf16[16,4096]{1,0:T(8,128)(2,1)S(1)} %add_convert_fusion.3), channel_id=1, source_target_pairs={{0,12},{4,8},{8,4},{12,0},{1,13},{5,9},{9,5},{13,1},{2,14},{6,10},... | collective-permute-start | bytes 393224 | tf_op jit(solution)/shard_map/ppermute | solution.py:398
  78.2 6.1 %collective-permute-start.27 = (bf16[16,4096]{1,0:T(8,128)(2,1)S(1)}, bf16[16,4096]{1,0:T(8,128)(2,1)S(1)}, u32[]{:S(2)}, u32[]{:S(2)}) collective-permute-start(bf16[16,4096]{1,0:T(8,128)(2,1)S(1)} %add_convert_fusion.1), channel_id=1, source_target_pairs={{0,4},{4,0},{8,12},{12,8},{1,5},{5,1},{9,13},{13,9},{2,6},{6,2},{1... | collective-permute-start | bytes 393224 | tf_op jit(solution)/shard_map/ppermute | solution.py:398
  79.6 5.6 %collective-permute-start.30 = (bf16[16,4096]{1,0:T(8,128)(2,1)S(1)}, bf16[16,4096]{1,0:T(8,128)(2,1)S(1)}, u32[]{:S(2)}, u32[]{:S(2)}) collective-permute-start(bf16[16,4096]{1,0:T(8,128)(2,1)S(1)} %add_convert_fusion), channel_id=1, source_target_pairs={{0,2},{1,3},{2,0},{3,1},{4,6},{5,7},{6,4},{7,5},{8,10},{9,11},{10,... | collective-permute-start | bytes 393224 | tf_op jit(solution)/shard_map/ppermute | solution.py:395
  (17 other events, 63.2 us)

commit v16 on v15

--- a/solution.py
+++ b/solution.py
@@ -91,6 +91,25 @@
         cost_estimate=EXPERT_COST,
         name="normalize",
     )(kept, got, hidden, gain)
+
+
+def join_kernel(count, *refs):
+    total = refs[0][...].astype(jnp.float32)
+    for ref in refs[1:count]:
+        total += ref[...].astype(jnp.float32)
+    refs[-1][...] = total
+
+
+def join_call(terms, after):
+    return pl.pallas_call(
+        lambda *refs: join_kernel(len(terms), *refs),
+        out_shape=jax.ShapeDtypeStruct(terms[0].shape, jnp.float32),
+        in_specs=[WHOLE] * len(terms) + [ANYWHERE] * len(after),
+        out_specs=WHOLE,
+        compiler_params=pltpu.CompilerParams(vmem_limit_bytes=VMEM_LIMIT),
+        cost_estimate=EXPERT_COST,
+        name="join",
+    )(*terms, *after)
 
 
 def prepare_kernel(ep_count, blocks, weight_at, lens, owners, place, *refs):
@@ -474,39 +493,53 @@
     own_have = [normed]
     for bit, piece in zip(bits + [1], early):
         own_have += [piece] + [exchange(part, bit) for part in own_have[1:]]
-
-    groups = [[step] for step in [ep_count // 2] + [step for step in reversed(range(1, ep_count)) if step != ep_count // 2] + [0]]
-    sums = {}
-    sent, given, finished = None, [], []
-    for turn, group in enumerate(groups):
-        after = [sent] if turn >= 1 else []
+    own_kept, sent = expert_call(
+        (0,), blocks, row_weights, own_have, held_gate_up, held_down, []
+    )
+    own_sum, own_got, own_given, _ = scatter(own_kept, sent)
+    own_sum = own_sum + own_got.astype(jnp.float32)
+    crossed = {0: normed}
+    for bit in ep_bits:
+        for step in list(crossed):
+            crossed[step ^ bit] = across(crossed[step], bit) if step else direct[bit]
+    leading = ep_bits[0]
+    forwarded = [step for step in crossed if step & (step - 1)]
+    lead_have = group_rows([crossed[leading]], bits[:1])
+    lead_have[1:], ahead, sent = lax.optimization_barrier(
+        (lead_have[1:], [crossed[step] for step in forwarded], sent)
+    )
+    crossed.update(zip(forwarded, ahead))
+    lead_have = group_rows(lead_have, bits[1:] + [1])
+
+    order = [leading] + [step for step in reversed(range(1, ep_count)) if step != leading]
+    mixture = resid_wide
+    given, finished = [], []
+    crossing = []
+    for turn, step in enumerate(order):
+        after = [sent]
         if turn == 1:
             after += []
-        elif turn == len(groups) - 1:
-            after += given[turn - 1 : turn]
         elif turn >= 2:
-            after += given[turn - 2 : turn]
-        haves = {0: own_have, leading: lead_have}
-        for step in group:
-            if step not in haves:
-                piece = crossed[step]
-                haves[step] = group_rows([piece], bits + [1], sent if turn == 1 else received)
-                reached = haves[step][1]
-        have = [haves[step][spot] for spot in range(blocks) for step in group]
+            after += given[:1]
+        if turn == 0:
+            have = lead_have
+        else:
+            piece = crossed[step]
+            if turn > 1 and bits:
+                piece, reached = lax.optimization_barrier((piece, reached))
+            have = group_rows([piece], bits + [1], sent if turn == 1 else received)
+            reached = have[1] if bits else piece
         kept, sent = expert_call(
-            tuple(group), blocks, row_weights, have, held_gate_up, held_down, after
+            (step,), blocks, row_weights, have, held_gate_up, held_down, after
         )
         own, got, gives, received = scatter(kept, sent)
-        own = own + got.astype(jnp.float32)
-        given.append(gives[0] if gives else own.astype(jnp.bfloat16))
-        finished.append(own.astype(jnp.bfloat16))
-        for spot, step in enumerate(group):
-            sums[step] = own[spot * row_count : (spot + 1) * row_count]
-    mixture = resid_wide
-    for step, own in sums.items():
-        if step:
-            own = across(own.astype(jnp.bfloat16), step).astype(jnp.float32)
-        mixture = mixture + own
+        own = (own + got.astype(jnp.float32)).astype(jnp.bfloat16)
+        given.append(gives[0] if gives else own)
+        finished.append(own)
+        crossing.append(across(own, step))
+    mixture = mixture + own_sum
+    for rows in crossing:
+        mixture = mixture + rows.astype(jnp.float32)
     layer_out = jnp.where(row_mask[:, None] > 0, mixture, 0.0).astype(jnp.bfloat16)
 
     if keyval_local == 1:

time: 86.4 us -> 86.2 us (level)
    ppermute x22, waiting for transfers between devices: 11.3 us -> 13.1 us  [local(): lax.ppermute(value, ('kv', 'tp'), [(i, i ^ bit) for i in range(blocks)])]
    ppermute x6, waiting for transfers between devices: 10.2 us -> 8.8 us  [local(): lax.ppermute(value, 'ep', [(i, i ^ step) for i in range(ep_count)])]
where the time goes in v16:
time: 86.2 us; the launch traced here: 85.8 us
  starting transfers between devices  27.7 us (32%)
  waiting for transfers between devices  22.3 us (26%)
  Pallas kernels  17.1 us (20%)
  local copies, waits for them, and re-layouts  14.1 us (16%)
  other arithmetic  3.62 us (4%)
  between operations  0.96 us (1%)
    ppermute x22, waiting for transfers between devices, local(): lax.ppermute(value, ('kv', 'tp'), [(i, i ^ bit) for i in range(blocks)])  13.1 us
    ppermute x22, starting transfers between devices, local(): lax.ppermute(value, ('kv', 'tp'), [(i, i ^ bit) for i in range(blocks)])  12.7 us
    pallas_call x4, Pallas kernels, expert_call(): pl.pallas_call(lambda *refs: expert_kernel(len(have), steps, blocks, *ref...  10.6 us
    unnamed x21, local copies, waits for them, and re-layouts  9.62 us
    ppermute x6, waiting for transfers between devices, local(): lax.ppermute(value, 'ep', [(i, i ^ step) for i in range(ep_count)])  8.8 us
    ppermute x6, starting transfers between devices, local(): lax.ppermute(value, 'ep', [(i, i ^ step) for i in range(ep_count)])  8.66 us
    ppermute x3, starting transfers between devices, local(): lax.ppermute(payload, 'ep', [(i, i ^ step) for i in range(ep_count)])  5.76 us
    pallas_call x1, Pallas kernels, attend_call(): pl.pallas_call(lambda *refs: attend_kernel(ep_count, held, tokens, blocks...  3.4 us
  transfers between devices with their start and end apart: 32, of which 14 were waited for; matrix products, arithmetic and copies ran while one was open for 5% of the time, Pallas kernels for 16%

profile of v16, /device:TPU:0, one launch (start us, length us, event | category | flops | bytes accessed | tf_op | source)
XLA Modules:
  0.0 85.8 jit_solution(13711586039572720388)
XLA Ops:
  4.8 5.1 %collective-permute-start.2 = (bf16[336,256]{1,0:T(8,128)(2,1)S(1)}, bf16[336,256]{1,0:T(8,128)(2,1)S(1)}, u32[]{:S(2)}, u32[]{:S(2)}) collective-permute-start(bf16[336,256]{1,0:T(8,128)(2,1)S(1)} %pad_maximum_fusion.refs_3_.refs_4_), channel_id=1, source_target_pairs={{0,12},{4,8},{8,4},{12,0},{1,13},{5,9},{9,5},{13,1},{2,14},{6,10},... | collective-permute-start | bytes 516104 | tf_op jit(solution)/shard_map/ppermute | solution.py:402
  13.5 3.4 %copy-done.1 = bf16[1024,4096]{1,0:T(8,128)(2,1)S(1)} copy-done((bf16[1024,4096]{1,0:T(8,128)(2,1)S(1)}, bf16[1024,4096]{1,0:T(8,128)(2,1)}, u32[]{:S(2)}) %copy-start.1) | copy-done | bytes 8388632
  16.9 2.8 %copy-done.2 = bf16[1,2,384,4096]{3,2,1,0:T(8,128)(2,1)S(1)} copy-done((bf16[1,2,384,4096]{3,2,1,0:T(8,128)(2,1)S(1)}, bf16[1,2,384,4096]{3,2,1,0:T(8,128)(2,1)}, u32[]{:S(2)}) %copy-start.2) | copy-done | bytes 6291480
  19.7 1.9 %copy-done.3 = bf16[1,384,4096]{2,1,0:T(8,128)(2,1)S(1)} copy-done((bf16[1,384,4096]{2,1,0:T(8,128)(2,1)S(1)}, bf16[1,384,4096]{2,1,0:T(8,128)(2,1)}, u32[]{:S(2)}) %copy-start.3) | copy-done | bytes 3145752
  22.3 1.8 %hold.1 = (bf16[1024,4096]{1,0:T(8,128)(2,1)S(1)}, bf16[1,2,384,4096]{3,2,1,0:T(8,128)(2,1)S(1)}, bf16[1,384,4096]{2,1,0:T(8,128)(2,1)S(1)}, f32[8,128]{1,0:T(8,128)}) custom-call(bf16[1024,4096]{1,0:T(8,128)(2,1)S(1)} %copy-done.1, bf16[1,2,384,4096]{3,2,1,0:T(8,128)(2,1)S(1)} %copy-done.2, bf16[1,384,4096]{2,1,0:T(8,128)(2,1)S(1)} %copy-done.3, ...), custom_call_target="tpu_custom_call" | custom-call | bytes 35651584 | tf_op jit(solution)/shard_map/hold/pallas_call | solution.py:62
  24.5 3.4 %attend.1 = (f32[32,4096]{1,0:T(8,128)S(1)}, bf16[32,4096]{1,0:T(8,128)(2,1)S(1)}) custom-call(s32[4]{0:T(128)S(1)} %copy-done.7, s32[2]{0:T(128)S(1)} %pad_add_fusion.refs_4_.refs_1_.refs_2_, s32[1]{0:T(128)} %constant.48.clone.1.refs_2_, bf16[64,1024]{1,0:T(8,128)(2,1)S(1)} %copy-done.4, bf16[336,256]{1,0:T(8,128)(2,1)S(1)} %pad_maximum_fusion.refs_3_.refs_4_, ...), custom_call_target="tpu_custom_call" | custom-call | flops 872415232 | bytes 8388608 | tf_op jit(solution)/shard_map/attend/pallas_call | solution.py:266
  28.0 1.5 %collective-permute-done.3 = bf16[32,4096]{1,0:T(8,128)(2,1)S(1)} collective-permute-done((bf16[32,4096]{1,0:T(8,128)(2,1)S(1)}, bf16[32,4096]{1,0:T(8,128)(2,1)S(1)}, u32[]{:S(2)}, u32[]{:S(2)}) %collective-permute-start.3) | collective-permute-done | bytes 262176 | tf_op jit(solution)/shard_map/ppermute | solution.py:414
  29.6 1.6 %collective-permute-start.4 = (bf16[16,4096]{1,0:T(8,128)(2,1)S(1)}, bf16[16,4096]{1,0:T(8,128)(2,1)S(1)}, u32[]{:S(2)}, u32[]{:S(2)}) collective-permute-start(bf16[16,4096]{1,0:T(8,128)(2,1)S(1)} %get-tuple-element.68), channel_id=1, source_target_pairs={{0,2},{1,3},{2,0},{3,1},{4,6},{5,7},{6,4},{7,5},{8,10},{9,11},{10,... | collective-permute-start | bytes 393224 | tf_op jit(solution)/shard_map/ppermute | solution.py:414
  31.1 4.1 %collective-permute-done.4.got = bf16[16,4096]{1,0:T(8,128)(2,1)S(1)} collective-permute-done((bf16[16,4096]{1,0:T(8,128)(2,1)S(1)}, bf16[16,4096]{1,0:T(8,128)(2,1)S(1)}, u32[]{:S(2)}, u32[]{:S(2)}) %collective-permute-start.4) | collective-permute-done | bytes 131104 | tf_op jit(solution)/shard_map/ppermute | solution.py:414
  36.5 2.9 %collective-permute-start.7 = (bf16[16,4096]{1,0:T(8,128)(2,1)S(1)}, bf16[16,4096]{1,0:T(8,128)(2,1)S(1)}, u32[]{:S(2)}, u32[]{:S(2)}) collective-permute-start(bf16[16,4096]{1,0:T(8,128)(2,1)S(1)} %get-tuple-element.38.refs_7_.refs_1_), channel_id=1, source_target_pairs={{0,8},{4,12},{8,0},{12,4},{1,9},{5,13},{9,1},{13,5},{2,10},{6,14},... | collective-permute-start | bytes 393224 | tf_op jit(solution)/shard_map/ppermute | solution.py:417
  42.6 2.4 %collective-permute-done.7.refs_1_ = bf16[16,4096]{1,0:T(8,128)(2,1)S(1)} collective-permute-done((bf16[16,4096]{1,0:T(8,128)(2,1)S(1)}, bf16[16,4096]{1,0:T(8,128)(2,1)S(1)}, u32[]{:S(2)}, u32[]{:S(2)}) %collective-permute-start.7) | collective-permute-done | bytes 131104 | tf_op jit(solution)/shard_map/ppermute | solution.py:417
  45.4 1.5 %collective-permute-start.12 = (bf16[16,4096]{1,0:T(8,128)(2,1)S(1)}, bf16[16,4096]{1,0:T(8,128)(2,1)S(1)}, u32[]{:S(2)}, u32[]{:S(2)}) collective-permute-start(bf16[16,4096]{1,0:T(8,128)(2,1)S(1)} %collective-permute-done.7.refs_1_), channel_id=1, source_target_pairs={{0,2},{1,3},{2,0},{3,1},{4,6},{5,7},{6,4},{7,5},{8,10},{9,11},{10,... | collective-permute-start | bytes 393224 | tf_op jit(solution)/shard_map/ppermute | solution.py:414
  47.1 2.7 %experts.4 = (bf16[32,4096]{1,0:T(8,128)(2,1)S(1)}, bf16[32,4096]{1,0:T(8,128)(2,1)S(1)}) custom-call(f32[256,128]{1,0:T(8,128)S(1)} %get-tuple-element.40.refs_0_, bf16[16,4096]{1,0:T(8,128)(2,1)S(1)} %get-tuple-element.38.refs_7_.refs_1_, bf16[16,4096]{1,0:T(8,128)(2,1)S(1)} %collective-permute-done.5.refs_2_, ...), custom_call_target="tpu_custom_call" | custom-call | flops 1024 | bytes 1024 | tf_op jit(solution)/shard_map/experts/pallas_call | solution.py:329
  49.7 1.5 %collective-permute-done.13.refs_1_ = bf16[16,4096]{1,0:T(8,128)(2,1)S(1)} collective-permute-done((bf16[16,4096]{1,0:T(8,128)(2,1)S(1)}, bf16[16,4096]{1,0:T(8,128)(2,1)S(1)}, u32[]{:S(2)}, u32[]{:S(2)}) %collective-permute-start.13) | collective-permute-done | bytes 131104 | tf_op jit(solution)/shard_map/ppermute | solution.py:417
  51.3 1.5 %collective-permute-start.19 = (bf16[16,4096]{1,0:T(8,128)(2,1)S(1)}, bf16[16,4096]{1,0:T(8,128)(2,1)S(1)}, u32[]{:S(2)}, u32[]{:S(2)}) collective-permute-start(bf16[16,4096]{1,0:T(8,128)(2,1)S(1)} %collective-permute-done.13.refs_1_), channel_id=1, source_target_pairs={{0,2},{1,3},{2,0},{3,1},{4,6},{5,7},{6,4},{7,5},{8,10},{9,11},{10,... | collective-permute-start | bytes 393224 | tf_op jit(solution)/shard_map/ppermute | solution.py:414
  53.3 2.7 %experts.5 = (bf16[32,4096]{1,0:T(8,128)(2,1)S(1)}, bf16[32,4096]{1,0:T(8,128)(2,1)S(1)}) custom-call(f32[256,128]{1,0:T(8,128)S(1)} %get-tuple-element.40.refs_0_, bf16[16,4096]{1,0:T(8,128)(2,1)S(1)} %collective-permute-done.7.refs_1_, bf16[16,4096]{1,0:T(8,128)(2,1)S(1)} %collective-permute-done.12.refs_2_, ...), custom_call_target="tpu_custom_call" | custom-call | flops 1024 | bytes 1024 | tf_op jit(solution)/shard_map/experts/pallas_call | solution.py:329
  57.8 1.5 %collective-permute-start.25 = (bf16[16,4096]{1,0:T(8,128)(2,1)S(1)}, bf16[16,4096]{1,0:T(8,128)(2,1)S(1)}, u32[]{:S(2)}, u32[]{:S(2)}) collective-permute-start(bf16[16,4096]{1,0:T(8,128)(2,1)S(1)} %collective-permute-done.8.refs_1_), channel_id=1, source_target_pairs={{0,2},{1,3},{2,0},{3,1},{4,6},{5,7},{6,4},{7,5},{8,10},{9,11},{10,... | collective-permute-start | bytes 393224 | tf_op jit(solution)/shard_map/ppermute | solution.py:414
  59.5 2.7 %experts.6 = (bf16[32,4096]{1,0:T(8,128)(2,1)S(1)}, bf16[32,4096]{1,0:T(8,128)(2,1)S(1)}) custom-call(f32[256,128]{1,0:T(8,128)S(1)} %get-tuple-element.40.refs_0_, bf16[16,4096]{1,0:T(8,128)(2,1)S(1)} %collective-permute-done.13.refs_1_, bf16[16,4096]{1,0:T(8,128)(2,1)S(1)} %collective-permute-done.19.refs_2_, ...), custom_call_target="tpu_custom_call" | custom-call | flops 1024 | bytes 1024 | tf_op jit(solution)/shard_map/experts/pallas_call | solution.py:329
  66.5 2.7 %experts.7 = (bf16[32,4096]{1,0:T(8,128)(2,1)S(1)}, bf16[32,4096]{1,0:T(8,128)(2,1)S(1)}) custom-call(f32[256,128]{1,0:T(8,128)S(1)} %get-tuple-element.40.refs_0_, bf16[16,4096]{1,0:T(8,128)(2,1)S(1)} %collective-permute-done.8.refs_1_, bf16[16,4096]{1,0:T(8,128)(2,1)S(1)} %collective-permute-done.25.refs_2_, ...), custom_call_target="tpu_custom_call" | custom-call | flops 1024 | bytes 1024 | tf_op jit(solution)/shard_map/experts/pallas_call | solution.py:329
  69.4 2.4 %collective-permute-done.17 = bf16[16,4096]{1,0:T(8,128)(2,1)S(1)} collective-permute-done((bf16[16,4096]{1,0:T(8,128)(2,1)S(1)}, bf16[16,4096]{1,0:T(8,128)(2,1)S(1)}, u32[]{:S(2)}, u32[]{:S(2)}) %collective-permute-start.17) | collective-permute-done | bytes 131104 | tf_op jit(solution)/shard_map/ppermute | solution.py:414
  71.9 2.4 %collective-permute-start.18 = (bf16[16,4096]{1,0:T(8,128)(2,1)S(1)}, bf16[16,4096]{1,0:T(8,128)(2,1)S(1)}, u32[]{:S(2)}, u32[]{:S(2)}) collective-permute-start(bf16[16,4096]{1,0:T(8,128)(2,1)S(1)} %add_convert_fusion.4), channel_id=1, source_target_pairs={{0,8},{4,12},{8,0},{12,4},{1,9},{5,13},{9,1},{13,5},{2,10},{6,14},... | collective-permute-start | bytes 393224 | tf_op jit(solution)/shard_map/ppermute | solution.py:417
  75.2 1.8 %collective-permute-start.24 = (bf16[16,4096]{1,0:T(8,128)(2,1)S(1)}, bf16[16,4096]{1,0:T(8,128)(2,1)S(1)}, u32[]{:S(2)}, u32[]{:S(2)}) collective-permute-start(bf16[16,4096]{1,0:T(8,128)(2,1)S(1)} %add_convert_fusion.2), channel_id=1, source_target_pairs={{0,12},{4,8},{8,4},{12,0},{1,13},{5,9},{9,5},{13,1},{2,14},{6,10},... | collective-permute-start | bytes 393224 | tf_op jit(solution)/shard_map/ppermute | solution.py:417
  77.0 2.4 %collective-permute-done.29 = bf16[16,4096]{1,0:T(8,128)(2,1)S(1)} collective-permute-done((bf16[16,4096]{1,0:T(8,128)(2,1)S(1)}, bf16[16,4096]{1,0:T(8,128)(2,1)S(1)}, u32[]{:S(2)}, u32[]{:S(2)}) %collective-permute-start.29) | collective-permute-done | bytes 131104 | tf_op jit(solution)/shard_map/ppermute | solution.py:414
  80.6 2.9 %collective-permute-done.18 = bf16[16,4096]{1,0:T(8,128)(2,1)S(1)} collective-permute-done((bf16[16,4096]{1,0:T(8,128)(2,1)S(1)}, bf16[16,4096]{1,0:T(8,128)(2,1)S(1)}, u32[]{:S(2)}, u32[]{:S(2)}) %collective-permute-start.18) | collective-permute-done | bytes 131104 | tf_op jit(solution)/shard_map/ppermute | solution.py:417
  (100 shorter events, 25.4 us)
Async XLA Ops:
  4.8 19.3 %collective-permute-start.2 = (bf16[336,256]{1,0:T(8,128)(2,1)S(1)}, bf16[336,256]{1,0:T(8,128)(2,1)S(1)}, u32[]{:S(2)}, u32[]{:S(2)}) collective-permute-start(bf16[336,256]{1,0:T(8,128)(2,1)S(1)} %pad_maximum_fusion.refs_3_.refs_4_), channel_id=1, source_target_pairs={{0,12},{4,8},{8,4},{12,0},{1,13},{5,9},{9,5},{13,1},{2,14},{6,10},... | collective-permute-start | bytes 516104 | tf_op jit(solution)/shard_map/ppermute | solution.py:402
  9.9 14.6 %collective-permute-start.1 = (bf16[336,256]{1,0:T(8,128)(2,1)S(1)}, bf16[336,256]{1,0:T(8,128)(2,1)S(1)}, u32[]{:S(2)}, u32[]{:S(2)}) collective-permute-start(bf16[336,256]{1,0:T(8,128)(2,1)S(1)} %pad_maximum_fusion.refs_3_.refs_4_), channel_id=1, source_target_pairs={{0,8},{4,12},{8,0},{12,4},{1,9},{5,13},{9,1},{13,5},{2,10},{6,14},... | collective-permute-start | bytes 516104 | tf_op jit(solution)/shard_map/ppermute | solution.py:402
  9.9 14.6 %collective-permute-start = (bf16[336,256]{1,0:T(8,128)(2,1)S(1)}, bf16[336,256]{1,0:T(8,128)(2,1)S(1)}, u32[]{:S(2)}, u32[]{:S(2)}) collective-permute-start(bf16[336,256]{1,0:T(8,128)(2,1)S(1)} %pad_maximum_fusion.refs_3_.refs_4_), channel_id=1, source_target_pairs={{0,4},{4,0},{8,12},{12,8},{1,5},{5,1},{9,13},{13,9},{2,6},{6,2},{1... | collective-permute-start | bytes 516104 | tf_op jit(solution)/shard_map/ppermute | solution.py:402
  29.6 5.6 %collective-permute-start.4 = (bf16[16,4096]{1,0:T(8,128)(2,1)S(1)}, bf16[16,4096]{1,0:T(8,128)(2,1)S(1)}, u32[]{:S(2)}, u32[]{:S(2)}) collective-permute-start(bf16[16,4096]{1,0:T(8,128)(2,1)S(1)} %get-tuple-element.68), channel_id=1, source_target_pairs={{0,2},{1,3},{2,0},{3,1},{4,6},{5,7},{6,4},{7,5},{8,10},{9,11},{10,... | collective-permute-start | bytes 393224 | tf_op jit(solution)/shard_map/ppermute | solution.py:414
  35.4 7.2 %collective-permute-start.8 = (bf16[16,4096]{1,0:T(8,128)(2,1)S(1)}, bf16[16,4096]{1,0:T(8,128)(2,1)S(1)}, u32[]{:S(2)}, u32[]{:S(2)}) collective-permute-start(bf16[16,4096]{1,0:T(8,128)(2,1)S(1)} %get-tuple-element.38.refs_7_.refs_1_), channel_id=1, source_target_pairs={{0,4},{4,0},{8,12},{12,8},{1,5},{5,1},{9,13},{13,9},{2,6},{6,2},{1... | collective-permute-start | bytes 393224 | tf_op jit(solution)/shard_map/ppermute | solution.py:417
  36.5 8.5 %collective-permute-start.7 = (bf16[16,4096]{1,0:T(8,128)(2,1)S(1)}, bf16[16,4096]{1,0:T(8,128)(2,1)S(1)}, u32[]{:S(2)}, u32[]{:S(2)}) collective-permute-start(bf16[16,4096]{1,0:T(8,128)(2,1)S(1)} %get-tuple-element.38.refs_7_.refs_1_), channel_id=1, source_target_pairs={{0,8},{4,12},{8,0},{12,4},{1,9},{5,13},{9,1},{13,5},{2,10},{6,14},... | collective-permute-start | bytes 393224 | tf_op jit(solution)/shard_map/ppermute | solution.py:417
  39.4 5.5 %collective-permute-start.6 = (bf16[16,4096]{1,0:T(8,128)(2,1)S(1)}, bf16[16,4096]{1,0:T(8,128)(2,1)S(1)}, u32[]{:S(2)}, u32[]{:S(2)}) collective-permute-start(bf16[16,4096]{1,0:T(8,128)(2,1)S(1)} %get-tuple-element.38.refs_7_.refs_1_), channel_id=1, source_target_pairs={{0,1},{1,0},{2,3},{3,2},{4,5},{5,4},{6,7},{7,6},{8,9},{9,8},{10,11... | collective-permute-start | bytes 393224 | tf_op jit(solution)/shard_map/ppermute | solution.py:414
  39.4 5.9 %collective-permute-start.5 = (bf16[16,4096]{1,0:T(8,128)(2,1)S(1)}, bf16[16,4096]{1,0:T(8,128)(2,1)S(1)}, u32[]{:S(2)}, u32[]{:S(2)}) collective-permute-start(bf16[16,4096]{1,0:T(8,128)(2,1)S(1)} %get-tuple-element.38.refs_7_.refs_1_), channel_id=1, source_target_pairs={{0,2},{1,3},{2,0},{3,1},{4,6},{5,7},{6,4},{7,5},{8,10},{9,11},{10,... | collective-permute-start | bytes 393224 | tf_op jit(solution)/shard_map/ppermute | solution.py:414
  45.3 5.9 %collective-permute-start.13 = (bf16[16,4096]{1,0:T(8,128)(2,1)S(1)}, bf16[16,4096]{1,0:T(8,128)(2,1)S(1)}, u32[]{:S(2)}, u32[]{:S(2)}) collective-permute-start(bf16[16,4096]{1,0:T(8,128)(2,1)S(1)} %collective-permute-done.7.refs_1_), channel_id=1, source_target_pairs={{0,4},{4,0},{8,12},{12,8},{1,5},{5,1},{9,13},{13,9},{2,6},{6,2},{1... | collective-permute-start | bytes 393224 | tf_op jit(solution)/shard_map/ppermute | solution.py:417
  45.4 5.8 %collective-permute-start.12 = (bf16[16,4096]{1,0:T(8,128)(2,1)S(1)}, bf16[16,4096]{1,0:T(8,128)(2,1)S(1)}, u32[]{:S(2)}, u32[]{:S(2)}) collective-permute-start(bf16[16,4096]{1,0:T(8,128)(2,1)S(1)} %collective-permute-done.7.refs_1_), channel_id=1, source_target_pairs={{0,2},{1,3},{2,0},{3,1},{4,6},{5,7},{6,4},{7,5},{8,10},{9,11},{10,... | collective-permute-start | bytes 393224 | tf_op jit(solution)/shard_map/ppermute | solution.py:414
  46.9 6.4 %collective-permute-start.14 = (bf16[16,4096]{1,0:T(8,128)(2,1)S(1)}, bf16[16,4096]{1,0:T(8,128)(2,1)S(1)}, u32[]{:S(2)}, u32[]{:S(2)}) collective-permute-start(bf16[16,4096]{1,0:T(8,128)(2,1)S(1)} %collective-permute-done.7.refs_1_), channel_id=1, source_target_pairs={{0,1},{1,0},{2,3},{3,2},{4,5},{5,4},{6,7},{7,6},{8,9},{9,8},{10,11... | collective-permute-start | bytes 393224 | tf_op jit(solution)/shard_map/ppermute | solution.py:414
  51.3 5.9 %collective-permute-start.19 = (bf16[16,4096]{1,0:T(8,128)(2,1)S(1)}, bf16[16,4096]{1,0:T(8,128)(2,1)S(1)}, u32[]{:S(2)}, u32[]{:S(2)}) collective-permute-start(bf16[16,4096]{1,0:T(8,128)(2,1)S(1)} %collective-permute-done.13.refs_1_), channel_id=1, source_target_pairs={{0,2},{1,3},{2,0},{3,1},{4,6},{5,7},{6,4},{7,5},{8,10},{9,11},{10,... | collective-permute-start | bytes 393224 | tf_op jit(solution)/shard_map/ppermute | solution.py:414
  52.7 5.1 %collective-permute-start.20 = (bf16[16,4096]{1,0:T(8,128)(2,1)S(1)}, bf16[16,4096]{1,0:T(8,128)(2,1)S(1)}, u32[]{:S(2)}, u32[]{:S(2)}) collective-permute-start(bf16[16,4096]{1,0:T(8,128)(2,1)S(1)} %collective-permute-done.13.refs_1_), channel_id=1, source_target_pairs={{0,1},{1,0},{2,3},{3,2},{4,5},{5,4},{6,7},{7,6},{8,9},{9,8},{10,11... | collective-permute-start | bytes 393224 | tf_op jit(solution)/shard_map/ppermute | solution.py:414
  53.0 9.2 %collective-permute-start.10 = (bf16[32,4096]{1,0:T(8,128)(2,1)S(1)}, bf16[32,4096]{1,0:T(8,128)(2,1)S(1)}, u32[]{:S(2)}, u32[]{:S(2)}) collective-permute-start(bf16[32,4096]{1,0:T(8,128)(2,1)S(1)} %get-tuple-element.49.refs_7_), channel_id=1, source_target_pairs={{0,1},{1,0},{2,3},{3,2},{4,5},{5,4},{6,7},{7,6},{8,9},{9,8},{10,11... | collective-permute-start | bytes 786440 | tf_op jit(solution)/shard_map/ppermute | solution.py:414
  57.2 22.6 %collective-permute-start.31 = (bf16[8,16,256]{2,1,0:T(8,128)(2,1)S(1)}, bf16[8,16,256]{2,1,0:T(8,128)(2,1)S(1)}, u32[]{:S(2)}, u32[]{:S(2)}) collective-permute-start(bf16[8,16,256]{2,1,0:T(8,128)(2,1)S(1)} %bitcast.26), channel_id=1, source_target_pairs={{0,1},{1,0},{2,3},{3,2},{4,5},{5,4},{6,7},{7,6},{8,9},{9,8},{10,11... | collective-permute-start | bytes 196616 | tf_op jit(solution)/shard_map/ppermute | solution.py:548
  57.8 7.5 %collective-permute-start.26 = (bf16[16,4096]{1,0:T(8,128)(2,1)S(1)}, bf16[16,4096]{1,0:T(8,128)(2,1)S(1)}, u32[]{:S(2)}, u32[]{:S(2)}) collective-permute-start(bf16[16,4096]{1,0:T(8,128)(2,1)S(1)} %collective-permute-done.8.refs_1_), channel_id=1, source_target_pairs={{0,1},{1,0},{2,3},{3,2},{4,5},{5,4},{6,7},{7,6},{8,9},{9,8},{10,11... | collective-permute-start | bytes 393224 | tf_op jit(solution)/shard_map/ppermute | solution.py:414
  57.8 5.8 %collective-permute-start.25 = (bf16[16,4096]{1,0:T(8,128)(2,1)S(1)}, bf16[16,4096]{1,0:T(8,128)(2,1)S(1)}, u32[]{:S(2)}, u32[]{:S(2)}) collective-permute-start(bf16[16,4096]{1,0:T(8,128)(2,1)S(1)} %collective-permute-done.8.refs_1_), channel_id=1, source_target_pairs={{0,2},{1,3},{2,0},{3,1},{4,6},{5,7},{6,4},{7,5},{8,10},{9,11},{10,... | collective-permute-start | bytes 393224 | tf_op jit(solution)/shard_map/ppermute | solution.py:414
  62.6 18.0 %collective-permute-start.11 = (bf16[16,4096]{1,0:T(8,128)(2,1)S(1)}, bf16[16,4096]{1,0:T(8,128)(2,1)S(1)}, u32[]{:S(2)}, u32[]{:S(2)}) collective-permute-start(bf16[16,4096]{1,0:T(8,128)(2,1)S(1)} %add_convert_fusion.6), channel_id=1, source_target_pairs={{0,2},{1,3},{2,0},{3,1},{4,6},{5,7},{6,4},{7,5},{8,10},{9,11},{10,... | collective-permute-start | bytes 393224 | tf_op jit(solution)/shard_map/ppermute | solution.py:414
  63.7 8.2 %collective-permute-start.17 = (bf16[16,4096]{1,0:T(8,128)(2,1)S(1)}, bf16[16,4096]{1,0:T(8,128)(2,1)S(1)}, u32[]{:S(2)}, u32[]{:S(2)}) collective-permute-start(bf16[16,4096]{1,0:T(8,128)(2,1)S(1)} %add_convert_fusion.5.refs_8_), channel_id=1, source_target_pairs={{0,2},{1,3},{2,0},{3,1},{4,6},{5,7},{6,4},{7,5},{8,10},{9,11},{10,... | collective-permute-start | bytes 393224 | tf_op jit(solution)/shard_map/ppermute | solution.py:414
  65.2 9.9 %collective-permute-start.23 = (bf16[16,4096]{1,0:T(8,128)(2,1)S(1)}, bf16[16,4096]{1,0:T(8,128)(2,1)S(1)}, u32[]{:S(2)}, u32[]{:S(2)}) collective-permute-start(bf16[16,4096]{1,0:T(8,128)(2,1)S(1)} %add_convert_fusion.3), channel_id=1, source_target_pairs={{0,2},{1,3},{2,0},{3,1},{4,6},{5,7},{6,4},{7,5},{8,10},{9,11},{10,... | collective-permute-start | bytes 393224 | tf_op jit(solution)/shard_map/ppermute | solution.py:414
  69.2 5.1 %collective-permute-start.28 = (bf16[32,4096]{1,0:T(8,128)(2,1)S(1)}, bf16[32,4096]{1,0:T(8,128)(2,1)S(1)}, u32[]{:S(2)}, u32[]{:S(2)}) collective-permute-start(bf16[32,4096]{1,0:T(8,128)(2,1)S(1)} %get-tuple-element.60), channel_id=1, source_target_pairs={{0,1},{1,0},{2,3},{3,2},{4,5},{5,4},{6,7},{7,6},{8,9},{9,8},{10,11... | collective-permute-start | bytes 786440 | tf_op jit(solution)/shard_map/ppermute | solution.py:414
  71.9 11.7 %collective-permute-start.18 = (bf16[16,4096]{1,0:T(8,128)(2,1)S(1)}, bf16[16,4096]{1,0:T(8,128)(2,1)S(1)}, u32[]{:S(2)}, u32[]{:S(2)}) collective-permute-start(bf16[16,4096]{1,0:T(8,128)(2,1)S(1)} %add_convert_fusion.4), channel_id=1, source_target_pairs={{0,8},{4,12},{8,0},{12,4},{1,9},{5,13},{9,1},{13,5},{2,10},{6,14},... | collective-permute-start | bytes 393224 | tf_op jit(solution)/shard_map/ppermute | solution.py:417
  75.2 8.4 %collective-permute-start.24 = (bf16[16,4096]{1,0:T(8,128)(2,1)S(1)}, bf16[16,4096]{1,0:T(8,128)(2,1)S(1)}, u32[]{:S(2)}, u32[]{:S(2)}) collective-permute-start(bf16[16,4096]{1,0:T(8,128)(2,1)S(1)} %add_convert_fusion.2), channel_id=1, source_target_pairs={{0,12},{4,8},{8,4},{12,0},{1,13},{5,9},{9,5},{13,1},{2,14},{6,10},... | collective-permute-start | bytes 393224 | tf_op jit(solution)/shard_map/ppermute | solution.py:417
  79.4 5.5 %collective-permute-start.30 = (bf16[16,4096]{1,0:T(8,128)(2,1)S(1)}, bf16[16,4096]{1,0:T(8,128)(2,1)S(1)}, u32[]{:S(2)}, u32[]{:S(2)}) collective-permute-start(bf16[16,4096]{1,0:T(8,128)(2,1)S(1)} %add_convert_fusion), channel_id=1, source_target_pairs={{0,4},{4,0},{8,12},{12,8},{1,5},{5,1},{9,13},{13,9},{2,6},{6,2},{1... | collective-permute-start | bytes 393224 | tf_op jit(solution)/shard_map/ppermute | solution.py:417
  (17 other events, 64.1 us)

commit v17 on v16

--- a/solution.py
+++ b/solution.py
@@ -91,25 +91,6 @@
         cost_estimate=EXPERT_COST,
         name="normalize",
     )(kept, got, hidden, gain)
-
-
-def join_kernel(count, *refs):
-    total = refs[0][...].astype(jnp.float32)
-    for ref in refs[1:count]:
-        total += ref[...].astype(jnp.float32)
-    refs[-1][...] = total
-
-
-def join_call(terms, after):
-    return pl.pallas_call(
-        lambda *refs: join_kernel(len(terms), *refs),
-        out_shape=jax.ShapeDtypeStruct(terms[0].shape, jnp.float32),
-        in_specs=[WHOLE] * len(terms) + [ANYWHERE] * len(after),
-        out_specs=WHOLE,
-        compiler_params=pltpu.CompilerParams(vmem_limit_bytes=VMEM_LIMIT),
-        cost_estimate=EXPERT_COST,
-        name="join",
-    )(*terms, *after)
 
 
 def prepare_kernel(ep_count, blocks, weight_at, lens, owners, place, *refs):
@@ -419,13 +400,16 @@
     )
     bits = [1 << place for place in range(1, blocks.bit_length() - 1)]
 
-    def scatter(kept, sent):
+    def scatter(kept, sent, before=None):
         got = received = exchange(sent, 1)
         gives = []
         for bit in reversed(bits):
             half = kept.shape[0] // 2
             give = kept[half:].astype(jnp.float32) + got[half:].astype(jnp.float32)
-            gives.append(give.astype(jnp.bfloat16))
+            give = give.astype(jnp.bfloat16)
+            if before is not None and not gives:
+                give, before = lax.optimization_barrier((give, before))
+            gives.append(give)
             kept = kept[:half].astype(jnp.float32) + got[:half].astype(jnp.float32)
             got = exchange(gives[-1], bit)
         return kept.astype(jnp.float32), got, gives, received
@@ -493,11 +477,10 @@
     own_have = [normed]
     for bit, piece in zip(bits + [1], early):
         own_have += [piece] + [exchange(part, bit) for part in own_have[1:]]
-    own_kept, sent = expert_call(
+    own_kept, own_sent = expert_call(
         (0,), blocks, row_weights, own_have, held_gate_up, held_down, []
     )
-    own_sum, own_got, own_given, _ = scatter(own_kept, sent)
-    own_sum = own_sum + own_got.astype(jnp.float32)
+    sent = own_sent
     crossed = {0: normed}
     for bit in ep_bits:
         for step in list(crossed):
@@ -537,7 +520,8 @@
         given.append(gives[0] if gives else own)
         finished.append(own)
         crossing.append(across(own, step))
-    mixture = mixture + own_sum
+    own_sum, own_got, _, _ = scatter(own_kept, own_sent, got)
+    mixture = mixture + own_sum + own_got.astype(jnp.float32)
     for rows in crossing:
         mixture = mixture + rows.astype(jnp.float32)
     layer_out = jnp.where(row_mask[:, None] > 0, mixture, 0.0).astype(jnp.bfloat16)

time: 86.2 us -> 84.6 us (0.981)
  waiting for transfers between devices: 22.3 us -> 20.2 us
    ppermute x22, waiting for transfers between devices: 13.1 us -> 11.1 us  [local(): lax.ppermute(value, ('kv', 'tp'), [(i, i ^ bit) for i in range(blocks)])]
where the time goes in v17:
time: 84.6 us; the launch traced here: 84.2 us
  starting transfers between devices  28.1 us (33%)
  waiting for transfers between devices  20.2 us (24%)
  Pallas kernels  17.1 us (20%)
  local copies, waits for them, and re-layouts  14.1 us (17%)
  other arithmetic  3.63 us (4%)
  between operations  0.96 us (1%)
    ppermute x22, starting transfers between devices, local(): lax.ppermute(value, ('kv', 'tp'), [(i, i ^ bit) for i in range(blocks)])  13 us
    ppermute x22, waiting for transfers between devices, local(): lax.ppermute(value, ('kv', 'tp'), [(i, i ^ bit) for i in range(blocks)])  11.1 us
    pallas_call x4, Pallas kernels, expert_call(): pl.pallas_call(lambda *refs: expert_kernel(len(have), steps, blocks, *ref...  10.6 us
    unnamed x21, local copies, waits for them, and re-layouts  9.62 us
    ppermute x6, starting transfers between devices, local(): lax.ppermute(value, 'ep', [(i, i ^ step) for i in range(ep_count)])  8.79 us
    ppermute x6, waiting for transfers between devices, local(): lax.ppermute(value, 'ep', [(i, i ^ step) for i in range(ep_count)])  8.71 us
    ppermute x3, starting transfers between devices, local(): lax.ppermute(payload, 'ep', [(i, i ^ step) for i in range(ep_count)])  5.76 us
    pallas_call x1, Pallas kernels, attend_call(): pl.pallas_call(lambda *refs: attend_kernel(ep_count, held, tokens, blocks...  3.4 us
  transfers between devices with their start and end apart: 32, of which 14 were waited for; matrix products, arithmetic and copies ran while one was open for 5% of the time, Pallas kernels for 16%

profile of v17, /device:TPU:0, one launch (start us, length us, event | category | flops | bytes accessed | tf_op | source)
XLA Modules:
  0.0 84.2 jit_solution(12313785487750512936)
XLA Ops:
  4.8 5.1 %collective-permute-start.2 = (bf16[336,256]{1,0:T(8,128)(2,1)S(1)}, bf16[336,256]{1,0:T(8,128)(2,1)S(1)}, u32[]{:S(2)}, u32[]{:S(2)}) collective-permute-start(bf16[336,256]{1,0:T(8,128)(2,1)S(1)} %pad_maximum_fusion.refs_3_.refs_4_), channel_id=1, source_target_pairs={{0,12},{4,8},{8,4},{12,0},{1,13},{5,9},{9,5},{13,1},{2,14},{6,10},... | collective-permute-start | bytes 516104 | tf_op jit(solution)/shard_map/ppermute | solution.py:383
  13.5 3.4 %copy-done.1 = bf16[1024,4096]{1,0:T(8,128)(2,1)S(1)} copy-done((bf16[1024,4096]{1,0:T(8,128)(2,1)S(1)}, bf16[1024,4096]{1,0:T(8,128)(2,1)}, u32[]{:S(2)}) %copy-start.1) | copy-done | bytes 8388632
  16.9 2.8 %copy-done.2 = bf16[1,2,384,4096]{3,2,1,0:T(8,128)(2,1)S(1)} copy-done((bf16[1,2,384,4096]{3,2,1,0:T(8,128)(2,1)S(1)}, bf16[1,2,384,4096]{3,2,1,0:T(8,128)(2,1)}, u32[]{:S(2)}) %copy-start.2) | copy-done | bytes 6291480
  19.7 1.9 %copy-done.3 = bf16[1,384,4096]{2,1,0:T(8,128)(2,1)S(1)} copy-done((bf16[1,384,4096]{2,1,0:T(8,128)(2,1)S(1)}, bf16[1,384,4096]{2,1,0:T(8,128)(2,1)}, u32[]{:S(2)}) %copy-start.3) | copy-done | bytes 3145752
  22.3 1.8 %hold.1 = (bf16[1024,4096]{1,0:T(8,128)(2,1)S(1)}, bf16[1,2,384,4096]{3,2,1,0:T(8,128)(2,1)S(1)}, bf16[1,384,4096]{2,1,0:T(8,128)(2,1)S(1)}, f32[8,128]{1,0:T(8,128)}) custom-call(bf16[1024,4096]{1,0:T(8,128)(2,1)S(1)} %copy-done.1, bf16[1,2,384,4096]{3,2,1,0:T(8,128)(2,1)S(1)} %copy-done.2, bf16[1,384,4096]{2,1,0:T(8,128)(2,1)S(1)} %copy-done.3, ...), custom_call_target="tpu_custom_call" | custom-call | bytes 35651584 | tf_op jit(solution)/shard_map/hold/pallas_call | solution.py:62
  24.5 3.4 %attend.1 = (f32[32,4096]{1,0:T(8,128)S(1)}, bf16[32,4096]{1,0:T(8,128)(2,1)S(1)}) custom-call(s32[4]{0:T(128)S(1)} %copy-done.7, s32[2]{0:T(128)S(1)} %pad_add_fusion.refs_4_.refs_1_.refs_2_, s32[1]{0:T(128)} %constant.48.clone.1.refs_2_, bf16[64,1024]{1,0:T(8,128)(2,1)S(1)} %copy-done.4, bf16[336,256]{1,0:T(8,128)(2,1)S(1)} %pad_maximum_fusion.refs_3_.refs_4_, ...), custom_call_target="tpu_custom_call" | custom-call | flops 872415232 | bytes 8388608 | tf_op jit(solution)/shard_map/attend/pallas_call | solution.py:247
  28.0 1.5 %collective-permute-done.3 = bf16[32,4096]{1,0:T(8,128)(2,1)S(1)} collective-permute-done((bf16[32,4096]{1,0:T(8,128)(2,1)S(1)}, bf16[32,4096]{1,0:T(8,128)(2,1)S(1)}, u32[]{:S(2)}, u32[]{:S(2)}) %collective-permute-start.3) | collective-permute-done | bytes 262176 | tf_op jit(solution)/shard_map/ppermute | solution.py:395
  29.6 1.6 %collective-permute-start.4 = (bf16[16,4096]{1,0:T(8,128)(2,1)S(1)}, bf16[16,4096]{1,0:T(8,128)(2,1)S(1)}, u32[]{:S(2)}, u32[]{:S(2)}) collective-permute-start(bf16[16,4096]{1,0:T(8,128)(2,1)S(1)} %get-tuple-element.70), channel_id=1, source_target_pairs={{0,2},{1,3},{2,0},{3,1},{4,6},{5,7},{6,4},{7,5},{8,10},{9,11},{10,... | collective-permute-start | bytes 393224 | tf_op jit(solution)/shard_map/ppermute | solution.py:395
  31.1 4.1 %collective-permute-done.4.got = bf16[16,4096]{1,0:T(8,128)(2,1)S(1)} collective-permute-done((bf16[16,4096]{1,0:T(8,128)(2,1)S(1)}, bf16[16,4096]{1,0:T(8,128)(2,1)S(1)}, u32[]{:S(2)}, u32[]{:S(2)}) %collective-permute-start.4) | collective-permute-done | bytes 131104 | tf_op jit(solution)/shard_map/ppermute | solution.py:395
  36.5 2.9 %collective-permute-start.7 = (bf16[16,4096]{1,0:T(8,128)(2,1)S(1)}, bf16[16,4096]{1,0:T(8,128)(2,1)S(1)}, u32[]{:S(2)}, u32[]{:S(2)}) collective-permute-start(bf16[16,4096]{1,0:T(8,128)(2,1)S(1)} %get-tuple-element.39.refs_7_.refs_1_), channel_id=1, source_target_pairs={{0,8},{4,12},{8,0},{12,4},{1,9},{5,13},{9,1},{13,5},{2,10},{6,14},... | collective-permute-start | bytes 393224 | tf_op jit(solution)/shard_map/ppermute | solution.py:398
  39.4 1.5 %collective-permute-start.5 = (bf16[16,4096]{1,0:T(8,128)(2,1)S(1)}, bf16[16,4096]{1,0:T(8,128)(2,1)S(1)}, u32[]{:S(2)}, u32[]{:S(2)}) collective-permute-start(bf16[16,4096]{1,0:T(8,128)(2,1)S(1)} %get-tuple-element.39.refs_7_.refs_1_), channel_id=1, source_target_pairs={{0,2},{1,3},{2,0},{3,1},{4,6},{5,7},{6,4},{7,5},{8,10},{9,11},{10,... | collective-permute-start | bytes 393224 | tf_op jit(solution)/shard_map/ppermute | solution.py:395
  42.6 2.4 %collective-permute-done.7.refs_1_ = bf16[16,4096]{1,0:T(8,128)(2,1)S(1)} collective-permute-done((bf16[16,4096]{1,0:T(8,128)(2,1)S(1)}, bf16[16,4096]{1,0:T(8,128)(2,1)S(1)}, u32[]{:S(2)}, u32[]{:S(2)}) %collective-permute-start.7) | collective-permute-done | bytes 131104 | tf_op jit(solution)/shard_map/ppermute | solution.py:398
  45.4 1.5 %collective-permute-start.11 = (bf16[16,4096]{1,0:T(8,128)(2,1)S(1)}, bf16[16,4096]{1,0:T(8,128)(2,1)S(1)}, u32[]{:S(2)}, u32[]{:S(2)}) collective-permute-start(bf16[16,4096]{1,0:T(8,128)(2,1)S(1)} %collective-permute-done.7.refs_1_), channel_id=1, source_target_pairs={{0,2},{1,3},{2,0},{3,1},{4,6},{5,7},{6,4},{7,5},{8,10},{9,11},{10,... | collective-permute-start | bytes 393224 | tf_op jit(solution)/shard_map/ppermute | solution.py:395
  47.1 2.7 %experts.4 = (bf16[32,4096]{1,0:T(8,128)(2,1)S(1)}, bf16[32,4096]{1,0:T(8,128)(2,1)S(1)}) custom-call(f32[256,128]{1,0:T(8,128)S(1)} %get-tuple-element.41.refs_0_, bf16[16,4096]{1,0:T(8,128)(2,1)S(1)} %get-tuple-element.39.refs_7_.refs_1_, bf16[16,4096]{1,0:T(8,128)(2,1)S(1)} %collective-permute-done.5.refs_2_, ...), custom_call_target="tpu_custom_call" | custom-call | flops 1024 | bytes 1024 | tf_op jit(solution)/shard_map/experts/pallas_call | solution.py:310
  49.7 1.5 %collective-permute-done.12.refs_1_ = bf16[16,4096]{1,0:T(8,128)(2,1)S(1)} collective-permute-done((bf16[16,4096]{1,0:T(8,128)(2,1)S(1)}, bf16[16,4096]{1,0:T(8,128)(2,1)S(1)}, u32[]{:S(2)}, u32[]{:S(2)}) %collective-permute-start.12) | collective-permute-done | bytes 131104 | tf_op jit(solution)/shard_map/ppermute | solution.py:398
  51.3 1.5 %collective-permute-start.13 = (bf16[16,4096]{1,0:T(8,128)(2,1)S(1)}, bf16[16,4096]{1,0:T(8,128)(2,1)S(1)}, u32[]{:S(2)}, u32[]{:S(2)}) collective-permute-start(bf16[16,4096]{1,0:T(8,128)(2,1)S(1)} %collective-permute-done.12.refs_1_), channel_id=1, source_target_pairs={{0,2},{1,3},{2,0},{3,1},{4,6},{5,7},{6,4},{7,5},{8,10},{9,11},{10,... | collective-permute-start | bytes 393224 | tf_op jit(solution)/shard_map/ppermute | solution.py:395
  53.3 2.7 %experts.5 = (bf16[32,4096]{1,0:T(8,128)(2,1)S(1)}, bf16[32,4096]{1,0:T(8,128)(2,1)S(1)}) custom-call(f32[256,128]{1,0:T(8,128)S(1)} %get-tuple-element.41.refs_0_, bf16[16,4096]{1,0:T(8,128)(2,1)S(1)} %collective-permute-done.7.refs_1_, bf16[16,4096]{1,0:T(8,128)(2,1)S(1)} %collective-permute-done.11.refs_2_, ...), custom_call_target="tpu_custom_call" | custom-call | flops 1024 | bytes 1024 | tf_op jit(solution)/shard_map/experts/pallas_call | solution.py:310
  57.8 1.5 %collective-permute-start.16 = (bf16[16,4096]{1,0:T(8,128)(2,1)S(1)}, bf16[16,4096]{1,0:T(8,128)(2,1)S(1)}, u32[]{:S(2)}, u32[]{:S(2)}) collective-permute-start(bf16[16,4096]{1,0:T(8,128)(2,1)S(1)} %collective-permute-done.8.refs_1_), channel_id=1, source_target_pairs={{0,2},{1,3},{2,0},{3,1},{4,6},{5,7},{6,4},{7,5},{8,10},{9,11},{10,... | collective-permute-start | bytes 393224 | tf_op jit(solution)/shard_map/ppermute | solution.py:395
  59.5 2.7 %experts.6 = (bf16[32,4096]{1,0:T(8,128)(2,1)S(1)}, bf16[32,4096]{1,0:T(8,128)(2,1)S(1)}) custom-call(f32[256,128]{1,0:T(8,128)S(1)} %get-tuple-element.41.refs_0_, bf16[16,4096]{1,0:T(8,128)(2,1)S(1)} %collective-permute-done.12.refs_1_, bf16[16,4096]{1,0:T(8,128)(2,1)S(1)} %collective-permute-done.13.refs_2_, ...), custom_call_target="tpu_custom_call" | custom-call | flops 1024 | bytes 1024 | tf_op jit(solution)/shard_map/experts/pallas_call | solution.py:310
  65.3 2.7 %experts.7 = (bf16[32,4096]{1,0:T(8,128)(2,1)S(1)}, bf16[32,4096]{1,0:T(8,128)(2,1)S(1)}) custom-call(f32[256,128]{1,0:T(8,128)S(1)} %get-tuple-element.41.refs_0_, bf16[16,4096]{1,0:T(8,128)(2,1)S(1)} %collective-permute-done.8.refs_1_, bf16[16,4096]{1,0:T(8,128)(2,1)S(1)} %collective-permute-done.16.refs_2_, ...), custom_call_target="tpu_custom_call" | custom-call | flops 1024 | bytes 1024 | tf_op jit(solution)/shard_map/experts/pallas_call | solution.py:310
  69.1 2.4 %collective-permute-start.27 = (bf16[16,4096]{1,0:T(8,128)(2,1)S(1)}, bf16[16,4096]{1,0:T(8,128)(2,1)S(1)}, u32[]{:S(2)}, u32[]{:S(2)}) collective-permute-start(bf16[16,4096]{1,0:T(8,128)(2,1)S(1)} %add_convert_fusion.3), channel_id=1, source_target_pairs={{0,8},{4,12},{8,0},{12,4},{1,9},{5,13},{9,1},{13,5},{2,10},{6,14},... | collective-permute-start | bytes 393224 | tf_op jit(solution)/shard_map/ppermute | solution.py:398
  72.1 1.8 %collective-permute-start.29 = (bf16[16,4096]{1,0:T(8,128)(2,1)S(1)}, bf16[16,4096]{1,0:T(8,128)(2,1)S(1)}, u32[]{:S(2)}, u32[]{:S(2)}) collective-permute-start(bf16[16,4096]{1,0:T(8,128)(2,1)S(1)} %add_convert_fusion.1), channel_id=1, source_target_pairs={{0,12},{4,8},{8,4},{12,0},{1,13},{5,9},{9,5},{13,1},{2,14},{6,10},... | collective-permute-start | bytes 393224 | tf_op jit(solution)/shard_map/ppermute | solution.py:398
  73.9 2.7 %collective-permute-done.24 = bf16[16,4096]{1,0:T(8,128)(2,1)S(1)} collective-permute-done((bf16[16,4096]{1,0:T(8,128)(2,1)S(1)}, bf16[16,4096]{1,0:T(8,128)(2,1)S(1)}, u32[]{:S(2)}, u32[]{:S(2)}) %collective-permute-start.24) | collective-permute-done | bytes 131104 | tf_op jit(solution)/shard_map/ppermute | solution.py:395
  79.2 2.8 %collective-permute-done.27 = bf16[16,4096]{1,0:T(8,128)(2,1)S(1)} collective-permute-done((bf16[16,4096]{1,0:T(8,128)(2,1)S(1)}, bf16[16,4096]{1,0:T(8,128)(2,1)S(1)}, u32[]{:S(2)}, u32[]{:S(2)}) %collective-permute-start.27) | collective-permute-done | bytes 131104 | tf_op jit(solution)/shard_map/ppermute | solution.py:398
  (100 shorter events, 24.6 us)
Async XLA Ops:
  4.8 19.3 %collective-permute-start.2 = (bf16[336,256]{1,0:T(8,128)(2,1)S(1)}, bf16[336,256]{1,0:T(8,128)(2,1)S(1)}, u32[]{:S(2)}, u32[]{:S(2)}) collective-permute-start(bf16[336,256]{1,0:T(8,128)(2,1)S(1)} %pad_maximum_fusion.refs_3_.refs_4_), channel_id=1, source_target_pairs={{0,12},{4,8},{8,4},{12,0},{1,13},{5,9},{9,5},{13,1},{2,14},{6,10},... | collective-permute-start | bytes 516104 | tf_op jit(solution)/shard_map/ppermute | solution.py:383
  9.9 14.6 %collective-permute-start.1 = (bf16[336,256]{1,0:T(8,128)(2,1)S(1)}, bf16[336,256]{1,0:T(8,128)(2,1)S(1)}, u32[]{:S(2)}, u32[]{:S(2)}) collective-permute-start(bf16[336,256]{1,0:T(8,128)(2,1)S(1)} %pad_maximum_fusion.refs_3_.refs_4_), channel_id=1, source_target_pairs={{0,8},{4,12},{8,0},{12,4},{1,9},{5,13},{9,1},{13,5},{2,10},{6,14},... | collective-permute-start | bytes 516104 | tf_op jit(solution)/shard_map/ppermute | solution.py:383
  9.9 14.6 %collective-permute-start = (bf16[336,256]{1,0:T(8,128)(2,1)S(1)}, bf16[336,256]{1,0:T(8,128)(2,1)S(1)}, u32[]{:S(2)}, u32[]{:S(2)}) collective-permute-start(bf16[336,256]{1,0:T(8,128)(2,1)S(1)} %pad_maximum_fusion.refs_3_.refs_4_), channel_id=1, source_target_pairs={{0,4},{4,0},{8,12},{12,8},{1,5},{5,1},{9,13},{13,9},{2,6},{6,2},{1... | collective-permute-start | bytes 516104 | tf_op jit(solution)/shard_map/ppermute | solution.py:383
  29.6 5.6 %collective-permute-start.4 = (bf16[16,4096]{1,0:T(8,128)(2,1)S(1)}, bf16[16,4096]{1,0:T(8,128)(2,1)S(1)}, u32[]{:S(2)}, u32[]{:S(2)}) collective-permute-start(bf16[16,4096]{1,0:T(8,128)(2,1)S(1)} %get-tuple-element.70), channel_id=1, source_target_pairs={{0,2},{1,3},{2,0},{3,1},{4,6},{5,7},{6,4},{7,5},{8,10},{9,11},{10,... | collective-permute-start | bytes 393224 | tf_op jit(solution)/shard_map/ppermute | solution.py:395
  35.4 7.2 %collective-permute-start.8 = (bf16[16,4096]{1,0:T(8,128)(2,1)S(1)}, bf16[16,4096]{1,0:T(8,128)(2,1)S(1)}, u32[]{:S(2)}, u32[]{:S(2)}) collective-permute-start(bf16[16,4096]{1,0:T(8,128)(2,1)S(1)} %get-tuple-element.39.refs_7_.refs_1_), channel_id=1, source_target_pairs={{0,4},{4,0},{8,12},{12,8},{1,5},{5,1},{9,13},{13,9},{2,6},{6,2},{1... | collective-permute-start | bytes 393224 | tf_op jit(solution)/shard_map/ppermute | solution.py:398
  36.5 8.5 %collective-permute-start.7 = (bf16[16,4096]{1,0:T(8,128)(2,1)S(1)}, bf16[16,4096]{1,0:T(8,128)(2,1)S(1)}, u32[]{:S(2)}, u32[]{:S(2)}) collective-permute-start(bf16[16,4096]{1,0:T(8,128)(2,1)S(1)} %get-tuple-element.39.refs_7_.refs_1_), channel_id=1, source_target_pairs={{0,8},{4,12},{8,0},{12,4},{1,9},{5,13},{9,1},{13,5},{2,10},{6,14},... | collective-permute-start | bytes 393224 | tf_op jit(solution)/shard_map/ppermute | solution.py:398
  39.4 5.5 %collective-permute-start.6 = (bf16[16,4096]{1,0:T(8,128)(2,1)S(1)}, bf16[16,4096]{1,0:T(8,128)(2,1)S(1)}, u32[]{:S(2)}, u32[]{:S(2)}) collective-permute-start(bf16[16,4096]{1,0:T(8,128)(2,1)S(1)} %get-tuple-element.39.refs_7_.refs_1_), channel_id=1, source_target_pairs={{0,1},{1,0},{2,3},{3,2},{4,5},{5,4},{6,7},{7,6},{8,9},{9,8},{10,11... | collective-permute-start | bytes 393224 | tf_op jit(solution)/shard_map/ppermute | solution.py:395
  39.4 5.9 %collective-permute-start.5 = (bf16[16,4096]{1,0:T(8,128)(2,1)S(1)}, bf16[16,4096]{1,0:T(8,128)(2,1)S(1)}, u32[]{:S(2)}, u32[]{:S(2)}) collective-permute-start(bf16[16,4096]{1,0:T(8,128)(2,1)S(1)} %get-tuple-element.39.refs_7_.refs_1_), channel_id=1, source_target_pairs={{0,2},{1,3},{2,0},{3,1},{4,6},{5,7},{6,4},{7,5},{8,10},{9,11},{10,... | collective-permute-start | bytes 393224 | tf_op jit(solution)/shard_map/ppermute | solution.py:395
  45.3 5.9 %collective-permute-start.12 = (bf16[16,4096]{1,0:T(8,128)(2,1)S(1)}, bf16[16,4096]{1,0:T(8,128)(2,1)S(1)}, u32[]{:S(2)}, u32[]{:S(2)}) collective-permute-start(bf16[16,4096]{1,0:T(8,128)(2,1)S(1)} %collective-permute-done.7.refs_1_), channel_id=1, source_target_pairs={{0,4},{4,0},{8,12},{12,8},{1,5},{5,1},{9,13},{13,9},{2,6},{6,2},{1... | collective-permute-start | bytes 393224 | tf_op jit(solution)/shard_map/ppermute | solution.py:398
  45.4 5.8 %collective-permute-start.11 = (bf16[16,4096]{1,0:T(8,128)(2,1)S(1)}, bf16[16,4096]{1,0:T(8,128)(2,1)S(1)}, u32[]{:S(2)}, u32[]{:S(2)}) collective-permute-start(bf16[16,4096]{1,0:T(8,128)(2,1)S(1)} %collective-permute-done.7.refs_1_), channel_id=1, source_target_pairs={{0,2},{1,3},{2,0},{3,1},{4,6},{5,7},{6,4},{7,5},{8,10},{9,11},{10,... | collective-permute-start | bytes 393224 | tf_op jit(solution)/shard_map/ppermute | solution.py:395
  46.9 6.4 %collective-permute-start.14 = (bf16[16,4096]{1,0:T(8,128)(2,1)S(1)}, bf16[16,4096]{1,0:T(8,128)(2,1)S(1)}, u32[]{:S(2)}, u32[]{:S(2)}) collective-permute-start(bf16[16,4096]{1,0:T(8,128)(2,1)S(1)} %collective-permute-done.7.refs_1_), channel_id=1, source_target_pairs={{0,1},{1,0},{2,3},{3,2},{4,5},{5,4},{6,7},{7,6},{8,9},{9,8},{10,11... | collective-permute-start | bytes 393224 | tf_op jit(solution)/shard_map/ppermute | solution.py:395
  51.3 5.9 %collective-permute-start.13 = (bf16[16,4096]{1,0:T(8,128)(2,1)S(1)}, bf16[16,4096]{1,0:T(8,128)(2,1)S(1)}, u32[]{:S(2)}, u32[]{:S(2)}) collective-permute-start(bf16[16,4096]{1,0:T(8,128)(2,1)S(1)} %collective-permute-done.12.refs_1_), channel_id=1, source_target_pairs={{0,2},{1,3},{2,0},{3,1},{4,6},{5,7},{6,4},{7,5},{8,10},{9,11},{10,... | collective-permute-start | bytes 393224 | tf_op jit(solution)/shard_map/ppermute | solution.py:395
  52.7 5.1 %collective-permute-start.17 = (bf16[16,4096]{1,0:T(8,128)(2,1)S(1)}, bf16[16,4096]{1,0:T(8,128)(2,1)S(1)}, u32[]{:S(2)}, u32[]{:S(2)}) collective-permute-start(bf16[16,4096]{1,0:T(8,128)(2,1)S(1)} %collective-permute-done.12.refs_1_), channel_id=1, source_target_pairs={{0,1},{1,0},{2,3},{3,2},{4,5},{5,4},{6,7},{7,6},{8,9},{9,8},{10,11... | collective-permute-start | bytes 393224 | tf_op jit(solution)/shard_map/ppermute | solution.py:395
  53.0 9.2 %collective-permute-start.10 = (bf16[32,4096]{1,0:T(8,128)(2,1)S(1)}, bf16[32,4096]{1,0:T(8,128)(2,1)S(1)}, u32[]{:S(2)}, u32[]{:S(2)}) collective-permute-start(bf16[32,4096]{1,0:T(8,128)(2,1)S(1)} %get-tuple-element.52.refs_7_), channel_id=1, source_target_pairs={{0,1},{1,0},{2,3},{3,2},{4,5},{5,4},{6,7},{7,6},{8,9},{9,8},{10,11... | collective-permute-start | bytes 786440 | tf_op jit(solution)/shard_map/ppermute | solution.py:395
  57.2 21.1 %collective-permute-start.31 = (bf16[8,16,256]{2,1,0:T(8,128)(2,1)S(1)}, bf16[8,16,256]{2,1,0:T(8,128)(2,1)S(1)}, u32[]{:S(2)}, u32[]{:S(2)}) collective-permute-start(bf16[8,16,256]{2,1,0:T(8,128)(2,1)S(1)} %bitcast.26), channel_id=1, source_target_pairs={{0,1},{1,0},{2,3},{3,2},{4,5},{5,4},{6,7},{7,6},{8,9},{9,8},{10,11... | collective-permute-start | bytes 196616 | tf_op jit(solution)/shard_map/ppermute | solution.py:532
  57.8 7.5 %collective-permute-start.20 = (bf16[16,4096]{1,0:T(8,128)(2,1)S(1)}, bf16[16,4096]{1,0:T(8,128)(2,1)S(1)}, u32[]{:S(2)}, u32[]{:S(2)}) collective-permute-start(bf16[16,4096]{1,0:T(8,128)(2,1)S(1)} %collective-permute-done.8.refs_1_), channel_id=1, source_target_pairs={{0,1},{1,0},{2,3},{3,2},{4,5},{5,4},{6,7},{7,6},{8,9},{9,8},{10,11... | collective-permute-start | bytes 393224 | tf_op jit(solution)/shard_map/ppermute | solution.py:395
  57.8 5.8 %collective-permute-start.16 = (bf16[16,4096]{1,0:T(8,128)(2,1)S(1)}, bf16[16,4096]{1,0:T(8,128)(2,1)S(1)}, u32[]{:S(2)}, u32[]{:S(2)}) collective-permute-start(bf16[16,4096]{1,0:T(8,128)(2,1)S(1)} %collective-permute-done.8.refs_1_), channel_id=1, source_target_pairs={{0,2},{1,3},{2,0},{3,1},{4,6},{5,7},{6,4},{7,5},{8,10},{9,11},{10,... | collective-permute-start | bytes 393224 | tf_op jit(solution)/shard_map/ppermute | solution.py:395
  62.7 6.4 %collective-permute-start.26 = (bf16[16,4096]{1,0:T(8,128)(2,1)S(1)}, bf16[16,4096]{1,0:T(8,128)(2,1)S(1)}, u32[]{:S(2)}, u32[]{:S(2)}) collective-permute-start(bf16[16,4096]{1,0:T(8,128)(2,1)S(1)} %add_convert_fusion.5.refs_8_), channel_id=1, source_target_pairs={{0,2},{1,3},{2,0},{3,1},{4,6},{5,7},{6,4},{7,5},{8,10},{9,11},{10,... | collective-permute-start | bytes 393224 | tf_op jit(solution)/shard_map/ppermute | solution.py:395
  64.2 7.9 %collective-permute-start.28 = (bf16[16,4096]{1,0:T(8,128)(2,1)S(1)}, bf16[16,4096]{1,0:T(8,128)(2,1)S(1)}, u32[]{:S(2)}, u32[]{:S(2)}) collective-permute-start(bf16[16,4096]{1,0:T(8,128)(2,1)S(1)} %add_convert_fusion.2), channel_id=1, source_target_pairs={{0,2},{1,3},{2,0},{3,1},{4,6},{5,7},{6,4},{7,5},{8,10},{9,11},{10,... | collective-permute-start | bytes 393224 | tf_op jit(solution)/shard_map/ppermute | solution.py:395
  69.1 12.8 %collective-permute-start.27 = (bf16[16,4096]{1,0:T(8,128)(2,1)S(1)}, bf16[16,4096]{1,0:T(8,128)(2,1)S(1)}, u32[]{:S(2)}, u32[]{:S(2)}) collective-permute-start(bf16[16,4096]{1,0:T(8,128)(2,1)S(1)} %add_convert_fusion.3), channel_id=1, source_target_pairs={{0,8},{4,12},{8,0},{12,4},{1,9},{5,13},{9,1},{13,5},{2,10},{6,14},... | collective-permute-start | bytes 393224 | tf_op jit(solution)/shard_map/ppermute | solution.py:398
  71.6 5.0 %collective-permute-start.24 = (bf16[16,4096]{1,0:T(8,128)(2,1)S(1)}, bf16[16,4096]{1,0:T(8,128)(2,1)S(1)}, u32[]{:S(2)}, u32[]{:S(2)}) collective-permute-start(bf16[16,4096]{1,0:T(8,128)(2,1)S(1)} %add_convert_fusion.4), channel_id=1, source_target_pairs={{0,2},{1,3},{2,0},{3,1},{4,6},{5,7},{6,4},{7,5},{8,10},{9,11},{10,... | collective-permute-start | bytes 393224 | tf_op jit(solution)/shard_map/ppermute | solution.py:395
  72.1 9.9 %collective-permute-start.29 = (bf16[16,4096]{1,0:T(8,128)(2,1)S(1)}, bf16[16,4096]{1,0:T(8,128)(2,1)S(1)}, u32[]{:S(2)}, u32[]{:S(2)}) collective-permute-start(bf16[16,4096]{1,0:T(8,128)(2,1)S(1)} %add_convert_fusion.1), channel_id=1, source_target_pairs={{0,12},{4,8},{8,4},{12,0},{1,13},{5,9},{9,5},{13,1},{2,14},{6,10},... | collective-permute-start | bytes 393224 | tf_op jit(solution)/shard_map/ppermute | solution.py:398
  76.7 6.7 %collective-permute-start.30 = (bf16[16,4096]{1,0:T(8,128)(2,1)S(1)}, bf16[16,4096]{1,0:T(8,128)(2,1)S(1)}, u32[]{:S(2)}, u32[]{:S(2)}) collective-permute-start(bf16[16,4096]{1,0:T(8,128)(2,1)S(1)} %add_convert_fusion), channel_id=1, source_target_pairs={{0,4},{4,0},{8,12},{12,8},{1,5},{5,1},{9,13},{13,9},{2,6},{6,2},{1... | collective-permute-start | bytes 393224 | tf_op jit(solution)/shard_map/ppermute | solution.py:398
  77.1 6.3 %collective-permute-start.25 = (bf16[16,4096]{1,0:T(8,128)(2,1)S(1)}, bf16[16,4096]{1,0:T(8,128)(2,1)S(1)}, u32[]{:S(2)}, u32[]{:S(2)}) collective-permute-start(bf16[16,4096]{1,0:T(8,128)(2,1)S(1)} %add_convert_fusion.6), channel_id=1, source_target_pairs={{0,2},{1,3},{2,0},{3,1},{4,6},{5,7},{6,4},{7,5},{8,10},{9,11},{10,... | collective-permute-start | bytes 393224 | tf_op jit(solution)/shard_map/ppermute | solution.py:395
  (17 other events, 61.4 us)

commit v18 on v17

--- a/solution.py
+++ b/solution.py
@@ -519,11 +519,17 @@
         own = (own + got.astype(jnp.float32)).astype(jnp.bfloat16)
         given.append(gives[0] if gives else own)
         finished.append(own)
-        crossing.append(across(own, step))
+        crossing.append(own)
     own_sum, own_got, _, _ = scatter(own_kept, own_sent, got)
     mixture = mixture + own_sum + own_got.astype(jnp.float32)
-    for rows in crossing:
-        mixture = mixture + rows.astype(jnp.float32)
+    sums = dict(zip(order, (rows.astype(jnp.float32) for rows in crossing)))
+    sums[0] = mixture
+    for bit in reversed(ep_bits):
+        for step in [step for step in sums if step & bit]:
+            sums[step ^ bit] = sums[step ^ bit] + across(
+                sums.pop(step).astype(jnp.bfloat16), bit
+            ).astype(jnp.float32)
+    mixture = sums[0]
     layer_out = jnp.where(row_mask[:, None] > 0, mixture, 0.0).astype(jnp.bfloat16)
 
     if keyval_local == 1:

time: 84.6 us -> 84.4 us (level)
    ppermute x22, waiting for transfers between devices: 11.1 us -> 9.71 us  [local(): lax.ppermute(value, ('kv', 'tp'), [(i, i ^ bit) for i in range(blocks)])]
    unnamed x21 -> x19, local copies, waits for them, and re-layouts: 9.62 us -> 9.61 us
  transfers between devices with their start and end apart: 32 -> 32, of which waited for: 14 -> 15; matrix products, arithmetic and copies ran while one was open for 5% -> 5% of each run, Pallas kernels for 16% -> 16%
where the time goes in v18:
time: 84.4 us; the launch traced here: 84 us
  starting transfers between devices  28.8 us (34%)
  waiting for transfers between devices  19.4 us (23%)
  Pallas kernels  17.1 us (20%)
  local copies, waits for them, and re-layouts  14.1 us (17%)
  other arithmetic  3.62 us (4%)
  between operations  0.95 us (1%)
    ppermute x22, starting transfers between devices, local(): lax.ppermute(value, ('kv', 'tp'), [(i, i ^ bit) for i in range(blocks)])  13.8 us
    pallas_call x4, Pallas kernels, expert_call(): pl.pallas_call(lambda *refs: expert_kernel(len(have), steps, blocks, *ref...  10.6 us
    ppermute x22, waiting for transfers between devices, local(): lax.ppermute(value, ('kv', 'tp'), [(i, i ^ bit) for i in range(blocks)])  9.71 us
    unnamed x19, local copies, waits for them, and re-layouts  9.61 us
    ppermute x6, waiting for transfers between devices, local(): lax.ppermute(value, 'ep', [(i, i ^ step) for i in range(ep_count)])  9.22 us
    ppermute x6, starting transfers between devices, local(): lax.ppermute(value, 'ep', [(i, i ^ step) for i in range(ep_count)])  8.7 us
    ppermute x3, starting transfers between devices, local(): lax.ppermute(payload, 'ep', [(i, i ^ step) for i in range(ep_count)])  5.76 us
    pallas_call x1, Pallas kernels, attend_call(): pl.pallas_call(lambda *refs: attend_kernel(ep_count, held, tokens, blocks...  3.4 us
  transfers between devices with their start and end apart: 32, of which 15 were waited for; matrix products, arithmetic and copies ran while one was open for 5% of the time, Pallas kernels for 16%

profile of v18, /device:TPU:0, one launch (start us, length us, event | category | flops | bytes accessed | tf_op | source)
XLA Modules:
  0.0 84.0 jit_solution(8872421000203346973)
XLA Ops:
  4.8 5.1 %collective-permute-start.2 = (bf16[336,256]{1,0:T(8,128)(2,1)S(1)}, bf16[336,256]{1,0:T(8,128)(2,1)S(1)}, u32[]{:S(2)}, u32[]{:S(2)}) collective-permute-start(bf16[336,256]{1,0:T(8,128)(2,1)S(1)} %pad_maximum_fusion.refs_3_.refs_4_), channel_id=1, source_target_pairs={{0,12},{4,8},{8,4},{12,0},{1,13},{5,9},{9,5},{13,1},{2,14},{6,10},... | collective-permute-start | bytes 516104 | tf_op jit(solution)/shard_map/ppermute | solution.py:383
  13.5 3.4 %copy-done.1 = bf16[1024,4096]{1,0:T(8,128)(2,1)S(1)} copy-done((bf16[1024,4096]{1,0:T(8,128)(2,1)S(1)}, bf16[1024,4096]{1,0:T(8,128)(2,1)}, u32[]{:S(2)}) %copy-start.1) | copy-done | bytes 8388632
  16.8 2.8 %copy-done.2 = bf16[1,2,384,4096]{3,2,1,0:T(8,128)(2,1)S(1)} copy-done((bf16[1,2,384,4096]{3,2,1,0:T(8,128)(2,1)S(1)}, bf16[1,2,384,4096]{3,2,1,0:T(8,128)(2,1)}, u32[]{:S(2)}) %copy-start.2) | copy-done | bytes 6291480
  19.6 1.9 %copy-done.3 = bf16[1,384,4096]{2,1,0:T(8,128)(2,1)S(1)} copy-done((bf16[1,384,4096]{2,1,0:T(8,128)(2,1)S(1)}, bf16[1,384,4096]{2,1,0:T(8,128)(2,1)}, u32[]{:S(2)}) %copy-start.3) | copy-done | bytes 3145752
  22.2 1.8 %hold.1 = (bf16[1024,4096]{1,0:T(8,128)(2,1)S(1)}, bf16[1,2,384,4096]{3,2,1,0:T(8,128)(2,1)S(1)}, bf16[1,384,4096]{2,1,0:T(8,128)(2,1)S(1)}, f32[8,128]{1,0:T(8,128)}) custom-call(bf16[1024,4096]{1,0:T(8,128)(2,1)S(1)} %copy-done.1, bf16[1,2,384,4096]{3,2,1,0:T(8,128)(2,1)S(1)} %copy-done.2, bf16[1,384,4096]{2,1,0:T(8,128)(2,1)S(1)} %copy-done.3, ...), custom_call_target="tpu_custom_call" | custom-call | bytes 35651584 | tf_op jit(solution)/shard_map/hold/pallas_call | solution.py:62
  24.5 3.4 %attend.1 = (f32[32,4096]{1,0:T(8,128)S(1)}, bf16[32,4096]{1,0:T(8,128)(2,1)S(1)}) custom-call(s32[4]{0:T(128)S(1)} %copy-done.6, s32[2]{0:T(128)S(1)} %pad_add_fusion.refs_4_.refs_1_.refs_2_, s32[1]{0:T(128)} %constant.48.clone.1.refs_2_, bf16[64,1024]{1,0:T(8,128)(2,1)S(1)} %copy-done.4, bf16[336,256]{1,0:T(8,128)(2,1)S(1)} %pad_maximum_fusion.refs_3_.refs_4_, ...), custom_call_target="tpu_custom_call" | custom-call | flops 872415232 | bytes 8388608 | tf_op jit(solution)/shard_map/attend/pallas_call | solution.py:247
  28.0 1.5 %collective-permute-done.3 = bf16[32,4096]{1,0:T(8,128)(2,1)S(1)} collective-permute-done((bf16[32,4096]{1,0:T(8,128)(2,1)S(1)}, bf16[32,4096]{1,0:T(8,128)(2,1)S(1)}, u32[]{:S(2)}, u32[]{:S(2)}) %collective-permute-start.3) | collective-permute-done | bytes 262176 | tf_op jit(solution)/shard_map/ppermute | solution.py:395
  29.6 1.6 %collective-permute-start.4 = (bf16[16,4096]{1,0:T(8,128)(2,1)S(1)}, bf16[16,4096]{1,0:T(8,128)(2,1)S(1)}, u32[]{:S(2)}, u32[]{:S(2)}) collective-permute-start(bf16[16,4096]{1,0:T(8,128)(2,1)S(1)} %get-tuple-element.70), channel_id=1, source_target_pairs={{0,2},{1,3},{2,0},{3,1},{4,6},{5,7},{6,4},{7,5},{8,10},{9,11},{10,... | collective-permute-start | bytes 393224 | tf_op jit(solution)/shard_map/ppermute | solution.py:395
  31.1 4.1 %collective-permute-done.4.got = bf16[16,4096]{1,0:T(8,128)(2,1)S(1)} collective-permute-done((bf16[16,4096]{1,0:T(8,128)(2,1)S(1)}, bf16[16,4096]{1,0:T(8,128)(2,1)S(1)}, u32[]{:S(2)}, u32[]{:S(2)}) %collective-permute-start.4) | collective-permute-done | bytes 131104 | tf_op jit(solution)/shard_map/ppermute | solution.py:395
  36.4 2.9 %collective-permute-start.7 = (bf16[16,4096]{1,0:T(8,128)(2,1)S(1)}, bf16[16,4096]{1,0:T(8,128)(2,1)S(1)}, u32[]{:S(2)}, u32[]{:S(2)}) collective-permute-start(bf16[16,4096]{1,0:T(8,128)(2,1)S(1)} %get-tuple-element.39.refs_7_.refs_1_), channel_id=1, source_target_pairs={{0,8},{4,12},{8,0},{12,4},{1,9},{5,13},{9,1},{13,5},{2,10},{6,14},... | collective-permute-start | bytes 393224 | tf_op jit(solution)/shard_map/ppermute | solution.py:398
  39.4 1.5 %collective-permute-start.5 = (bf16[16,4096]{1,0:T(8,128)(2,1)S(1)}, bf16[16,4096]{1,0:T(8,128)(2,1)S(1)}, u32[]{:S(2)}, u32[]{:S(2)}) collective-permute-start(bf16[16,4096]{1,0:T(8,128)(2,1)S(1)} %get-tuple-element.39.refs_7_.refs_1_), channel_id=1, source_target_pairs={{0,2},{1,3},{2,0},{3,1},{4,6},{5,7},{6,4},{7,5},{8,10},{9,11},{10,... | collective-permute-start | bytes 393224 | tf_op jit(solution)/shard_map/ppermute | solution.py:395
  42.6 2.3 %collective-permute-done.7.refs_1_ = bf16[16,4096]{1,0:T(8,128)(2,1)S(1)} collective-permute-done((bf16[16,4096]{1,0:T(8,128)(2,1)S(1)}, bf16[16,4096]{1,0:T(8,128)(2,1)S(1)}, u32[]{:S(2)}, u32[]{:S(2)}) %collective-permute-start.7) | collective-permute-done | bytes 131104 | tf_op jit(solution)/shard_map/ppermute | solution.py:398
  45.3 1.5 %collective-permute-start.11 = (bf16[16,4096]{1,0:T(8,128)(2,1)S(1)}, bf16[16,4096]{1,0:T(8,128)(2,1)S(1)}, u32[]{:S(2)}, u32[]{:S(2)}) collective-permute-start(bf16[16,4096]{1,0:T(8,128)(2,1)S(1)} %collective-permute-done.7.refs_1_), channel_id=1, source_target_pairs={{0,2},{1,3},{2,0},{3,1},{4,6},{5,7},{6,4},{7,5},{8,10},{9,11},{10,... | collective-permute-start | bytes 393224 | tf_op jit(solution)/shard_map/ppermute | solution.py:395
  47.0 2.7 %experts.4 = (bf16[32,4096]{1,0:T(8,128)(2,1)S(1)}, bf16[32,4096]{1,0:T(8,128)(2,1)S(1)}) custom-call(f32[256,128]{1,0:T(8,128)S(1)} %get-tuple-element.41.refs_0_, bf16[16,4096]{1,0:T(8,128)(2,1)S(1)} %get-tuple-element.39.refs_7_.refs_1_, bf16[16,4096]{1,0:T(8,128)(2,1)S(1)} %collective-permute-done.5.refs_2_, ...), custom_call_target="tpu_custom_call" | custom-call | flops 1024 | bytes 1024 | tf_op jit(solution)/shard_map/experts/pallas_call | solution.py:310
  49.7 1.5 %collective-permute-done.12.refs_1_ = bf16[16,4096]{1,0:T(8,128)(2,1)S(1)} collective-permute-done((bf16[16,4096]{1,0:T(8,128)(2,1)S(1)}, bf16[16,4096]{1,0:T(8,128)(2,1)S(1)}, u32[]{:S(2)}, u32[]{:S(2)}) %collective-permute-start.12) | collective-permute-done | bytes 131104 | tf_op jit(solution)/shard_map/ppermute | solution.py:398
  51.2 1.5 %collective-permute-start.13 = (bf16[16,4096]{1,0:T(8,128)(2,1)S(1)}, bf16[16,4096]{1,0:T(8,128)(2,1)S(1)}, u32[]{:S(2)}, u32[]{:S(2)}) collective-permute-start(bf16[16,4096]{1,0:T(8,128)(2,1)S(1)} %collective-permute-done.12.refs_1_), channel_id=1, source_target_pairs={{0,2},{1,3},{2,0},{3,1},{4,6},{5,7},{6,4},{7,5},{8,10},{9,11},{10,... | collective-permute-start | bytes 393224 | tf_op jit(solution)/shard_map/ppermute | solution.py:395
  53.2 2.7 %experts.5 = (bf16[32,4096]{1,0:T(8,128)(2,1)S(1)}, bf16[32,4096]{1,0:T(8,128)(2,1)S(1)}) custom-call(f32[256,128]{1,0:T(8,128)S(1)} %get-tuple-element.41.refs_0_, bf16[16,4096]{1,0:T(8,128)(2,1)S(1)} %collective-permute-done.7.refs_1_, bf16[16,4096]{1,0:T(8,128)(2,1)S(1)} %collective-permute-done.11.refs_2_, ...), custom_call_target="tpu_custom_call" | custom-call | flops 1024 | bytes 1024 | tf_op jit(solution)/shard_map/experts/pallas_call | solution.py:310
  57.8 1.5 %collective-permute-start.16 = (bf16[16,4096]{1,0:T(8,128)(2,1)S(1)}, bf16[16,4096]{1,0:T(8,128)(2,1)S(1)}, u32[]{:S(2)}, u32[]{:S(2)}) collective-permute-start(bf16[16,4096]{1,0:T(8,128)(2,1)S(1)} %collective-permute-done.8.refs_1_), channel_id=1, source_target_pairs={{0,2},{1,3},{2,0},{3,1},{4,6},{5,7},{6,4},{7,5},{8,10},{9,11},{10,... | collective-permute-start | bytes 393224 | tf_op jit(solution)/shard_map/ppermute | solution.py:395
  59.5 2.7 %experts.6 = (bf16[32,4096]{1,0:T(8,128)(2,1)S(1)}, bf16[32,4096]{1,0:T(8,128)(2,1)S(1)}) custom-call(f32[256,128]{1,0:T(8,128)S(1)} %get-tuple-element.41.refs_0_, bf16[16,4096]{1,0:T(8,128)(2,1)S(1)} %collective-permute-done.12.refs_1_, bf16[16,4096]{1,0:T(8,128)(2,1)S(1)} %collective-permute-done.13.refs_2_, ...), custom_call_target="tpu_custom_call" | custom-call | flops 1024 | bytes 1024 | tf_op jit(solution)/shard_map/experts/pallas_call | solution.py:310
  66.5 2.7 %experts.7 = (bf16[32,4096]{1,0:T(8,128)(2,1)S(1)}, bf16[32,4096]{1,0:T(8,128)(2,1)S(1)}) custom-call(f32[256,128]{1,0:T(8,128)S(1)} %get-tuple-element.41.refs_0_, bf16[16,4096]{1,0:T(8,128)(2,1)S(1)} %collective-permute-done.8.refs_1_, bf16[16,4096]{1,0:T(8,128)(2,1)S(1)} %collective-permute-done.16.refs_2_, ...), custom_call_target="tpu_custom_call" | custom-call | flops 1024 | bytes 1024 | tf_op jit(solution)/shard_map/experts/pallas_call | solution.py:310
  70.2 1.8 %collective-permute-start.29 = (bf16[16,4096]{1,0:T(8,128)(2,1)S(1)}, bf16[16,4096]{1,0:T(8,128)(2,1)S(1)}, u32[]{:S(2)}, u32[]{:S(2)}) collective-permute-start(bf16[16,4096]{1,0:T(8,128)(2,1)S(1)} %add_convert_fusion.1), channel_id=1, source_target_pairs={{0,4},{4,0},{8,12},{12,8},{1,5},{5,1},{9,13},{13,9},{2,6},{6,2},{1... | collective-permute-start | bytes 393224 | tf_op jit(solution)/shard_map/ppermute | solution.py:398
  73.4 1.9 %collective-permute-done.29 = bf16[16,4096]{1,0:T(8,128)(2,1)S(1)} collective-permute-done((bf16[16,4096]{1,0:T(8,128)(2,1)S(1)}, bf16[16,4096]{1,0:T(8,128)(2,1)S(1)}, u32[]{:S(2)}, u32[]{:S(2)}) %collective-permute-start.29) | collective-permute-done | bytes 131104 | tf_op jit(solution)/shard_map/ppermute | solution.py:398
  75.3 2.4 %collective-permute-start.30 = (bf16[16,4096]{1,0:T(8,128)(2,1)S(1)}, bf16[16,4096]{1,0:T(8,128)(2,1)S(1)}, u32[]{:S(2)}, u32[]{:S(2)}) collective-permute-start(bf16[16,4096]{1,0:T(8,128)(2,1)S(1)} %add_convert_fusion), channel_id=1, source_target_pairs={{0,8},{4,12},{8,0},{12,4},{1,9},{5,13},{9,1},{13,5},{2,10},{6,14},... | collective-permute-start | bytes 393224 | tf_op jit(solution)/shard_map/ppermute | solution.py:398
  80.2 1.8 %collective-permute-done.30 = bf16[16,4096]{1,0:T(8,128)(2,1)S(1)} collective-permute-done((bf16[16,4096]{1,0:T(8,128)(2,1)S(1)}, bf16[16,4096]{1,0:T(8,128)(2,1)S(1)}, u32[]{:S(2)}, u32[]{:S(2)}) %collective-permute-start.30) | collective-permute-done | bytes 131104 | tf_op jit(solution)/shard_map/ppermute | solution.py:398
  (98 shorter events, 26.4 us)
Async XLA Ops:
  4.8 19.2 %collective-permute-start.2 = (bf16[336,256]{1,0:T(8,128)(2,1)S(1)}, bf16[336,256]{1,0:T(8,128)(2,1)S(1)}, u32[]{:S(2)}, u32[]{:S(2)}) collective-permute-start(bf16[336,256]{1,0:T(8,128)(2,1)S(1)} %pad_maximum_fusion.refs_3_.refs_4_), channel_id=1, source_target_pairs={{0,12},{4,8},{8,4},{12,0},{1,13},{5,9},{9,5},{13,1},{2,14},{6,10},... | collective-permute-start | bytes 516104 | tf_op jit(solution)/shard_map/ppermute | solution.py:383
  9.9 14.6 %collective-permute-start.1 = (bf16[336,256]{1,0:T(8,128)(2,1)S(1)}, bf16[336,256]{1,0:T(8,128)(2,1)S(1)}, u32[]{:S(2)}, u32[]{:S(2)}) collective-permute-start(bf16[336,256]{1,0:T(8,128)(2,1)S(1)} %pad_maximum_fusion.refs_3_.refs_4_), channel_id=1, source_target_pairs={{0,8},{4,12},{8,0},{12,4},{1,9},{5,13},{9,1},{13,5},{2,10},{6,14},... | collective-permute-start | bytes 516104 | tf_op jit(solution)/shard_map/ppermute | solution.py:383
  9.9 14.6 %collective-permute-start = (bf16[336,256]{1,0:T(8,128)(2,1)S(1)}, bf16[336,256]{1,0:T(8,128)(2,1)S(1)}, u32[]{:S(2)}, u32[]{:S(2)}) collective-permute-start(bf16[336,256]{1,0:T(8,128)(2,1)S(1)} %pad_maximum_fusion.refs_3_.refs_4_), channel_id=1, source_target_pairs={{0,4},{4,0},{8,12},{12,8},{1,5},{5,1},{9,13},{13,9},{2,6},{6,2},{1... | collective-permute-start | bytes 516104 | tf_op jit(solution)/shard_map/ppermute | solution.py:383
  29.6 5.6 %collective-permute-start.4 = (bf16[16,4096]{1,0:T(8,128)(2,1)S(1)}, bf16[16,4096]{1,0:T(8,128)(2,1)S(1)}, u32[]{:S(2)}, u32[]{:S(2)}) collective-permute-start(bf16[16,4096]{1,0:T(8,128)(2,1)S(1)} %get-tuple-element.70), channel_id=1, source_target_pairs={{0,2},{1,3},{2,0},{3,1},{4,6},{5,7},{6,4},{7,5},{8,10},{9,11},{10,... | collective-permute-start | bytes 393224 | tf_op jit(solution)/shard_map/ppermute | solution.py:395
  35.4 7.2 %collective-permute-start.8 = (bf16[16,4096]{1,0:T(8,128)(2,1)S(1)}, bf16[16,4096]{1,0:T(8,128)(2,1)S(1)}, u32[]{:S(2)}, u32[]{:S(2)}) collective-permute-start(bf16[16,4096]{1,0:T(8,128)(2,1)S(1)} %get-tuple-element.39.refs_7_.refs_1_), channel_id=1, source_target_pairs={{0,4},{4,0},{8,12},{12,8},{1,5},{5,1},{9,13},{13,9},{2,6},{6,2},{1... | collective-permute-start | bytes 393224 | tf_op jit(solution)/shard_map/ppermute | solution.py:398
  36.4 8.5 %collective-permute-start.7 = (bf16[16,4096]{1,0:T(8,128)(2,1)S(1)}, bf16[16,4096]{1,0:T(8,128)(2,1)S(1)}, u32[]{:S(2)}, u32[]{:S(2)}) collective-permute-start(bf16[16,4096]{1,0:T(8,128)(2,1)S(1)} %get-tuple-element.39.refs_7_.refs_1_), channel_id=1, source_target_pairs={{0,8},{4,12},{8,0},{12,4},{1,9},{5,13},{9,1},{13,5},{2,10},{6,14},... | collective-permute-start | bytes 393224 | tf_op jit(solution)/shard_map/ppermute | solution.py:398
  39.4 5.5 %collective-permute-start.6 = (bf16[16,4096]{1,0:T(8,128)(2,1)S(1)}, bf16[16,4096]{1,0:T(8,128)(2,1)S(1)}, u32[]{:S(2)}, u32[]{:S(2)}) collective-permute-start(bf16[16,4096]{1,0:T(8,128)(2,1)S(1)} %get-tuple-element.39.refs_7_.refs_1_), channel_id=1, source_target_pairs={{0,1},{1,0},{2,3},{3,2},{4,5},{5,4},{6,7},{7,6},{8,9},{9,8},{10,11... | collective-permute-start | bytes 393224 | tf_op jit(solution)/shard_map/ppermute | solution.py:395
  39.4 5.9 %collective-permute-start.5 = (bf16[16,4096]{1,0:T(8,128)(2,1)S(1)}, bf16[16,4096]{1,0:T(8,128)(2,1)S(1)}, u32[]{:S(2)}, u32[]{:S(2)}) collective-permute-start(bf16[16,4096]{1,0:T(8,128)(2,1)S(1)} %get-tuple-element.39.refs_7_.refs_1_), channel_id=1, source_target_pairs={{0,2},{1,3},{2,0},{3,1},{4,6},{5,7},{6,4},{7,5},{8,10},{9,11},{10,... | collective-permute-start | bytes 393224 | tf_op jit(solution)/shard_map/ppermute | solution.py:395
  45.3 5.9 %collective-permute-start.12 = (bf16[16,4096]{1,0:T(8,128)(2,1)S(1)}, bf16[16,4096]{1,0:T(8,128)(2,1)S(1)}, u32[]{:S(2)}, u32[]{:S(2)}) collective-permute-start(bf16[16,4096]{1,0:T(8,128)(2,1)S(1)} %collective-permute-done.7.refs_1_), channel_id=1, source_target_pairs={{0,4},{4,0},{8,12},{12,8},{1,5},{5,1},{9,13},{13,9},{2,6},{6,2},{1... | collective-permute-start | bytes 393224 | tf_op jit(solution)/shard_map/ppermute | solution.py:398
  45.3 5.8 %collective-permute-start.11 = (bf16[16,4096]{1,0:T(8,128)(2,1)S(1)}, bf16[16,4096]{1,0:T(8,128)(2,1)S(1)}, u32[]{:S(2)}, u32[]{:S(2)}) collective-permute-start(bf16[16,4096]{1,0:T(8,128)(2,1)S(1)} %collective-permute-done.7.refs_1_), channel_id=1, source_target_pairs={{0,2},{1,3},{2,0},{3,1},{4,6},{5,7},{6,4},{7,5},{8,10},{9,11},{10,... | collective-permute-start | bytes 393224 | tf_op jit(solution)/shard_map/ppermute | solution.py:395
  46.8 6.4 %collective-permute-start.14 = (bf16[16,4096]{1,0:T(8,128)(2,1)S(1)}, bf16[16,4096]{1,0:T(8,128)(2,1)S(1)}, u32[]{:S(2)}, u32[]{:S(2)}) collective-permute-start(bf16[16,4096]{1,0:T(8,128)(2,1)S(1)} %collective-permute-done.7.refs_1_), channel_id=1, source_target_pairs={{0,1},{1,0},{2,3},{3,2},{4,5},{5,4},{6,7},{7,6},{8,9},{9,8},{10,11... | collective-permute-start | bytes 393224 | tf_op jit(solution)/shard_map/ppermute | solution.py:395
  51.2 5.9 %collective-permute-start.13 = (bf16[16,4096]{1,0:T(8,128)(2,1)S(1)}, bf16[16,4096]{1,0:T(8,128)(2,1)S(1)}, u32[]{:S(2)}, u32[]{:S(2)}) collective-permute-start(bf16[16,4096]{1,0:T(8,128)(2,1)S(1)} %collective-permute-done.12.refs_1_), channel_id=1, source_target_pairs={{0,2},{1,3},{2,0},{3,1},{4,6},{5,7},{6,4},{7,5},{8,10},{9,11},{10,... | collective-permute-start | bytes 393224 | tf_op jit(solution)/shard_map/ppermute | solution.py:395
  52.7 5.1 %collective-permute-start.17 = (bf16[16,4096]{1,0:T(8,128)(2,1)S(1)}, bf16[16,4096]{1,0:T(8,128)(2,1)S(1)}, u32[]{:S(2)}, u32[]{:S(2)}) collective-permute-start(bf16[16,4096]{1,0:T(8,128)(2,1)S(1)} %collective-permute-done.12.refs_1_), channel_id=1, source_target_pairs={{0,1},{1,0},{2,3},{3,2},{4,5},{5,4},{6,7},{7,6},{8,9},{9,8},{10,11... | collective-permute-start | bytes 393224 | tf_op jit(solution)/shard_map/ppermute | solution.py:395
  52.9 9.2 %collective-permute-start.10 = (bf16[32,4096]{1,0:T(8,128)(2,1)S(1)}, bf16[32,4096]{1,0:T(8,128)(2,1)S(1)}, u32[]{:S(2)}, u32[]{:S(2)}) collective-permute-start(bf16[32,4096]{1,0:T(8,128)(2,1)S(1)} %get-tuple-element.52.refs_7_), channel_id=1, source_target_pairs={{0,1},{1,0},{2,3},{3,2},{4,5},{5,4},{6,7},{7,6},{8,9},{9,8},{10,11... | collective-permute-start | bytes 786440 | tf_op jit(solution)/shard_map/ppermute | solution.py:395
  57.1 22.3 %collective-permute-start.31 = (bf16[8,16,256]{2,1,0:T(8,128)(2,1)S(1)}, bf16[8,16,256]{2,1,0:T(8,128)(2,1)S(1)}, u32[]{:S(2)}, u32[]{:S(2)}) collective-permute-start(bf16[8,16,256]{2,1,0:T(8,128)(2,1)S(1)} %bitcast.26), channel_id=1, source_target_pairs={{0,1},{1,0},{2,3},{3,2},{4,5},{5,4},{6,7},{7,6},{8,9},{9,8},{10,11... | collective-permute-start | bytes 196616 | tf_op jit(solution)/shard_map/ppermute | solution.py:538
  57.7 8.3 %collective-permute-start.20 = (bf16[16,4096]{1,0:T(8,128)(2,1)S(1)}, bf16[16,4096]{1,0:T(8,128)(2,1)S(1)}, u32[]{:S(2)}, u32[]{:S(2)}) collective-permute-start(bf16[16,4096]{1,0:T(8,128)(2,1)S(1)} %collective-permute-done.8.refs_1_), channel_id=1, source_target_pairs={{0,1},{1,0},{2,3},{3,2},{4,5},{5,4},{6,7},{7,6},{8,9},{9,8},{10,11... | collective-permute-start | bytes 393224 | tf_op jit(solution)/shard_map/ppermute | solution.py:395
  57.8 6.0 %collective-permute-start.16 = (bf16[16,4096]{1,0:T(8,128)(2,1)S(1)}, bf16[16,4096]{1,0:T(8,128)(2,1)S(1)}, u32[]{:S(2)}, u32[]{:S(2)}) collective-permute-start(bf16[16,4096]{1,0:T(8,128)(2,1)S(1)} %collective-permute-done.8.refs_1_), channel_id=1, source_target_pairs={{0,2},{1,3},{2,0},{3,1},{4,6},{5,7},{6,4},{7,5},{8,10},{9,11},{10,... | collective-permute-start | bytes 393224 | tf_op jit(solution)/shard_map/ppermute | solution.py:395
  59.3 5.9 %collective-permute-start.22 = (bf16[32,4096]{1,0:T(8,128)(2,1)S(1)}, bf16[32,4096]{1,0:T(8,128)(2,1)S(1)}, u32[]{:S(2)}, u32[]{:S(2)}) collective-permute-start(bf16[32,4096]{1,0:T(8,128)(2,1)S(1)} %get-tuple-element.53.refs_7_), channel_id=1, source_target_pairs={{0,1},{1,0},{2,3},{3,2},{4,5},{5,4},{6,7},{7,6},{8,9},{9,8},{10,11... | collective-permute-start | bytes 786440 | tf_op jit(solution)/shard_map/ppermute | solution.py:395
  63.8 6.4 %collective-permute-start.28 = (bf16[16,4096]{1,0:T(8,128)(2,1)S(1)}, bf16[16,4096]{1,0:T(8,128)(2,1)S(1)}, u32[]{:S(2)}, u32[]{:S(2)}) collective-permute-start(bf16[16,4096]{1,0:T(8,128)(2,1)S(1)} %add_convert_fusion.2), channel_id=1, source_target_pairs={{0,2},{1,3},{2,0},{3,1},{4,6},{5,7},{6,4},{7,5},{8,10},{9,11},{10,... | collective-permute-start | bytes 393224 | tf_op jit(solution)/shard_map/ppermute | solution.py:395
  65.2 8.2 %collective-permute-start.27 = (bf16[16,4096]{1,0:T(8,128)(2,1)S(1)}, bf16[16,4096]{1,0:T(8,128)(2,1)S(1)}, u32[]{:S(2)}, u32[]{:S(2)}) collective-permute-start(bf16[16,4096]{1,0:T(8,128)(2,1)S(1)} %add_convert_fusion.6.refs_8_), channel_id=1, source_target_pairs={{0,2},{1,3},{2,0},{3,1},{4,6},{5,7},{6,4},{7,5},{8,10},{9,11},{10,... | collective-permute-start | bytes 393224 | tf_op jit(solution)/shard_map/ppermute | solution.py:395
  70.2 5.0 %collective-permute-start.29 = (bf16[16,4096]{1,0:T(8,128)(2,1)S(1)}, bf16[16,4096]{1,0:T(8,128)(2,1)S(1)}, u32[]{:S(2)}, u32[]{:S(2)}) collective-permute-start(bf16[16,4096]{1,0:T(8,128)(2,1)S(1)} %add_convert_fusion.1), channel_id=1, source_target_pairs={{0,4},{4,0},{8,12},{12,8},{1,5},{5,1},{9,13},{13,9},{2,6},{6,2},{1... | collective-permute-start | bytes 393224 | tf_op jit(solution)/shard_map/ppermute | solution.py:398
  72.0 5.7 %collective-permute-start.24 = (bf16[16,4096]{1,0:T(8,128)(2,1)S(1)}, bf16[16,4096]{1,0:T(8,128)(2,1)S(1)}, u32[]{:S(2)}, u32[]{:S(2)}) collective-permute-start(bf16[16,4096]{1,0:T(8,128)(2,1)S(1)} %add_convert_fusion.5), channel_id=1, source_target_pairs={{0,2},{1,3},{2,0},{3,1},{4,6},{5,7},{6,4},{7,5},{8,10},{9,11},{10,... | collective-permute-start | bytes 393224 | tf_op jit(solution)/shard_map/ppermute | solution.py:395
  75.3 6.7 %collective-permute-start.30 = (bf16[16,4096]{1,0:T(8,128)(2,1)S(1)}, bf16[16,4096]{1,0:T(8,128)(2,1)S(1)}, u32[]{:S(2)}, u32[]{:S(2)}) collective-permute-start(bf16[16,4096]{1,0:T(8,128)(2,1)S(1)} %add_convert_fusion), channel_id=1, source_target_pairs={{0,8},{4,12},{8,0},{12,4},{1,9},{5,13},{9,1},{13,5},{2,10},{6,14},... | collective-permute-start | bytes 393224 | tf_op jit(solution)/shard_map/ppermute | solution.py:398
  77.8 5.3 %collective-permute-start.26 = (bf16[16,4096]{1,0:T(8,128)(2,1)S(1)}, bf16[16,4096]{1,0:T(8,128)(2,1)S(1)}, u32[]{:S(2)}, u32[]{:S(2)}) collective-permute-start(bf16[16,4096]{1,0:T(8,128)(2,1)S(1)} %add_convert_fusion.4), channel_id=1, source_target_pairs={{0,4},{4,0},{8,12},{12,8},{1,5},{5,1},{9,13},{13,9},{2,6},{6,2},{1... | collective-permute-start | bytes 393224 | tf_op jit(solution)/shard_map/ppermute | solution.py:398
  (16 other events, 51.2 us)
